TPU v7x, 32 devices: a whole 2x2x4 slice. The times are simulated.
32 devices in a mesh: grp: 2 (over x), row: 8 (over z, y), col: 2 (over core).
Axes of the slice: x: 2, y: 2, z: 4, core: 2. Of those that a mesh axis runs over, the one named last changes fastest.
Arguments:
- pair_act: bfloat16 [352, 176, 128], P(('grp', 'row'), 'col'), parts along dimension 0, may hold values from -6 to 6
- chain_lengths: int32 [16], P('grp'), parts along dimension 0, may hold values from 1 to 44, 176 in all
- resolved: int32 [16], P('grp'), parts along dimension 0, may hold values from 22 to 44
- in_gain: float32 [128], replicated, may hold values from 0.1 to 1.9
- out_gain: float32 [128], replicated, may hold values from 0.1 to 1.9
- w_left: bfloat16 [128, 256], replicated, may hold values from -0.5 to 0.5
- w_right: bfloat16 [128, 256], replicated, may hold values from -0.5 to 0.5
- w_gate: bfloat16 [128, 128], replicated, may hold values from -0.5 to 0.5
- w_out: bfloat16 [128, 128], replicated, may hold values from -0.5 to 0.5
Outputs:
- update: bfloat16 [352, 176, 128], P(('grp', 'row'), 'col'), parts along dimension 0
There are 2 independent parts, one for each index of `grp`. A program takes and returns all parts, laid end to end along the dimension named above; an argument that names none is the same for every part. Nothing has to cross between parts.
Inputs may be any that keep to these rules, and one draw needn't show every extreme that they name: chain_lengths sum to 176; the longest chain has exactly 44 residues.
All inputs are finite; a program needn't handle non-finite values.
Results may differ from a plain program's by a relative error of at most 0.0079.
Values may be sent and summed in bfloat16 or wider, within the bound.
No kernel may reach another device: no remote copies, remote signals or barrier semaphores. Data moves between devices by JAX's collectives and lax.ppermute only.
A program may use at most 64 MiB of HBM per device.

v0:
```python
import jax
import jax.numpy as jnp
from jax import lax
from jax.sharding import PartitionSpec as P


def layer_norm(values, gain):
    mean = jnp.mean(values, axis=-1, keepdims=True)
    centred = values - mean
    variance = jnp.mean(centred * centred, axis=-1, keepdims=True)
    return centred * lax.rsqrt(variance + 1e-05) * gain


def valid_residues(chain_lengths, resolved, first, count):
    ends = jnp.cumsum(chain_lengths)
    starts = ends - chain_lengths
    position = first + jnp.arange(count, dtype=jnp.int32)
    inside = (position[:, None] >= starts[None, :]) & (position[:, None] < ends[None, :])
    kept = inside & (position[:, None] - starts[None, :] < resolved[None, :])
    return jnp.any(kept, axis=1).astype(jnp.float32)


def edges(normed, weight, mask, hidden):
    projected = jnp.einsum("ijc,cd->ijd", normed, weight, preferred_element_type=jnp.float32)
    return (
        mask[..., None] * jax.nn.sigmoid(projected[..., :hidden]) * projected[..., hidden:]
    ).astype(jnp.bfloat16)


def shards(pair_act, chain_lengths, resolved, in_gain, out_gain, w_left, w_right, w_gate, w_out):
    rows_here = pair_act.shape[0]
    cols_here = pair_act.shape[1]
    hidden = w_out.shape[0]
    row_first = lax.axis_index("row") * rows_here
    col_first = lax.axis_index("col") * cols_here
    valid_rows = valid_residues(chain_lengths, resolved, row_first, rows_here)
    valid_cols = valid_residues(chain_lengths, resolved, col_first, cols_here)
    mask = valid_rows[:, None] * valid_cols[None, :]
    normed = layer_norm(pair_act.astype(jnp.float32), in_gain).astype(jnp.bfloat16)
    left_edge = edges(normed, w_left, mask, hidden)
    right_edge = edges(normed, w_right, mask, hidden)
    gate_values = jax.nn.sigmoid(
        jnp.einsum("ijc,cd->ijd", normed, w_gate, preferred_element_type=jnp.float32)
    )
    n_rows = lax.axis_size("row")
    n_cols = lax.axis_size("col")
    per_dev = hidden // (n_rows * n_cols)
    total = rows_here * n_rows
    left_first = jnp.transpose(left_edge, (2, 0, 1))
    right_first = jnp.transpose(right_edge, (2, 0, 1))
    left_got, right_got = (
        lax.all_to_all(left_first, ("row", "col"), split_axis=0, concat_axis=0, tiled=True),
        lax.all_to_all(right_first, ("row", "col"), split_axis=0, concat_axis=0, tiled=True),
    )

    def arrange(received):
        blocks = received.reshape(n_rows, n_cols, per_dev, rows_here, cols_here)
        return jnp.transpose(blocks, (2, 0, 3, 1, 4)).reshape(per_dev, total, total)

    left_full = arrange(left_got)
    right_full = arrange(right_got)
    channel_prod = jnp.einsum(
        "cik,cjk->cij", left_full, right_full, preferred_element_type=jnp.float32
    )
    outgoing = channel_prod.reshape(per_dev, n_rows, rows_here, n_cols, cols_here)
    outgoing = jnp.transpose(outgoing, (1, 3, 0, 2, 4)).reshape(
        n_rows * n_cols * per_dev, rows_here, cols_here
    )
    returned = lax.all_to_all(outgoing, ("row", "col"), split_axis=0, concat_axis=0, tiled=True)
    product = jnp.transpose(returned, (1, 2, 0))
    normed_out = layer_norm(product, out_gain).astype(jnp.bfloat16)
    projected = jnp.einsum("ijc,cd->ijd", normed_out, w_out, preferred_element_type=jnp.float32)
    return (gate_values * projected).astype(jnp.bfloat16)


def solution(mesh):
    return jax.shard_map(
        shards,
        mesh=mesh,
        in_specs=(P(("grp", "row"), "col", None), P("grp"), P("grp"), P(), P(), P(), P(), P(), P()),
        out_specs=P(("grp", "row"), "col", None),
        check_vma=False,
    )
```

profile of v0, /device:TPU:15, one launch (start us, length us, event | category | flops | bytes accessed | tf_op | source)
XLA Modules:
  0.0 110.4 jit_solution(1638733292883919318)
XLA Ops:
  0.0 0.0 copy-start
  0.0 0.9 reduce-window.8
  0.9 0.7 bitcast_subtract_fusion.1
  1.5 0.7 fusion.32
  2.3 0.7 fusion.34
  3.0 1.3 %convert_reduce_fusion = f32[22,88]{1,0:T(8,128)S(1)} fusion(bf16[22,88,128]{2,1,0:T(8,128)(2,1)} %param.9), kind=kLoop, calls=%fused_computation.11 | loop fusion | flops 493680 | bytes 503360 | tf_op jit(solution)/shard_map/reduce_sum | solution.py:8
  4.4 0.0 copy-start.1
  4.4 0.0 copy-start.3
  4.4 0.0 copy-start.5
  4.4 1.8 %fusion.6 = f32[22,88]{1,0:T(8,128)S(1)} fusion(bf16[22,88,128]{2,1,0:T(8,128)(2,1)} %param.9, f32[22,88]{1,0:T(8,128)S(1)} %broadcast_multiply_fusion.2), kind=kLoop, calls=%fused_computation.14 | loop fusion | flops 989296 | bytes 511104 | tf_op jit(solution)/shard_map/reduce_sum | solution.py:10
  6.2 0.0 copy-done
  6.2 1.8 %fusion.22 = f32[22,88,256]{2,1,0:T(8,128)S(1)} fusion(bf16[22,88,128]{2,1,0:T(8,128)(2,1)} %param.9, f32[128]{0:T(128)} %param.12, f32[22,88]{1,0:T(8,128)S(1)} %add_rsqrt_fusion.1, f32[22,88]{1,0:T(8,128)S(1)} %broadcast_multiply_fusion.2, bf16[128,256]{1,0:T(8,128)(2,1)S(1)} %copy-done), kind=kOutput, calls=%fused_computation.34 | convolution fusion | flops 128116736 | bytes 2559616 | tf_op jit(solution)/shard_map/ijc,cd->ijd/dot_general | solution.py:24
  8.0 0.0 copy-done.1
  8.0 0.0 copy-done.3
  8.0 0.0 copy-done.5
  8.0 1.0 fusion.24
  9.0 0.1 broadcast_multiply_fusion
  9.1 0.6 fusion.21
  9.6 1.3 %copy.28 = bf16[128,22,88]{2,1,0:T(8,128)(2,1)} copy(bf16[128,22,88]{0,2,1:T(8,128)(2,1)S(1)} %get-tuple-element.6) | data formatting | bytes 991232 | tf_op jit(solution)/shard_map/transpose | solution.py:49
  10.9 6.6 %all-to-all-start = ((bf16[128,22,88]{2,1,0:T(8,128)(2,1)}), bf16[128,22,88]{2,1,0:T(8,128)(2,1)S(1)}, u32[]{:S(2)}, u32[]{:S(2)}) async-start(bf16[128,22,88]{2,1,0:T(8,128)(2,1)} %copy.28), calls=%async_computation | async-start | bytes 1572864 | tf_op jit(solution)/shard_map/all_to_all | solution.py:52
  17.5 1.3 %copy.31 = bf16[128,22,88]{2,1,0:T(8,128)(2,1)} copy(bf16[128,22,88]{0,2,1:T(8,128)(2,1)S(1)} %get-tuple-element.5) | data formatting | bytes 991232 | tf_op jit(solution)/shard_map/transpose | solution.py:50
  18.7 18.0 %all-to-all-done = bf16[128,22,88]{2,1,0:T(8,128)(2,1)S(1)} async-done(((bf16[128,22,88]{2,1,0:T(8,128)(2,1)}), bf16[128,22,88]{2,1,0:T(8,128)(2,1)S(1)}, u32[]{:S(2)}, u32[]{:S(2)}) %all-to-all-start) | async-done | bytes 495648 | tf_op jit(solution)/shard_map/all_to_all | solution.py:52
  36.7 5.0 %all-to-all-start.1 = ((bf16[128,22,88]{2,1,0:T(8,128)(2,1)}), bf16[128,22,88]{2,1,0:T(8,128)(2,1)S(1)}, u32[]{:S(2)}, u32[]{:S(2)}) async-start(bf16[128,22,88]{2,1,0:T(8,128)(2,1)} %copy.31), calls=%async_computation.1 | async-start | bytes 1572864 | tf_op jit(solution)/shard_map/all_to_all | solution.py:53
  41.7 0.7 copy.30
  42.4 1.3 %reshape.113 = bf16[8,176,176]{2,1,0:T(8,128)(2,1)} reshape(bf16[8,8,22,2,88]{4,3,2,1,0:T(2,128)(2,1)S(1)} %copy.30) | data formatting | bytes 991232 | tf_op jit(solution)/shard_map/reshape | solution.py:58
  43.7 0.0 copy-start.2
  43.7 17.2 %all-to-all-done.1 = bf16[128,22,88]{2,1,0:T(8,128)(2,1)S(1)} async-done(((bf16[128,22,88]{2,1,0:T(8,128)(2,1)}), bf16[128,22,88]{2,1,0:T(8,128)(2,1)S(1)}, u32[]{:S(2)}, u32[]{:S(2)}) %all-to-all-start.1) | async-done | bytes 495648 | tf_op jit(solution)/shard_map/all_to_all | solution.py:53
  60.9 0.7 copy.33
  61.7 1.3 %reshape.115 = bf16[8,176,176]{2,1,0:T(8,128)(2,1)} reshape(bf16[8,8,22,2,88]{4,3,2,1,0:T(2,128)(2,1)S(1)} %copy.33) | data formatting | bytes 991232 | tf_op jit(solution)/shard_map/reshape | solution.py:58
  62.9 0.0 copy-done.2
  62.9 1.5 %fusion.35 = f32[8,176,176]{2,1,0:T(8,128)S(1)} fusion(bf16[8,176,176]{2,1,0:T(8,128)(2,1)S(1)} %copy-done.2, bf16[8,176,176]{2,1,0:T(8,128)(2,1)} %reshape.115), kind=kOutput, calls=%fused_computation.54 | convolution fusion | flops 87228416 | bytes 1982464 | tf_op jit(solution)/shard_map/cik,cjk->cij/dot_general | solution.py:62
  64.4 0.9 reshape.116
  65.4 1.3 %copy.39 = f32[8,8,22,2,88]{4,2,0,3,1:T(8,128)} copy(f32[8,8,22,2,88]{4,3,2,1,0:T(2,128)S(1)} %reshape.116) | data formatting | bytes 1982464 | tf_op jit(solution)/shard_map/reshape | solution.py:66
  66.7 0.0 copy-start.7
  66.7 5.1 %all-to-all-start.2 = ((f32[128,22,88]{2,1,0:T(8,128)}), f32[128,22,88]{2,1,0:T(8,128)S(1)}, u32[]{:S(2)}, u32[]{:S(2)}) async-start(f32[128,22,88]{2,1,0:T(8,128)} %bitcast.37), calls=%async_computation.2 | async-start | bytes 3145728 | tf_op jit(solution)/shard_map/all_to_all | solution.py:69
  71.8 0.0 copy-done.7
  71.8 1.0 fusion.2
  72.8 0.0 copy-start.6
  72.8 35.2 %all-to-all-done.2 = f32[128,22,88]{2,1,0:T(8,128)S(1)} async-done(((f32[128,22,88]{2,1,0:T(8,128)}), f32[128,22,88]{2,1,0:T(8,128)S(1)}, u32[]{:S(2)}, u32[]{:S(2)}) %all-to-all-start.2) | async-done | bytes 991264 | tf_op jit(solution)/shard_map/all_to_all | solution.py:69
  108.0 0.2 bitcast_reduce_fusion
  108.1 0.3 multiply_reduce_fusion
  108.4 0.0 copy-start.4
  108.4 0.0 copy-done.6
  108.4 0.3 multiply_convert_fusion
  108.7 0.5 copy-done.4
  109.2 1.2 %fusion.3 = bf16[22,88,128]{2,1,0:T(8,128)(2,1)} fusion(f32[22,88,128]{2,1,0:T(8,128)S(1)} %fusion.2, bf16[22,88,128]{1,0,2:T(8,128)(2,1)S(1)} %multiply_convert_fusion, bf16[128,128]{1,0:T(8,128)(2,1)S(1)} %copy-done.4), kind=kOutput, calls=%fused_computation.9 | convolution fusion | flops 63934464 | bytes 2015232 | tf_op jit(solution)/shard_map/ijc,cd->ijd/dot_general | solution.py:72
  (8 shorter events, 0.0 us)
Async XLA Ops:
  0.0 6.2 %copy-start = (bf16[128,256]{1,0:T(8,128)(2,1)S(1)}, bf16[128,256]{1,0:T(8,128)(2,1)}, u32[]{:S(2)}) copy-start(bf16[128,256]{1,0:T(8,128)(2,1)} %param.15) | copy-start | bytes 196612
  4.4 3.7 %copy-start.1 = (bf16[22,88,128]{2,1,0:T(8,128)(2,1)S(1)}, bf16[22,88,128]{2,1,0:T(8,128)(2,1)}, u32[]{:S(2)}) copy-start(bf16[22,88,128]{2,1,0:T(8,128)(2,1)} %param.9) | copy-start | bytes 1486852
  4.4 3.6 %copy-start.3 = (bf16[128,256]{1,0:T(8,128)(2,1)S(1)}, bf16[128,256]{1,0:T(8,128)(2,1)}, u32[]{:S(2)}) copy-start(bf16[128,256]{1,0:T(8,128)(2,1)} %param.14) | copy-start | bytes 196612
  4.4 3.6 %copy-start.5 = (f32[128]{0:T(128)S(1)}, f32[128]{0:T(128)}, u32[]{:S(2)}) copy-start(f32[128]{0:T(128)} %param.12) | copy-start | bytes 1540
  10.9 25.8 %all-to-all-start = ((bf16[128,22,88]{2,1,0:T(8,128)(2,1)}), bf16[128,22,88]{2,1,0:T(8,128)(2,1)S(1)}, u32[]{:S(2)}, u32[]{:S(2)}) async-start(bf16[128,22,88]{2,1,0:T(8,128)(2,1)} %copy.28), calls=%async_computation | async-start | bytes 1572864 | tf_op jit(solution)/shard_map/all_to_all | solution.py:52
  36.7 24.2 %all-to-all-start.1 = ((bf16[128,22,88]{2,1,0:T(8,128)(2,1)}), bf16[128,22,88]{2,1,0:T(8,128)(2,1)S(1)}, u32[]{:S(2)}, u32[]{:S(2)}) async-start(bf16[128,22,88]{2,1,0:T(8,128)(2,1)} %copy.31), calls=%async_computation.1 | async-start | bytes 1572864 | tf_op jit(solution)/shard_map/all_to_all | solution.py:53
  43.7 19.2 %copy-start.2 = (bf16[8,176,176]{2,1,0:T(8,128)(2,1)S(1)}, bf16[8,176,176]{2,1,0:T(8,128)(2,1)}, u32[]{:S(2)}) copy-start(bf16[8,176,176]{2,1,0:T(8,128)(2,1)} %reshape.113) | copy-start | bytes 1486852
  66.7 5.1 %copy-start.7 = (bf16[128,128]{1,0:T(8,128)(2,1)S(1)}, bf16[128,128]{1,0:T(8,128)(2,1)}, u32[]{:S(2)}) copy-start(bf16[128,128]{1,0:T(8,128)(2,1)} %param.16) | copy-start | bytes 98308
  66.7 41.3 %all-to-all-start.2 = ((f32[128,22,88]{2,1,0:T(8,128)}), f32[128,22,88]{2,1,0:T(8,128)S(1)}, u32[]{:S(2)}, u32[]{:S(2)}) async-start(f32[128,22,88]{2,1,0:T(8,128)} %bitcast.37), calls=%async_computation.2 | async-start | bytes 3145728 | tf_op jit(solution)/shard_map/all_to_all | solution.py:69
  72.8 35.6 %copy-start.6 = (f32[128]{0:T(128)S(1)}, f32[128]{0:T(128)}, u32[]{:S(2)}) copy-start(f32[128]{0:T(128)} %param.13) | copy-start | bytes 1540
  108.4 0.8 copy-start.4
where the time goes:
time: 111 us; the launch traced here: 110 us
  waiting for transfers between devices  70.4 us (63%)
  starting transfers between devices  16.6 us (15%)
  local copies, waits for them, and re-layouts  9.34 us (8%)
  other arithmetic  7.49 us (7%)
  matrix products  6.43 us (6%)
    all_to_all x1, waiting for transfers between devices, shards(): lax.all_to_all(outgoing, ('row', 'col'), split_axis=0, concat_axis=0, til...  35.2 us
    all_to_all x1, waiting for transfers between devices, shards(): lax.all_to_all(left_first, ('row', 'col'), split_axis=0, concat_axis=0, t...  18 us
    all_to_all x1, waiting for transfers between devices, shards(): lax.all_to_all(right_first, ('row', 'col'), split_axis=0, concat_axis=0,...  17.2 us
    all_to_all x1, starting transfers between devices, shards(): lax.all_to_all(left_first, ('row', 'col'), split_axis=0, concat_axis=0, t...  6.55 us
    all_to_all x1, starting transfers between devices, shards(): lax.all_to_all(outgoing, ('row', 'col'), split_axis=0, concat_axis=0, til...  5.08 us
    all_to_all x1, starting transfers between devices, shards(): lax.all_to_all(right_first, ('row', 'col'), split_axis=0, concat_axis=0,...  4.95 us
    dot_general x2, matrix products, edges(): jnp.einsum('ijc,cd->ijd', normed, weight, preferred_element_type=jnp.floa...  2.72 us
    reshape x2, local copies, waits for them, and re-layouts, arrange(): return jnp.transpose(blocks, (2, 0, 3, 1, 4)).reshape(per_dev, total, total)  2.54 us
  transfers between devices with their start and end apart: 3, of which 3 were waited for; matrix products, arithmetic and copies ran while one was open for 4% of the time, Pallas kernels for 0%

commit v1 on v0

v1 whole, which is shorter than its diff:
```python
import functools

import jax
import jax.numpy as jnp
from jax import lax
from jax.experimental import pallas as pl
from jax.experimental.pallas import tpu as pltpu
from jax.sharding import PartitionSpec as P

EPS = 1e-05
LANES = 128
VMEM_LIMIT = 48 * 1024 * 1024


def ceil_to(n, m):
    return -(-n // m) * m


def edges_kernel(rows, cols, n_dev, chains, lens_ref, res_ref, first_ref, x_ref, gain_ref, wl_ref, wr_ref,
                 edge_ref, normed_ref):
    block = x_ref.shape[0]
    hidden = wl_ref.shape[1] // 2
    x = x_ref[...].astype(jnp.float32)
    mean = jnp.mean(x, axis=-1, keepdims=True)
    centred = x - mean
    variance = jnp.mean(centred * centred, axis=-1, keepdims=True)
    normed = (centred * lax.rsqrt(variance + EPS) * gain_ref[...]).astype(jnp.bfloat16)
    normed_ref[...] = normed
    position = pl.program_id(0) * block + lax.broadcasted_iota(jnp.int32, (8, block), 1)
    i_here = jnp.floor((position.astype(jnp.float32) + 0.5) * (1.0 / cols)).astype(jnp.int32)
    k_here = position - i_here * cols
    i_at = first_ref[0] + i_here
    k_at = first_ref[1] + k_here
    i_ok = jnp.zeros((8, block), jnp.float32)
    k_ok = jnp.zeros((8, block), jnp.float32)
    start = 0
    for q in range(chains):
        length = lens_ref[q]
        stop = start + jnp.minimum(length, res_ref[q])
        i_ok = jnp.where((i_at >= start) & (i_at < stop), 1.0, i_ok)
        k_ok = jnp.where((k_at >= start) & (k_at < stop), 1.0, k_ok)
        start = start + length
    mask = i_ok * k_ok
    parts = []
    for w_ref in (wl_ref, wr_ref):
        projected = lax.dot_general(
            w_ref[...], normed, (((0,), (1,)), ((), ())), preferred_element_type=jnp.float32
        )
        edge = jax.nn.sigmoid(projected[:hidden]) * projected[hidden:]
        parts.append(edge.reshape(n_dev, hidden // n_dev, block))
    both = jnp.concatenate(parts, axis=1)
    if both.shape[1] % 8 == 0:
        both = (both.reshape(-1, 8, block) * mask[None]).reshape(both.shape)
    else:
        both = both * mask[None, : 1]
    edge_ref[...] = both.astype(jnp.bfloat16)


def make_edges(pair, lens, resolved, first, gain, w_left, w_right, n_dev, rows, cols):
    count, channels = pair.shape
    hidden = w_left.shape[1] // 2
    per_dev = hidden // n_dev
    block = 512
    smem = pl.BlockSpec(memory_space=pltpu.SMEM)
    return pl.pallas_call(
        functools.partial(edges_kernel, rows, cols, n_dev, lens.shape[0]),
        grid=(pl.cdiv(count, block),),
        in_specs=[
            smem, smem, smem,
            pl.BlockSpec((block, channels), lambda b: (b, 0)),
            pl.BlockSpec((1, channels), lambda b: (0, 0)),
            pl.BlockSpec(w_left.shape, lambda b: (0, 0)),
            pl.BlockSpec(w_right.shape, lambda b: (0, 0)),
        ],
        out_specs=[
            pl.BlockSpec((n_dev, 2 * per_dev, block), lambda b: (0, 0, b)),
            pl.BlockSpec((block, channels), lambda b: (b, 0)),
        ],
        out_shape=[
            jax.ShapeDtypeStruct((n_dev, 2 * per_dev, count), jnp.bfloat16),
            jax.ShapeDtypeStruct((count, channels), jnp.bfloat16),
        ],
        compiler_params=pltpu.CompilerParams(vmem_limit_bytes=VMEM_LIMIT),
    )(lens, resolved, first, pair, gain, w_left, w_right)


def product_kernel(n_rows, n_cols, rows, cols, got_ref, out_ref, left_s, right_s, prod_s):
    ch = out_ref.shape[1]
    step = left_s.shape[1] // (n_rows * rows)
    total = n_rows * rows
    tiles = pl.cdiv(cols, LANES)
    flat = rows * cols
    lane = lax.broadcasted_iota(jnp.int32, (2 * ch, LANES), 1)
    lane_out = lax.broadcasted_iota(jnp.int32, (ch, LANES), 1)

    def unpack(r, carry):
        for c in range(n_cols):
            src = r * n_cols + c
            held = {}

            def tile_of(t):
                if t not in held:
                    width = min(LANES, flat - t * LANES)
                    got = got_ref[src, :, pl.ds(t * LANES, width)].astype(jnp.float32)
                    if width < LANES:
                        got = jnp.concatenate([got, jnp.zeros((2 * ch, LANES - width), jnp.float32)], axis=1)
                    held[t] = got
                return held[t]

            for i in range(rows):
                for tt in range(tiles):
                    at = cols * i + LANES * tt
                    length = min(LANES, cols - LANES * tt)
                    t0, off = divmod(at, LANES)
                    piece = tile_of(t0)
                    if off:
                        piece = pltpu.roll(piece, LANES - off, 1)
                    if off + length > LANES:
                        piece = jnp.where(lane < LANES - off, piece, pltpu.roll(tile_of(t0 + 1), LANES - off, 1))
                    if length < LANES:
                        piece = jnp.where(lane < length, piece, 0.0)
                    base = pl.multiple_of((r * rows + i) * step, 8)
                    left_s[c * tiles + tt, pl.ds(base, ch), :] = piece[:ch]
                    right_s[c * tiles + tt, pl.ds(base, ch), :] = piece[ch:]
        return carry

    lax.fori_loop(0, n_rows, unpack, 0)

    pad = tiles * LANES - cols
    for d in range(ch):
        left = jnp.concatenate(
            [left_s[t, pl.ds(d, total, stride=step), :] for t in range(n_cols * tiles)], axis=1
        ).astype(jnp.bfloat16)
        right = jnp.concatenate(
            [right_s[t, pl.ds(d, total, stride=step), :] for t in range(n_cols * tiles)], axis=1
        )
        pieces = []
        for c in range(n_cols):
            pieces.append(right[c * cols:(c + 1) * cols])
            if pad:
                pieces.append(jnp.zeros((pad, right.shape[1]), jnp.float32))
        right = jnp.concatenate(pieces, axis=0).astype(jnp.bfloat16)
        prod = lax.dot_general(left, right, (((1,), (1,)), ((), ())), preferred_element_type=jnp.float32)
        for t in range(n_cols * tiles):
            prod_s[t, pl.ds(d, total, stride=step), :] = prod[:, t * LANES:(t + 1) * LANES]

    def pack(r, carry):
        for c in range(n_cols):
            for t in range(pl.cdiv(flat, LANES)):
                tile = None
                for i in range(rows):
                    for tt in range(tiles):
                        shift = cols * i + LANES * tt - LANES * t
                        length = min(LANES, cols - LANES * tt)
                        if shift >= LANES or shift + length <= 0:
                            continue
                        base = pl.multiple_of((r * rows + i) * step, 8)
                        piece = prod_s[c * tiles + tt, pl.ds(base, ch), :]
                        if shift % LANES:
                            piece = pltpu.roll(piece, shift % LANES, 1)
                        tile = piece if tile is None else jnp.where(lane_out < shift, tile, piece)
                width = min(LANES, flat - t * LANES)
                out_ref[r * n_cols + c, :, pl.ds(t * LANES, width)] = tile[:, :width].astype(out_ref.dtype)
        return carry

    lax.fori_loop(0, n_rows, pack, 0)


def make_product(got, n_rows, n_cols, rows, cols):
    n_dev, both, flat = got.shape
    ch = both // 2
    step = ceil_to(ch, 8)
    tiles = n_cols * pl.cdiv(cols, LANES)
    held = pltpu.VMEM((tiles, n_rows * rows * step, LANES), jnp.float32)
    whole = pl.BlockSpec(memory_space=pltpu.VMEM)
    return pl.pallas_call(
        functools.partial(product_kernel, n_rows, n_cols, rows, cols),
        in_specs=[whole],
        out_specs=whole,
        out_shape=jax.ShapeDtypeStruct((n_dev, ch, flat), jnp.bfloat16),
        scratch_shapes=[held, held, held],
        compiler_params=pltpu.CompilerParams(vmem_limit_bytes=VMEM_LIMIT),
    )(got)


def update_kernel(prod_ref, gain_ref, w_ref, gate_ref, out_ref):
    prod = prod_ref[...].astype(jnp.float32).reshape(-1, prod_ref.shape[2])
    mean = jnp.mean(prod, axis=0, keepdims=True)
    centred = prod - mean
    variance = jnp.mean(centred * centred, axis=0, keepdims=True)
    normed = (centred * lax.rsqrt(variance + EPS) * gain_ref[...]).astype(jnp.bfloat16)
    projected = lax.dot_general(normed, w_ref[...], (((0,), (0,)), ((), ())), preferred_element_type=jnp.float32)
    out_ref[...] = (gate_ref[...] * projected).astype(out_ref.dtype)


def make_update(prod, gain, w_out, gate):
    n_dev, ch, count = prod.shape
    channels = w_out.shape[1]
    block = 512
    return pl.pallas_call(
        update_kernel,
        grid=(pl.cdiv(count, block),),
        in_specs=[
            pl.BlockSpec((n_dev, ch, block), lambda b: (0, 0, b)),
            pl.BlockSpec((n_dev * ch, 1), lambda b: (0, 0)),
            pl.BlockSpec(w_out.shape, lambda b: (0, 0)),
            pl.BlockSpec((block, channels), lambda b: (b, 0)),
        ],
        out_specs=pl.BlockSpec((block, channels), lambda b: (b, 0)),
        out_shape=jax.ShapeDtypeStruct((count, channels), jnp.bfloat16),
        compiler_params=pltpu.CompilerParams(vmem_limit_bytes=VMEM_LIMIT),
    )(prod, gain, w_out, gate)


def shards(pair_act, chain_lengths, resolved, in_gain, out_gain, w_left, w_right, w_gate, w_out):
    rows, cols, channels = pair_act.shape
    hidden = w_out.shape[0]
    n_rows = lax.axis_size("row")
    n_cols = lax.axis_size("col")
    n_dev = n_rows * n_cols
    first = jnp.stack([lax.axis_index("row") * rows, lax.axis_index("col") * cols]).astype(jnp.int32)
    edges, normed = make_edges(
        pair_act.reshape(rows * cols, channels), chain_lengths, resolved, first,
        in_gain.reshape(1, channels), w_left, w_right, n_dev, rows, cols,
    )
    got = lax.all_to_all(edges, ("row", "col"), split_axis=0, concat_axis=0, tiled=True)
    gate = jax.nn.sigmoid(jnp.dot(normed, w_gate, preferred_element_type=jnp.float32))
    outgoing = make_product(got, n_rows, n_cols, rows, cols)
    returned = lax.all_to_all(outgoing, ("row", "col"), split_axis=0, concat_axis=0, tiled=True)
    update = make_update(returned, out_gain.reshape(hidden, 1), w_out, gate)
    return update.reshape(rows, cols, channels)


def solution(mesh):
    return jax.shard_map(
        shards,
        mesh=mesh,
        in_specs=(P(("grp", "row"), "col", None), P("grp"), P("grp"), P(), P(), P(), P(), P(), P()),
        out_specs=P(("grp", "row"), "col", None),
        check_vma=False,
    )
```

time: 111 us -> 64.3 us (0.58)
  the two profiles are of different devices: /device:TPU:15 before, /device:TPU:0 now
where the time goes in v1:
time: 64.3 us; the launch traced here: 63.8 us
  blocking collectives  32 us (50%)
  waiting for transfers between devices  13.3 us (21%)
  Pallas kernels  8.81 us (14%)
  starting transfers between devices  4.99 us (8%)
  local copies, waits for them, and re-layouts  4.17 us (6%)
    all_to_all x1, blocking collectives, shards(): lax.all_to_all(edges, ('row', 'col'), split_axis=0, concat_axis=0, tiled=...  32 us
    all_to_all x1, waiting for transfers between devices, shards(): lax.all_to_all(outgoing, ('row', 'col'), split_axis=0, concat_axis=0, til...  13.3 us
    all_to_all x1, starting transfers between devices, shards(): lax.all_to_all(outgoing, ('row', 'col'), split_axis=0, concat_axis=0, til...  4.99 us
    unnamed x18, local copies, waits for them, and re-layouts  4.05 us
    pallas_call x1, Pallas kernels, make_product(): pl.pallas_call(functools.partial(product_kernel, n_rows, n_cols, rows, co...  3.44 us
    pallas_call x1, Pallas kernels, make_edges(): pl.pallas_call(functools.partial(edges_kernel, rows, cols, n_dev, lens.sh...  3.11 us
    pallas_call x1, Pallas kernels, make_update(): pl.pallas_call(update_kernel, grid=(pl.cdiv(count, block),), in_specs=[pl...  2.25 us
  transfers between devices with their start and end apart: 1, of which 1 were waited for; matrix products, arithmetic and copies ran while one was open for 1% of the time, Pallas kernels for 0%

profile of v1, /device:TPU:0, one launch (start us, length us, event | category | flops | bytes accessed | tf_op | source)
XLA Modules:
  0.0 63.8 jit_solution(2832848115325009286)
XLA Ops:
  0.0 0.0 copy-start
  0.0 0.1 pad_add_fusion.first_ref
  0.1 0.0 copy-start.5
  0.1 0.0 copy-start.6
  0.1 0.0 copy-start.7
  0.1 0.6 %copy-done.5 = s32[8]{0:T(128)S(1)} copy-done((s32[8]{0:T(128)S(1)}, s32[8]{0:T(128)}, u32[]{:S(2)}) %copy-start.5) | copy-done | bytes 56
  0.7 0.0 copy-done.6
  0.8 0.0 copy-done.7
  0.8 0.0 copy-start.1
  0.8 1.0 %copy-done.1 = bf16[22,88,128]{2,1,0:T(8,128)(2,1)S(1)} copy-done((bf16[22,88,128]{2,1,0:T(8,128)(2,1)S(1)}, bf16[22,88,128]{2,1,0:T(8,128)(2,1)}, u32[]{:S(2)}) %copy-start.1) | copy-done | bytes 495640
  1.8 0.0 copy-start.2
  1.8 0.8 %copy-done.2 = bf16[128,256]{1,0:T(8,128)(2,1)S(1)} copy-done((bf16[128,256]{1,0:T(8,128)(2,1)S(1)}, bf16[128,256]{1,0:T(8,128)(2,1)}, u32[]{:S(2)}) %copy-start.2) | copy-done | bytes 65560
  2.6 0.0 copy-start.3
  2.6 0.8 %copy-done.3 = bf16[128,256]{1,0:T(8,128)(2,1)S(1)} copy-done((bf16[128,256]{1,0:T(8,128)(2,1)S(1)}, bf16[128,256]{1,0:T(8,128)(2,1)}, u32[]{:S(2)}) %copy-start.3) | copy-done | bytes 65560
  3.5 3.1 %shard_map.91 = (bf16[16,16,1936]{2,1,0:T(8,128)(2,1)S(1)}, bf16[1936,128]{1,0:T(8,128)(2,1)S(1)}) custom-call(s32[8]{0:T(128)S(1)} %copy-done.5, s32[8]{0:T(128)S(1)} %copy-done.6, s32[2]{0:T(128)S(1)} %pad_add_fusion.first_ref, bf16[1936,128]{1,0:T(8,128)(2,1)S(1)} %bitcast.8, f32[1,128]{1,0:T(1,128)S(1)} %bitcast.9, bf16[128,256]{1,0:T(8,128)(2,1)S(1)} %copy-done.2, ...), custom_call_target="tpu_custom_call" | custom-call | tf_op jit(solution)/shard_map/pallas_call | solution.py:65
  6.6 32.0 %all_to_all.10.got_ref = bf16[16,16,1936]{2,1,0:T(8,128)(2,1)S(1)} all-to-all(bf16[16,16,1936]{2,1,0:T(8,128)(2,1)S(1)} %get-tuple-element.7), channel_id=1, replica_groups=mesh['grp'=2,'row'=8,'col'=2] {'row','col'}, dimensions={0} | all-to-all | bytes 1982464 | tf_op jit(solution)/shard_map/all_to_all | solution.py:226
  38.6 3.4 %shard_map.92 = bf16[16,8,1936]{2,1,0:T(8,128)(2,1)} custom-call(bf16[16,16,1936]{2,1,0:T(8,128)(2,1)S(1)} %all_to_all.10.got_ref), custom_call_target="tpu_custom_call" | custom-call | tf_op jit(solution)/shard_map/pallas_call | solution.py:176
  42.1 5.0 %all-to-all-start.1 = ((bf16[16,8,1936]{2,1,0:T(8,128)(2,1)}), bf16[16,8,1936]{2,1,0:T(8,128)(2,1)S(1)}, u32[]{:S(2)}, u32[]{:S(2)}) async-start(bf16[16,8,1936]{2,1,0:T(8,128)(2,1)} %shard_map.92), calls=%async_computation.1 | async-start | bytes 1048576 | tf_op jit(solution)/shard_map/all_to_all | solution.py:229
  47.1 0.0 copy-start.8
  47.1 0.6 %copy-done.8 = f32[128]{0:T(128)S(1)} copy-done((f32[128]{0:T(128)S(1)}, f32[128]{0:T(128)}, u32[]{:S(2)}) %copy-start.8) | copy-done | bytes 536
  47.7 0.1 copy.10.gain_ref
  47.8 0.0 copy-done
  47.8 0.0 copy-start.4
  47.9 0.4 fusion.2.gate_ref
  48.3 13.3 %all-to-all-done.1.prod_ref = bf16[16,8,1936]{2,1,0:T(8,128)(2,1)S(1)} async-done(((bf16[16,8,1936]{2,1,0:T(8,128)(2,1)}), bf16[16,8,1936]{2,1,0:T(8,128)(2,1)S(1)}, u32[]{:S(2)}, u32[]{:S(2)}) %all-to-all-start.1) | async-done | bytes 495648 | tf_op jit(solution)/shard_map/all_to_all | solution.py:229
  61.5 0.0 copy-done.4
  61.5 2.3 %shard_map.93 = bf16[1936,128]{1,0:T(8,128)(2,1)} custom-call(bf16[16,8,1936]{2,1,0:T(8,128)(2,1)S(1)} %all-to-all-done.1.prod_ref, f32[128,1]{1,0:T(8,128)S(1)} %copy.10.gain_ref, bf16[128,128]{1,0:T(8,128)(2,1)S(1)} %copy-done.4, f32[1936,128]{1,0:T(8,128)S(1)} %fusion.2.gate_ref), custom_call_target="tpu_custom_call" | custom-call | tf_op jit(solution)/shard_map/pallas_call | solution.py:200
Async XLA Ops:
  0.0 47.8 %copy-start = (bf16[128,128]{1,0:T(8,128)(2,1)S(1)}, bf16[128,128]{1,0:T(8,128)(2,1)}, u32[]{:S(2)}) copy-start(bf16[128,128]{1,0:T(8,128)(2,1)} %param.16) | copy-start | bytes 98308
  0.1 0.7 %copy-start.5 = (s32[8]{0:T(128)S(1)}, s32[8]{0:T(128)}, u32[]{:S(2)}) copy-start(s32[8]{0:T(128)} %lens_ref.1) | copy-start | bytes 100
  0.1 0.7 %copy-start.6 = (s32[8]{0:T(128)S(1)}, s32[8]{0:T(128)}, u32[]{:S(2)}) copy-start(s32[8]{0:T(128)} %res_ref.1) | copy-start | bytes 100
  0.1 0.7 %copy-start.7 = (f32[128]{0:T(128)S(1)}, f32[128]{0:T(128)}, u32[]{:S(2)}) copy-start(f32[128]{0:T(128)} %param.12) | copy-start | bytes 1540
  0.8 1.0 %copy-start.1 = (bf16[22,88,128]{2,1,0:T(8,128)(2,1)S(1)}, bf16[22,88,128]{2,1,0:T(8,128)(2,1)}, u32[]{:S(2)}) copy-start(bf16[22,88,128]{2,1,0:T(8,128)(2,1)} %param.9) | copy-start | bytes 1486852
  1.8 0.8 %copy-start.2 = (bf16[128,256]{1,0:T(8,128)(2,1)S(1)}, bf16[128,256]{1,0:T(8,128)(2,1)}, u32[]{:S(2)}) copy-start(bf16[128,256]{1,0:T(8,128)(2,1)} %wl_ref.1) | copy-start | bytes 196612
  2.6 0.8 %copy-start.3 = (bf16[128,256]{1,0:T(8,128)(2,1)S(1)}, bf16[128,256]{1,0:T(8,128)(2,1)}, u32[]{:S(2)}) copy-start(bf16[128,256]{1,0:T(8,128)(2,1)} %wr_ref.1) | copy-start | bytes 196612
  42.1 19.5 %all-to-all-start.1 = ((bf16[16,8,1936]{2,1,0:T(8,128)(2,1)}), bf16[16,8,1936]{2,1,0:T(8,128)(2,1)S(1)}, u32[]{:S(2)}, u32[]{:S(2)}) async-start(bf16[16,8,1936]{2,1,0:T(8,128)(2,1)} %shard_map.92), calls=%async_computation.1 | async-start | bytes 1048576 | tf_op jit(solution)/shard_map/all_to_all | solution.py:229
  47.1 0.7 %copy-start.8 = (f32[128]{0:T(128)S(1)}, f32[128]{0:T(128)}, u32[]{:S(2)}) copy-start(f32[128]{0:T(128)} %param.13) | copy-start | bytes 1540
  47.8 13.7 %copy-start.4 = (bf16[128,128]{1,0:T(8,128)(2,1)S(1)}, bf16[128,128]{1,0:T(8,128)(2,1)}, u32[]{:S(2)}) copy-start(bf16[128,128]{1,0:T(8,128)(2,1)} %w_ref.1) | copy-start | bytes 98308

commit v2 on v1

--- a/solution.py
+++ b/solution.py
@@ -9,7 +9,8 @@
 
 EPS = 1e-05
 LANES = 128
-VMEM_LIMIT = 48 * 1024 * 1024
+VMEM_LIMIT = 32 * 1024 * 1024
+VMEM_FIRST = 60 * 1024 * 1024
 
 
 def ceil_to(n, m):
@@ -17,7 +18,8 @@
 
 
 def edges_kernel(rows, cols, n_dev, chains, lens_ref, res_ref, first_ref, x_ref, gain_ref, wl_ref, wr_ref,
-                 edge_ref, normed_ref):
+                 normed_ref, *refs):
+    edge_refs, held = refs[:n_dev], refs[n_dev]
     block = x_ref.shape[0]
     hidden = wl_ref.shape[1] // 2
     x = x_ref[...].astype(jnp.float32)
@@ -53,7 +55,9 @@
         both = (both.reshape(-1, 8, block) * mask[None]).reshape(both.shape)
     else:
         both = both * mask[None, : 1]
-    edge_ref[...] = both.astype(jnp.bfloat16)
+    held[...] = both.astype(jnp.bfloat16)
+    for s in range(n_dev):
+        edge_refs[s][...] = held[jnp.bitwise_xor(first_ref[2], s)]
 
 
 def make_edges(pair, lens, resolved, first, gain, w_left, w_right, n_dev, rows, cols):
@@ -72,20 +76,20 @@
             pl.BlockSpec(w_left.shape, lambda b: (0, 0)),
             pl.BlockSpec(w_right.shape, lambda b: (0, 0)),
         ],
-        out_specs=[
-            pl.BlockSpec((n_dev, 2 * per_dev, block), lambda b: (0, 0, b)),
-            pl.BlockSpec((block, channels), lambda b: (b, 0)),
-        ],
-        out_shape=[
-            jax.ShapeDtypeStruct((n_dev, 2 * per_dev, count), jnp.bfloat16),
-            jax.ShapeDtypeStruct((count, channels), jnp.bfloat16),
-        ],
-        compiler_params=pltpu.CompilerParams(vmem_limit_bytes=VMEM_LIMIT),
+        out_specs=[pl.BlockSpec((block, channels), lambda b: (b, 0))]
+        + [pl.BlockSpec((2 * per_dev, block), lambda b: (0, b))] * n_dev,
+        out_shape=[jax.ShapeDtypeStruct((count, channels), jnp.bfloat16)]
+        + [jax.ShapeDtypeStruct((2 * per_dev, count), jnp.bfloat16)] * n_dev,
+        scratch_shapes=[pltpu.VMEM((n_dev, 2 * per_dev, block), jnp.bfloat16)],
+        compiler_params=pltpu.CompilerParams(vmem_limit_bytes=VMEM_FIRST),
     )(lens, resolved, first, pair, gain, w_left, w_right)
 
 
-def product_kernel(n_rows, n_cols, rows, cols, got_ref, out_ref, left_s, right_s, prod_s):
-    ch = out_ref.shape[1]
+def product_kernel(n_rows, n_cols, rows, cols, me_ref, *refs):
+    n_dev = n_rows * n_cols
+    got_refs, out_refs = refs[:n_dev], refs[n_dev:2 * n_dev]
+    left_s, right_s, prod_s = refs[2 * n_dev:]
+    ch = out_refs[0].shape[0]
     step = left_s.shape[1] // (n_rows * rows)
     total = n_rows * rows
     tiles = pl.cdiv(cols, LANES)
@@ -93,15 +97,17 @@
     lane = lax.broadcasted_iota(jnp.int32, (2 * ch, LANES), 1)
     lane_out = lax.broadcasted_iota(jnp.int32, (ch, LANES), 1)
 
-    def unpack(r, carry):
-        for c in range(n_cols):
-            src = r * n_cols + c
+    for s in range(n_dev):
+        src = jnp.bitwise_xor(me_ref[2], s)
+        r, c = src // n_cols, lax.rem(src, n_cols)
+        got_ref = got_refs[s]
+        if True:
             held = {}
 
             def tile_of(t):
                 if t not in held:
                     width = min(LANES, flat - t * LANES)
-                    got = got_ref[src, :, pl.ds(t * LANES, width)].astype(jnp.float32)
+                    got = got_ref[:, pl.ds(t * LANES, width)].astype(jnp.float32)
                     if width < LANES:
                         got = jnp.concatenate([got, jnp.zeros((2 * ch, LANES - width), jnp.float32)], axis=1)
                     held[t] = got
@@ -122,9 +128,6 @@
                     base = pl.multiple_of((r * rows + i) * step, 8)
                     left_s[c * tiles + tt, pl.ds(base, ch), :] = piece[:ch]
                     right_s[c * tiles + tt, pl.ds(base, ch), :] = piece[ch:]
-        return carry
-
-    lax.fori_loop(0, n_rows, unpack, 0)
 
     pad = tiles * LANES - cols
     for d in range(ch):
@@ -144,8 +147,10 @@
         for t in range(n_cols * tiles):
             prod_s[t, pl.ds(d, total, stride=step), :] = prod[:, t * LANES:(t + 1) * LANES]
 
-    def pack(r, carry):
-        for c in range(n_cols):
+    for s in range(n_dev):
+        dst = jnp.bitwise_xor(me_ref[2], s)
+        r, c = dst // n_cols, lax.rem(dst, n_cols)
+        if True:
             for t in range(pl.cdiv(flat, LANES)):
                 tile = None
                 for i in range(rows):
@@ -160,14 +165,12 @@
                             piece = pltpu.roll(piece, shift % LANES, 1)
                         tile = piece if tile is None else jnp.where(lane_out < shift, tile, piece)
                 width = min(LANES, flat - t * LANES)
-                out_ref[r * n_cols + c, :, pl.ds(t * LANES, width)] = tile[:, :width].astype(out_ref.dtype)
-        return carry
-
-    lax.fori_loop(0, n_rows, pack, 0)
-
-
-def make_product(got, n_rows, n_cols, rows, cols):
-    n_dev, both, flat = got.shape
+                out_refs[s][:, pl.ds(t * LANES, width)] = tile[:, :width].astype(jnp.bfloat16)
+
+
+def make_product(got, first, n_rows, n_cols, rows, cols):
+    n_dev = len(got)
+    both, flat = got[0].shape
     ch = both // 2
     step = ceil_to(ch, 8)
     tiles = n_cols * pl.cdiv(cols, LANES)
@@ -175,16 +178,19 @@
     whole = pl.BlockSpec(memory_space=pltpu.VMEM)
     return pl.pallas_call(
         functools.partial(product_kernel, n_rows, n_cols, rows, cols),
-        in_specs=[whole],
-        out_specs=whole,
-        out_shape=jax.ShapeDtypeStruct((n_dev, ch, flat), jnp.bfloat16),
+        in_specs=[pl.BlockSpec(memory_space=pltpu.SMEM)] + [whole] * n_dev,
+        out_specs=[whole] * n_dev,
+        out_shape=[jax.ShapeDtypeStruct((ch, flat), jnp.bfloat16)] * n_dev,
         scratch_shapes=[held, held, held],
         compiler_params=pltpu.CompilerParams(vmem_limit_bytes=VMEM_LIMIT),
-    )(got)
-
-
-def update_kernel(prod_ref, gain_ref, w_ref, gate_ref, out_ref):
-    prod = prod_ref[...].astype(jnp.float32).reshape(-1, prod_ref.shape[2])
+    )(first, *got)
+
+
+def update_kernel(n_dev, first_ref, gain_ref, w_ref, gate_ref, *refs):
+    prod_refs, out_ref, held = refs[:n_dev], refs[n_dev], refs[n_dev + 1]
+    for s in range(n_dev):
+        held[jnp.bitwise_xor(first_ref[2], s)] = prod_refs[s][...].astype(jnp.float32)
+    prod = held[...].reshape(-1, held.shape[2])
     mean = jnp.mean(prod, axis=0, keepdims=True)
     centred = prod - mean
     variance = jnp.mean(centred * centred, axis=0, keepdims=True)
@@ -193,23 +199,33 @@
     out_ref[...] = (gate_ref[...] * projected).astype(out_ref.dtype)
 
 
-def make_update(prod, gain, w_out, gate):
-    n_dev, ch, count = prod.shape
+def make_update(prods, first, gain, w_out, gate):
+    n_dev = len(prods)
+    ch, count = prods[0].shape
     channels = w_out.shape[1]
     block = 512
     return pl.pallas_call(
-        update_kernel,
+        functools.partial(update_kernel, n_dev),
         grid=(pl.cdiv(count, block),),
         in_specs=[
-            pl.BlockSpec((n_dev, ch, block), lambda b: (0, 0, b)),
+            pl.BlockSpec(memory_space=pltpu.SMEM),
             pl.BlockSpec((n_dev * ch, 1), lambda b: (0, 0)),
             pl.BlockSpec(w_out.shape, lambda b: (0, 0)),
             pl.BlockSpec((block, channels), lambda b: (b, 0)),
-        ],
+        ]
+        + [pl.BlockSpec((ch, block), lambda b: (0, b))] * n_dev,
         out_specs=pl.BlockSpec((block, channels), lambda b: (b, 0)),
         out_shape=jax.ShapeDtypeStruct((count, channels), jnp.bfloat16),
+        scratch_shapes=[pltpu.VMEM((n_dev, ch, block), jnp.float32)],
         compiler_params=pltpu.CompilerParams(vmem_limit_bytes=VMEM_LIMIT),
-    )(prod, gain, w_out, gate)
+    )(first, gain, w_out, gate, *prods)
+
+
+def exchange(blocks):
+    n_dev = len(blocks)
+    return [blocks[0]] + [
+        lax.ppermute(blocks[s], ("row", "col"), [(d, d ^ s) for d in range(n_dev)]) for s in range(1, n_dev)
+    ]
 
 
 def shards(pair_act, chain_lengths, resolved, in_gain, out_gain, w_left, w_right, w_gate, w_out):
@@ -218,16 +234,17 @@
     n_rows = lax.axis_size("row")
     n_cols = lax.axis_size("col")
     n_dev = n_rows * n_cols
-    first = jnp.stack([lax.axis_index("row") * rows, lax.axis_index("col") * cols]).astype(jnp.int32)
-    edges, normed = make_edges(
+    row, col = lax.axis_index("row"), lax.axis_index("col")
+    first = jnp.stack([row * rows, col * cols, row * n_cols + col]).astype(jnp.int32)
+    normed, *edges = make_edges(
         pair_act.reshape(rows * cols, channels), chain_lengths, resolved, first,
         in_gain.reshape(1, channels), w_left, w_right, n_dev, rows, cols,
     )
-    got = lax.all_to_all(edges, ("row", "col"), split_axis=0, concat_axis=0, tiled=True)
+    got = exchange(edges)
     gate = jax.nn.sigmoid(jnp.dot(normed, w_gate, preferred_element_type=jnp.float32))
-    outgoing = make_product(got, n_rows, n_cols, rows, cols)
-    returned = lax.all_to_all(outgoing, ("row", "col"), split_axis=0, concat_axis=0, tiled=True)
-    update = make_update(returned, out_gain.reshape(hidden, 1), w_out, gate)
+    outgoing = make_product(got, first, n_rows, n_cols, rows, cols)
+    returned = exchange(outgoing)
+    update = make_update(returned, first, out_gain.reshape(hidden, 1), w_out, gate)
     return update.reshape(rows, cols, channels)
 
 

time: 64.3 us -> 72.6 us (1.13)
  starting transfers between devices: 4.99 us -> 49.1 us
  blocking collectives: 32 us -> 0 us
  local copies, waits for them, and re-layouts: 4.17 us -> 1.62 us
  waiting for transfers between devices: 13.3 us -> 11.1 us
    ppermute x0 -> x30, starting transfers between devices: none -> 49.1 us  [exchange(): lax.ppermute(blocks[s], ('row', 'col'), [(d, d ^ s) for d in range(n_dev)])]
    all_to_all x1 -> x0, blocking collectives: 32 us -> none  [shards(): lax.all_to_all(edges, ('row', 'col'), split_axis=0, concat_axis=0, tiled=...]
    all_to_all x1 -> x0, waiting for transfers between devices: 13.3 us -> none  [shards(): lax.all_to_all(outgoing, ('row', 'col'), split_axis=0, concat_axis=0, til...]
    ppermute x0 -> x30, waiting for transfers between devices: none -> 11.1 us  [exchange(): lax.ppermute(blocks[s], ('row', 'col'), [(d, d ^ s) for d in range(n_dev)])]
    all_to_all x1 -> x0, starting transfers between devices: 4.99 us -> none  [shards(): lax.all_to_all(outgoing, ('row', 'col'), split_axis=0, concat_axis=0, til...]
    unnamed x18 -> x12, local copies, waits for them, and re-layouts: 4.05 us -> 1.51 us
    pallas_call x1, Pallas kernels: 3.11 us -> 4.49 us  [make_edges(): pl.pallas_call(functools.partial(edges_kernel, rows, cols, n_dev, lens.sh...]
    pallas_call x1, Pallas kernels: 3.44 us -> 2.18 us  [make_product(): pl.pallas_call(functools.partial(product_kernel, n_rows, n_cols, rows, co...]
  transfers between devices with their start and end apart: 1 -> 30, of which waited for: 1 -> 5; matrix products, arithmetic and copies ran while one was open for 1% -> 1% of each run, Pallas kernels for 0% -> 0%
where the time goes in v2:
time: 72.6 us; the launch traced here: 72.4 us
  starting transfers between devices  49.1 us (68%)
  waiting for transfers between devices  11.1 us (15%)
  Pallas kernels  9.48 us (13%)
  local copies, waits for them, and re-layouts  1.62 us (2%)
    ppermute x30, starting transfers between devices, exchange(): lax.ppermute(blocks[s], ('row', 'col'), [(d, d ^ s) for d in range(n_dev)])  49.1 us
    ppermute x30, waiting for transfers between devices, exchange(): lax.ppermute(blocks[s], ('row', 'col'), [(d, d ^ s) for d in range(n_dev)])  11.1 us
    pallas_call x1, Pallas kernels, make_edges(): pl.pallas_call(functools.partial(edges_kernel, rows, cols, n_dev, lens.sh...  4.49 us
    pallas_call x1, Pallas kernels, make_update(): pl.pallas_call(functools.partial(update_kernel, n_dev), grid=(pl.cdiv(cou...  2.82 us
    pallas_call x1, Pallas kernels, make_product(): pl.pallas_call(functools.partial(product_kernel, n_rows, n_cols, rows, co...  2.18 us
    unnamed x12, local copies, waits for them, and re-layouts  1.51 us
  transfers between devices with their start and end apart: 30, of which 5 were waited for; matrix products, arithmetic and copies ran while one was open for 1% of the time, Pallas kernels for 0%

profile of v2, /device:TPU:0, one launch (start us, length us, event | category | flops | bytes accessed | tf_op | source)
XLA Modules:
  0.0 72.4 jit_solution(6651882201980771987)
XLA Ops:
  0.0 0.6 pad_add_fusion.first_ref.me_ref
  0.6 4.5 %shard_map.91 = (bf16[1936,128]{1,0:T(8,128)(2,1)}, bf16[16,1936]{1,0:T(8,128)(2,1)}, bf16[16,1936]{1,0:T(8,128)(2,1)}, bf16[16,1936]{1,0:T(8,128)(2,1)}, bf16[1...) custom-call(s32[8]{0:T(128)} %lens_ref.1, ...), custom_call_target="tpu_custom_call" | custom-call | tf_op jit(solution)/shard_map/pallas_call | solution.py:69
  5.1 0.5 collective-permute-start
  5.6 2.6 %collective-permute-start.1 = (bf16[16,1936]{1,0:T(8,128)(2,1)}, bf16[16,1936]{1,0:T(8,128)(2,1)S(1)}, u32[]{:S(2)}, u32[]{:S(2)}) collective-permute-start(bf16[16,1936]{1,0:T(8,128)(2,1)} %get-tuple-element.41), channel_id=1, source_target_pairs={{0,2},{1,3},{2,0},{3,1},{4,6},{5,7},{6,4},{7,5},{8,10},{9,11},{10,... | collective-permute-start | bytes 185864 | tf_op jit(solution)/shard_map/ppermute | solution.py:227
  8.2 2.3 %collective-permute-start.10 = (bf16[16,1936]{1,0:T(8,128)(2,1)}, bf16[16,1936]{1,0:T(8,128)(2,1)S(1)}, u32[]{:S(2)}, u32[]{:S(2)}) collective-permute-start(bf16[16,1936]{1,0:T(8,128)(2,1)} %get-tuple-element.50), channel_id=1, source_target_pairs={{0,11},{1,10},{2,9},{3,8},{4,15},{5,14},{6,13},{7,12},{8,3},{9,2},... | collective-permute-start | bytes 185864 | tf_op jit(solution)/shard_map/ppermute | solution.py:227
  10.5 1.3 %collective-permute-start.11 = (bf16[16,1936]{1,0:T(8,128)(2,1)}, bf16[16,1936]{1,0:T(8,128)(2,1)S(1)}, u32[]{:S(2)}, u32[]{:S(2)}) collective-permute-start(bf16[16,1936]{1,0:T(8,128)(2,1)} %get-tuple-element.51), channel_id=1, source_target_pairs={{0,12},{1,13},{2,14},{3,15},{4,8},{5,9},{6,10},{7,11},{8,4},{9,5},... | collective-permute-start | bytes 185864 | tf_op jit(solution)/shard_map/ppermute | solution.py:227
  11.9 2.1 %collective-permute-start.12 = (bf16[16,1936]{1,0:T(8,128)(2,1)}, bf16[16,1936]{1,0:T(8,128)(2,1)S(1)}, u32[]{:S(2)}, u32[]{:S(2)}) collective-permute-start(bf16[16,1936]{1,0:T(8,128)(2,1)} %get-tuple-element.52), channel_id=1, source_target_pairs={{0,13},{1,12},{2,15},{3,14},{4,9},{5,8},{6,11},{7,10},{8,5},{9,4},... | collective-permute-start | bytes 185864 | tf_op jit(solution)/shard_map/ppermute | solution.py:227
  14.0 0.0 collective-permute-done.refs_1_
  14.0 2.3 %collective-permute-start.13 = (bf16[16,1936]{1,0:T(8,128)(2,1)}, bf16[16,1936]{1,0:T(8,128)(2,1)S(1)}, u32[]{:S(2)}, u32[]{:S(2)}) collective-permute-start(bf16[16,1936]{1,0:T(8,128)(2,1)} %get-tuple-element.53), channel_id=1, source_target_pairs={{0,14},{1,15},{2,12},{3,13},{4,10},{5,11},{6,8},{7,9},{8,6},{9,7},... | collective-permute-start | bytes 185864 | tf_op jit(solution)/shard_map/ppermute | solution.py:227
  16.3 2.2 %collective-permute-start.14 = (bf16[16,1936]{1,0:T(8,128)(2,1)}, bf16[16,1936]{1,0:T(8,128)(2,1)S(1)}, u32[]{:S(2)}, u32[]{:S(2)}) collective-permute-start(bf16[16,1936]{1,0:T(8,128)(2,1)} %get-tuple-element.54), channel_id=1, source_target_pairs={{0,15},{1,14},{2,13},{3,12},{4,11},{5,10},{6,9},{7,8},{8,7},{9,6},... | collective-permute-start | bytes 185864 | tf_op jit(solution)/shard_map/ppermute | solution.py:227
  18.5 1.5 %collective-permute-start.2 = (bf16[16,1936]{1,0:T(8,128)(2,1)}, bf16[16,1936]{1,0:T(8,128)(2,1)S(1)}, u32[]{:S(2)}, u32[]{:S(2)}) collective-permute-start(bf16[16,1936]{1,0:T(8,128)(2,1)} %get-tuple-element.42), channel_id=1, source_target_pairs={{0,3},{1,2},{2,1},{3,0},{4,7},{5,6},{6,5},{7,4},{8,11},{9,10},{10,... | collective-permute-start | bytes 185864 | tf_op jit(solution)/shard_map/ppermute | solution.py:227
  20.0 2.9 %collective-permute-start.3 = (bf16[16,1936]{1,0:T(8,128)(2,1)}, bf16[16,1936]{1,0:T(8,128)(2,1)S(1)}, u32[]{:S(2)}, u32[]{:S(2)}) collective-permute-start(bf16[16,1936]{1,0:T(8,128)(2,1)} %get-tuple-element.43), channel_id=1, source_target_pairs={{0,4},{1,5},{2,6},{3,7},{4,0},{5,1},{6,2},{7,3},{8,12},{9,13},{10,... | collective-permute-start | bytes 185864 | tf_op jit(solution)/shard_map/ppermute | solution.py:227
  22.9 1.1 %collective-permute-start.4 = (bf16[16,1936]{1,0:T(8,128)(2,1)}, bf16[16,1936]{1,0:T(8,128)(2,1)S(1)}, u32[]{:S(2)}, u32[]{:S(2)}) collective-permute-start(bf16[16,1936]{1,0:T(8,128)(2,1)} %get-tuple-element.44), channel_id=1, source_target_pairs={{0,5},{1,4},{2,7},{3,6},{4,1},{5,0},{6,3},{7,2},{8,13},{9,12},{10,... | collective-permute-start | bytes 185864 | tf_op jit(solution)/shard_map/ppermute | solution.py:227
  23.9 2.7 %collective-permute-start.5 = (bf16[16,1936]{1,0:T(8,128)(2,1)}, bf16[16,1936]{1,0:T(8,128)(2,1)S(1)}, u32[]{:S(2)}, u32[]{:S(2)}) collective-permute-start(bf16[16,1936]{1,0:T(8,128)(2,1)} %get-tuple-element.45), channel_id=1, source_target_pairs={{0,6},{1,7},{2,4},{3,5},{4,2},{5,3},{6,0},{7,1},{8,14},{9,15},{10,... | collective-permute-start | bytes 185864 | tf_op jit(solution)/shard_map/ppermute | solution.py:227
  26.6 0.0 collective-permute-done.14.refs_15_
  26.7 1.1 %collective-permute-start.6 = (bf16[16,1936]{1,0:T(8,128)(2,1)}, bf16[16,1936]{1,0:T(8,128)(2,1)S(1)}, u32[]{:S(2)}, u32[]{:S(2)}) collective-permute-start(bf16[16,1936]{1,0:T(8,128)(2,1)} %get-tuple-element.46), channel_id=1, source_target_pairs={{0,7},{1,6},{2,5},{3,4},{4,3},{5,2},{6,1},{7,0},{8,15},{9,14},{10,... | collective-permute-start | bytes 185864 | tf_op jit(solution)/shard_map/ppermute | solution.py:227
  27.7 0.0 collective-permute-done.2.refs_3_
  27.7 3.1 %collective-permute-start.7 = (bf16[16,1936]{1,0:T(8,128)(2,1)}, bf16[16,1936]{1,0:T(8,128)(2,1)S(1)}, u32[]{:S(2)}, u32[]{:S(2)}) collective-permute-start(bf16[16,1936]{1,0:T(8,128)(2,1)} %get-tuple-element.47), channel_id=1, source_target_pairs={{0,8},{1,9},{2,10},{3,11},{4,12},{5,13},{6,14},{7,15},{8,0},{9,1},... | collective-permute-start | bytes 185864 | tf_op jit(solution)/shard_map/ppermute | solution.py:227
  30.8 0.0 collective-permute-done.3.refs_4_
  30.8 0.4 collective-permute-start.8
  31.2 2.5 %collective-permute-start.9 = (bf16[16,1936]{1,0:T(8,128)(2,1)}, bf16[16,1936]{1,0:T(8,128)(2,1)S(1)}, u32[]{:S(2)}, u32[]{:S(2)}) collective-permute-start(bf16[16,1936]{1,0:T(8,128)(2,1)} %get-tuple-element.49), channel_id=1, source_target_pairs={{0,10},{1,11},{2,8},{3,9},{4,14},{5,15},{6,12},{7,13},{8,2},{9,3},... | collective-permute-start | bytes 185864 | tf_op jit(solution)/shard_map/ppermute | solution.py:227
  33.7 0.5 collective-permute-done.7.refs_8_
  34.2 5.3 %collective-permute-done.8.refs_9_ = bf16[16,1936]{1,0:T(8,128)(2,1)S(1)} collective-permute-done((bf16[16,1936]{1,0:T(8,128)(2,1)}, bf16[16,1936]{1,0:T(8,128)(2,1)S(1)}, u32[]{:S(2)}, u32[]{:S(2)}) %collective-permute-start.8) | collective-permute-done | bytes 61984 | tf_op jit(solution)/shard_map/ppermute | solution.py:227
  39.5 2.1 %collective-permute-done.9.refs_10_ = bf16[16,1936]{1,0:T(8,128)(2,1)S(1)} collective-permute-done((bf16[16,1936]{1,0:T(8,128)(2,1)}, bf16[16,1936]{1,0:T(8,128)(2,1)S(1)}, u32[]{:S(2)}, u32[]{:S(2)}) %collective-permute-start.9) | collective-permute-done | bytes 61984 | tf_op jit(solution)/shard_map/ppermute | solution.py:227
  41.7 0.8 %copy-done.1 = bf16[16,1936]{1,0:T(8,128)(2,1)S(1)} copy-done((bf16[16,1936]{1,0:T(8,128)(2,1)S(1)}, bf16[16,1936]{1,0:T(8,128)(2,1)}, u32[]{:S(2)}) %copy-start.1) | copy-done | bytes 61976
  42.5 2.2 %shard_map.92 = (bf16[8,1936]{1,0:T(8,128)(2,1)S(1)}, bf16[8,1936]{1,0:T(8,128)(2,1)S(1)}, bf16[8,1936]{1,0:T(8,128)(2,1)S(1)}, bf16[8,1936]{1,0:T(8,128)(2,1)S(...) custom-call(s32[3]{0:T(128)S(1)} %copy-done.3, ...), custom_call_target="tpu_custom_call" | custom-call | tf_op jit(solution)/shard_map/pallas_call | solution.py:179
  44.7 0.1 collective-permute-start.15
  44.8 0.8 %collective-permute-start.16 = (bf16[8,1936]{1,0:T(8,128)(2,1)S(1)}, bf16[8,1936]{1,0:T(8,128)(2,1)S(1)}, u32[]{:S(2)}, u32[]{:S(2)}) collective-permute-start(bf16[8,1936]{1,0:T(8,128)(2,1)S(1)} %get-tuple-element.57), channel_id=1, source_target_pairs={{0,2},{1,3},{2,0},{3,1},{4,6},{5,7},{6,4},{7,5},{8,10},{9,11},{10,... | collective-permute-start | bytes 92936 | tf_op jit(solution)/shard_map/ppermute | solution.py:227
  45.6 1.0 %collective-permute-start.17 = (bf16[8,1936]{1,0:T(8,128)(2,1)S(1)}, bf16[8,1936]{1,0:T(8,128)(2,1)S(1)}, u32[]{:S(2)}, u32[]{:S(2)}) collective-permute-start(bf16[8,1936]{1,0:T(8,128)(2,1)S(1)} %get-tuple-element.58), channel_id=1, source_target_pairs={{0,3},{1,2},{2,1},{3,0},{4,7},{5,6},{6,5},{7,4},{8,11},{9,10},{10,... | collective-permute-start | bytes 92936 | tf_op jit(solution)/shard_map/ppermute | solution.py:227
  46.6 1.7 %collective-permute-start.19 = (bf16[8,1936]{1,0:T(8,128)(2,1)S(1)}, bf16[8,1936]{1,0:T(8,128)(2,1)S(1)}, u32[]{:S(2)}, u32[]{:S(2)}) collective-permute-start(bf16[8,1936]{1,0:T(8,128)(2,1)S(1)} %get-tuple-element.60), channel_id=1, source_target_pairs={{0,5},{1,4},{2,7},{3,6},{4,1},{5,0},{6,3},{7,2},{8,13},{9,12},{10,... | collective-permute-start | bytes 92936 | tf_op jit(solution)/shard_map/ppermute | solution.py:227
  48.3 0.5 collective-permute-start.20
  48.9 0.0 collective-permute-done.16.refs_2_
  48.9 2.1 %collective-permute-start.21 = (bf16[8,1936]{1,0:T(8,128)(2,1)S(1)}, bf16[8,1936]{1,0:T(8,128)(2,1)S(1)}, u32[]{:S(2)}, u32[]{:S(2)}) collective-permute-start(bf16[8,1936]{1,0:T(8,128)(2,1)S(1)} %get-tuple-element.62), channel_id=1, source_target_pairs={{0,7},{1,6},{2,5},{3,4},{4,3},{5,2},{6,1},{7,0},{8,15},{9,14},{10,... | collective-permute-start | bytes 92936 | tf_op jit(solution)/shard_map/ppermute | solution.py:227
  51.0 1.3 %collective-permute-start.22 = (bf16[8,1936]{1,0:T(8,128)(2,1)S(1)}, bf16[8,1936]{1,0:T(8,128)(2,1)S(1)}, u32[]{:S(2)}, u32[]{:S(2)}) collective-permute-start(bf16[8,1936]{1,0:T(8,128)(2,1)S(1)} %get-tuple-element.63), channel_id=1, source_target_pairs={{0,8},{1,9},{2,10},{3,11},{4,12},{5,13},{6,14},{7,15},{8,0},{9,1},... | collective-permute-start | bytes 92936 | tf_op jit(solution)/shard_map/ppermute | solution.py:227
  52.4 1.2 %collective-permute-start.23 = (bf16[8,1936]{1,0:T(8,128)(2,1)S(1)}, bf16[8,1936]{1,0:T(8,128)(2,1)S(1)}, u32[]{:S(2)}, u32[]{:S(2)}) collective-permute-start(bf16[8,1936]{1,0:T(8,128)(2,1)S(1)} %get-tuple-element.64), channel_id=1, source_target_pairs={{0,9},{1,8},{2,11},{3,10},{4,13},{5,12},{6,15},{7,14},{8,1},{9,0},... | collective-permute-start | bytes 92936 | tf_op jit(solution)/shard_map/ppermute | solution.py:227
  53.6 2.1 %collective-permute-start.24 = (bf16[8,1936]{1,0:T(8,128)(2,1)S(1)}, bf16[8,1936]{1,0:T(8,128)(2,1)S(1)}, u32[]{:S(2)}, u32[]{:S(2)}) collective-permute-start(bf16[8,1936]{1,0:T(8,128)(2,1)S(1)} %get-tuple-element.65), channel_id=1, source_target_pairs={{0,10},{1,11},{2,8},{3,9},{4,14},{5,15},{6,12},{7,13},{8,2},{9,3},... | collective-permute-start | bytes 92936 | tf_op jit(solution)/shard_map/ppermute | solution.py:227
  55.7 1.5 %collective-permute-start.25 = (bf16[8,1936]{1,0:T(8,128)(2,1)S(1)}, bf16[8,1936]{1,0:T(8,128)(2,1)S(1)}, u32[]{:S(2)}, u32[]{:S(2)}) collective-permute-start(bf16[8,1936]{1,0:T(8,128)(2,1)S(1)} %get-tuple-element.66), channel_id=1, source_target_pairs={{0,11},{1,10},{2,9},{3,8},{4,15},{5,14},{6,13},{7,12},{8,3},{9,2},... | collective-permute-start | bytes 92936 | tf_op jit(solution)/shard_map/ppermute | solution.py:227
  57.2 2.8 %collective-permute-start.26 = (bf16[8,1936]{1,0:T(8,128)(2,1)S(1)}, bf16[8,1936]{1,0:T(8,128)(2,1)S(1)}, u32[]{:S(2)}, u32[]{:S(2)}) collective-permute-start(bf16[8,1936]{1,0:T(8,128)(2,1)S(1)} %get-tuple-element.67), channel_id=1, source_target_pairs={{0,12},{1,13},{2,14},{3,15},{4,8},{5,9},{6,10},{7,11},{8,4},{9,5},... | collective-permute-start | bytes 92936 | tf_op jit(solution)/shard_map/ppermute | solution.py:227
  60.0 0.7 collective-permute-start.27
  60.7 2.8 %collective-permute-start.28 = (bf16[8,1936]{1,0:T(8,128)(2,1)S(1)}, bf16[8,1936]{1,0:T(8,128)(2,1)S(1)}, u32[]{:S(2)}, u32[]{:S(2)}) collective-permute-start(bf16[8,1936]{1,0:T(8,128)(2,1)S(1)} %get-tuple-element.69), channel_id=1, source_target_pairs={{0,14},{1,15},{2,12},{3,13},{4,10},{5,11},{6,8},{7,9},{8,6},{9,7},... | collective-permute-start | bytes 92936 | tf_op jit(solution)/shard_map/ppermute | solution.py:227
  63.5 1.7 %collective-permute-start.29 = (bf16[8,1936]{1,0:T(8,128)(2,1)S(1)}, bf16[8,1936]{1,0:T(8,128)(2,1)S(1)}, u32[]{:S(2)}, u32[]{:S(2)}) collective-permute-start(bf16[8,1936]{1,0:T(8,128)(2,1)S(1)} %get-tuple-element.70), channel_id=1, source_target_pairs={{0,15},{1,14},{2,13},{3,12},{4,11},{5,10},{6,9},{7,8},{8,7},{9,6},... | collective-permute-start | bytes 92936 | tf_op jit(solution)/shard_map/ppermute | solution.py:227
  65.3 0.4 fusion.2.gate_ref
  65.7 0.0 copy-start.4
  65.7 0.6 copy-done.4
  66.3 0.1 copy.10.gain_ref
  66.5 0.9 %collective-permute-done.28.refs_14_ = bf16[8,1936]{1,0:T(8,128)(2,1)S(1)} collective-permute-done((bf16[8,1936]{1,0:T(8,128)(2,1)S(1)}, bf16[8,1936]{1,0:T(8,128)(2,1)S(1)}, u32[]{:S(2)}, u32[]{:S(2)}) %collective-permute-start.28) | collective-permute-done | bytes 31008 | tf_op jit(solution)/shard_map/ppermute | solution.py:227
  67.3 2.2 %collective-permute-done.29.refs_15_ = bf16[8,1936]{1,0:T(8,128)(2,1)S(1)} collective-permute-done((bf16[8,1936]{1,0:T(8,128)(2,1)S(1)}, bf16[8,1936]{1,0:T(8,128)(2,1)S(1)}, u32[]{:S(2)}, u32[]{:S(2)}) %collective-permute-start.29) | collective-permute-done | bytes 31008 | tf_op jit(solution)/shard_map/ppermute | solution.py:227
  69.6 2.8 %shard_map.93 = bf16[1936,128]{1,0:T(8,128)(2,1)} custom-call(s32[3]{0:T(128)S(1)} %copy-done.3, f32[128,1]{1,0:T(8,128)S(1)} %copy.10.gain_ref, bf16[128,128]{1,0:T(8,128)(2,1)S(1)} %copy-done.2, f32[1936,128]{1,0:T(8,128)S(1)} %fusion.2.gate_ref, bf16[8,1936]{1,0:T(8,128)(2,1)S(1)} %get-tuple-element.55.refs_0_, ...), custom_call_target="tpu_custom_call" | custom-call | tf_op jit(solution)/shard_map/pallas_call | solution.py:207
  (30 shorter events, 0.1 us)
Async XLA Ops:
  0.0 65.2 %copy-start = (bf16[128,128]{1,0:T(8,128)(2,1)S(1)}, bf16[128,128]{1,0:T(8,128)(2,1)}, u32[]{:S(2)}) copy-start(bf16[128,128]{1,0:T(8,128)(2,1)} %param.16) | copy-start | bytes 98308
  5.1 8.9 %collective-permute-start = (bf16[16,1936]{1,0:T(8,128)(2,1)}, bf16[16,1936]{1,0:T(8,128)(2,1)S(1)}, u32[]{:S(2)}, u32[]{:S(2)}) collective-permute-start(bf16[16,1936]{1,0:T(8,128)(2,1)} %get-tuple-element.40), channel_id=1, source_target_pairs={{0,1},{1,0},{2,3},{3,2},{4,5},{5,4},{6,7},{7,6},{8,9},{9,8},{10,11... | collective-permute-start | bytes 185864 | tf_op jit(solution)/shard_map/ppermute | solution.py:227
  5.6 10.7 %collective-permute-start.1 = (bf16[16,1936]{1,0:T(8,128)(2,1)}, bf16[16,1936]{1,0:T(8,128)(2,1)S(1)}, u32[]{:S(2)}, u32[]{:S(2)}) collective-permute-start(bf16[16,1936]{1,0:T(8,128)(2,1)} %get-tuple-element.41), channel_id=1, source_target_pairs={{0,2},{1,3},{2,0},{3,1},{4,6},{5,7},{6,4},{7,5},{8,10},{9,11},{10,... | collective-permute-start | bytes 185864 | tf_op jit(solution)/shard_map/ppermute | solution.py:227
  8.2 10.3 %collective-permute-start.10 = (bf16[16,1936]{1,0:T(8,128)(2,1)}, bf16[16,1936]{1,0:T(8,128)(2,1)S(1)}, u32[]{:S(2)}, u32[]{:S(2)}) collective-permute-start(bf16[16,1936]{1,0:T(8,128)(2,1)} %get-tuple-element.50), channel_id=1, source_target_pairs={{0,11},{1,10},{2,9},{3,8},{4,15},{5,14},{6,13},{7,12},{8,3},{9,2},... | collective-permute-start | bytes 185864 | tf_op jit(solution)/shard_map/ppermute | solution.py:227
  10.5 9.5 %collective-permute-start.11 = (bf16[16,1936]{1,0:T(8,128)(2,1)}, bf16[16,1936]{1,0:T(8,128)(2,1)S(1)}, u32[]{:S(2)}, u32[]{:S(2)}) collective-permute-start(bf16[16,1936]{1,0:T(8,128)(2,1)} %get-tuple-element.51), channel_id=1, source_target_pairs={{0,12},{1,13},{2,14},{3,15},{4,8},{5,9},{6,10},{7,11},{8,4},{9,5},... | collective-permute-start | bytes 185864 | tf_op jit(solution)/shard_map/ppermute | solution.py:227
  11.9 11.0 %collective-permute-start.12 = (bf16[16,1936]{1,0:T(8,128)(2,1)}, bf16[16,1936]{1,0:T(8,128)(2,1)S(1)}, u32[]{:S(2)}, u32[]{:S(2)}) collective-permute-start(bf16[16,1936]{1,0:T(8,128)(2,1)} %get-tuple-element.52), channel_id=1, source_target_pairs={{0,13},{1,12},{2,15},{3,14},{4,9},{5,8},{6,11},{7,10},{8,5},{9,4},... | collective-permute-start | bytes 185864 | tf_op jit(solution)/shard_map/ppermute | solution.py:227
  14.0 9.9 %collective-permute-start.13 = (bf16[16,1936]{1,0:T(8,128)(2,1)}, bf16[16,1936]{1,0:T(8,128)(2,1)S(1)}, u32[]{:S(2)}, u32[]{:S(2)}) collective-permute-start(bf16[16,1936]{1,0:T(8,128)(2,1)} %get-tuple-element.53), channel_id=1, source_target_pairs={{0,14},{1,15},{2,12},{3,13},{4,10},{5,11},{6,8},{7,9},{8,6},{9,7},... | collective-permute-start | bytes 185864 | tf_op jit(solution)/shard_map/ppermute | solution.py:227
  16.3 10.3 %collective-permute-start.14 = (bf16[16,1936]{1,0:T(8,128)(2,1)}, bf16[16,1936]{1,0:T(8,128)(2,1)S(1)}, u32[]{:S(2)}, u32[]{:S(2)}) collective-permute-start(bf16[16,1936]{1,0:T(8,128)(2,1)} %get-tuple-element.54), channel_id=1, source_target_pairs={{0,15},{1,14},{2,13},{3,12},{4,11},{5,10},{6,9},{7,8},{8,7},{9,6},... | collective-permute-start | bytes 185864 | tf_op jit(solution)/shard_map/ppermute | solution.py:227
  18.5 9.2 %collective-permute-start.2 = (bf16[16,1936]{1,0:T(8,128)(2,1)}, bf16[16,1936]{1,0:T(8,128)(2,1)S(1)}, u32[]{:S(2)}, u32[]{:S(2)}) collective-permute-start(bf16[16,1936]{1,0:T(8,128)(2,1)} %get-tuple-element.42), channel_id=1, source_target_pairs={{0,3},{1,2},{2,1},{3,0},{4,7},{5,6},{6,5},{7,4},{8,11},{9,10},{10,... | collective-permute-start | bytes 185864 | tf_op jit(solution)/shard_map/ppermute | solution.py:227
  20.0 10.8 %collective-permute-start.3 = (bf16[16,1936]{1,0:T(8,128)(2,1)}, bf16[16,1936]{1,0:T(8,128)(2,1)S(1)}, u32[]{:S(2)}, u32[]{:S(2)}) collective-permute-start(bf16[16,1936]{1,0:T(8,128)(2,1)} %get-tuple-element.43), channel_id=1, source_target_pairs={{0,4},{1,5},{2,6},{3,7},{4,0},{5,1},{6,2},{7,3},{8,12},{9,13},{10,... | collective-permute-start | bytes 185864 | tf_op jit(solution)/shard_map/ppermute | solution.py:227
  22.9 8.3 %collective-permute-start.4 = (bf16[16,1936]{1,0:T(8,128)(2,1)}, bf16[16,1936]{1,0:T(8,128)(2,1)S(1)}, u32[]{:S(2)}, u32[]{:S(2)}) collective-permute-start(bf16[16,1936]{1,0:T(8,128)(2,1)} %get-tuple-element.44), channel_id=1, source_target_pairs={{0,5},{1,4},{2,7},{3,6},{4,1},{5,0},{6,3},{7,2},{8,13},{9,12},{10,... | collective-permute-start | bytes 185864 | tf_op jit(solution)/shard_map/ppermute | solution.py:227
  23.9 9.8 %collective-permute-start.5 = (bf16[16,1936]{1,0:T(8,128)(2,1)}, bf16[16,1936]{1,0:T(8,128)(2,1)S(1)}, u32[]{:S(2)}, u32[]{:S(2)}) collective-permute-start(bf16[16,1936]{1,0:T(8,128)(2,1)} %get-tuple-element.45), channel_id=1, source_target_pairs={{0,6},{1,7},{2,4},{3,5},{4,2},{5,3},{6,0},{7,1},{8,14},{9,15},{10,... | collective-permute-start | bytes 185864 | tf_op jit(solution)/shard_map/ppermute | solution.py:227
  26.7 7.1 %collective-permute-start.6 = (bf16[16,1936]{1,0:T(8,128)(2,1)}, bf16[16,1936]{1,0:T(8,128)(2,1)S(1)}, u32[]{:S(2)}, u32[]{:S(2)}) collective-permute-start(bf16[16,1936]{1,0:T(8,128)(2,1)} %get-tuple-element.46), channel_id=1, source_target_pairs={{0,7},{1,6},{2,5},{3,4},{4,3},{5,2},{6,1},{7,0},{8,15},{9,14},{10,... | collective-permute-start | bytes 185864 | tf_op jit(solution)/shard_map/ppermute | solution.py:227
  27.7 6.5 %collective-permute-start.7 = (bf16[16,1936]{1,0:T(8,128)(2,1)}, bf16[16,1936]{1,0:T(8,128)(2,1)S(1)}, u32[]{:S(2)}, u32[]{:S(2)}) collective-permute-start(bf16[16,1936]{1,0:T(8,128)(2,1)} %get-tuple-element.47), channel_id=1, source_target_pairs={{0,8},{1,9},{2,10},{3,11},{4,12},{5,13},{6,14},{7,15},{8,0},{9,1},... | collective-permute-start | bytes 185864 | tf_op jit(solution)/shard_map/ppermute | solution.py:227
  30.8 8.7 %collective-permute-start.8 = (bf16[16,1936]{1,0:T(8,128)(2,1)}, bf16[16,1936]{1,0:T(8,128)(2,1)S(1)}, u32[]{:S(2)}, u32[]{:S(2)}) collective-permute-start(bf16[16,1936]{1,0:T(8,128)(2,1)} %get-tuple-element.48), channel_id=1, source_target_pairs={{0,9},{1,8},{2,11},{3,10},{4,13},{5,12},{6,15},{7,14},{8,1},{9,0},... | collective-permute-start | bytes 185864 | tf_op jit(solution)/shard_map/ppermute | solution.py:227
  31.2 10.5 %copy-start.3 = (s32[3]{0:T(128)S(1)}, s32[3]{0:T(128)}, u32[]{:S(2)}) copy-start(s32[3]{0:T(128)} %pad_add_fusion.first_ref.me_ref) | copy-start | bytes 40
  31.2 10.5 %collective-permute-start.9 = (bf16[16,1936]{1,0:T(8,128)(2,1)}, bf16[16,1936]{1,0:T(8,128)(2,1)S(1)}, u32[]{:S(2)}, u32[]{:S(2)}) collective-permute-start(bf16[16,1936]{1,0:T(8,128)(2,1)} %get-tuple-element.49), channel_id=1, source_target_pairs={{0,10},{1,11},{2,8},{3,9},{4,14},{5,15},{6,12},{7,13},{8,2},{9,3},... | collective-permute-start | bytes 185864 | tf_op jit(solution)/shard_map/ppermute | solution.py:227
  41.7 0.8 %copy-start.1 = (bf16[16,1936]{1,0:T(8,128)(2,1)S(1)}, bf16[16,1936]{1,0:T(8,128)(2,1)}, u32[]{:S(2)}) copy-start(bf16[16,1936]{1,0:T(8,128)(2,1)} %get-tuple-element.39.refs_0_) | copy-start | bytes 185860
  42.5 22.8 %copy-start.5 = (bf16[1936,128]{1,0:T(8,128)(2,1)S(1)}, bf16[1936,128]{1,0:T(8,128)(2,1)}, u32[]{:S(2)}) copy-start(bf16[1936,128]{1,0:T(8,128)(2,1)} %get-tuple-element.38) | copy-start | bytes 1486852
  44.7 3.6 %collective-permute-start.15 = (bf16[8,1936]{1,0:T(8,128)(2,1)S(1)}, bf16[8,1936]{1,0:T(8,128)(2,1)S(1)}, u32[]{:S(2)}, u32[]{:S(2)}) collective-permute-start(bf16[8,1936]{1,0:T(8,128)(2,1)S(1)} %get-tuple-element.56), channel_id=1, source_target_pairs={{0,1},{1,0},{2,3},{3,2},{4,5},{5,4},{6,7},{7,6},{8,9},{9,8},{10,11... | collective-permute-start | bytes 92936 | tf_op jit(solution)/shard_map/ppermute | solution.py:227
  44.8 4.1 %collective-permute-start.16 = (bf16[8,1936]{1,0:T(8,128)(2,1)S(1)}, bf16[8,1936]{1,0:T(8,128)(2,1)S(1)}, u32[]{:S(2)}, u32[]{:S(2)}) collective-permute-start(bf16[8,1936]{1,0:T(8,128)(2,1)S(1)} %get-tuple-element.57), channel_id=1, source_target_pairs={{0,2},{1,3},{2,0},{3,1},{4,6},{5,7},{6,4},{7,5},{8,10},{9,11},{10,... | collective-permute-start | bytes 92936 | tf_op jit(solution)/shard_map/ppermute | solution.py:227
  45.6 5.4 %collective-permute-start.17 = (bf16[8,1936]{1,0:T(8,128)(2,1)S(1)}, bf16[8,1936]{1,0:T(8,128)(2,1)S(1)}, u32[]{:S(2)}, u32[]{:S(2)}) collective-permute-start(bf16[8,1936]{1,0:T(8,128)(2,1)S(1)} %get-tuple-element.58), channel_id=1, source_target_pairs={{0,3},{1,2},{2,1},{3,0},{4,7},{5,6},{6,5},{7,4},{8,11},{9,10},{10,... | collective-permute-start | bytes 92936 | tf_op jit(solution)/shard_map/ppermute | solution.py:227
  46.6 5.8 %collective-permute-start.18 = (bf16[8,1936]{1,0:T(8,128)(2,1)S(1)}, bf16[8,1936]{1,0:T(8,128)(2,1)S(1)}, u32[]{:S(2)}, u32[]{:S(2)}) collective-permute-start(bf16[8,1936]{1,0:T(8,128)(2,1)S(1)} %get-tuple-element.59), channel_id=1, source_target_pairs={{0,4},{1,5},{2,6},{3,7},{4,0},{5,1},{6,2},{7,3},{8,12},{9,13},{10,... | collective-permute-start | bytes 92936 | tf_op jit(solution)/shard_map/ppermute | solution.py:227
  46.6 7.0 %collective-permute-start.19 = (bf16[8,1936]{1,0:T(8,128)(2,1)S(1)}, bf16[8,1936]{1,0:T(8,128)(2,1)S(1)}, u32[]{:S(2)}, u32[]{:S(2)}) collective-permute-start(bf16[8,1936]{1,0:T(8,128)(2,1)S(1)} %get-tuple-element.60), channel_id=1, source_target_pairs={{0,5},{1,4},{2,7},{3,6},{4,1},{5,0},{6,3},{7,2},{8,13},{9,12},{10,... | collective-permute-start | bytes 92936 | tf_op jit(solution)/shard_map/ppermute | solution.py:227
  48.3 7.4 %collective-permute-start.20 = (bf16[8,1936]{1,0:T(8,128)(2,1)S(1)}, bf16[8,1936]{1,0:T(8,128)(2,1)S(1)}, u32[]{:S(2)}, u32[]{:S(2)}) collective-permute-start(bf16[8,1936]{1,0:T(8,128)(2,1)S(1)} %get-tuple-element.61), channel_id=1, source_target_pairs={{0,6},{1,7},{2,4},{3,5},{4,2},{5,3},{6,0},{7,1},{8,14},{9,15},{10,... | collective-permute-start | bytes 92936 | tf_op jit(solution)/shard_map/ppermute | solution.py:227
  48.9 8.3 %collective-permute-start.21 = (bf16[8,1936]{1,0:T(8,128)(2,1)S(1)}, bf16[8,1936]{1,0:T(8,128)(2,1)S(1)}, u32[]{:S(2)}, u32[]{:S(2)}) collective-permute-start(bf16[8,1936]{1,0:T(8,128)(2,1)S(1)} %get-tuple-element.62), channel_id=1, source_target_pairs={{0,7},{1,6},{2,5},{3,4},{4,3},{5,2},{6,1},{7,0},{8,15},{9,14},{10,... | collective-permute-start | bytes 92936 | tf_op jit(solution)/shard_map/ppermute | solution.py:227
  51.0 9.0 %collective-permute-start.22 = (bf16[8,1936]{1,0:T(8,128)(2,1)S(1)}, bf16[8,1936]{1,0:T(8,128)(2,1)S(1)}, u32[]{:S(2)}, u32[]{:S(2)}) collective-permute-start(bf16[8,1936]{1,0:T(8,128)(2,1)S(1)} %get-tuple-element.63), channel_id=1, source_target_pairs={{0,8},{1,9},{2,10},{3,11},{4,12},{5,13},{6,14},{7,15},{8,0},{9,1},... | collective-permute-start | bytes 92936 | tf_op jit(solution)/shard_map/ppermute | solution.py:227
  52.4 8.3 %collective-permute-start.23 = (bf16[8,1936]{1,0:T(8,128)(2,1)S(1)}, bf16[8,1936]{1,0:T(8,128)(2,1)S(1)}, u32[]{:S(2)}, u32[]{:S(2)}) collective-permute-start(bf16[8,1936]{1,0:T(8,128)(2,1)S(1)} %get-tuple-element.64), channel_id=1, source_target_pairs={{0,9},{1,8},{2,11},{3,10},{4,13},{5,12},{6,15},{7,14},{8,1},{9,0},... | collective-permute-start | bytes 92936 | tf_op jit(solution)/shard_map/ppermute | solution.py:227
  53.6 9.9 %collective-permute-start.24 = (bf16[8,1936]{1,0:T(8,128)(2,1)S(1)}, bf16[8,1936]{1,0:T(8,128)(2,1)S(1)}, u32[]{:S(2)}, u32[]{:S(2)}) collective-permute-start(bf16[8,1936]{1,0:T(8,128)(2,1)S(1)} %get-tuple-element.65), channel_id=1, source_target_pairs={{0,10},{1,11},{2,8},{3,9},{4,14},{5,15},{6,12},{7,13},{8,2},{9,3},... | collective-permute-start | bytes 92936 | tf_op jit(solution)/shard_map/ppermute | solution.py:227
  55.7 10.7 %collective-permute-start.25 = (bf16[8,1936]{1,0:T(8,128)(2,1)S(1)}, bf16[8,1936]{1,0:T(8,128)(2,1)S(1)}, u32[]{:S(2)}, u32[]{:S(2)}) collective-permute-start(bf16[8,1936]{1,0:T(8,128)(2,1)S(1)} %get-tuple-element.66), channel_id=1, source_target_pairs={{0,11},{1,10},{2,9},{3,8},{4,15},{5,14},{6,13},{7,12},{8,3},{9,2},... | collective-permute-start | bytes 92936 | tf_op jit(solution)/shard_map/ppermute | solution.py:227
  57.2 9.2 %collective-permute-start.26 = (bf16[8,1936]{1,0:T(8,128)(2,1)S(1)}, bf16[8,1936]{1,0:T(8,128)(2,1)S(1)}, u32[]{:S(2)}, u32[]{:S(2)}) collective-permute-start(bf16[8,1936]{1,0:T(8,128)(2,1)S(1)} %get-tuple-element.67), channel_id=1, source_target_pairs={{0,12},{1,13},{2,14},{3,15},{4,8},{5,9},{6,10},{7,11},{8,4},{9,5},... | collective-permute-start | bytes 92936 | tf_op jit(solution)/shard_map/ppermute | solution.py:227
  60.0 6.4 %collective-permute-start.27 = (bf16[8,1936]{1,0:T(8,128)(2,1)S(1)}, bf16[8,1936]{1,0:T(8,128)(2,1)S(1)}, u32[]{:S(2)}, u32[]{:S(2)}) collective-permute-start(bf16[8,1936]{1,0:T(8,128)(2,1)S(1)} %get-tuple-element.68), channel_id=1, source_target_pairs={{0,13},{1,12},{2,15},{3,14},{4,9},{5,8},{6,11},{7,10},{8,5},{9,4},... | collective-permute-start | bytes 92936 | tf_op jit(solution)/shard_map/ppermute | solution.py:227
  60.7 6.6 %collective-permute-start.28 = (bf16[8,1936]{1,0:T(8,128)(2,1)S(1)}, bf16[8,1936]{1,0:T(8,128)(2,1)S(1)}, u32[]{:S(2)}, u32[]{:S(2)}) collective-permute-start(bf16[8,1936]{1,0:T(8,128)(2,1)S(1)} %get-tuple-element.69), channel_id=1, source_target_pairs={{0,14},{1,15},{2,12},{3,13},{4,10},{5,11},{6,8},{7,9},{8,6},{9,7},... | collective-permute-start | bytes 92936 | tf_op jit(solution)/shard_map/ppermute | solution.py:227
  63.5 6.0 %collective-permute-start.29 = (bf16[8,1936]{1,0:T(8,128)(2,1)S(1)}, bf16[8,1936]{1,0:T(8,128)(2,1)S(1)}, u32[]{:S(2)}, u32[]{:S(2)}) collective-permute-start(bf16[8,1936]{1,0:T(8,128)(2,1)S(1)} %get-tuple-element.70), channel_id=1, source_target_pairs={{0,15},{1,14},{2,13},{3,12},{4,11},{5,10},{6,9},{7,8},{8,7},{9,6},... | collective-permute-start | bytes 92936 | tf_op jit(solution)/shard_map/ppermute | solution.py:227
  65.7 0.7 copy-start.4
  66.3 3.2 %copy-start.2 = (bf16[128,128]{1,0:T(8,128)(2,1)S(1)}, bf16[128,128]{1,0:T(8,128)(2,1)}, u32[]{:S(2)}) copy-start(bf16[128,128]{1,0:T(8,128)(2,1)} %w_ref.1) | copy-start | bytes 98308

commit v3 on v2

v3 whole, which is shorter than its diff:
```python
import functools

import jax
import jax.numpy as jnp
from jax import lax
from jax.experimental import pallas as pl
from jax.experimental.pallas import tpu as pltpu
from jax.sharding import PartitionSpec as P

EPS = 1e-05
LANES = 128
VMEM_LIMIT = 32 * 1024 * 1024
VMEM_FIRST = 60 * 1024 * 1024


def ceil_to(n, m):
    return -(-n // m) * m


def edges_kernel(cols, groups, chains, lens_ref, res_ref, place_ref, x_ref, gain_ref, wl_ref, wr_ref,
                 normed_ref, *refs):
    both_refs, right_refs, held = refs[:groups], refs[groups:2 * groups], refs[2 * groups]
    block = x_ref.shape[0]
    hidden = wl_ref.shape[1] // 2
    x = x_ref[...].astype(jnp.float32)
    mean = jnp.mean(x, axis=-1, keepdims=True)
    centred = x - mean
    variance = jnp.mean(centred * centred, axis=-1, keepdims=True)
    normed = (centred * lax.rsqrt(variance + EPS) * gain_ref[...]).astype(jnp.bfloat16)
    normed_ref[...] = normed
    position = pl.program_id(0) * block + lax.broadcasted_iota(jnp.int32, (8, block), 1)
    i_here = jnp.floor((position.astype(jnp.float32) + 0.5) * (1.0 / cols)).astype(jnp.int32)
    k_here = position - i_here * cols
    i_at = place_ref[0] + i_here
    k_at = place_ref[1] + k_here
    i_ok = jnp.zeros((8, block), jnp.float32)
    k_ok = jnp.zeros((8, block), jnp.float32)
    start = 0
    for q in range(chains):
        length = lens_ref[q]
        stop = start + jnp.minimum(length, res_ref[q])
        i_ok = jnp.where((i_at >= start) & (i_at < stop), 1.0, i_ok)
        k_ok = jnp.where((k_at >= start) & (k_at < stop), 1.0, k_ok)
        start = start + length
    mask = i_ok * k_ok
    parts = []
    for w_ref in (wl_ref, wr_ref):
        projected = lax.dot_general(
            w_ref[...], normed, (((0,), (1,)), ((), ())), preferred_element_type=jnp.float32
        )
        edge = jax.nn.sigmoid(projected[:hidden]) * projected[hidden:]
        parts.append(edge.reshape(groups, hidden // groups, block))
    both = jnp.concatenate(parts, axis=1)
    held[...] = (both.reshape(-1, 8, block) * mask[None]).reshape(both.shape).astype(jnp.bfloat16)
    own = hidden // groups
    for u in range(groups):
        group = jnp.bitwise_xor(place_ref[2], u)
        both_refs[u][...] = held[group]
        right_refs[u][...] = held[group, own:]


def make_edges(pair, lens, resolved, place, gain, w_left, w_right, groups, cols):
    count, channels = pair.shape
    own = w_left.shape[1] // 2 // groups
    block = 512
    smem = pl.BlockSpec(memory_space=pltpu.SMEM)
    return pl.pallas_call(
        functools.partial(edges_kernel, cols, groups, lens.shape[0]),
        grid=(pl.cdiv(count, block),),
        in_specs=[
            smem, smem, smem,
            pl.BlockSpec((block, channels), lambda b: (b, 0)),
            pl.BlockSpec((1, channels), lambda b: (0, 0)),
            pl.BlockSpec(w_left.shape, lambda b: (0, 0)),
            pl.BlockSpec(w_right.shape, lambda b: (0, 0)),
        ],
        out_specs=[pl.BlockSpec((block, channels), lambda b: (b, 0))]
        + [pl.BlockSpec((2 * own, block), lambda b: (0, b))] * groups
        + [pl.BlockSpec((own, block), lambda b: (0, b))] * groups,
        out_shape=[jax.ShapeDtypeStruct((count, channels), jnp.bfloat16)]
        + [jax.ShapeDtypeStruct((2 * own, count), jnp.bfloat16)] * groups
        + [jax.ShapeDtypeStruct((own, count), jnp.bfloat16)] * groups,
        scratch_shapes=[pltpu.VMEM((groups, 2 * own, block), jnp.bfloat16)],
        compiler_params=pltpu.CompilerParams(vmem_limit_bytes=VMEM_FIRST),
    )(lens, resolved, place, pair, gain, w_left, w_right)


def unpack(got_ref, held_refs, block, rows, cols, step):
    tiles = pl.cdiv(cols, LANES)
    flat = rows * cols
    height = got_ref.shape[0]
    ch = height // len(held_refs)
    lane = lax.broadcasted_iota(jnp.int32, (height, LANES), 1)
    seen = {}

    def tile_of(t):
        if t not in seen:
            width = min(LANES, flat - t * LANES)
            got = got_ref[:, pl.ds(t * LANES, width)].astype(jnp.float32)
            if width < LANES:
                got = jnp.concatenate([got, jnp.zeros((height, LANES - width), jnp.float32)], axis=1)
            seen[t] = got
        return seen[t]

    for i in range(rows):
        for tt in range(tiles):
            length = min(LANES, cols - LANES * tt)
            t0, off = divmod(cols * i + LANES * tt, LANES)
            piece = tile_of(t0)
            if off:
                piece = pltpu.roll(piece, LANES - off, 1)
            if off + length > LANES:
                piece = jnp.where(lane < LANES - off, piece, pltpu.roll(tile_of(t0 + 1), LANES - off, 1))
            if length < LANES:
                piece = jnp.where(lane < length, piece, 0.0)
            base = pl.multiple_of((block * rows + i) * step, 8)
            for n, held in enumerate(held_refs):
                held[tt, pl.ds(base, ch), :] = piece[n * ch:(n + 1) * ch]


def pack(held, store, block, rows, cols, step, ch):
    tiles = pl.cdiv(cols, LANES)
    flat = rows * cols
    lane = lax.broadcasted_iota(jnp.int32, (ch, LANES), 1)
    for t in range(pl.cdiv(flat, LANES)):
        tile = None
        for i in range(rows):
            for tt in range(tiles):
                shift = cols * i + LANES * tt - LANES * t
                length = min(LANES, cols - LANES * tt)
                if shift >= LANES or shift + length <= 0:
                    continue
                base = pl.multiple_of((block * rows + i) * step, 8)
                piece = held[tt, pl.ds(base, ch), :]
                if shift % LANES:
                    piece = pltpu.roll(piece, shift % LANES, 1)
                tile = piece if tile is None else jnp.where(lane < shift, tile, piece)
        width = min(LANES, flat - t * LANES)
        store(t, width, tile[:, :width].astype(jnp.bfloat16))


def channel_of(held, d, count, step):
    lines = [held[t, pl.ds(d, count, stride=step), :] for t in range(held.shape[0])]
    return jnp.concatenate(lines, axis=1)


def multiply(left_ref, right_s, prod_s, ch, step):
    count = left_ref.shape[1]
    pad = right_s.shape[0] * LANES - count
    for d in range(ch):
        right = channel_of(right_s, d, count, step)
        if pad:
            right = jnp.concatenate([right, jnp.zeros((pad, right.shape[1]), jnp.float32)], axis=0)
        prod = lax.dot_general(
            left_ref[d], right.astype(jnp.bfloat16), (((1,), (1,)), ((), ())), preferred_element_type=jnp.float32
        )
        for t in range(prod_s.shape[0]):
            prod_s[t, pl.ds(d, count, stride=step), :] = prod[:, t * LANES:(t + 1) * LANES]


def near_kernel(groups, rows, cols, place_ref, *refs):
    got_refs = refs[:groups]
    left_ref, near_ref, left_s, right_s, prod_s = refs[groups:]
    ch = near_ref.shape[1]
    step = left_s.shape[1] // (groups * rows)
    for u in range(groups):
        unpack(got_refs[u], (left_s, right_s), jnp.bitwise_xor(place_ref[2], u), rows, cols, step)
    for d in range(ch):
        left_ref[d] = channel_of(left_s, d, groups * rows, step).astype(jnp.bfloat16)
    multiply(left_ref, right_s, prod_s, ch, step)
    for u in range(groups):
        def store(t, width, tile):
            near_ref[u, :, pl.ds(t * LANES, width)] = tile
        pack(prod_s, store, jnp.bitwise_xor(place_ref[2], u), rows, cols, step, ch)


def far_kernel(groups, rows, cols, place_ref, left_ref, near_ref, *refs):
    got_refs = refs[:groups]
    keep_ref, send_ref, right_s, prod_s, pair_s = refs[groups:]
    ch = near_ref.shape[1]
    step = right_s.shape[1] // (groups * rows)
    far_at = place_ref[3]
    pair_s[1 - far_at] = near_ref[...]
    for u in range(groups):
        unpack(got_refs[u], (right_s,), jnp.bitwise_xor(place_ref[2], u), rows, cols, step)
    multiply(left_ref, right_s, prod_s, ch, step)
    for u in range(groups):
        def store(t, width, tile):
            pair_s[far_at, u, :, pl.ds(t * LANES, width)] = tile
        pack(prod_s, store, jnp.bitwise_xor(place_ref[2], u), rows, cols, step, ch)
    keep_ref[...] = pair_s[0]
    send_ref[...] = pair_s[1]


def make_near(got, place, rows, cols):
    groups = len(got)
    both, flat = got[0].shape
    ch = both // 2
    count = groups * rows
    tiles = pl.cdiv(cols, LANES)
    held = pltpu.VMEM((tiles, count * ceil_to(ch, 8), LANES), jnp.float32)
    whole = pl.BlockSpec(memory_space=pltpu.VMEM)
    return pl.pallas_call(
        functools.partial(near_kernel, groups, rows, cols),
        in_specs=[pl.BlockSpec(memory_space=pltpu.SMEM)] + [whole] * groups,
        out_specs=[whole] * 2,
        out_shape=[
            jax.ShapeDtypeStruct((ch, count, tiles * LANES), jnp.bfloat16),
            jax.ShapeDtypeStruct((groups, ch, flat), jnp.bfloat16),
        ],
        scratch_shapes=[held, held, held],
        compiler_params=pltpu.CompilerParams(vmem_limit_bytes=VMEM_LIMIT),
    )(place, *got)


def make_far(got, place, left, near, rows, cols):
    groups = len(got)
    ch, flat = got[0].shape
    tiles = pl.cdiv(cols, LANES)
    held = pltpu.VMEM((tiles, groups * rows * ceil_to(ch, 8), LANES), jnp.float32)
    whole = pl.BlockSpec(memory_space=pltpu.VMEM)
    return pl.pallas_call(
        functools.partial(far_kernel, groups, rows, cols),
        in_specs=[pl.BlockSpec(memory_space=pltpu.SMEM)] + [whole] * (groups + 2),
        out_specs=[whole] * 2,
        out_shape=[jax.ShapeDtypeStruct((groups, ch, flat), jnp.bfloat16)] * 2,
        scratch_shapes=[held, held, pltpu.VMEM((2, groups, ch, flat), jnp.bfloat16)],
        compiler_params=pltpu.CompilerParams(vmem_limit_bytes=VMEM_LIMIT),
    )(place, left, near, *got)


def add_kernel(a_ref, b_ref, *out_refs):
    for u, out_ref in enumerate(out_refs):
        out_ref[...] = (a_ref[u].astype(jnp.float32) + b_ref[u].astype(jnp.float32)).astype(out_ref.dtype)


def make_sums(a, b):
    groups, ch, flat = a.shape
    whole = pl.BlockSpec(memory_space=pltpu.VMEM)
    return pl.pallas_call(
        add_kernel,
        in_specs=[whole] * 2,
        out_specs=[whole] * groups,
        out_shape=[jax.ShapeDtypeStruct((ch, flat), a.dtype)] * groups,
        compiler_params=pltpu.CompilerParams(vmem_limit_bytes=VMEM_LIMIT),
    )(a, b)


def update_kernel(n_dev, place_ref, gain_ref, w_ref, gate_ref, *refs):
    prod_refs, out_ref, held = refs[:n_dev], refs[n_dev], refs[n_dev + 1]
    for s in range(n_dev):
        held[jnp.bitwise_xor(place_ref[2], s)] = prod_refs[s][...].astype(jnp.float32)
    prod = held[...].reshape(-1, held.shape[2])
    mean = jnp.mean(prod, axis=0, keepdims=True)
    centred = prod - mean
    variance = jnp.mean(centred * centred, axis=0, keepdims=True)
    normed = (centred * lax.rsqrt(variance + EPS) * gain_ref[...]).astype(jnp.bfloat16)
    projected = lax.dot_general(normed, w_ref[...], (((0,), (0,)), ((), ())), preferred_element_type=jnp.float32)
    out_ref[...] = (gate_ref[...] * projected).astype(out_ref.dtype)


def make_update(prods, place, gain, w_out, gate):
    n_dev = len(prods)
    ch, count = prods[0].shape
    channels = w_out.shape[1]
    block = 512
    return pl.pallas_call(
        functools.partial(update_kernel, n_dev),
        grid=(pl.cdiv(count, block),),
        in_specs=[
            pl.BlockSpec(memory_space=pltpu.SMEM),
            pl.BlockSpec((n_dev * ch, 1), lambda b: (0, 0)),
            pl.BlockSpec(w_out.shape, lambda b: (0, 0)),
            pl.BlockSpec((block, channels), lambda b: (b, 0)),
        ]
        + [pl.BlockSpec((ch, block), lambda b: (0, b))] * n_dev,
        out_specs=pl.BlockSpec((block, channels), lambda b: (b, 0)),
        out_shape=jax.ShapeDtypeStruct((count, channels), jnp.bfloat16),
        scratch_shapes=[pltpu.VMEM((n_dev, ch, block), jnp.float32)],
        compiler_params=pltpu.CompilerParams(vmem_limit_bytes=VMEM_LIMIT),
    )(place, gain, w_out, gate, *prods)


def swap(value, shift):
    return lax.ppermute(value, "row", [(r, r ^ shift) for r in range(lax.axis_size("row"))])


def shards(pair_act, chain_lengths, resolved, in_gain, out_gain, w_left, w_right, w_gate, w_out):
    rows, cols, channels = pair_act.shape
    hidden = w_out.shape[0]
    groups = lax.axis_size("row") // 2
    row, col = lax.axis_index("row"), lax.axis_index("col")
    far_at = (col == row // groups).astype(jnp.int32)
    place = jnp.stack([row * rows, col * cols, lax.rem(row, groups), far_at]).astype(jnp.int32)
    normed, *edges = make_edges(
        pair_act.reshape(rows * cols, channels), chain_lengths, resolved, place,
        in_gain.reshape(1, channels), w_left, w_right, groups, cols,
    )
    both, right = edges[:groups], edges[groups:]
    far_got = [swap(right[u], groups + u) for u in range(groups)]
    near_got = [both[0]] + [swap(both[u], u) for u in range(1, groups)]
    gate = jax.nn.sigmoid(jnp.dot(normed, w_gate, preferred_element_type=jnp.float32))
    left, near = make_near(near_got, place, rows, cols)
    keep, send = make_far(far_got, place, left, near, rows, cols)
    sums = make_sums(keep, lax.ppermute(send, "col", [(0, 1), (1, 0)]))
    returned = [sums[0]] + [swap(sums[u], u) for u in range(1, groups)]
    update = make_update(returned, place, out_gain.reshape(hidden, 1), w_out, gate)
    return update.reshape(rows, cols, channels)


def solution(mesh):
    return jax.shard_map(
        shards,
        mesh=mesh,
        in_specs=(P(("grp", "row"), "col", None), P("grp"), P("grp"), P(), P(), P(), P(), P(), P()),
        out_specs=P(("grp", "row"), "col", None),
        check_vma=False,
    )
```

time: 72.6 us -> 54.4 us (0.75)
  the two profiles are of different devices: /device:TPU:0 before, /device:TPU:26 now
where the time goes in v3:
time: 54.4 us; the launch traced here: 54.2 us
  waiting for transfers between devices  25.3 us (47%)
  Pallas kernels  14.9 us (27%)
  starting transfers between devices  11.2 us (21%)
  local copies, waits for them, and re-layouts  1.73 us (3%)
  other arithmetic  0.55 us (1%)
    ppermute x10, waiting for transfers between devices, swap(): lax.ppermute(value, 'row', [(r, r ^ shift) for r in range(lax.axis_size('...  23.4 us
    ppermute x10, starting transfers between devices, swap(): lax.ppermute(value, 'row', [(r, r ^ shift) for r in range(lax.axis_size('...  11.2 us
    pallas_call x1, Pallas kernels, make_edges(): pl.pallas_call(functools.partial(edges_kernel, cols, groups, lens.shape[0...  4.54 us
    pallas_call x1, Pallas kernels, make_near(): pl.pallas_call(functools.partial(near_kernel, groups, rows, cols), in_spe...  4.24 us
    pallas_call x1, Pallas kernels, make_far(): pl.pallas_call(functools.partial(far_kernel, groups, rows, cols), in_spec...  3.16 us
    pallas_call x1, Pallas kernels, make_update(): pl.pallas_call(functools.partial(update_kernel, n_dev), grid=(pl.cdiv(cou...  2.83 us
    ppermute x1, waiting for transfers between devices, shards(): sums = make_sums(keep, lax.ppermute(send, 'col', [(0, 1), (1, 0)]))  1.9 us
    unnamed x12, local copies, waits for them, and re-layouts  1.62 us
  transfers between devices with their start and end apart: 11, of which 7 were waited for; matrix products, arithmetic and copies ran while one was open for 1% of the time, Pallas kernels for 8%

profile of v3, /device:TPU:26, one launch (start us, length us, event | category | flops | bytes accessed | tf_op | source)
XLA Modules:
  0.0 54.2 jit_solution(8441591803271950791)
XLA Ops:
  0.0 0.0 copy-start
  0.0 0.6 %pad_add_fusion.place_ref = s32[4]{0:T(128)} fusion(s32[1]{0:T(128)} %bitcast.3, s32[1]{0:T(128)} %bitcast.2, s32[1]{0:T(128)} %bitcast.1, s32[1]{0:T(128)} %bitcast), kind=kLoop, calls=%fused_computation.4 | loop fusion | flops 12 | bytes 32 | tf_op jit(solution)/shard_map/stack | solution.py:294
  0.6 4.5 %shard_map.91 = (bf16[1936,128]{1,0:T(8,128)(2,1)}, bf16[64,1936]{1,0:T(8,128)(2,1)}, bf16[64,1936]{1,0:T(8,128)(2,1)}, bf16[64,1936]{1,0:T(8,128)(2,1)}, bf16[6...) custom-call(s32[8]{0:T(128)} %lens_ref.1, ...), custom_call_target="tpu_custom_call" | custom-call | tf_op jit(solution)/shard_map/pallas_call | solution.py:67
  5.1 1.6 %collective-permute-start = (bf16[64,1936]{1,0:T(8,128)(2,1)}, bf16[64,1936]{1,0:T(8,128)(2,1)S(1)}, u32[]{:S(2)}, u32[]{:S(2)}) collective-permute-start(bf16[64,1936]{1,0:T(8,128)(2,1)} %get-tuple-element.24), channel_id=1, source_target_pairs={{0,2},{2,0},{4,6},{6,4},{8,10},{10,8},{12,14},{14,12},{1,3},{3,1},... | collective-permute-start | bytes 743432 | tf_op jit(solution)/shard_map/ppermute | solution.py:285
  6.7 0.5 collective-permute-start.1
  7.1 1.5 %collective-permute-start.2 = (bf16[64,1936]{1,0:T(8,128)(2,1)}, bf16[64,1936]{1,0:T(8,128)(2,1)S(1)}, u32[]{:S(2)}, u32[]{:S(2)}) collective-permute-start(bf16[64,1936]{1,0:T(8,128)(2,1)} %get-tuple-element.26), channel_id=1, source_target_pairs={{0,6},{2,4},{4,2},{6,0},{8,14},{10,12},{12,10},{14,8},{1,7},{3,5},... | collective-permute-start | bytes 743432 | tf_op jit(solution)/shard_map/ppermute | solution.py:285
  8.6 0.3 collective-permute-start.3
  9.0 3.5 %collective-permute-start.4 = (bf16[32,1936]{1,0:T(8,128)(2,1)}, bf16[32,1936]{1,0:T(8,128)(2,1)S(1)}, u32[]{:S(2)}, u32[]{:S(2)}) collective-permute-start(bf16[32,1936]{1,0:T(8,128)(2,1)} %get-tuple-element.30), channel_id=1, source_target_pairs={{0,10},{2,8},{4,14},{6,12},{8,2},{10,0},{12,6},{14,4},{1,11},{3,9}... | collective-permute-start | bytes 371720 | tf_op jit(solution)/shard_map/ppermute | solution.py:285
  12.5 1.1 %collective-permute-done.refs_1_ = bf16[64,1936]{1,0:T(8,128)(2,1)S(1)} collective-permute-done((bf16[64,1936]{1,0:T(8,128)(2,1)}, bf16[64,1936]{1,0:T(8,128)(2,1)S(1)}, u32[]{:S(2)}, u32[]{:S(2)}) %collective-permute-start) | collective-permute-done | bytes 247840 | tf_op jit(solution)/shard_map/ppermute | solution.py:285
  13.6 0.0 collective-permute-start.5
  13.6 8.1 %collective-permute-done.1.refs_2_ = bf16[64,1936]{1,0:T(8,128)(2,1)S(1)} collective-permute-done((bf16[64,1936]{1,0:T(8,128)(2,1)}, bf16[64,1936]{1,0:T(8,128)(2,1)S(1)}, u32[]{:S(2)}, u32[]{:S(2)}) %collective-permute-start.1) | collective-permute-done | bytes 247840 | tf_op jit(solution)/shard_map/ppermute | solution.py:285
  21.7 0.0 copy-start.3
  21.7 0.2 collective-permute-start.6
  21.9 9.6 %collective-permute-done.2.refs_3_ = bf16[64,1936]{1,0:T(8,128)(2,1)S(1)} collective-permute-done((bf16[64,1936]{1,0:T(8,128)(2,1)}, bf16[64,1936]{1,0:T(8,128)(2,1)S(1)}, u32[]{:S(2)}, u32[]{:S(2)}) %collective-permute-start.2) | collective-permute-done | bytes 247840 | tf_op jit(solution)/shard_map/ppermute | solution.py:285
  31.5 0.0 copy-done.3
  31.5 0.0 copy-start.1
  31.5 0.9 %copy-done.1 = bf16[64,1936]{1,0:T(8,128)(2,1)S(1)} copy-done((bf16[64,1936]{1,0:T(8,128)(2,1)S(1)}, bf16[64,1936]{1,0:T(8,128)(2,1)}, u32[]{:S(2)}) %copy-start.1) | copy-done | bytes 247832
  32.4 4.2 %shard_map.92 = (bf16[32,88,128]{2,1,0:T(8,128)(2,1)S(1)}, bf16[4,32,1936]{2,1,0:T(8,128)(2,1)S(1)}) custom-call(s32[4]{0:T(128)S(1)} %copy-done.3, bf16[64,1936]{1,0:T(8,128)(2,1)S(1)} %copy-done.1, bf16[64,1936]{1,0:T(8,128)(2,1)S(1)} %collective-permute-done.refs_1_, bf16[64,1936]{1,0:T(8,128)(2,1)S(1)} %collective-permute-done.1.refs_2_, ...), custom_call_target="tpu_custom_call" | custom-call | tf_op jit(solution)/shard_map/pallas_call | solution.py:203
  36.7 0.0 collective-permute-done.3.refs_0_
  36.7 0.0 collective-permute-done.4.refs_1_
  36.7 0.0 collective-permute-done.5.refs_2_
  36.7 0.0 collective-permute-done.6.refs_3_
  36.7 3.2 %shard_map.93 = (bf16[4,32,1936]{2,1,0:T(8,128)(2,1)S(1)}, bf16[4,32,1936]{2,1,0:T(8,128)(2,1)S(1)}) custom-call(s32[4]{0:T(128)S(1)} %copy-done.3, bf16[32,88,128]{2,1,0:T(8,128)(2,1)S(1)} %get-tuple-element.27.left_ref, bf16[4,32,1936]{2,1,0:T(8,128)(2,1)S(1)} %get-tuple-element.28.near_ref, bf16[32,1936]{1,0:T(8,128)(2,1)S(1)} %collective-permute-done.3.refs_0_, ...), custom_call_target="tpu_custom_call" | custom-call | tf_op jit(solution)/shard_map/pallas_call | solution.py:222
  39.9 0.1 collective-permute-start.7
  40.0 1.9 %collective-permute-done.7.b_ref = bf16[4,32,1936]{2,1,0:T(8,128)(2,1)S(1)} collective-permute-done((bf16[4,32,1936]{2,1,0:T(8,128)(2,1)S(1)}, bf16[4,32,1936]{2,1,0:T(8,128)(2,1)S(1)}, u32[]{:S(2)}, u32[]{:S(2)}) %collective-permute-start.7) | collective-permute-done | bytes 495648 | tf_op jit(solution)/shard_map/ppermute | solution.py:305
  41.8 0.0 copy-start.5
  41.9 0.1 shard_map.94
  42.0 0.1 collective-permute-start.10
  42.1 1.6 %collective-permute-start.8 = (bf16[32,1936]{1,0:T(8,128)(2,1)S(1)}, bf16[32,1936]{1,0:T(8,128)(2,1)S(1)}, u32[]{:S(2)}, u32[]{:S(2)}) collective-permute-start(bf16[32,1936]{1,0:T(8,128)(2,1)S(1)} %get-tuple-element.36), channel_id=1, source_target_pairs={{0,2},{2,0},{4,6},{6,4},{8,10},{10,8},{12,14},{14,12},{1,3},{3,1},... | collective-permute-start | bytes 371720 | tf_op jit(solution)/shard_map/ppermute | solution.py:285
  43.6 1.9 %collective-permute-start.9 = (bf16[32,1936]{1,0:T(8,128)(2,1)S(1)}, bf16[32,1936]{1,0:T(8,128)(2,1)S(1)}, u32[]{:S(2)}, u32[]{:S(2)}) collective-permute-start(bf16[32,1936]{1,0:T(8,128)(2,1)S(1)} %get-tuple-element.37), channel_id=1, source_target_pairs={{0,4},{2,6},{4,0},{6,2},{8,12},{10,14},{12,8},{14,10},{1,5},{3,7},... | collective-permute-start | bytes 371720 | tf_op jit(solution)/shard_map/ppermute | solution.py:285
  45.5 0.0 copy-done
  45.5 0.0 copy-done.5
  45.5 0.4 fusion.2.gate_ref
  46.0 0.0 copy-start.4
  46.0 0.6 %copy-done.4 = f32[128]{0:T(128)S(1)} copy-done((f32[128]{0:T(128)S(1)}, f32[128]{0:T(128)}, u32[]{:S(2)}) %copy-start.4) | copy-done | bytes 536
  46.6 0.0 copy-start.2
  46.6 0.1 copy.10.gain_ref
  46.7 2.6 %collective-permute-done.10.refs_3_ = bf16[32,1936]{1,0:T(8,128)(2,1)S(1)} collective-permute-done((bf16[32,1936]{1,0:T(8,128)(2,1)S(1)}, bf16[32,1936]{1,0:T(8,128)(2,1)S(1)}, u32[]{:S(2)}, u32[]{:S(2)}) %collective-permute-start.10) | collective-permute-done | bytes 123936 | tf_op jit(solution)/shard_map/ppermute | solution.py:285
  49.3 1.1 %collective-permute-done.8.refs_1_ = bf16[32,1936]{1,0:T(8,128)(2,1)S(1)} collective-permute-done((bf16[32,1936]{1,0:T(8,128)(2,1)S(1)}, bf16[32,1936]{1,0:T(8,128)(2,1)S(1)}, u32[]{:S(2)}, u32[]{:S(2)}) %collective-permute-start.8) | collective-permute-done | bytes 123936 | tf_op jit(solution)/shard_map/ppermute | solution.py:285
  50.5 0.9 %collective-permute-done.9.refs_2_ = bf16[32,1936]{1,0:T(8,128)(2,1)S(1)} collective-permute-done((bf16[32,1936]{1,0:T(8,128)(2,1)S(1)}, bf16[32,1936]{1,0:T(8,128)(2,1)S(1)}, u32[]{:S(2)}, u32[]{:S(2)}) %collective-permute-start.9) | collective-permute-done | bytes 123936 | tf_op jit(solution)/shard_map/ppermute | solution.py:285
  51.4 0.0 copy-done.2
  51.4 2.8 %shard_map.95 = bf16[1936,128]{1,0:T(8,128)(2,1)} custom-call(s32[4]{0:T(128)S(1)} %copy-done.3, f32[128,1]{1,0:T(8,128)S(1)} %copy.10.gain_ref, bf16[128,128]{1,0:T(8,128)(2,1)S(1)} %copy-done.2, f32[1936,128]{1,0:T(8,128)S(1)} %fusion.2.gate_ref, bf16[32,1936]{1,0:T(8,128)(2,1)S(1)} %get-tuple-element.35.refs_0_, ...), custom_call_target="tpu_custom_call" | custom-call | tf_op jit(solution)/shard_map/pallas_call | solution.py:267
Async XLA Ops:
  0.0 45.5 %copy-start = (bf16[128,128]{1,0:T(8,128)(2,1)S(1)}, bf16[128,128]{1,0:T(8,128)(2,1)}, u32[]{:S(2)}) copy-start(bf16[128,128]{1,0:T(8,128)(2,1)} %param.16) | copy-start | bytes 98308
  5.1 8.5 %collective-permute-start = (bf16[64,1936]{1,0:T(8,128)(2,1)}, bf16[64,1936]{1,0:T(8,128)(2,1)S(1)}, u32[]{:S(2)}, u32[]{:S(2)}) collective-permute-start(bf16[64,1936]{1,0:T(8,128)(2,1)} %get-tuple-element.24), channel_id=1, source_target_pairs={{0,2},{2,0},{4,6},{6,4},{8,10},{10,8},{12,14},{14,12},{1,3},{3,1},... | collective-permute-start | bytes 743432 | tf_op jit(solution)/shard_map/ppermute | solution.py:285
  6.7 15.1 %collective-permute-start.1 = (bf16[64,1936]{1,0:T(8,128)(2,1)}, bf16[64,1936]{1,0:T(8,128)(2,1)S(1)}, u32[]{:S(2)}, u32[]{:S(2)}) collective-permute-start(bf16[64,1936]{1,0:T(8,128)(2,1)} %get-tuple-element.25), channel_id=1, source_target_pairs={{0,4},{2,6},{4,0},{6,2},{8,12},{10,14},{12,8},{14,10},{1,5},{3,7},... | collective-permute-start | bytes 743432 | tf_op jit(solution)/shard_map/ppermute | solution.py:285
  7.1 24.3 %collective-permute-start.2 = (bf16[64,1936]{1,0:T(8,128)(2,1)}, bf16[64,1936]{1,0:T(8,128)(2,1)S(1)}, u32[]{:S(2)}, u32[]{:S(2)}) collective-permute-start(bf16[64,1936]{1,0:T(8,128)(2,1)} %get-tuple-element.26), channel_id=1, source_target_pairs={{0,6},{2,4},{4,2},{6,0},{8,14},{10,12},{12,10},{14,8},{1,7},{3,5},... | collective-permute-start | bytes 743432 | tf_op jit(solution)/shard_map/ppermute | solution.py:285
  8.6 28.0 %collective-permute-start.3 = (bf16[32,1936]{1,0:T(8,128)(2,1)}, bf16[32,1936]{1,0:T(8,128)(2,1)S(1)}, u32[]{:S(2)}, u32[]{:S(2)}) collective-permute-start(bf16[32,1936]{1,0:T(8,128)(2,1)} %get-tuple-element.29), channel_id=1, source_target_pairs={{0,8},{2,10},{4,12},{6,14},{8,0},{10,2},{12,4},{14,6},{1,9},{3,11}... | collective-permute-start | bytes 371720 | tf_op jit(solution)/shard_map/ppermute | solution.py:285
  9.0 27.7 %collective-permute-start.4 = (bf16[32,1936]{1,0:T(8,128)(2,1)}, bf16[32,1936]{1,0:T(8,128)(2,1)S(1)}, u32[]{:S(2)}, u32[]{:S(2)}) collective-permute-start(bf16[32,1936]{1,0:T(8,128)(2,1)} %get-tuple-element.30), channel_id=1, source_target_pairs={{0,10},{2,8},{4,14},{6,12},{8,2},{10,0},{12,6},{14,4},{1,11},{3,9}... | collective-permute-start | bytes 371720 | tf_op jit(solution)/shard_map/ppermute | solution.py:285
  13.6 23.1 %collective-permute-start.5 = (bf16[32,1936]{1,0:T(8,128)(2,1)}, bf16[32,1936]{1,0:T(8,128)(2,1)S(1)}, u32[]{:S(2)}, u32[]{:S(2)}) collective-permute-start(bf16[32,1936]{1,0:T(8,128)(2,1)} %get-tuple-element.31), channel_id=1, source_target_pairs={{0,12},{2,14},{4,8},{6,10},{8,4},{10,6},{12,0},{14,2},{1,13},{3,15... | collective-permute-start | bytes 371720 | tf_op jit(solution)/shard_map/ppermute | solution.py:285
  21.7 9.7 %copy-start.3 = (s32[4]{0:T(128)S(1)}, s32[4]{0:T(128)}, u32[]{:S(2)}) copy-start(s32[4]{0:T(128)} %pad_add_fusion.place_ref) | copy-start | bytes 52
  21.7 15.0 %collective-permute-start.6 = (bf16[32,1936]{1,0:T(8,128)(2,1)}, bf16[32,1936]{1,0:T(8,128)(2,1)S(1)}, u32[]{:S(2)}, u32[]{:S(2)}) collective-permute-start(bf16[32,1936]{1,0:T(8,128)(2,1)} %get-tuple-element.32), channel_id=1, source_target_pairs={{0,14},{2,12},{4,10},{6,8},{8,6},{10,4},{12,2},{14,0},{1,15},{3,13... | collective-permute-start | bytes 371720 | tf_op jit(solution)/shard_map/ppermute | solution.py:285
  31.5 1.0 %copy-start.1 = (bf16[64,1936]{1,0:T(8,128)(2,1)S(1)}, bf16[64,1936]{1,0:T(8,128)(2,1)}, u32[]{:S(2)}) copy-start(bf16[64,1936]{1,0:T(8,128)(2,1)} %get-tuple-element.23.refs_0_) | copy-start | bytes 743428
  39.9 2.0 %collective-permute-start.7 = (bf16[4,32,1936]{2,1,0:T(8,128)(2,1)S(1)}, bf16[4,32,1936]{2,1,0:T(8,128)(2,1)S(1)}, u32[]{:S(2)}, u32[]{:S(2)}) collective-permute-start(bf16[4,32,1936]{2,1,0:T(8,128)(2,1)S(1)} %get-tuple-element.34), channel_id=1, source_target_pairs={{0,1},{1,0},{2,3},{3,2},{4,5},{5,4},{6,7},{7,6},{8,9},{9,8},{10,11... | collective-permute-start | bytes 1486856 | tf_op jit(solution)/shard_map/ppermute | solution.py:305
  41.8 3.7 %copy-start.5 = (bf16[1936,128]{1,0:T(8,128)(2,1)S(1)}, bf16[1936,128]{1,0:T(8,128)(2,1)}, u32[]{:S(2)}) copy-start(bf16[1936,128]{1,0:T(8,128)(2,1)} %get-tuple-element.22) | copy-start | bytes 1486852
  42.0 7.3 %collective-permute-start.10 = (bf16[32,1936]{1,0:T(8,128)(2,1)S(1)}, bf16[32,1936]{1,0:T(8,128)(2,1)S(1)}, u32[]{:S(2)}, u32[]{:S(2)}) collective-permute-start(bf16[32,1936]{1,0:T(8,128)(2,1)S(1)} %get-tuple-element.38), channel_id=1, source_target_pairs={{0,6},{2,4},{4,2},{6,0},{8,14},{10,12},{12,10},{14,8},{1,7},{3,5},... | collective-permute-start | bytes 371720 | tf_op jit(solution)/shard_map/ppermute | solution.py:285
  42.1 8.4 %collective-permute-start.8 = (bf16[32,1936]{1,0:T(8,128)(2,1)S(1)}, bf16[32,1936]{1,0:T(8,128)(2,1)S(1)}, u32[]{:S(2)}, u32[]{:S(2)}) collective-permute-start(bf16[32,1936]{1,0:T(8,128)(2,1)S(1)} %get-tuple-element.36), channel_id=1, source_target_pairs={{0,2},{2,0},{4,6},{6,4},{8,10},{10,8},{12,14},{14,12},{1,3},{3,1},... | collective-permute-start | bytes 371720 | tf_op jit(solution)/shard_map/ppermute | solution.py:285
  43.6 7.8 %collective-permute-start.9 = (bf16[32,1936]{1,0:T(8,128)(2,1)S(1)}, bf16[32,1936]{1,0:T(8,128)(2,1)S(1)}, u32[]{:S(2)}, u32[]{:S(2)}) collective-permute-start(bf16[32,1936]{1,0:T(8,128)(2,1)S(1)} %get-tuple-element.37), channel_id=1, source_target_pairs={{0,4},{2,6},{4,0},{6,2},{8,12},{10,14},{12,8},{14,10},{1,5},{3,7},... | collective-permute-start | bytes 371720 | tf_op jit(solution)/shard_map/ppermute | solution.py:285
  46.0 0.7 %copy-start.4 = (f32[128]{0:T(128)S(1)}, f32[128]{0:T(128)}, u32[]{:S(2)}) copy-start(f32[128]{0:T(128)} %param.13) | copy-start | bytes 1540
  46.6 4.8 %copy-start.2 = (bf16[128,128]{1,0:T(8,128)(2,1)S(1)}, bf16[128,128]{1,0:T(8,128)(2,1)}, u32[]{:S(2)}) copy-start(bf16[128,128]{1,0:T(8,128)(2,1)} %w_ref.1) | copy-start | bytes 98308

commit v4 on v3

v4 whole, which is shorter than its diff:
```python
import functools

import jax
import jax.numpy as jnp
from jax import lax
from jax.experimental import pallas as pl
from jax.experimental.pallas import tpu as pltpu
from jax.sharding import PartitionSpec as P

EPS = 1e-05
LANES = 128
VMEM_LIMIT = 32 * 1024 * 1024
VMEM_FIRST = 60 * 1024 * 1024


def ceil_to(n, m):
    return -(-n // m) * m


def place_of(groups, rows, cols):
    row, col = lax.axis_index("row"), lax.axis_index("col")
    return row * rows, col * cols, lax.rem(row, groups), row // groups, col


def mask_of(cols, first_row, first_col, lens_ref, res_ref, block):
    position = pl.program_id(0) * block + lax.broadcasted_iota(jnp.int32, (8, block), 1)
    i_here = jnp.floor((position.astype(jnp.float32) + 0.5) * (1.0 / cols)).astype(jnp.int32)
    i_at = first_row + i_here
    k_at = first_col + position - i_here * cols
    i_ok = jnp.zeros((8, block), jnp.float32)
    k_ok = jnp.zeros((8, block), jnp.float32)
    start = 0
    for q in range(lens_ref.shape[0]):
        length = lens_ref[q]
        stop = start + jnp.minimum(length, res_ref[q])
        i_ok = jnp.where((i_at >= start) & (i_at < stop), 1.0, i_ok)
        k_ok = jnp.where((k_at >= start) & (k_at < stop), 1.0, k_ok)
        start = start + length
    return i_ok * k_ok


def edge_of(normed, w_ref, mask, groups):
    hidden = w_ref.shape[1] // 2
    block = normed.shape[0]
    projected = lax.dot_general(w_ref[...], normed, (((0,), (1,)), ((), ())), preferred_element_type=jnp.float32)
    edge = jax.nn.sigmoid(projected[:hidden]) * projected[hidden:]
    edge = edge.reshape(hidden // 8, 8, block) * mask[None]
    return edge.reshape(groups, hidden // groups, block).astype(jnp.bfloat16)


def right_kernel(groups, rows, cols, lens_ref, res_ref, x_ref, gain_ref, w_ref, normed_ref, *refs):
    right_refs, held = refs[:groups], refs[groups]
    first_row, first_col, mine, _, _ = place_of(groups, rows, cols)
    x = x_ref[...].astype(jnp.float32)
    mean = jnp.mean(x, axis=-1, keepdims=True)
    centred = x - mean
    variance = jnp.mean(centred * centred, axis=-1, keepdims=True)
    normed = (centred * lax.rsqrt(variance + EPS) * gain_ref[...]).astype(jnp.bfloat16)
    normed_ref[...] = normed
    mask = mask_of(cols, first_row, first_col, lens_ref, res_ref, x.shape[0])
    held[...] = edge_of(normed, w_ref, mask, groups)
    for u in range(groups):
        right_refs[u][...] = held[jnp.bitwise_xor(mine, u)]


def left_kernel(groups, rows, cols, lens_ref, res_ref, normed_ref, w_ref, *refs):
    right_refs, both_ref = refs[:groups], refs[groups]
    first_row, first_col, mine, _, _ = place_of(groups, rows, cols)
    own = both_ref.shape[1] // 2
    mask = mask_of(cols, first_row, first_col, lens_ref, res_ref, normed_ref.shape[0])
    both_ref[:, :own] = edge_of(normed_ref[...], w_ref, mask, groups)
    for u in range(groups):
        both_ref[jnp.bitwise_xor(mine, u), own:] = right_refs[u][...]


def make_right(pair, lens, resolved, gain, w_right, groups, rows, cols):
    count, channels = pair.shape
    own = w_right.shape[1] // 2 // groups
    block = 512
    smem = pl.BlockSpec(memory_space=pltpu.SMEM)
    return pl.pallas_call(
        functools.partial(right_kernel, groups, rows, cols),
        grid=(pl.cdiv(count, block),),
        in_specs=[
            smem, smem,
            pl.BlockSpec((block, channels), lambda b: (b, 0)),
            pl.BlockSpec((1, channels), lambda b: (0, 0)),
            pl.BlockSpec(w_right.shape, lambda b: (0, 0)),
        ],
        out_specs=[pl.BlockSpec((block, channels), lambda b: (b, 0))]
        + [pl.BlockSpec((own, block), lambda b: (0, b))] * groups,
        out_shape=[jax.ShapeDtypeStruct((count, channels), jnp.bfloat16)]
        + [jax.ShapeDtypeStruct((own, count), jnp.bfloat16)] * groups,
        scratch_shapes=[pltpu.VMEM((groups, own, block), jnp.bfloat16)],
        compiler_params=pltpu.CompilerParams(vmem_limit_bytes=VMEM_FIRST),
    )(lens, resolved, pair, gain, w_right)


def make_left(normed, lens, resolved, w_left, right, rows, cols):
    groups = len(right)
    count, channels = normed.shape
    own = w_left.shape[1] // 2 // groups
    block = 512
    smem = pl.BlockSpec(memory_space=pltpu.SMEM)
    return pl.pallas_call(
        functools.partial(left_kernel, groups, rows, cols),
        grid=(pl.cdiv(count, block),),
        in_specs=[
            smem, smem,
            pl.BlockSpec((block, channels), lambda b: (b, 0)),
            pl.BlockSpec(w_left.shape, lambda b: (0, 0)),
        ]
        + [pl.BlockSpec((own, block), lambda b: (0, b))] * groups,
        out_specs=pl.BlockSpec((groups, 2 * own, block), lambda b: (0, 0, b)),
        out_shape=jax.ShapeDtypeStruct((groups, 2 * own, count), jnp.bfloat16),
        compiler_params=pltpu.CompilerParams(vmem_limit_bytes=VMEM_FIRST),
    )(lens, resolved, normed, w_left, *right)


def unpack(got_ref, held_refs, block, rows, cols, step):
    tiles = pl.cdiv(cols, LANES)
    flat = rows * cols
    height = got_ref.shape[0]
    ch = height // len(held_refs)
    lane = lax.broadcasted_iota(jnp.int32, (height, LANES), 1)
    seen = {}

    def tile_of(t):
        if t not in seen:
            width = min(LANES, flat - t * LANES)
            got = got_ref[:, pl.ds(t * LANES, width)].astype(jnp.float32)
            if width < LANES:
                got = jnp.concatenate([got, jnp.zeros((height, LANES - width), jnp.float32)], axis=1)
            seen[t] = got
        return seen[t]

    for i in range(rows):
        for tt in range(tiles):
            length = min(LANES, cols - LANES * tt)
            t0, off = divmod(cols * i + LANES * tt, LANES)
            piece = tile_of(t0)
            if off:
                piece = pltpu.roll(piece, LANES - off, 1)
            if off + length > LANES:
                piece = jnp.where(lane < LANES - off, piece, pltpu.roll(tile_of(t0 + 1), LANES - off, 1))
            if length < LANES:
                piece = jnp.where(lane < length, piece, 0.0)
            base = pl.multiple_of((block * rows + i) * step, 8)
            for n, held in enumerate(held_refs):
                held[tt, pl.ds(base, ch), :] = piece[n * ch:(n + 1) * ch]


def pack(held, store, block, rows, cols, step, ch):
    tiles = pl.cdiv(cols, LANES)
    flat = rows * cols
    lane = lax.broadcasted_iota(jnp.int32, (ch, LANES), 1)
    for t in range(pl.cdiv(flat, LANES)):
        tile = None
        for i in range(rows):
            for tt in range(tiles):
                shift = cols * i + LANES * tt - LANES * t
                length = min(LANES, cols - LANES * tt)
                if shift >= LANES or shift + length <= 0:
                    continue
                base = pl.multiple_of((block * rows + i) * step, 8)
                piece = held[tt, pl.ds(base, ch), :]
                if shift % LANES:
                    piece = pltpu.roll(piece, shift % LANES, 1)
                tile = piece if tile is None else jnp.where(lane < shift, tile, piece)
        width = min(LANES, flat - t * LANES)
        store(t, width, tile[:, :width].astype(jnp.bfloat16))


def channel_of(held, d, count, step):
    lines = [held[t, pl.ds(d, count, stride=step), :] for t in range(held.shape[0])]
    return jnp.concatenate(lines, axis=1)


def multiply(left_ref, right_s, prod_s, ch, step):
    count = left_ref.shape[1]
    pad = right_s.shape[0] * LANES - count
    for d in range(ch):
        right = channel_of(right_s, d, count, step)
        if pad:
            right = jnp.concatenate([right, jnp.zeros((pad, right.shape[1]), jnp.float32)], axis=0)
        prod = lax.dot_general(
            left_ref[d], right.astype(jnp.bfloat16), (((1,), (1,)), ((), ())), preferred_element_type=jnp.float32
        )
        for t in range(prod_s.shape[0]):
            prod_s[t, pl.ds(d, count, stride=step), :] = prod[:, t * LANES:(t + 1) * LANES]


def near_kernel(groups, rows, cols, got_ref, left_ref, near_ref, left_s, right_s, prod_s):
    mine = place_of(groups, rows, cols)[2]
    ch = near_ref.shape[1]
    step = left_s.shape[1] // (groups * rows)
    for u in range(groups):
        unpack(got_ref.at[u], (left_s, right_s), u, rows, cols, step)
    for d in range(ch):
        left_ref[d] = channel_of(left_s, d, groups * rows, step).astype(jnp.bfloat16)
    multiply(left_ref, right_s, prod_s, ch, step)
    for u in range(groups):
        def store(t, width, tile):
            near_ref[u, :, pl.ds(t * LANES, width)] = tile
        pack(prod_s, store, jnp.bitwise_xor(mine, u), rows, cols, step, ch)


def far_kernel(groups, rows, cols, left_ref, near_ref, *refs):
    got_refs = refs[:groups]
    keep_ref, send_ref, right_s, prod_s, pair_s = refs[groups:]
    ch = near_ref.shape[1]
    step = right_s.shape[1] // (groups * rows)
    _, _, mine, half, col = place_of(groups, rows, cols)
    far_at = (col == half).astype(jnp.int32)
    pair_s[1 - far_at] = near_ref[...]
    for u in range(groups):
        unpack(got_refs[u], (right_s,), jnp.bitwise_xor(mine, u), rows, cols, step)
    multiply(left_ref, right_s, prod_s, ch, step)
    for u in range(groups):
        def store(t, width, tile):
            pair_s[far_at, u, :, pl.ds(t * LANES, width)] = tile
        pack(prod_s, store, jnp.bitwise_xor(mine, u), rows, cols, step, ch)
    keep_ref[...] = pair_s[0]
    send_ref[...] = pair_s[1]


def make_near(got, rows, cols):
    groups, both, flat = got.shape
    ch = both // 2
    count = groups * rows
    tiles = pl.cdiv(cols, LANES)
    held = pltpu.VMEM((tiles, count * ceil_to(ch, 8), LANES), jnp.float32)
    whole = pl.BlockSpec(memory_space=pltpu.VMEM)
    return pl.pallas_call(
        functools.partial(near_kernel, groups, rows, cols),
        in_specs=[whole],
        out_specs=[whole] * 2,
        out_shape=[
            jax.ShapeDtypeStruct((ch, count, tiles * LANES), jnp.bfloat16),
            jax.ShapeDtypeStruct((groups, ch, flat), jnp.bfloat16),
        ],
        scratch_shapes=[held, held, held],
        compiler_params=pltpu.CompilerParams(vmem_limit_bytes=VMEM_LIMIT),
    )(got)


def make_far(got, left, near, rows, cols):
    groups = len(got)
    ch, flat = got[0].shape
    tiles = pl.cdiv(cols, LANES)
    held = pltpu.VMEM((tiles, groups * rows * ceil_to(ch, 8), LANES), jnp.float32)
    whole = pl.BlockSpec(memory_space=pltpu.VMEM)
    return pl.pallas_call(
        functools.partial(far_kernel, groups, rows, cols),
        in_specs=[whole] * (groups + 2),
        out_specs=[whole] * 2,
        out_shape=[jax.ShapeDtypeStruct((groups, ch, flat), jnp.bfloat16)] * 2,
        scratch_shapes=[held, held, pltpu.VMEM((2, groups, ch, flat), jnp.bfloat16)],
        compiler_params=pltpu.CompilerParams(vmem_limit_bytes=VMEM_LIMIT),
    )(left, near, *got)


def add_kernel(a_ref, b_ref, *out_refs):
    for u, out_ref in enumerate(out_refs):
        out_ref[...] = (a_ref[u].astype(jnp.float32) + b_ref[u].astype(jnp.float32)).astype(out_ref.dtype)


def make_sums(a, b):
    groups, ch, flat = a.shape
    whole = pl.BlockSpec(memory_space=pltpu.VMEM)
    return pl.pallas_call(
        add_kernel,
        in_specs=[whole] * 2,
        out_specs=[whole] * groups,
        out_shape=[jax.ShapeDtypeStruct((ch, flat), a.dtype)] * groups,
        compiler_params=pltpu.CompilerParams(vmem_limit_bytes=VMEM_LIMIT),
    )(a, b)


def update_kernel(groups, rows, cols, gain_ref, w_ref, gate_ref, *refs):
    prod_refs, out_ref, held = refs[:groups], refs[groups], refs[groups + 1]
    mine = place_of(groups, rows, cols)[2]
    for u in range(groups):
        held[jnp.bitwise_xor(mine, u)] = prod_refs[u][...].astype(jnp.float32)
    prod = held[...].reshape(-1, held.shape[2])
    mean = jnp.mean(prod, axis=0, keepdims=True)
    centred = prod - mean
    variance = jnp.mean(centred * centred, axis=0, keepdims=True)
    normed = (centred * lax.rsqrt(variance + EPS) * gain_ref[...]).astype(jnp.bfloat16)
    projected = lax.dot_general(normed, w_ref[...], (((0,), (0,)), ((), ())), preferred_element_type=jnp.float32)
    out_ref[...] = (gate_ref[...] * projected).astype(out_ref.dtype)


def make_update(prods, gain, w_out, gate, rows, cols):
    groups = len(prods)
    ch, count = prods[0].shape
    channels = w_out.shape[1]
    block = 512
    return pl.pallas_call(
        functools.partial(update_kernel, groups, rows, cols),
        grid=(pl.cdiv(count, block),),
        in_specs=[
            pl.BlockSpec((groups * ch, 1), lambda b: (0, 0)),
            pl.BlockSpec(w_out.shape, lambda b: (0, 0)),
            pl.BlockSpec((block, channels), lambda b: (b, 0)),
        ]
        + [pl.BlockSpec((ch, block), lambda b: (0, b))] * groups,
        out_specs=pl.BlockSpec((block, channels), lambda b: (b, 0)),
        out_shape=jax.ShapeDtypeStruct((count, channels), jnp.bfloat16),
        scratch_shapes=[pltpu.VMEM((groups, ch, block), jnp.float32)],
        compiler_params=pltpu.CompilerParams(vmem_limit_bytes=VMEM_LIMIT),
    )(gain, w_out, gate, *prods)


def swap(value, shift):
    return lax.ppermute(value, "row", [(r, r ^ shift) for r in range(lax.axis_size("row"))])


def shards(pair_act, chain_lengths, resolved, in_gain, out_gain, w_left, w_right, w_gate, w_out):
    rows, cols, channels = pair_act.shape
    hidden = w_out.shape[0]
    groups = lax.axis_size("row") // 2
    halves = [[h * groups + r for r in range(groups)] for h in range(2)]
    normed, *right = make_right(
        pair_act.reshape(rows * cols, channels), chain_lengths, resolved,
        in_gain.reshape(1, channels), w_right, groups, rows, cols,
    )
    far_got = [swap(right[u], groups + u) for u in range(groups)]
    both = make_left(normed, chain_lengths, resolved, w_left, right, rows, cols)
    near_got = lax.all_to_all(both, "row", split_axis=0, concat_axis=0, tiled=True, axis_index_groups=halves)
    gate = jax.nn.sigmoid(jnp.dot(normed, w_gate, preferred_element_type=jnp.float32))
    left, near = make_near(near_got, rows, cols)
    keep, send = make_far(far_got, left, near, rows, cols)
    sums = make_sums(keep, lax.ppermute(send, "col", [(0, 1), (1, 0)]))
    returned = [sums[0]] + [swap(sums[u], u) for u in range(1, groups)]
    update = make_update(returned, out_gain.reshape(hidden, 1), w_out, gate, rows, cols)
    return update.reshape(rows, cols, channels)


def solution(mesh):
    return jax.shard_map(
        shards,
        mesh=mesh,
        in_specs=(P(("grp", "row"), "col", None), P("grp"), P("grp"), P(), P(), P(), P(), P(), P()),
        out_specs=P(("grp", "row"), "col", None),
        check_vma=False,
    )
```

time: 54.4 us -> 58.3 us (1.072)
  the two profiles are of different devices: /device:TPU:26 before, /device:TPU:0 now
where the time goes in v4:
time: 58.3 us; the launch traced here: 58 us
  waiting for transfers between devices  23.1 us (40%)
  starting transfers between devices  17 us (29%)
  Pallas kernels  16.6 us (28%)
  local copies, waits for them, and re-layouts  0.79 us (1%)
    ppermute x7, starting transfers between devices, swap(): lax.ppermute(value, 'row', [(r, r ^ shift) for r in range(lax.axis_size('...  11.5 us
    all_to_all x1, waiting for transfers between devices, shards(): lax.all_to_all(both, 'row', split_axis=0, concat_axis=0, tiled=True, axis...  11.3 us
    ppermute x7, waiting for transfers between devices, swap(): lax.ppermute(value, 'row', [(r, r ^ shift) for r in range(lax.axis_size('...  9.87 us
    all_to_all x1, starting transfers between devices, shards(): lax.all_to_all(both, 'row', split_axis=0, concat_axis=0, tiled=True, axis...  5.4 us
    pallas_call x1, Pallas kernels, make_right(): pl.pallas_call(functools.partial(right_kernel, groups, rows, cols), grid=...  4.12 us
    pallas_call x1, Pallas kernels, make_left(): pl.pallas_call(functools.partial(left_kernel, groups, rows, cols), grid=(...  3.94 us
    pallas_call x1, Pallas kernels, make_near(): pl.pallas_call(functools.partial(near_kernel, groups, rows, cols), in_spe...  3.47 us
    pallas_call x1, Pallas kernels, make_far(): pl.pallas_call(functools.partial(far_kernel, groups, rows, cols), in_spec...  2.67 us
  transfers between devices with their start and end apart: 9, of which 7 were waited for; matrix products, arithmetic and copies ran while one was open for 1% of the time, Pallas kernels for 6%

profile of v4, /device:TPU:0, one launch (start us, length us, event | category | flops | bytes accessed | tf_op | source)
XLA Modules:
  0.0 58.0 jit_solution(8148928692328021481)
XLA Ops:
  0.0 0.0 copy-start
  0.0 4.1 %shard_map.91 = (bf16[1936,128]{1,0:T(8,128)(2,1)}, bf16[32,1936]{1,0:T(8,128)(2,1)}, bf16[32,1936]{1,0:T(8,128)(2,1)}, bf16[32,1936]{1,0:T(8,128)(2,1)}, bf16[32,1936]{1,0:T(8,128)(2,1)}) custom-call(s32[8]{0:T(128)} %lens_ref.3, s32[8]{0:T(128)} %res_ref.3, bf16[1936,128]{1,0:T(8,128)(2,1)} %bitcast.6, f32[1,128]{1,0:T(1,128)} %bitcast.7, ...), custom_call_target="tpu_custom_call" | custom-call | tf_op jit(solution)/shard_map/pallas_call | solution.py:81
  4.1 3.9 %shard_map.92 = bf16[4,64,1936]{2,1,0:T(8,128)(2,1)} custom-call(s32[8]{0:T(128)} %lens_ref.3, s32[8]{0:T(128)} %res_ref.3, bf16[1936,128]{1,0:T(8,128)(2,1)} %get-tuple-element.18.normed_ref, bf16[128,256]{1,0:T(8,128)(2,1)} %w_ref.4, bf16[32,1936]{1,0:T(8,128)(2,1)} %get-tuple-element.19.refs_0_, bf16[32,1936]{1,0:T(8,128)(2,1)} %get-tuple-element.20.refs_1_, ...), custom_call_target="tpu_custom_call" | custom-call | tf_op jit(solution)/shard_map/pallas_call | solution.py:105
  8.1 0.0 copy-start.6
  8.1 0.0 copy-start.5
  8.1 0.0 copy-start.4
  8.1 0.0 copy-start.3
  8.1 5.4 %all-to-all-start = ((bf16[4,64,1936]{2,1,0:T(8,128)(2,1)}), bf16[4,64,1936]{2,1,0:T(8,128)(2,1)S(1)}, u32[]{:S(2)}, u32[]{:S(2)}) async-start(bf16[4,64,1936]{2,1,0:T(8,128)(2,1)} %shard_map.92), calls=%async_computation | async-start | bytes 2097152 | tf_op jit(solution)/shard_map/all_to_all | solution.py:330
  13.5 0.0 copy-done.6
  13.5 2.6 %collective-permute-start = (bf16[32,1936]{1,0:T(8,128)(2,1)S(1)}, bf16[32,1936]{1,0:T(8,128)(2,1)S(1)}, u32[]{:S(2)}, u32[]{:S(2)}) collective-permute-start(bf16[32,1936]{1,0:T(8,128)(2,1)S(1)} %copy-done.6), channel_id=1, source_target_pairs={{0,8},{2,10},{4,12},{6,14},{8,0},{10,2},{12,4},{14,6},{1,9},{3,11}... | collective-permute-start | bytes 371720 | tf_op jit(solution)/shard_map/ppermute | solution.py:316
  16.1 0.0 copy-done.5
  16.1 1.8 %collective-permute-start.1 = (bf16[32,1936]{1,0:T(8,128)(2,1)S(1)}, bf16[32,1936]{1,0:T(8,128)(2,1)S(1)}, u32[]{:S(2)}, u32[]{:S(2)}) collective-permute-start(bf16[32,1936]{1,0:T(8,128)(2,1)S(1)} %copy-done.5), channel_id=1, source_target_pairs={{0,10},{2,8},{4,14},{6,12},{8,2},{10,0},{12,6},{14,4},{1,11},{3,9}... | collective-permute-start | bytes 371720 | tf_op jit(solution)/shard_map/ppermute | solution.py:316
  17.9 0.0 copy-done.4
  17.9 3.5 %collective-permute-start.2 = (bf16[32,1936]{1,0:T(8,128)(2,1)S(1)}, bf16[32,1936]{1,0:T(8,128)(2,1)S(1)}, u32[]{:S(2)}, u32[]{:S(2)}) collective-permute-start(bf16[32,1936]{1,0:T(8,128)(2,1)S(1)} %copy-done.4), channel_id=1, source_target_pairs={{0,12},{2,14},{4,8},{6,10},{8,4},{10,6},{12,0},{14,2},{1,13},{3,15... | collective-permute-start | bytes 371720 | tf_op jit(solution)/shard_map/ppermute | solution.py:316
  21.4 0.0 copy-done.3
  21.4 0.1 collective-permute-start.3
  21.5 11.3 %all-to-all-done.got_ref = bf16[4,64,1936]{2,1,0:T(8,128)(2,1)S(1)} async-done(((bf16[4,64,1936]{2,1,0:T(8,128)(2,1)}), bf16[4,64,1936]{2,1,0:T(8,128)(2,1)S(1)}, u32[]{:S(2)}, u32[]{:S(2)}) %all-to-all-start) | async-done | bytes 991264 | tf_op jit(solution)/shard_map/all_to_all | solution.py:330
  32.8 3.5 %shard_map.93 = (bf16[32,88,128]{2,1,0:T(8,128)(2,1)S(1)}, bf16[4,32,1936]{2,1,0:T(8,128)(2,1)S(1)}) custom-call(bf16[4,64,1936]{2,1,0:T(8,128)(2,1)S(1)} %all-to-all-done.got_ref), custom_call_target="tpu_custom_call" | custom-call | tf_op jit(solution)/shard_map/pallas_call | solution.py:234
  36.2 0.0 collective-permute-done.refs_0_
  36.2 0.0 collective-permute-done.1.refs_1_
  36.3 2.7 %collective-permute-done.2.refs_2_ = bf16[32,1936]{1,0:T(8,128)(2,1)S(1)} collective-permute-done((bf16[32,1936]{1,0:T(8,128)(2,1)S(1)}, bf16[32,1936]{1,0:T(8,128)(2,1)S(1)}, u32[]{:S(2)}, u32[]{:S(2)}) %collective-permute-start.2) | collective-permute-done | bytes 123936 | tf_op jit(solution)/shard_map/ppermute | solution.py:316
  39.0 2.3 %collective-permute-done.3.refs_3_ = bf16[32,1936]{1,0:T(8,128)(2,1)S(1)} collective-permute-done((bf16[32,1936]{1,0:T(8,128)(2,1)S(1)}, bf16[32,1936]{1,0:T(8,128)(2,1)S(1)}, u32[]{:S(2)}, u32[]{:S(2)}) %collective-permute-start.3) | collective-permute-done | bytes 123936 | tf_op jit(solution)/shard_map/ppermute | solution.py:316
  41.3 2.7 %shard_map.94 = (bf16[4,32,1936]{2,1,0:T(8,128)(2,1)S(1)}, bf16[4,32,1936]{2,1,0:T(8,128)(2,1)S(1)}) custom-call(bf16[32,88,128]{2,1,0:T(8,128)(2,1)S(1)} %get-tuple-element.23.left_ref, bf16[4,32,1936]{2,1,0:T(8,128)(2,1)S(1)} %get-tuple-element.24.near_ref, bf16[32,1936]{1,0:T(8,128)(2,1)S(1)} %collective-permute-done.refs_0_, ...), custom_call_target="tpu_custom_call" | custom-call | tf_op jit(solution)/shard_map/pallas_call | solution.py:253
  44.0 0.1 collective-permute-start.4
  44.0 1.9 %collective-permute-done.4.b_ref = bf16[4,32,1936]{2,1,0:T(8,128)(2,1)S(1)} collective-permute-done((bf16[4,32,1936]{2,1,0:T(8,128)(2,1)S(1)}, bf16[4,32,1936]{2,1,0:T(8,128)(2,1)S(1)}, u32[]{:S(2)}, u32[]{:S(2)}) %collective-permute-start.4) | collective-permute-done | bytes 495648 | tf_op jit(solution)/shard_map/ppermute | solution.py:334
  45.9 0.0 copy-start.2
  45.9 0.1 shard_map.95
  46.1 0.6 %collective-permute-start.5 = (bf16[32,1936]{1,0:T(8,128)(2,1)S(1)}, bf16[32,1936]{1,0:T(8,128)(2,1)S(1)}, u32[]{:S(2)}, u32[]{:S(2)}) collective-permute-start(bf16[32,1936]{1,0:T(8,128)(2,1)S(1)} %get-tuple-element.28), channel_id=1, source_target_pairs={{0,2},{2,0},{4,6},{6,4},{8,10},{10,8},{12,14},{14,12},{1,3},{3,1},... | collective-permute-start | bytes 371720 | tf_op jit(solution)/shard_map/ppermute | solution.py:316
  46.7 0.0 collective-permute-start.6
  46.7 2.9 %collective-permute-start.7 = (bf16[32,1936]{1,0:T(8,128)(2,1)S(1)}, bf16[32,1936]{1,0:T(8,128)(2,1)S(1)}, u32[]{:S(2)}, u32[]{:S(2)}) collective-permute-start(bf16[32,1936]{1,0:T(8,128)(2,1)S(1)} %get-tuple-element.30), channel_id=1, source_target_pairs={{0,6},{2,4},{4,2},{6,0},{8,14},{10,12},{12,10},{14,8},{1,7},{3,5},... | collective-permute-start | bytes 371720 | tf_op jit(solution)/shard_map/ppermute | solution.py:316
  49.6 0.0 copy-done
  49.6 0.0 copy-done.2
  49.6 0.4 fusion.2.gate_ref
  50.0 0.0 copy-start.7
  50.1 0.6 %copy-done.7 = f32[128]{0:T(128)S(1)} copy-done((f32[128]{0:T(128)S(1)}, f32[128]{0:T(128)}, u32[]{:S(2)}) %copy-start.7) | copy-done | bytes 536
  50.7 0.0 copy-start.1
  50.7 0.1 copy.10.gain_ref
  50.8 0.8 %collective-permute-done.5.refs_1_ = bf16[32,1936]{1,0:T(8,128)(2,1)S(1)} collective-permute-done((bf16[32,1936]{1,0:T(8,128)(2,1)S(1)}, bf16[32,1936]{1,0:T(8,128)(2,1)S(1)}, u32[]{:S(2)}, u32[]{:S(2)}) %collective-permute-start.5) | collective-permute-done | bytes 123936 | tf_op jit(solution)/shard_map/ppermute | solution.py:316
  51.7 1.4 %collective-permute-done.6.refs_2_ = bf16[32,1936]{1,0:T(8,128)(2,1)S(1)} collective-permute-done((bf16[32,1936]{1,0:T(8,128)(2,1)S(1)}, bf16[32,1936]{1,0:T(8,128)(2,1)S(1)}, u32[]{:S(2)}, u32[]{:S(2)}) %collective-permute-start.6) | collective-permute-done | bytes 123936 | tf_op jit(solution)/shard_map/ppermute | solution.py:316
  53.1 2.6 %collective-permute-done.7.refs_3_ = bf16[32,1936]{1,0:T(8,128)(2,1)S(1)} collective-permute-done((bf16[32,1936]{1,0:T(8,128)(2,1)S(1)}, bf16[32,1936]{1,0:T(8,128)(2,1)S(1)}, u32[]{:S(2)}, u32[]{:S(2)}) %collective-permute-start.7) | collective-permute-done | bytes 123936 | tf_op jit(solution)/shard_map/ppermute | solution.py:316
  55.7 0.0 copy-done.1
  55.7 2.3 %shard_map.96 = bf16[1936,128]{1,0:T(8,128)(2,1)} custom-call(f32[128,1]{1,0:T(8,128)S(1)} %copy.10.gain_ref, bf16[128,128]{1,0:T(8,128)(2,1)S(1)} %copy-done.1, f32[1936,128]{1,0:T(8,128)S(1)} %fusion.2.gate_ref, bf16[32,1936]{1,0:T(8,128)(2,1)S(1)} %get-tuple-element.27.refs_0_, bf16[32,1936]{1,0:T(8,128)(2,1)S(1)} %collective-permute-done.5.refs_1_, ...), custom_call_target="tpu_custom_call" | custom-call | tf_op jit(solution)/shard_map/pallas_call | solution.py:299
Async XLA Ops:
  0.0 49.6 %copy-start = (bf16[128,128]{1,0:T(8,128)(2,1)S(1)}, bf16[128,128]{1,0:T(8,128)(2,1)}, u32[]{:S(2)}) copy-start(bf16[128,128]{1,0:T(8,128)(2,1)} %param.16) | copy-start | bytes 98308
  8.1 5.4 %copy-start.6 = (bf16[32,1936]{1,0:T(8,128)(2,1)S(1)}, bf16[32,1936]{1,0:T(8,128)(2,1)}, u32[]{:S(2)}) copy-start(bf16[32,1936]{1,0:T(8,128)(2,1)} %get-tuple-element.19.refs_0_) | copy-start | bytes 371716
  8.1 8.0 %copy-start.5 = (bf16[32,1936]{1,0:T(8,128)(2,1)S(1)}, bf16[32,1936]{1,0:T(8,128)(2,1)}, u32[]{:S(2)}) copy-start(bf16[32,1936]{1,0:T(8,128)(2,1)} %get-tuple-element.20.refs_1_) | copy-start | bytes 371716
  8.1 9.8 %copy-start.4 = (bf16[32,1936]{1,0:T(8,128)(2,1)S(1)}, bf16[32,1936]{1,0:T(8,128)(2,1)}, u32[]{:S(2)}) copy-start(bf16[32,1936]{1,0:T(8,128)(2,1)} %get-tuple-element.21.refs_2_) | copy-start | bytes 371716
  8.1 13.3 %copy-start.3 = (bf16[32,1936]{1,0:T(8,128)(2,1)S(1)}, bf16[32,1936]{1,0:T(8,128)(2,1)}, u32[]{:S(2)}) copy-start(bf16[32,1936]{1,0:T(8,128)(2,1)} %get-tuple-element.22.refs_3_) | copy-start | bytes 371716
  8.1 24.7 %all-to-all-start = ((bf16[4,64,1936]{2,1,0:T(8,128)(2,1)}), bf16[4,64,1936]{2,1,0:T(8,128)(2,1)S(1)}, u32[]{:S(2)}, u32[]{:S(2)}) async-start(bf16[4,64,1936]{2,1,0:T(8,128)(2,1)} %shard_map.92), calls=%async_computation | async-start | bytes 2097152 | tf_op jit(solution)/shard_map/all_to_all | solution.py:330
  13.5 22.7 %collective-permute-start = (bf16[32,1936]{1,0:T(8,128)(2,1)S(1)}, bf16[32,1936]{1,0:T(8,128)(2,1)S(1)}, u32[]{:S(2)}, u32[]{:S(2)}) collective-permute-start(bf16[32,1936]{1,0:T(8,128)(2,1)S(1)} %copy-done.6), channel_id=1, source_target_pairs={{0,8},{2,10},{4,12},{6,14},{8,0},{10,2},{12,4},{14,6},{1,9},{3,11}... | collective-permute-start | bytes 371720 | tf_op jit(solution)/shard_map/ppermute | solution.py:316
  16.1 20.2 %collective-permute-start.1 = (bf16[32,1936]{1,0:T(8,128)(2,1)S(1)}, bf16[32,1936]{1,0:T(8,128)(2,1)S(1)}, u32[]{:S(2)}, u32[]{:S(2)}) collective-permute-start(bf16[32,1936]{1,0:T(8,128)(2,1)S(1)} %copy-done.5), channel_id=1, source_target_pairs={{0,10},{2,8},{4,14},{6,12},{8,2},{10,0},{12,6},{14,4},{1,11},{3,9}... | collective-permute-start | bytes 371720 | tf_op jit(solution)/shard_map/ppermute | solution.py:316
  17.9 21.1 %collective-permute-start.2 = (bf16[32,1936]{1,0:T(8,128)(2,1)S(1)}, bf16[32,1936]{1,0:T(8,128)(2,1)S(1)}, u32[]{:S(2)}, u32[]{:S(2)}) collective-permute-start(bf16[32,1936]{1,0:T(8,128)(2,1)S(1)} %copy-done.4), channel_id=1, source_target_pairs={{0,12},{2,14},{4,8},{6,10},{8,4},{10,6},{12,0},{14,2},{1,13},{3,15... | collective-permute-start | bytes 371720 | tf_op jit(solution)/shard_map/ppermute | solution.py:316
  21.4 19.9 %collective-permute-start.3 = (bf16[32,1936]{1,0:T(8,128)(2,1)S(1)}, bf16[32,1936]{1,0:T(8,128)(2,1)S(1)}, u32[]{:S(2)}, u32[]{:S(2)}) collective-permute-start(bf16[32,1936]{1,0:T(8,128)(2,1)S(1)} %copy-done.3), channel_id=1, source_target_pairs={{0,14},{2,12},{4,10},{6,8},{8,6},{10,4},{12,2},{14,0},{1,15},{3,13... | collective-permute-start | bytes 371720 | tf_op jit(solution)/shard_map/ppermute | solution.py:316
  44.0 2.0 %collective-permute-start.4 = (bf16[4,32,1936]{2,1,0:T(8,128)(2,1)S(1)}, bf16[4,32,1936]{2,1,0:T(8,128)(2,1)S(1)}, u32[]{:S(2)}, u32[]{:S(2)}) collective-permute-start(bf16[4,32,1936]{2,1,0:T(8,128)(2,1)S(1)} %get-tuple-element.26), channel_id=1, source_target_pairs={{0,1},{1,0},{2,3},{3,2},{4,5},{5,4},{6,7},{7,6},{8,9},{9,8},{10,11... | collective-permute-start | bytes 1486856 | tf_op jit(solution)/shard_map/ppermute | solution.py:334
  45.9 3.7 %copy-start.2 = (bf16[1936,128]{1,0:T(8,128)(2,1)S(1)}, bf16[1936,128]{1,0:T(8,128)(2,1)}, u32[]{:S(2)}) copy-start(bf16[1936,128]{1,0:T(8,128)(2,1)} %get-tuple-element.18.normed_ref) | copy-start | bytes 1486852
  46.1 5.6 %collective-permute-start.5 = (bf16[32,1936]{1,0:T(8,128)(2,1)S(1)}, bf16[32,1936]{1,0:T(8,128)(2,1)S(1)}, u32[]{:S(2)}, u32[]{:S(2)}) collective-permute-start(bf16[32,1936]{1,0:T(8,128)(2,1)S(1)} %get-tuple-element.28), channel_id=1, source_target_pairs={{0,2},{2,0},{4,6},{6,4},{8,10},{10,8},{12,14},{14,12},{1,3},{3,1},... | collective-permute-start | bytes 371720 | tf_op jit(solution)/shard_map/ppermute | solution.py:316
  46.7 6.4 %collective-permute-start.6 = (bf16[32,1936]{1,0:T(8,128)(2,1)S(1)}, bf16[32,1936]{1,0:T(8,128)(2,1)S(1)}, u32[]{:S(2)}, u32[]{:S(2)}) collective-permute-start(bf16[32,1936]{1,0:T(8,128)(2,1)S(1)} %get-tuple-element.29), channel_id=1, source_target_pairs={{0,4},{2,6},{4,0},{6,2},{8,12},{10,14},{12,8},{14,10},{1,5},{3,7},... | collective-permute-start | bytes 371720 | tf_op jit(solution)/shard_map/ppermute | solution.py:316
  46.7 9.0 %collective-permute-start.7 = (bf16[32,1936]{1,0:T(8,128)(2,1)S(1)}, bf16[32,1936]{1,0:T(8,128)(2,1)S(1)}, u32[]{:S(2)}, u32[]{:S(2)}) collective-permute-start(bf16[32,1936]{1,0:T(8,128)(2,1)S(1)} %get-tuple-element.30), channel_id=1, source_target_pairs={{0,6},{2,4},{4,2},{6,0},{8,14},{10,12},{12,10},{14,8},{1,7},{3,5},... | collective-permute-start | bytes 371720 | tf_op jit(solution)/shard_map/ppermute | solution.py:316
  50.0 0.7 %copy-start.7 = (f32[128]{0:T(128)S(1)}, f32[128]{0:T(128)}, u32[]{:S(2)}) copy-start(f32[128]{0:T(128)} %param.13) | copy-start | bytes 1540
  50.7 5.0 %copy-start.1 = (bf16[128,128]{1,0:T(8,128)(2,1)S(1)}, bf16[128,128]{1,0:T(8,128)(2,1)}, u32[]{:S(2)}) copy-start(bf16[128,128]{1,0:T(8,128)(2,1)} %w_ref.5) | copy-start | bytes 98308

commit v5 on v0

v5 whole, which is shorter than its diff:
```python
import functools

import jax
import jax.numpy as jnp
from jax import lax
from jax.experimental import pallas as pl
from jax.experimental.pallas import tpu as pltpu
from jax.sharding import PartitionSpec as P

EPS = 1e-05
LANES = 128
VMEM_LIMIT = 32 * 1024 * 1024
VMEM_FIRST = 60 * 1024 * 1024


def ceil_to(n, m):
    return -(-n // m) * m


def place_of(groups, rows, cols):
    row, col = lax.axis_index("row"), lax.axis_index("col")
    return row * rows, col * cols, lax.rem(row, groups), row // groups, col


def sigmoid(x):
    return 0.5 + 0.5 * jnp.tanh(0.5 * x)


def mask_of(cols, first_row, first_col, lens_ref, res_ref, at, block):
    position = at + lax.broadcasted_iota(jnp.int32, (8, block), 1)
    i_here = jnp.floor((position.astype(jnp.float32) + 0.5) * (1.0 / cols)).astype(jnp.int32)
    i_at = first_row + i_here
    k_at = first_col + position - i_here * cols
    i_ok = jnp.zeros((8, block), jnp.float32)
    k_ok = jnp.zeros((8, block), jnp.float32)
    start = 0
    for q in range(lens_ref.shape[0]):
        length = lens_ref[q]
        stop = start + jnp.minimum(length, res_ref[q])
        i_ok = jnp.where((i_at >= start) & (i_at < stop), 1.0, i_ok)
        k_ok = jnp.where((k_at >= start) & (k_at < stop), 1.0, k_ok)
        start = start + length
    return i_ok * k_ok


def edge_of(normed, w_ref, mask, groups):
    hidden = w_ref.shape[1] // 2
    block = normed.shape[0]
    projected = lax.dot_general(w_ref[...], normed, (((0,), (1,)), ((), ())), preferred_element_type=jnp.float32)
    edge = sigmoid(projected[:hidden]) * projected[hidden:]
    edge = edge.reshape(hidden // 8, 8, block) * mask[None]
    return edge.reshape(groups, hidden // groups, block).astype(jnp.bfloat16)


def edges_kernel(groups, rows, cols, chunks, pair_ref, gain_ref, wl_ref, wr_ref, lens_ref, res_ref, normed_ref, *refs):
    both_refs, right_refs = refs[:groups], refs[groups:2 * groups]
    x_s, gain_s, wl_s, wr_s, lens_s, res_s, normed_s, held, in_sems, out_sems = refs[2 * groups:]
    count = rows * cols
    first_row, first_col, mine, _, _ = place_of(groups, rows, cols)
    own = wl_ref.shape[1] // 2 // groups
    loads = [
        pltpu.make_async_copy(src, dst, in_sems.at[n])
        for n, (src, dst) in enumerate(
            [(gain_ref, gain_s), (lens_ref, lens_s), (res_ref, res_s), (wr_ref, wr_s), (wl_ref, wl_s)]
        )
    ]
    pieces = [
        pltpu.make_async_copy(pair_ref.at[pl.ds(at, size)], x_s.at[pl.ds(at, size)], in_sems.at[len(loads) + n])
        for n, (at, size) in enumerate(chunks)
    ]
    for copy in pieces[:1] + loads + pieces[1:]:
        copy.start()
    block = chunks[0][1]
    spare = x_s.shape[0] - count
    if spare:
        x_s[pl.ds(count, spare)] = jnp.zeros((spare, x_s.shape[1]), x_s.dtype)
    stores = []
    for n, (at, size) in enumerate(chunks):
        pieces[n].wait()
        x = x_s[pl.ds(at, block)].astype(jnp.float32)
        mean = jnp.mean(x, axis=-1, keepdims=True)
        centred = x - mean
        variance = jnp.mean(centred * centred, axis=-1, keepdims=True)
        if n == 0:
            for copy in loads:
                copy.wait()
        normed = (centred * lax.rsqrt(variance + EPS) * gain_s[...]).astype(jnp.bfloat16)
        normed_s[pl.ds(at, block)] = normed
        mask = mask_of(cols, first_row, first_col, lens_s, res_s, at, block)
        lanes = pl.ds(at, block)
        held[:, own:, lanes] = edge_of(normed, wr_s, mask, groups)
        held[:, :own, lanes] = edge_of(normed, wl_s, mask, groups)
        sent = [(normed_s.at[pl.ds(at, size)], normed_ref.at[pl.ds(at, size)])]
        for u in range(groups):
            group = jnp.bitwise_xor(mine, u)
            sent.append((held.at[group, pl.ds(own, own), lanes], right_refs[u].at[:, lanes]))
            sent.append((held.at[group, :, lanes], both_refs[u].at[:, lanes]))
        for m, (src, dst) in enumerate(sent):
            stores.append(pltpu.make_async_copy(src, dst, out_sems.at[n, m]))
            stores[-1].start()
    for copy in stores:
        copy.wait()


def make_edges(pair, lens, resolved, gain, w_left, w_right, groups, rows, cols):
    count, channels = pair.shape
    own = w_left.shape[1] // 2 // groups
    block = 512
    flat = ceil_to(count, block)
    chunks = [(at, min(block, count - at)) for at in range(0, count, block)]
    here = pl.BlockSpec(memory_space=pltpu.HBM)
    return pl.pallas_call(
        functools.partial(edges_kernel, groups, rows, cols, chunks),
        in_specs=[here] * 6,
        out_specs=[here] * (1 + 2 * groups),
        out_shape=[jax.ShapeDtypeStruct((count, channels), jnp.bfloat16)]
        + [jax.ShapeDtypeStruct((2 * own, flat), jnp.bfloat16)] * groups
        + [jax.ShapeDtypeStruct((own, flat), jnp.bfloat16)] * groups,
        scratch_shapes=[
            pltpu.VMEM((flat, channels), pair.dtype),
            pltpu.VMEM(gain.shape, gain.dtype),
            pltpu.VMEM(w_left.shape, w_left.dtype),
            pltpu.VMEM(w_right.shape, w_right.dtype),
            pltpu.SMEM(lens.shape, lens.dtype),
            pltpu.SMEM(resolved.shape, resolved.dtype),
            pltpu.VMEM((flat, channels), jnp.bfloat16),
            pltpu.VMEM((groups, 2 * own, flat), jnp.bfloat16),
            pltpu.SemaphoreType.DMA((5 + len(chunks),)),
            pltpu.SemaphoreType.DMA((len(chunks), 1 + 2 * groups)),
        ],
        compiler_params=pltpu.CompilerParams(vmem_limit_bytes=VMEM_FIRST),
    )(pair, gain, w_left, w_right, lens, resolved)


def unpack(got_ref, held_refs, block, rows, cols, step):
    tiles = pl.cdiv(cols, LANES)
    ch = got_ref.shape[0] // len(held_refs)
    lane = lax.broadcasted_iota(jnp.int32, (ch, LANES), 1)
    for n, held in enumerate(held_refs):
        seen = {}

        def tile_of(t):
            if t not in seen:
                seen[t] = got_ref[n * ch:(n + 1) * ch, pl.ds(t * LANES, LANES)].astype(jnp.float32)
            return seen[t]

        for i in range(rows):
            for tt in range(tiles):
                length = min(LANES, cols - LANES * tt)
                t0, off = divmod(cols * i + LANES * tt, LANES)
                piece = tile_of(t0)
                if off:
                    piece = pltpu.roll(piece, LANES - off, 1)
                if off + length > LANES:
                    piece = jnp.where(lane < LANES - off, piece, pltpu.roll(tile_of(t0 + 1), LANES - off, 1))
                if length < LANES and n == 0:
                    piece = jnp.where(lane < length, piece, 0.0)
                base = pl.multiple_of((block * rows + i) * step, 8)
                held[tt, pl.ds(base, ch), :] = piece


def pack(held, out_ref, u, block, rows, cols, step):
    tiles = pl.cdiv(cols, LANES)
    ch = out_ref.shape[1]
    lane = lax.broadcasted_iota(jnp.int32, (ch, LANES), 1)
    for t in range(out_ref.shape[2] // LANES):
        tile = None
        for i in range(rows):
            for tt in range(tiles):
                shift = cols * i + LANES * tt - LANES * t
                length = min(LANES, cols - LANES * tt)
                if shift >= LANES or shift + length <= 0:
                    continue
                base = pl.multiple_of((block * rows + i) * step, 8)
                piece = held[tt, pl.ds(base, ch), :]
                if shift % LANES:
                    piece = pltpu.roll(piece, shift % LANES, 1)
                tile = piece if tile is None else jnp.where(lane < shift, tile, piece)
        if tile is None:
            tile = jnp.zeros((ch, LANES), jnp.float32)
        out_ref[u, :, pl.ds(t * LANES, LANES)] = tile.astype(jnp.bfloat16)


def channel_of(held, d, count, step):
    lines = [held[t, pl.ds(d, count, stride=step), :] for t in range(held.shape[0])]
    return jnp.concatenate(lines, axis=1).astype(jnp.bfloat16)


def near_kernel(groups, rows, cols, after_ref, *refs):
    got_refs = refs[:groups]
    left_ref, near_ref, left_s, right_s, prod_s = refs[groups:]
    mine = place_of(groups, rows, cols)[2]
    step = left_s.shape[1] // (groups * rows)
    for u in range(groups):
        unpack(got_refs[u], (left_s, right_s), jnp.bitwise_xor(mine, u), rows, cols, step)
    for d in range(near_ref.shape[1]):
        left_ref[d] = channel_of(left_s, d, groups * rows, step)
        multiply(left_ref[d], channel_of(right_s, d, groups * rows, step), prod_s, d, step)
    for u in range(groups):
        pack(prod_s, near_ref, u, jnp.bitwise_xor(mine, u), rows, cols, step)


def lines_kernel(groups, rows, cols, count, *refs):
    got_refs, lines_ref = refs[:count], refs[-1]
    mine = place_of(groups, rows, cols)[2]
    step = lines_ref.shape[1] // (count * rows)
    for u in range(count):
        block = jnp.bitwise_and(jnp.bitwise_xor(mine, u), count - 1)
        unpack(got_refs[u], (lines_ref,), block, rows, cols, step)


def multiply(left, right, prod_s, d, step):
    count = left.shape[0]
    pad = prod_s.shape[0] * LANES - count
    if pad:
        right = jnp.concatenate([right, jnp.zeros((pad, right.shape[1]), right.dtype)], axis=0)
    prod = lax.dot_general(left, right, (((1,), (1,)), ((), ())), preferred_element_type=jnp.float32)
    for t in range(prod_s.shape[0]):
        prod_s[t, pl.ds(d, count, stride=step), :] = prod[:, t * LANES:(t + 1) * LANES]


def cross_kernel(groups, rows, cols, left_ref, near_ref, early_ref, late_ref, keep_ref, send_ref, right_s, prod_s, pair_s):
    _, _, mine, half, col = place_of(groups, rows, cols)
    step = prod_s.shape[1] // (groups * rows)
    size = early_ref.shape[1]
    base = pl.multiple_of(mine // (groups // 2) * size, 8)
    right_s[:, pl.ds(base, size), :] = early_ref[...]
    right_s[:, pl.ds(pl.multiple_of(size - base, 8), size), :] = late_ref[...]
    for d in range(keep_ref.shape[1]):
        multiply(left_ref[d], channel_of(right_s, d, groups * rows, step), prod_s, d, step)
    for u in range(groups):
        pack(prod_s, pair_s, u, jnp.bitwise_xor(mine, u), rows, cols, step)
    near_kept = col == half
    keep_ref[...] = jnp.where(near_kept, near_ref[...], pair_s[...])
    send_ref[...] = jnp.where(near_kept, pair_s[...], near_ref[...])


def make_near(got, after, rows, cols):
    groups = len(got)
    both, flat = got[0].shape
    ch = both // 2
    count = groups * rows
    tiles = pl.cdiv(cols, LANES)
    held = pltpu.VMEM((tiles, count * ceil_to(ch, 8), LANES), jnp.float32)
    whole = pl.BlockSpec(memory_space=pltpu.VMEM)
    return pl.pallas_call(
        functools.partial(near_kernel, groups, rows, cols),
        in_specs=[pl.BlockSpec(memory_space=pl.ANY)] + [whole] * groups,
        out_specs=[whole] * 2,
        out_shape=[
            jax.ShapeDtypeStruct((ch, count, tiles * LANES), jnp.bfloat16),
            jax.ShapeDtypeStruct((groups, ch, flat), jnp.bfloat16),
        ],
        scratch_shapes=[held, held, held],
        compiler_params=pltpu.CompilerParams(vmem_limit_bytes=VMEM_LIMIT),
        cost_estimate=pl.CostEstimate(flops=10 ** 5, bytes_accessed=10 ** 5, transcendentals=0),
    )(after, *got)


def make_lines(got, groups, rows, cols, cost, after=()):
    ch = got[0].shape[0]
    whole = pl.BlockSpec(memory_space=pltpu.VMEM)
    lines = (pl.cdiv(cols, LANES), len(got) * rows * ceil_to(ch, 8), LANES)
    return pl.pallas_call(
        functools.partial(lines_kernel, groups, rows, cols, len(got)),
        in_specs=[whole] * len(got) + [pl.BlockSpec(memory_space=pl.ANY)] * len(after),
        out_specs=whole,
        out_shape=jax.ShapeDtypeStruct(lines, jnp.float32),
        compiler_params=pltpu.CompilerParams(vmem_limit_bytes=VMEM_LIMIT),
        cost_estimate=pl.CostEstimate(flops=10 ** 5, bytes_accessed=cost, transcendentals=0),
    )(*got, *after)


def make_cross(left, near, early, late, rows, cols):
    groups, ch, flat = near.shape
    whole = pl.BlockSpec(memory_space=pltpu.VMEM)
    held = pltpu.VMEM((pl.cdiv(cols, LANES), groups * rows * ceil_to(ch, 8), LANES), jnp.float32)
    return pl.pallas_call(
        functools.partial(cross_kernel, groups, rows, cols),
        in_specs=[whole] * 4,
        out_specs=[whole] * 2,
        out_shape=[jax.ShapeDtypeStruct(near.shape, near.dtype)] * 2,
        scratch_shapes=[held, held, pltpu.VMEM(near.shape, near.dtype)],
        compiler_params=pltpu.CompilerParams(vmem_limit_bytes=VMEM_LIMIT),
        cost_estimate=pl.CostEstimate(flops=10 ** 5, bytes_accessed=8 * 10 ** 6, transcendentals=0),
    )(left, near, early, late)


def add_kernel(a_ref, b_ref, *out_refs):
    for u, out_ref in enumerate(out_refs):
        out_ref[...] = (a_ref[u].astype(jnp.float32) + b_ref[u].astype(jnp.float32)).astype(out_ref.dtype)


def make_sums(a, b):
    groups, ch, flat = a.shape
    whole = pl.BlockSpec(memory_space=pltpu.VMEM)
    return pl.pallas_call(
        add_kernel,
        in_specs=[whole] * 2,
        out_specs=[whole] * groups,
        out_shape=[jax.ShapeDtypeStruct((ch, flat), a.dtype)] * groups,
        compiler_params=pltpu.CompilerParams(vmem_limit_bytes=VMEM_LIMIT),
        cost_estimate=pl.CostEstimate(flops=10 ** 5, bytes_accessed=10 ** 5, transcendentals=0),
    )(a, b)


def update_kernel(groups, rows, cols, chunks, gain_ref, w_ref, gate_ref, *refs):
    prod_refs = refs[:groups]
    out_ref, held, out_s, sems = refs[groups:]
    mine = place_of(groups, rows, cols)[2]
    ch = held.shape[1]
    block = held.shape[2]
    stores = []
    for n, (at, size) in enumerate(chunks):
        lanes = pl.ds(at, block)
        for u in range(groups):
            held[jnp.bitwise_xor(mine, u)] = prod_refs[u][:, lanes].astype(jnp.float32)
        prod = held[...].reshape(groups * ch, block)
        mean = jnp.mean(prod, axis=0, keepdims=True)
        centred = prod - mean
        variance = jnp.mean(centred * centred, axis=0, keepdims=True)
        normed = (centred * lax.rsqrt(variance + EPS) * gain_ref[...]).astype(jnp.bfloat16)
        projected = lax.dot_general(normed, w_ref[...], (((0,), (0,)), ((), ())), preferred_element_type=jnp.float32)
        out_s[pl.ds(at, size)] = (gate_ref[pl.ds(at, size)] * projected[:size]).astype(out_s.dtype)
        stores.append(pltpu.make_async_copy(out_s.at[pl.ds(at, size)], out_ref.at[pl.ds(at, size)], sems.at[n]))
        stores[-1].start()
    for copy in stores:
        copy.wait()


def make_update(prods, gain, w_out, gate, rows, cols):
    groups = len(prods)
    ch = prods[0].shape[0]
    count, channels = gate.shape
    block = 512
    chunks = [(at, min(block, count - at)) for at in range(0, count, block)]
    whole = pl.BlockSpec(memory_space=pltpu.VMEM)
    return pl.pallas_call(
        functools.partial(update_kernel, groups, rows, cols, chunks),
        in_specs=[whole] * (3 + groups),
        out_specs=pl.BlockSpec(memory_space=pltpu.HBM),
        out_shape=jax.ShapeDtypeStruct((count, channels), jnp.bfloat16),
        scratch_shapes=[
            pltpu.VMEM((groups, ch, block), jnp.float32),
            pltpu.VMEM((count, channels), jnp.bfloat16),
            pltpu.SemaphoreType.DMA((len(chunks),)),
        ],
        compiler_params=pltpu.CompilerParams(vmem_limit_bytes=VMEM_LIMIT),
    )(gain, w_out, gate, *prods)


def swap(value, shift):
    return lax.ppermute(value, "row", [(r, r ^ shift) for r in range(lax.axis_size("row"))])


def shards(pair_act, chain_lengths, resolved, in_gain, out_gain, w_left, w_right, w_gate, w_out):
    rows, cols, channels = pair_act.shape
    hidden = w_out.shape[0]
    groups = lax.axis_size("row") // 2
    normed, *edges = make_edges(
        pair_act.reshape(rows * cols, channels), chain_lengths, resolved,
        in_gain.reshape(1, channels), w_left, w_right, groups, rows, cols,
    )
    both, right = edges[:groups], edges[groups:]
    far_got = [swap(right[u], groups + u) for u in range(groups)]
    near_got = [both[0]] + [swap(both[u], u) for u in range(1, groups)]
    gate = jax.nn.sigmoid(jnp.dot(normed, w_gate, preferred_element_type=jnp.float32))
    half = groups // 2
    early = make_lines(far_got[:half], groups, rows, cols, 10 ** 8)
    left, near = make_near(near_got, early, rows, cols)
    late = make_lines(far_got[half:], groups, rows, cols, 10 ** 5, (left,))
    keep, send = make_cross(left, near, early, late, rows, cols)
    sums = make_sums(keep, lax.ppermute(send, "col", [(0, 1), (1, 0)]))
    returned = [sums[0]] + [swap(sums[u], u) for u in range(1, groups)]
    update = make_update(returned, out_gain.reshape(hidden, 1), w_out, gate, rows, cols)
    return update.reshape(rows, cols, channels)


def solution(mesh):
    return jax.shard_map(
        shards,
        mesh=mesh,
        in_specs=(P(("grp", "row"), "col", None), P("grp"), P("grp"), P(), P(), P(), P(), P(), P()),
        out_specs=P(("grp", "row"), "col", None),
        check_vma=False,
    )
```

time: 111 us -> 51.1 us (0.46)
  the two profiles are of different devices: /device:TPU:15 before, /device:TPU:0 now
where the time goes in v5:
time: 51.1 us; the launch traced here: 50.9 us
  waiting for transfers between devices  19.1 us (37%)
  starting transfers between devices  18.4 us (36%)
  Pallas kernels  12.2 us (24%)
  local copies, waits for them, and re-layouts  0.78 us (2%)
    ppermute x10, starting transfers between devices, swap(): lax.ppermute(value, 'row', [(r, r ^ shift) for r in range(lax.axis_size('...  18.3 us
    ppermute x10, waiting for transfers between devices, swap(): lax.ppermute(value, 'row', [(r, r ^ shift) for r in range(lax.axis_size('...  17.2 us
    pallas_call x1, Pallas kernels, make_edges(): pl.pallas_call(functools.partial(edges_kernel, groups, rows, cols, chunks...  4.16 us
    pallas_call x1, Pallas kernels, make_near(): pl.pallas_call(functools.partial(near_kernel, groups, rows, cols), in_spe...  3.66 us
    pallas_call x1, Pallas kernels, make_cross(): pl.pallas_call(functools.partial(cross_kernel, groups, rows, cols), in_sp...  2.38 us
    ppermute x1, waiting for transfers between devices, shards(): sums = make_sums(keep, lax.ppermute(send, 'col', [(0, 1), (1, 0)]))  1.9 us
    pallas_call x1, Pallas kernels, make_update(): pl.pallas_call(functools.partial(update_kernel, groups, rows, cols, chunk...  1.42 us
  transfers between devices with their start and end apart: 11, of which 7 were waited for; matrix products, arithmetic and copies ran while one was open for 1% of the time, Pallas kernels for 8%

profile of v5, /device:TPU:0, one launch (start us, length us, event | category | flops | bytes accessed | tf_op | source)
XLA Modules:
  0.0 50.9 jit_solution(9749703085082745383)
XLA Ops:
  0.0 0.0 copy-start
  0.0 4.2 %shard_map.91 = (bf16[1936,128]{1,0:T(8,128)(2,1)}, bf16[64,2048]{1,0:T(8,128)(2,1)}, bf16[64,2048]{1,0:T(8,128)(2,1)}, bf16[64,2048]{1,0:T(8,128)(2,1)}, bf16[6...) custom-call(bf16[1936,128]{1,0:T(8,128)(2,1)} %bitcast.6, ...), custom_call_target="tpu_custom_call" | custom-call | tf_op jit(solution)/shard_map/pallas_call | solution.py:112
  4.2 4.1 %collective-permute-start = (bf16[32,2048]{1,0:T(8,128)(2,1)}, bf16[32,2048]{1,0:T(8,128)(2,1)S(1)}, u32[]{:S(2)}, u32[]{:S(2)}) collective-permute-start(bf16[32,2048]{1,0:T(8,128)(2,1)} %get-tuple-element.23), channel_id=1, source_target_pairs={{0,8},{2,10},{4,12},{6,14},{8,0},{10,2},{12,4},{14,6},{1,9},{3,11}... | collective-permute-start | bytes 393224 | tf_op jit(solution)/shard_map/ppermute | solution.py:353
  8.3 1.5 %collective-permute-start.2 = (bf16[64,2048]{1,0:T(8,128)(2,1)}, bf16[64,2048]{1,0:T(8,128)(2,1)S(1)}, u32[]{:S(2)}, u32[]{:S(2)}) collective-permute-start(bf16[64,2048]{1,0:T(8,128)(2,1)} %get-tuple-element.26), channel_id=1, source_target_pairs={{0,2},{2,0},{4,6},{6,4},{8,10},{10,8},{12,14},{14,12},{1,3},{3,1},... | collective-permute-start | bytes 786440 | tf_op jit(solution)/shard_map/ppermute | solution.py:353
  9.8 1.6 %collective-permute-start.3 = (bf16[64,2048]{1,0:T(8,128)(2,1)}, bf16[64,2048]{1,0:T(8,128)(2,1)S(1)}, u32[]{:S(2)}, u32[]{:S(2)}) collective-permute-start(bf16[64,2048]{1,0:T(8,128)(2,1)} %get-tuple-element.27), channel_id=1, source_target_pairs={{0,4},{2,6},{4,0},{6,2},{8,12},{10,14},{12,8},{14,10},{1,5},{3,7},... | collective-permute-start | bytes 786440 | tf_op jit(solution)/shard_map/ppermute | solution.py:353
  11.4 0.4 collective-permute-start.4
  11.8 1.3 %collective-permute-start.1 = (bf16[32,2048]{1,0:T(8,128)(2,1)}, bf16[32,2048]{1,0:T(8,128)(2,1)S(1)}, u32[]{:S(2)}, u32[]{:S(2)}) collective-permute-start(bf16[32,2048]{1,0:T(8,128)(2,1)} %get-tuple-element.24), channel_id=1, source_target_pairs={{0,10},{2,8},{4,14},{6,12},{8,2},{10,0},{12,6},{14,4},{1,11},{3,9}... | collective-permute-start | bytes 393224 | tf_op jit(solution)/shard_map/ppermute | solution.py:353
  13.1 1.8 %collective-permute-done.refs_0_ = bf16[32,2048]{1,0:T(8,128)(2,1)S(1)} collective-permute-done((bf16[32,2048]{1,0:T(8,128)(2,1)}, bf16[32,2048]{1,0:T(8,128)(2,1)S(1)}, u32[]{:S(2)}, u32[]{:S(2)}) %collective-permute-start) | collective-permute-done | bytes 131104 | tf_op jit(solution)/shard_map/ppermute | solution.py:353
  14.9 3.6 %collective-permute-start.5 = (bf16[32,2048]{1,0:T(8,128)(2,1)}, bf16[32,2048]{1,0:T(8,128)(2,1)S(1)}, u32[]{:S(2)}, u32[]{:S(2)}) collective-permute-start(bf16[32,2048]{1,0:T(8,128)(2,1)} %get-tuple-element.31), channel_id=1, source_target_pairs={{0,12},{2,14},{4,8},{6,10},{8,4},{10,6},{12,0},{14,2},{1,13},{3,15... | collective-permute-start | bytes 393224 | tf_op jit(solution)/shard_map/ppermute | solution.py:353
  18.5 8.3 %collective-permute-done.1.refs_1_ = bf16[32,2048]{1,0:T(8,128)(2,1)S(1)} collective-permute-done((bf16[32,2048]{1,0:T(8,128)(2,1)}, bf16[32,2048]{1,0:T(8,128)(2,1)S(1)}, u32[]{:S(2)}, u32[]{:S(2)}) %collective-permute-start.1) | collective-permute-done | bytes 131104 | tf_op jit(solution)/shard_map/ppermute | solution.py:353
  26.8 0.0 copy-start.1
  26.8 2.0 %collective-permute-start.6 = (bf16[32,2048]{1,0:T(8,128)(2,1)}, bf16[32,2048]{1,0:T(8,128)(2,1)S(1)}, u32[]{:S(2)}, u32[]{:S(2)}) collective-permute-start(bf16[32,2048]{1,0:T(8,128)(2,1)} %get-tuple-element.32), channel_id=1, source_target_pairs={{0,14},{2,12},{4,10},{6,8},{8,6},{10,4},{12,2},{14,0},{1,15},{3,13... | collective-permute-start | bytes 393224 | tf_op jit(solution)/shard_map/ppermute | solution.py:353
  28.8 0.2 shard_map.92.after_ref.early_ref
  29.1 0.0 collective-permute-done.2.refs_1_
  29.1 0.0 collective-permute-done.3.refs_2_
  29.1 0.0 collective-permute-done.4.refs_3_
  29.1 0.0 copy-done.1
  29.1 3.7 %shard_map.93 = (bf16[32,88,128]{2,1,0:T(8,128)(2,1)S(1)}, bf16[4,32,2048]{2,1,0:T(8,128)(2,1)S(1)}) custom-call(f32[1,1408,128]{2,1,0:T(8,128)S(1)} %shard_map.92.after_ref.early_ref, bf16[64,2048]{1,0:T(8,128)(2,1)S(1)} %copy-done.1, bf16[64,2048]{1,0:T(8,128)(2,1)S(1)} %collective-permute-done.2.refs_1_, ...), custom_call_target="tpu_custom_call" | custom-call | flops 100000 | bytes 100000 | tf_op jit(solution)/shard_map/pallas_call | solution.py:246
  32.8 0.0 collective-permute-done.5.refs_0_
  32.8 2.1 %collective-permute-done.6.refs_1_ = bf16[32,2048]{1,0:T(8,128)(2,1)S(1)} collective-permute-done((bf16[32,2048]{1,0:T(8,128)(2,1)}, bf16[32,2048]{1,0:T(8,128)(2,1)S(1)}, u32[]{:S(2)}, u32[]{:S(2)}) %collective-permute-start.6) | collective-permute-done | bytes 131104 | tf_op jit(solution)/shard_map/ppermute | solution.py:353
  34.8 0.2 shard_map.94.late_ref
  35.0 2.4 %shard_map.95 = (bf16[4,32,2048]{2,1,0:T(8,128)(2,1)S(1)}, bf16[4,32,2048]{2,1,0:T(8,128)(2,1)S(1)}) custom-call(bf16[32,88,128]{2,1,0:T(8,128)(2,1)S(1)} %get-tuple-element.29.refs_2_.left_ref, bf16[4,32,2048]{2,1,0:T(8,128)(2,1)S(1)} %get-tuple-element.30.near_ref, f32[1,1408,128]{2,1,0:T(8,128)S(1)} %shard_map.92.after_ref.early_ref, ...), custom_call_target="tpu_custom_call" | custom-call | flops 100000 | bytes 8000000 | tf_op jit(solution)/shard_map/pallas_call | solution.py:278
  37.4 0.1 collective-permute-start.7
  37.5 1.9 %collective-permute-done.7.b_ref = bf16[4,32,2048]{2,1,0:T(8,128)(2,1)S(1)} collective-permute-done((bf16[4,32,2048]{2,1,0:T(8,128)(2,1)S(1)}, bf16[4,32,2048]{2,1,0:T(8,128)(2,1)S(1)}, u32[]{:S(2)}, u32[]{:S(2)}) %collective-permute-start.7) | collective-permute-done | bytes 524320 | tf_op jit(solution)/shard_map/ppermute | solution.py:373
  39.4 0.0 copy-start.4
  39.4 0.1 shard_map.96
  39.5 2.4 %collective-permute-start.10 = (bf16[32,2048]{1,0:T(8,128)(2,1)S(1)}, bf16[32,2048]{1,0:T(8,128)(2,1)S(1)}, u32[]{:S(2)}, u32[]{:S(2)}) collective-permute-start(bf16[32,2048]{1,0:T(8,128)(2,1)S(1)} %get-tuple-element.38), channel_id=1, source_target_pairs={{0,6},{2,4},{4,2},{6,0},{8,14},{10,12},{12,10},{14,8},{1,7},{3,5},... | collective-permute-start | bytes 393224 | tf_op jit(solution)/shard_map/ppermute | solution.py:353
  42.0 1.4 %collective-permute-start.8 = (bf16[32,2048]{1,0:T(8,128)(2,1)S(1)}, bf16[32,2048]{1,0:T(8,128)(2,1)S(1)}, u32[]{:S(2)}, u32[]{:S(2)}) collective-permute-start(bf16[32,2048]{1,0:T(8,128)(2,1)S(1)} %get-tuple-element.36), channel_id=1, source_target_pairs={{0,2},{2,0},{4,6},{6,4},{8,10},{10,8},{12,14},{14,12},{1,3},{3,1},... | collective-permute-start | bytes 393224 | tf_op jit(solution)/shard_map/ppermute | solution.py:353
  43.3 0.0 collective-permute-start.9
  43.3 0.0 copy-done
  43.3 0.0 copy-done.4
  43.3 0.4 fusion.2.gate_ref
  43.8 0.0 copy-start.3
  43.8 0.6 %copy-done.3 = f32[128]{0:T(128)S(1)} copy-done((f32[128]{0:T(128)S(1)}, f32[128]{0:T(128)}, u32[]{:S(2)}) %copy-start.3) | copy-done | bytes 536
  44.4 0.0 copy-start.2
  44.4 0.1 copy.10.gain_ref
  44.5 1.9 %collective-permute-done.10.refs_3_ = bf16[32,2048]{1,0:T(8,128)(2,1)S(1)} collective-permute-done((bf16[32,2048]{1,0:T(8,128)(2,1)S(1)}, bf16[32,2048]{1,0:T(8,128)(2,1)S(1)}, u32[]{:S(2)}, u32[]{:S(2)}) %collective-permute-start.10) | collective-permute-done | bytes 131104 | tf_op jit(solution)/shard_map/ppermute | solution.py:353
  46.4 2.4 %collective-permute-done.8.refs_1_ = bf16[32,2048]{1,0:T(8,128)(2,1)S(1)} collective-permute-done((bf16[32,2048]{1,0:T(8,128)(2,1)S(1)}, bf16[32,2048]{1,0:T(8,128)(2,1)S(1)}, u32[]{:S(2)}, u32[]{:S(2)}) %collective-permute-start.8) | collective-permute-done | bytes 131104 | tf_op jit(solution)/shard_map/ppermute | solution.py:353
  48.8 0.7 %collective-permute-done.9.refs_2_ = bf16[32,2048]{1,0:T(8,128)(2,1)S(1)} collective-permute-done((bf16[32,2048]{1,0:T(8,128)(2,1)S(1)}, bf16[32,2048]{1,0:T(8,128)(2,1)S(1)}, u32[]{:S(2)}, u32[]{:S(2)}) %collective-permute-start.9) | collective-permute-done | bytes 131104 | tf_op jit(solution)/shard_map/ppermute | solution.py:353
  49.5 0.0 copy-done.2
  49.5 1.4 %shard_map.97 = bf16[1936,128]{1,0:T(8,128)(2,1)} custom-call(f32[128,1]{1,0:T(8,128)S(1)} %copy.10.gain_ref, bf16[128,128]{1,0:T(8,128)(2,1)S(1)} %copy-done.2, f32[1936,128]{1,0:T(8,128)S(1)} %fusion.2.gate_ref, bf16[32,2048]{1,0:T(8,128)(2,1)S(1)} %get-tuple-element.35.refs_0_, bf16[32,2048]{1,0:T(8,128)(2,1)S(1)} %collective-permute-done.8.refs_1_, ...), custom_call_target="tpu_custom_call" | custom-call | tf_op jit(solution)/shard_map/pallas_call | solution.py:338
Async XLA Ops:
  0.0 43.3 %copy-start = (bf16[128,128]{1,0:T(8,128)(2,1)S(1)}, bf16[128,128]{1,0:T(8,128)(2,1)}, u32[]{:S(2)}) copy-start(bf16[128,128]{1,0:T(8,128)(2,1)} %param.16) | copy-start | bytes 98308
  4.2 10.7 %collective-permute-start = (bf16[32,2048]{1,0:T(8,128)(2,1)}, bf16[32,2048]{1,0:T(8,128)(2,1)S(1)}, u32[]{:S(2)}, u32[]{:S(2)}) collective-permute-start(bf16[32,2048]{1,0:T(8,128)(2,1)} %get-tuple-element.23), channel_id=1, source_target_pairs={{0,8},{2,10},{4,12},{6,14},{8,0},{10,2},{12,4},{14,6},{1,9},{3,11}... | collective-permute-start | bytes 393224 | tf_op jit(solution)/shard_map/ppermute | solution.py:353
  8.3 20.8 %collective-permute-start.2 = (bf16[64,2048]{1,0:T(8,128)(2,1)}, bf16[64,2048]{1,0:T(8,128)(2,1)S(1)}, u32[]{:S(2)}, u32[]{:S(2)}) collective-permute-start(bf16[64,2048]{1,0:T(8,128)(2,1)} %get-tuple-element.26), channel_id=1, source_target_pairs={{0,2},{2,0},{4,6},{6,4},{8,10},{10,8},{12,14},{14,12},{1,3},{3,1},... | collective-permute-start | bytes 786440 | tf_op jit(solution)/shard_map/ppermute | solution.py:353
  9.8 19.3 %collective-permute-start.3 = (bf16[64,2048]{1,0:T(8,128)(2,1)}, bf16[64,2048]{1,0:T(8,128)(2,1)S(1)}, u32[]{:S(2)}, u32[]{:S(2)}) collective-permute-start(bf16[64,2048]{1,0:T(8,128)(2,1)} %get-tuple-element.27), channel_id=1, source_target_pairs={{0,4},{2,6},{4,0},{6,2},{8,12},{10,14},{12,8},{14,10},{1,5},{3,7},... | collective-permute-start | bytes 786440 | tf_op jit(solution)/shard_map/ppermute | solution.py:353
  11.4 17.7 %collective-permute-start.4 = (bf16[64,2048]{1,0:T(8,128)(2,1)}, bf16[64,2048]{1,0:T(8,128)(2,1)S(1)}, u32[]{:S(2)}, u32[]{:S(2)}) collective-permute-start(bf16[64,2048]{1,0:T(8,128)(2,1)} %get-tuple-element.28), channel_id=1, source_target_pairs={{0,6},{2,4},{4,2},{6,0},{8,14},{10,12},{12,10},{14,8},{1,7},{3,5},... | collective-permute-start | bytes 786440 | tf_op jit(solution)/shard_map/ppermute | solution.py:353
  11.8 15.1 %collective-permute-start.1 = (bf16[32,2048]{1,0:T(8,128)(2,1)}, bf16[32,2048]{1,0:T(8,128)(2,1)S(1)}, u32[]{:S(2)}, u32[]{:S(2)}) collective-permute-start(bf16[32,2048]{1,0:T(8,128)(2,1)} %get-tuple-element.24), channel_id=1, source_target_pairs={{0,10},{2,8},{4,14},{6,12},{8,2},{10,0},{12,6},{14,4},{1,11},{3,9}... | collective-permute-start | bytes 393224 | tf_op jit(solution)/shard_map/ppermute | solution.py:353
  14.9 17.9 %collective-permute-start.5 = (bf16[32,2048]{1,0:T(8,128)(2,1)}, bf16[32,2048]{1,0:T(8,128)(2,1)S(1)}, u32[]{:S(2)}, u32[]{:S(2)}) collective-permute-start(bf16[32,2048]{1,0:T(8,128)(2,1)} %get-tuple-element.31), channel_id=1, source_target_pairs={{0,12},{2,14},{4,8},{6,10},{8,4},{10,6},{12,0},{14,2},{1,13},{3,15... | collective-permute-start | bytes 393224 | tf_op jit(solution)/shard_map/ppermute | solution.py:353
  26.8 2.2 %copy-start.1 = (bf16[64,2048]{1,0:T(8,128)(2,1)S(1)}, bf16[64,2048]{1,0:T(8,128)(2,1)}, u32[]{:S(2)}) copy-start(bf16[64,2048]{1,0:T(8,128)(2,1)} %get-tuple-element.25.refs_0_) | copy-start | bytes 786436
  26.8 8.0 %collective-permute-start.6 = (bf16[32,2048]{1,0:T(8,128)(2,1)}, bf16[32,2048]{1,0:T(8,128)(2,1)S(1)}, u32[]{:S(2)}, u32[]{:S(2)}) collective-permute-start(bf16[32,2048]{1,0:T(8,128)(2,1)} %get-tuple-element.32), channel_id=1, source_target_pairs={{0,14},{2,12},{4,10},{6,8},{8,6},{10,4},{12,2},{14,0},{1,15},{3,13... | collective-permute-start | bytes 393224 | tf_op jit(solution)/shard_map/ppermute | solution.py:353
  37.4 2.0 %collective-permute-start.7 = (bf16[4,32,2048]{2,1,0:T(8,128)(2,1)S(1)}, bf16[4,32,2048]{2,1,0:T(8,128)(2,1)S(1)}, u32[]{:S(2)}, u32[]{:S(2)}) collective-permute-start(bf16[4,32,2048]{2,1,0:T(8,128)(2,1)S(1)} %get-tuple-element.34), channel_id=1, source_target_pairs={{0,1},{1,0},{2,3},{3,2},{4,5},{5,4},{6,7},{7,6},{8,9},{9,8},{10,11... | collective-permute-start | bytes 1572872 | tf_op jit(solution)/shard_map/ppermute | solution.py:373
  39.4 3.9 %copy-start.4 = (bf16[1936,128]{1,0:T(8,128)(2,1)S(1)}, bf16[1936,128]{1,0:T(8,128)(2,1)}, u32[]{:S(2)}) copy-start(bf16[1936,128]{1,0:T(8,128)(2,1)} %get-tuple-element.22) | copy-start | bytes 1486852
  39.5 6.9 %collective-permute-start.10 = (bf16[32,2048]{1,0:T(8,128)(2,1)S(1)}, bf16[32,2048]{1,0:T(8,128)(2,1)S(1)}, u32[]{:S(2)}, u32[]{:S(2)}) collective-permute-start(bf16[32,2048]{1,0:T(8,128)(2,1)S(1)} %get-tuple-element.38), channel_id=1, source_target_pairs={{0,6},{2,4},{4,2},{6,0},{8,14},{10,12},{12,10},{14,8},{1,7},{3,5},... | collective-permute-start | bytes 393224 | tf_op jit(solution)/shard_map/ppermute | solution.py:353
  42.0 6.9 %collective-permute-start.8 = (bf16[32,2048]{1,0:T(8,128)(2,1)S(1)}, bf16[32,2048]{1,0:T(8,128)(2,1)S(1)}, u32[]{:S(2)}, u32[]{:S(2)}) collective-permute-start(bf16[32,2048]{1,0:T(8,128)(2,1)S(1)} %get-tuple-element.36), channel_id=1, source_target_pairs={{0,2},{2,0},{4,6},{6,4},{8,10},{10,8},{12,14},{14,12},{1,3},{3,1},... | collective-permute-start | bytes 393224 | tf_op jit(solution)/shard_map/ppermute | solution.py:353
  43.3 6.2 %collective-permute-start.9 = (bf16[32,2048]{1,0:T(8,128)(2,1)S(1)}, bf16[32,2048]{1,0:T(8,128)(2,1)S(1)}, u32[]{:S(2)}, u32[]{:S(2)}) collective-permute-start(bf16[32,2048]{1,0:T(8,128)(2,1)S(1)} %get-tuple-element.37), channel_id=1, source_target_pairs={{0,4},{2,6},{4,0},{6,2},{8,12},{10,14},{12,8},{14,10},{1,5},{3,7},... | collective-permute-start | bytes 393224 | tf_op jit(solution)/shard_map/ppermute | solution.py:353
  43.8 0.7 %copy-start.3 = (f32[128]{0:T(128)S(1)}, f32[128]{0:T(128)}, u32[]{:S(2)}) copy-start(f32[128]{0:T(128)} %param.13) | copy-start | bytes 1540
  44.4 5.1 %copy-start.2 = (bf16[128,128]{1,0:T(8,128)(2,1)S(1)}, bf16[128,128]{1,0:T(8,128)(2,1)}, u32[]{:S(2)}) copy-start(bf16[128,128]{1,0:T(8,128)(2,1)} %w_ref.1) | copy-start | bytes 98308

commit v6 on v5

--- a/solution.py
+++ b/solution.py
@@ -15,6 +15,10 @@
 
 def ceil_to(n, m):
     return -(-n // m) * m
+
+
+def line_step(ch):
+    return (ceil_to(ch, 8) // 8 | 1) * 8
 
 
 def place_of(groups, rows, cols):
@@ -53,8 +57,8 @@
 
 
 def edges_kernel(groups, rows, cols, chunks, pair_ref, gain_ref, wl_ref, wr_ref, lens_ref, res_ref, normed_ref, *refs):
-    both_refs, right_refs = refs[:groups], refs[groups:2 * groups]
-    x_s, gain_s, wl_s, wr_s, lens_s, res_s, normed_s, held, in_sems, out_sems = refs[2 * groups:]
+    both_ref, right_refs = refs[0], refs[1:1 + groups]
+    x_s, gain_s, wl_s, wr_s, lens_s, res_s, normed_s, held, in_sems, out_sems = refs[1 + groups:]
     count = rows * cols
     first_row, first_col, mine, _, _ = place_of(groups, rows, cols)
     own = wl_ref.shape[1] // 2 // groups
@@ -71,16 +75,20 @@
     for copy in pieces[:1] + loads + pieces[1:]:
         copy.start()
     block = chunks[0][1]
+    channels = x_s.shape[1]
+    average = jnp.full((2 * channels, channels), 1.0 / channels, jnp.bfloat16)
     spare = x_s.shape[0] - count
     if spare:
         x_s[pl.ds(count, spare)] = jnp.zeros((spare, x_s.shape[1]), x_s.dtype)
     stores = []
     for n, (at, size) in enumerate(chunks):
         pieces[n].wait()
-        x = x_s[pl.ds(at, block)].astype(jnp.float32)
-        mean = jnp.mean(x, axis=-1, keepdims=True)
-        centred = x - mean
-        variance = jnp.mean(centred * centred, axis=-1, keepdims=True)
+        x = x_s[pl.ds(at, block)]
+        centred = x.astype(jnp.float32) - jnp.dot(x, average[:channels], preferred_element_type=jnp.float32)
+        square = centred * centred
+        high = square.astype(jnp.bfloat16)
+        low = (square - high.astype(jnp.float32)).astype(jnp.bfloat16)
+        variance = jnp.dot(jnp.concatenate([high, low], axis=1), average, preferred_element_type=jnp.float32)
         if n == 0:
             for copy in loads:
                 copy.wait()
@@ -90,11 +98,12 @@
         lanes = pl.ds(at, block)
         held[:, own:, lanes] = edge_of(normed, wr_s, mask, groups)
         held[:, :own, lanes] = edge_of(normed, wl_s, mask, groups)
-        sent = [(normed_s.at[pl.ds(at, size)], normed_ref.at[pl.ds(at, size)])]
-        for u in range(groups):
-            group = jnp.bitwise_xor(mine, u)
-            sent.append((held.at[group, pl.ds(own, own), lanes], right_refs[u].at[:, lanes]))
-            sent.append((held.at[group, :, lanes], both_refs[u].at[:, lanes]))
+        sent = [
+            (held.at[jnp.bitwise_xor(mine, u), pl.ds(own, own), lanes], right_refs[u].at[:, lanes])
+            for u in range(groups)
+        ]
+        sent.append((held.at[:, :, lanes], both_ref.at[:, :, lanes]))
+        sent.append((normed_s.at[pl.ds(at, size)], normed_ref.at[pl.ds(at, size)]))
         for m, (src, dst) in enumerate(sent):
             stores.append(pltpu.make_async_copy(src, dst, out_sems.at[n, m]))
             stores[-1].start()
@@ -112,9 +121,9 @@
     return pl.pallas_call(
         functools.partial(edges_kernel, groups, rows, cols, chunks),
         in_specs=[here] * 6,
-        out_specs=[here] * (1 + 2 * groups),
+        out_specs=[here] * (2 + groups),
         out_shape=[jax.ShapeDtypeStruct((count, channels), jnp.bfloat16)]
-        + [jax.ShapeDtypeStruct((2 * own, flat), jnp.bfloat16)] * groups
+        + [jax.ShapeDtypeStruct((groups, 2 * own, flat), jnp.bfloat16)]
         + [jax.ShapeDtypeStruct((own, flat), jnp.bfloat16)] * groups,
         scratch_shapes=[
             pltpu.VMEM((flat, channels), pair.dtype),
@@ -126,7 +135,7 @@
             pltpu.VMEM((flat, channels), jnp.bfloat16),
             pltpu.VMEM((groups, 2 * own, flat), jnp.bfloat16),
             pltpu.SemaphoreType.DMA((5 + len(chunks),)),
-            pltpu.SemaphoreType.DMA((len(chunks), 1 + 2 * groups)),
+            pltpu.SemaphoreType.DMA((len(chunks), 2 + groups)),
         ],
         compiler_params=pltpu.CompilerParams(vmem_limit_bytes=VMEM_FIRST),
     )(pair, gain, w_left, w_right, lens, resolved)
@@ -186,13 +195,11 @@
     return jnp.concatenate(lines, axis=1).astype(jnp.bfloat16)
 
 
-def near_kernel(groups, rows, cols, after_ref, *refs):
-    got_refs = refs[:groups]
-    left_ref, near_ref, left_s, right_s, prod_s = refs[groups:]
+def near_kernel(groups, rows, cols, after_ref, got_ref, left_ref, near_ref, left_s, right_s, prod_s):
     mine = place_of(groups, rows, cols)[2]
     step = left_s.shape[1] // (groups * rows)
     for u in range(groups):
-        unpack(got_refs[u], (left_s, right_s), jnp.bitwise_xor(mine, u), rows, cols, step)
+        unpack(got_ref.at[u], (left_s, right_s), u, rows, cols, step)
     for d in range(near_ref.shape[1]):
         left_ref[d] = channel_of(left_s, d, groups * rows, step)
         multiply(left_ref[d], channel_of(right_s, d, groups * rows, step), prod_s, d, step)
@@ -236,16 +243,15 @@
 
 
 def make_near(got, after, rows, cols):
-    groups = len(got)
-    both, flat = got[0].shape
+    groups, both, flat = got.shape
     ch = both // 2
     count = groups * rows
     tiles = pl.cdiv(cols, LANES)
-    held = pltpu.VMEM((tiles, count * ceil_to(ch, 8), LANES), jnp.float32)
+    held = pltpu.VMEM((tiles, count * line_step(ch), LANES), jnp.float32)
     whole = pl.BlockSpec(memory_space=pltpu.VMEM)
     return pl.pallas_call(
         functools.partial(near_kernel, groups, rows, cols),
-        in_specs=[pl.BlockSpec(memory_space=pl.ANY)] + [whole] * groups,
+        in_specs=[pl.BlockSpec(memory_space=pl.ANY), whole],
         out_specs=[whole] * 2,
         out_shape=[
             jax.ShapeDtypeStruct((ch, count, tiles * LANES), jnp.bfloat16),
@@ -254,13 +260,13 @@
         scratch_shapes=[held, held, held],
         compiler_params=pltpu.CompilerParams(vmem_limit_bytes=VMEM_LIMIT),
         cost_estimate=pl.CostEstimate(flops=10 ** 5, bytes_accessed=10 ** 5, transcendentals=0),
-    )(after, *got)
+    )(after, got)
 
 
 def make_lines(got, groups, rows, cols, cost, after=()):
     ch = got[0].shape[0]
     whole = pl.BlockSpec(memory_space=pltpu.VMEM)
-    lines = (pl.cdiv(cols, LANES), len(got) * rows * ceil_to(ch, 8), LANES)
+    lines = (pl.cdiv(cols, LANES), len(got) * rows * line_step(ch), LANES)
     return pl.pallas_call(
         functools.partial(lines_kernel, groups, rows, cols, len(got)),
         in_specs=[whole] * len(got) + [pl.BlockSpec(memory_space=pl.ANY)] * len(after),
@@ -274,7 +280,7 @@
 def make_cross(left, near, early, late, rows, cols):
     groups, ch, flat = near.shape
     whole = pl.BlockSpec(memory_space=pltpu.VMEM)
-    held = pltpu.VMEM((pl.cdiv(cols, LANES), groups * rows * ceil_to(ch, 8), LANES), jnp.float32)
+    held = pltpu.VMEM((pl.cdiv(cols, LANES), groups * rows * line_step(ch), LANES), jnp.float32)
     return pl.pallas_call(
         functools.partial(cross_kernel, groups, rows, cols),
         in_specs=[whole] * 4,
@@ -361,9 +367,10 @@
         pair_act.reshape(rows * cols, channels), chain_lengths, resolved,
         in_gain.reshape(1, channels), w_left, w_right, groups, rows, cols,
     )
-    both, right = edges[:groups], edges[groups:]
+    both, right = edges[0], edges[1:]
+    halves = [[h * groups + r for r in range(groups)] for h in range(2)]
     far_got = [swap(right[u], groups + u) for u in range(groups)]
-    near_got = [both[0]] + [swap(both[u], u) for u in range(1, groups)]
+    near_got = lax.all_to_all(both, "row", split_axis=0, concat_axis=0, tiled=True, axis_index_groups=halves)
     gate = jax.nn.sigmoid(jnp.dot(normed, w_gate, preferred_element_type=jnp.float32))
     half = groups // 2
     early = make_lines(far_got[:half], groups, rows, cols, 10 ** 8)

time: 51.1 us -> 52.8 us (1.033)
  waiting for transfers between devices: 19.1 us -> 24.6 us
  Pallas kernels: 12.2 us -> 9.75 us
  starting transfers between devices: 18.4 us -> 17 us
    ppermute x10 -> x7, starting transfers between devices: 18.3 us -> 11.5 us  [swap(): lax.ppermute(value, 'row', [(r, r ^ shift) for r in range(lax.axis_size('...]
    all_to_all x0 -> x1, starting transfers between devices: none -> 5.39 us  [shards(): lax.all_to_all(both, 'row', split_axis=0, concat_axis=0, tiled=True, axis...]
    ppermute x10 -> x7, waiting for transfers between devices: 17.2 us -> 21.9 us  [swap(): lax.ppermute(value, 'row', [(r, r ^ shift) for r in range(lax.axis_size('...]
    pallas_call x1, Pallas kernels: 3.66 us -> 1.75 us  [make_near(): pl.pallas_call(functools.partial(near_kernel, groups, rows, cols), in_spe...]
    pallas_call x1, Pallas kernels: 2.38 us -> 1.28 us  [make_cross(): pl.pallas_call(functools.partial(cross_kernel, groups, rows, cols), in_sp...]
    all_to_all x0 -> x1, waiting for transfers between devices: none -> 0.79 us  [shards(): lax.all_to_all(both, 'row', split_axis=0, concat_axis=0, tiled=True, axis...]
    pallas_call x1, Pallas kernels: 4.16 us -> 4.76 us  [make_edges(): pl.pallas_call(functools.partial(edges_kernel, groups, rows, cols, chunks...]
  transfers between devices with their start and end apart: 11 -> 9, of which waited for: 7 -> 9; matrix products, arithmetic and copies ran while one was open for 1% -> 1% of each run, Pallas kernels for 8% -> 4%
where the time goes in v6:
time: 52.8 us; the launch traced here: 52.6 us
  waiting for transfers between devices  24.6 us (47%)
  starting transfers between devices  17 us (32%)
  Pallas kernels  9.75 us (18%)
  local copies, waits for them, and re-layouts  0.79 us (1%)
    ppermute x7, waiting for transfers between devices, swap(): lax.ppermute(value, 'row', [(r, r ^ shift) for r in range(lax.axis_size('...  21.9 us
    ppermute x7, starting transfers between devices, swap(): lax.ppermute(value, 'row', [(r, r ^ shift) for r in range(lax.axis_size('...  11.5 us
    all_to_all x1, starting transfers between devices, shards(): lax.all_to_all(both, 'row', split_axis=0, concat_axis=0, tiled=True, axis...  5.39 us
    pallas_call x1, Pallas kernels, make_edges(): pl.pallas_call(functools.partial(edges_kernel, groups, rows, cols, chunks...  4.76 us
    ppermute x1, waiting for transfers between devices, shards(): sums = make_sums(keep, lax.ppermute(send, 'col', [(0, 1), (1, 0)]))  1.9 us
    pallas_call x1, Pallas kernels, make_near(): pl.pallas_call(functools.partial(near_kernel, groups, rows, cols), in_spe...  1.75 us
    pallas_call x1, Pallas kernels, make_update(): pl.pallas_call(functools.partial(update_kernel, groups, rows, cols, chunk...  1.41 us
    pallas_call x1, Pallas kernels, make_cross(): pl.pallas_call(functools.partial(cross_kernel, groups, rows, cols), in_sp...  1.28 us
  transfers between devices with their start and end apart: 9, of which 9 were waited for; matrix products, arithmetic and copies ran while one was open for 1% of the time, Pallas kernels for 4%

profile of v6, /device:TPU:0, one launch (start us, length us, event | category | flops | bytes accessed | tf_op | source)
XLA Modules:
  0.0 52.6 jit_solution(17761351505298135337)
XLA Ops:
  0.0 0.0 copy-start
  0.0 4.8 %shard_map.91 = (bf16[1936,128]{1,0:T(8,128)(2,1)}, bf16[4,64,2048]{2,1,0:T(8,128)(2,1)}, bf16[32,2048]{1,0:T(8,128)(2,1)}, bf16[32,2048]{1,0:T(8,128)(2,1)}, bf...) custom-call(bf16[1936,128]{1,0:T(8,128)(2,1)} %bitcast.6, f32[1,128]{1,0:T(1,128)} %bitcast.8, bf16[128,256]{1,0:T(8,128)(2,1)} %wl_ref.1, ...), custom_call_target="tpu_custom_call" | custom-call | tf_op jit(solution)/shard_map/pallas_call | solution.py:121
  4.8 0.0 copy-start.7
  4.8 0.0 copy-start.6
  4.8 0.0 copy-start.5
  4.8 0.0 copy-start.4
  4.8 5.4 %all-to-all-start = ((bf16[4,64,2048]{2,1,0:T(8,128)(2,1)}), bf16[4,64,2048]{2,1,0:T(8,128)(2,1)S(1)}, u32[]{:S(2)}, u32[]{:S(2)}) async-start(bf16[4,64,2048]{2,1,0:T(8,128)(2,1)} %get-tuple-element.22), calls=%async_computation | async-start | bytes 2097152 | tf_op jit(solution)/shard_map/all_to_all | solution.py:373
  10.2 0.0 copy-done.7
  10.2 2.6 %collective-permute-start = (bf16[32,2048]{1,0:T(8,128)(2,1)S(1)}, bf16[32,2048]{1,0:T(8,128)(2,1)S(1)}, u32[]{:S(2)}, u32[]{:S(2)}) collective-permute-start(bf16[32,2048]{1,0:T(8,128)(2,1)S(1)} %copy-done.7), channel_id=1, source_target_pairs={{0,8},{2,10},{4,12},{6,14},{8,0},{10,2},{12,4},{14,6},{1,9},{3,11}... | collective-permute-start | bytes 393224 | tf_op jit(solution)/shard_map/ppermute | solution.py:359
  12.8 0.0 copy-done.6
  12.8 1.8 %collective-permute-start.1 = (bf16[32,2048]{1,0:T(8,128)(2,1)S(1)}, bf16[32,2048]{1,0:T(8,128)(2,1)S(1)}, u32[]{:S(2)}, u32[]{:S(2)}) collective-permute-start(bf16[32,2048]{1,0:T(8,128)(2,1)S(1)} %copy-done.6), channel_id=1, source_target_pairs={{0,10},{2,8},{4,14},{6,12},{8,2},{10,0},{12,6},{14,4},{1,11},{3,9}... | collective-permute-start | bytes 393224 | tf_op jit(solution)/shard_map/ppermute | solution.py:359
  14.6 0.0 copy-done.5
  14.6 3.5 %collective-permute-start.2 = (bf16[32,2048]{1,0:T(8,128)(2,1)S(1)}, bf16[32,2048]{1,0:T(8,128)(2,1)S(1)}, u32[]{:S(2)}, u32[]{:S(2)}) collective-permute-start(bf16[32,2048]{1,0:T(8,128)(2,1)S(1)} %copy-done.5), channel_id=1, source_target_pairs={{0,12},{2,14},{4,8},{6,10},{8,4},{10,6},{12,0},{14,2},{1,13},{3,15... | collective-permute-start | bytes 393224 | tf_op jit(solution)/shard_map/ppermute | solution.py:359
  18.1 0.0 copy-done.4
  18.1 0.1 collective-permute-start.3
  18.2 7.5 %collective-permute-done.refs_0_ = bf16[32,2048]{1,0:T(8,128)(2,1)S(1)} collective-permute-done((bf16[32,2048]{1,0:T(8,128)(2,1)S(1)}, bf16[32,2048]{1,0:T(8,128)(2,1)S(1)}, u32[]{:S(2)}, u32[]{:S(2)}) %collective-permute-start) | collective-permute-done | bytes 131104 | tf_op jit(solution)/shard_map/ppermute | solution.py:359
  25.6 2.8 %collective-permute-done.1.refs_1_ = bf16[32,2048]{1,0:T(8,128)(2,1)S(1)} collective-permute-done((bf16[32,2048]{1,0:T(8,128)(2,1)S(1)}, bf16[32,2048]{1,0:T(8,128)(2,1)S(1)}, u32[]{:S(2)}, u32[]{:S(2)}) %collective-permute-start.1) | collective-permute-done | bytes 131104 | tf_op jit(solution)/shard_map/ppermute | solution.py:359
  28.5 0.2 shard_map.92.after_ref.early_ref
  28.7 0.8 %all-to-all-done.got_ref = bf16[4,64,2048]{2,1,0:T(8,128)(2,1)S(1)} async-done(((bf16[4,64,2048]{2,1,0:T(8,128)(2,1)}), bf16[4,64,2048]{2,1,0:T(8,128)(2,1)S(1)}, u32[]{:S(2)}, u32[]{:S(2)}) %all-to-all-start) | async-done | bytes 1048608 | tf_op jit(solution)/shard_map/all_to_all | solution.py:373
  29.5 1.8 %shard_map.93 = (bf16[32,88,128]{2,1,0:T(8,128)(2,1)S(1)}, bf16[4,32,2048]{2,1,0:T(8,128)(2,1)S(1)}) custom-call(f32[1,1760,128]{2,1,0:T(8,128)S(1)} %shard_map.92.after_ref.early_ref, bf16[4,64,2048]{2,1,0:T(8,128)(2,1)S(1)} %all-to-all-done.got_ref), custom_call_target="tpu_custom_call" | custom-call | flops 100000 | bytes 100000 | tf_op jit(solution)/shard_map/pallas_call | solution.py:252
  31.2 4.5 %collective-permute-done.2.refs_0_ = bf16[32,2048]{1,0:T(8,128)(2,1)S(1)} collective-permute-done((bf16[32,2048]{1,0:T(8,128)(2,1)S(1)}, bf16[32,2048]{1,0:T(8,128)(2,1)S(1)}, u32[]{:S(2)}, u32[]{:S(2)}) %collective-permute-start.2) | collective-permute-done | bytes 131104 | tf_op jit(solution)/shard_map/ppermute | solution.py:359
  35.7 2.3 %collective-permute-done.3.refs_1_ = bf16[32,2048]{1,0:T(8,128)(2,1)S(1)} collective-permute-done((bf16[32,2048]{1,0:T(8,128)(2,1)S(1)}, bf16[32,2048]{1,0:T(8,128)(2,1)S(1)}, u32[]{:S(2)}, u32[]{:S(2)}) %collective-permute-start.3) | collective-permute-done | bytes 131104 | tf_op jit(solution)/shard_map/ppermute | solution.py:359
  38.0 0.2 shard_map.94.late_ref
  38.2 1.3 %shard_map.95 = (bf16[4,32,2048]{2,1,0:T(8,128)(2,1)S(1)}, bf16[4,32,2048]{2,1,0:T(8,128)(2,1)S(1)}) custom-call(bf16[32,88,128]{2,1,0:T(8,128)(2,1)S(1)} %get-tuple-element.23.refs_2_.left_ref, bf16[4,32,2048]{2,1,0:T(8,128)(2,1)S(1)} %get-tuple-element.24.near_ref, f32[1,1760,128]{2,1,0:T(8,128)S(1)} %shard_map.92.after_ref.early_ref, ...), custom_call_target="tpu_custom_call" | custom-call | flops 100000 | bytes 8000000 | tf_op jit(solution)/shard_map/pallas_call | solution.py:284
  39.5 0.1 collective-permute-start.4
  39.6 1.9 %collective-permute-done.4.b_ref = bf16[4,32,2048]{2,1,0:T(8,128)(2,1)S(1)} collective-permute-done((bf16[4,32,2048]{2,1,0:T(8,128)(2,1)S(1)}, bf16[4,32,2048]{2,1,0:T(8,128)(2,1)S(1)}, u32[]{:S(2)}, u32[]{:S(2)}) %collective-permute-start.4) | collective-permute-done | bytes 524320 | tf_op jit(solution)/shard_map/ppermute | solution.py:380
  41.5 0.0 copy-start.3
  41.5 0.1 shard_map.96
  41.6 0.6 %collective-permute-start.5 = (bf16[32,2048]{1,0:T(8,128)(2,1)S(1)}, bf16[32,2048]{1,0:T(8,128)(2,1)S(1)}, u32[]{:S(2)}, u32[]{:S(2)}) collective-permute-start(bf16[32,2048]{1,0:T(8,128)(2,1)S(1)} %get-tuple-element.30), channel_id=1, source_target_pairs={{0,2},{2,0},{4,6},{6,4},{8,10},{10,8},{12,14},{14,12},{1,3},{3,1},... | collective-permute-start | bytes 393224 | tf_op jit(solution)/shard_map/ppermute | solution.py:359
  42.2 0.0 collective-permute-start.6
  42.2 2.9 %collective-permute-start.7 = (bf16[32,2048]{1,0:T(8,128)(2,1)S(1)}, bf16[32,2048]{1,0:T(8,128)(2,1)S(1)}, u32[]{:S(2)}, u32[]{:S(2)}) collective-permute-start(bf16[32,2048]{1,0:T(8,128)(2,1)S(1)} %get-tuple-element.32), channel_id=1, source_target_pairs={{0,6},{2,4},{4,2},{6,0},{8,14},{10,12},{12,10},{14,8},{1,7},{3,5},... | collective-permute-start | bytes 393224 | tf_op jit(solution)/shard_map/ppermute | solution.py:359
  45.2 0.0 copy-done
  45.2 0.0 copy-done.3
  45.2 0.4 fusion.2.gate_ref
  45.6 0.0 copy-start.2
  45.6 0.6 %copy-done.2 = f32[128]{0:T(128)S(1)} copy-done((f32[128]{0:T(128)S(1)}, f32[128]{0:T(128)}, u32[]{:S(2)}) %copy-start.2) | copy-done | bytes 536
  46.2 0.0 copy-start.1
  46.2 0.1 copy.10.gain_ref
  46.4 0.8 %collective-permute-done.5.refs_1_ = bf16[32,2048]{1,0:T(8,128)(2,1)S(1)} collective-permute-done((bf16[32,2048]{1,0:T(8,128)(2,1)S(1)}, bf16[32,2048]{1,0:T(8,128)(2,1)S(1)}, u32[]{:S(2)}, u32[]{:S(2)}) %collective-permute-start.5) | collective-permute-done | bytes 131104 | tf_op jit(solution)/shard_map/ppermute | solution.py:359
  47.2 1.4 %collective-permute-done.6.refs_2_ = bf16[32,2048]{1,0:T(8,128)(2,1)S(1)} collective-permute-done((bf16[32,2048]{1,0:T(8,128)(2,1)S(1)}, bf16[32,2048]{1,0:T(8,128)(2,1)S(1)}, u32[]{:S(2)}, u32[]{:S(2)}) %collective-permute-start.6) | collective-permute-done | bytes 131104 | tf_op jit(solution)/shard_map/ppermute | solution.py:359
  48.6 2.6 %collective-permute-done.7.refs_3_ = bf16[32,2048]{1,0:T(8,128)(2,1)S(1)} collective-permute-done((bf16[32,2048]{1,0:T(8,128)(2,1)S(1)}, bf16[32,2048]{1,0:T(8,128)(2,1)S(1)}, u32[]{:S(2)}, u32[]{:S(2)}) %collective-permute-start.7) | collective-permute-done | bytes 131104 | tf_op jit(solution)/shard_map/ppermute | solution.py:359
  51.2 0.0 copy-done.1
  51.2 1.4 %shard_map.97 = bf16[1936,128]{1,0:T(8,128)(2,1)} custom-call(f32[128,1]{1,0:T(8,128)S(1)} %copy.10.gain_ref, bf16[128,128]{1,0:T(8,128)(2,1)S(1)} %copy-done.1, f32[1936,128]{1,0:T(8,128)S(1)} %fusion.2.gate_ref, bf16[32,2048]{1,0:T(8,128)(2,1)S(1)} %get-tuple-element.29.refs_0_, bf16[32,2048]{1,0:T(8,128)(2,1)S(1)} %collective-permute-done.5.refs_1_, ...), custom_call_target="tpu_custom_call" | custom-call | tf_op jit(solution)/shard_map/pallas_call | solution.py:344
Async XLA Ops:
  0.0 45.2 %copy-start = (bf16[128,128]{1,0:T(8,128)(2,1)S(1)}, bf16[128,128]{1,0:T(8,128)(2,1)}, u32[]{:S(2)}) copy-start(bf16[128,128]{1,0:T(8,128)(2,1)} %param.16) | copy-start | bytes 98308
  4.8 5.4 %copy-start.7 = (bf16[32,2048]{1,0:T(8,128)(2,1)S(1)}, bf16[32,2048]{1,0:T(8,128)(2,1)}, u32[]{:S(2)}) copy-start(bf16[32,2048]{1,0:T(8,128)(2,1)} %get-tuple-element.20) | copy-start | bytes 393220
  4.8 8.0 %copy-start.6 = (bf16[32,2048]{1,0:T(8,128)(2,1)S(1)}, bf16[32,2048]{1,0:T(8,128)(2,1)}, u32[]{:S(2)}) copy-start(bf16[32,2048]{1,0:T(8,128)(2,1)} %get-tuple-element.21) | copy-start | bytes 393220
  4.8 9.8 %copy-start.5 = (bf16[32,2048]{1,0:T(8,128)(2,1)S(1)}, bf16[32,2048]{1,0:T(8,128)(2,1)}, u32[]{:S(2)}) copy-start(bf16[32,2048]{1,0:T(8,128)(2,1)} %get-tuple-element.25) | copy-start | bytes 393220
  4.8 13.3 %copy-start.4 = (bf16[32,2048]{1,0:T(8,128)(2,1)S(1)}, bf16[32,2048]{1,0:T(8,128)(2,1)}, u32[]{:S(2)}) copy-start(bf16[32,2048]{1,0:T(8,128)(2,1)} %get-tuple-element.26) | copy-start | bytes 393220
  4.8 24.7 %all-to-all-start = ((bf16[4,64,2048]{2,1,0:T(8,128)(2,1)}), bf16[4,64,2048]{2,1,0:T(8,128)(2,1)S(1)}, u32[]{:S(2)}, u32[]{:S(2)}) async-start(bf16[4,64,2048]{2,1,0:T(8,128)(2,1)} %get-tuple-element.22), calls=%async_computation | async-start | bytes 2097152 | tf_op jit(solution)/shard_map/all_to_all | solution.py:373
  10.2 15.4 %collective-permute-start = (bf16[32,2048]{1,0:T(8,128)(2,1)S(1)}, bf16[32,2048]{1,0:T(8,128)(2,1)S(1)}, u32[]{:S(2)}, u32[]{:S(2)}) collective-permute-start(bf16[32,2048]{1,0:T(8,128)(2,1)S(1)} %copy-done.7), channel_id=1, source_target_pairs={{0,8},{2,10},{4,12},{6,14},{8,0},{10,2},{12,4},{14,6},{1,9},{3,11}... | collective-permute-start | bytes 393224 | tf_op jit(solution)/shard_map/ppermute | solution.py:359
  12.8 15.7 %collective-permute-start.1 = (bf16[32,2048]{1,0:T(8,128)(2,1)S(1)}, bf16[32,2048]{1,0:T(8,128)(2,1)S(1)}, u32[]{:S(2)}, u32[]{:S(2)}) collective-permute-start(bf16[32,2048]{1,0:T(8,128)(2,1)S(1)} %copy-done.6), channel_id=1, source_target_pairs={{0,10},{2,8},{4,14},{6,12},{8,2},{10,0},{12,6},{14,4},{1,11},{3,9}... | collective-permute-start | bytes 393224 | tf_op jit(solution)/shard_map/ppermute | solution.py:359
  14.6 21.1 %collective-permute-start.2 = (bf16[32,2048]{1,0:T(8,128)(2,1)S(1)}, bf16[32,2048]{1,0:T(8,128)(2,1)S(1)}, u32[]{:S(2)}, u32[]{:S(2)}) collective-permute-start(bf16[32,2048]{1,0:T(8,128)(2,1)S(1)} %copy-done.5), channel_id=1, source_target_pairs={{0,12},{2,14},{4,8},{6,10},{8,4},{10,6},{12,0},{14,2},{1,13},{3,15... | collective-permute-start | bytes 393224 | tf_op jit(solution)/shard_map/ppermute | solution.py:359
  18.1 19.9 %collective-permute-start.3 = (bf16[32,2048]{1,0:T(8,128)(2,1)S(1)}, bf16[32,2048]{1,0:T(8,128)(2,1)S(1)}, u32[]{:S(2)}, u32[]{:S(2)}) collective-permute-start(bf16[32,2048]{1,0:T(8,128)(2,1)S(1)} %copy-done.4), channel_id=1, source_target_pairs={{0,14},{2,12},{4,10},{6,8},{8,6},{10,4},{12,2},{14,0},{1,15},{3,13... | collective-permute-start | bytes 393224 | tf_op jit(solution)/shard_map/ppermute | solution.py:359
  39.5 2.0 %collective-permute-start.4 = (bf16[4,32,2048]{2,1,0:T(8,128)(2,1)S(1)}, bf16[4,32,2048]{2,1,0:T(8,128)(2,1)S(1)}, u32[]{:S(2)}, u32[]{:S(2)}) collective-permute-start(bf16[4,32,2048]{2,1,0:T(8,128)(2,1)S(1)} %get-tuple-element.28), channel_id=1, source_target_pairs={{0,1},{1,0},{2,3},{3,2},{4,5},{5,4},{6,7},{7,6},{8,9},{9,8},{10,11... | collective-permute-start | bytes 1572872 | tf_op jit(solution)/shard_map/ppermute | solution.py:380
  41.5 3.7 %copy-start.3 = (bf16[1936,128]{1,0:T(8,128)(2,1)S(1)}, bf16[1936,128]{1,0:T(8,128)(2,1)}, u32[]{:S(2)}) copy-start(bf16[1936,128]{1,0:T(8,128)(2,1)} %get-tuple-element.19) | copy-start | bytes 1486852
  41.6 5.6 %collective-permute-start.5 = (bf16[32,2048]{1,0:T(8,128)(2,1)S(1)}, bf16[32,2048]{1,0:T(8,128)(2,1)S(1)}, u32[]{:S(2)}, u32[]{:S(2)}) collective-permute-start(bf16[32,2048]{1,0:T(8,128)(2,1)S(1)} %get-tuple-element.30), channel_id=1, source_target_pairs={{0,2},{2,0},{4,6},{6,4},{8,10},{10,8},{12,14},{14,12},{1,3},{3,1},... | collective-permute-start | bytes 393224 | tf_op jit(solution)/shard_map/ppermute | solution.py:359
  42.2 6.4 %collective-permute-start.6 = (bf16[32,2048]{1,0:T(8,128)(2,1)S(1)}, bf16[32,2048]{1,0:T(8,128)(2,1)S(1)}, u32[]{:S(2)}, u32[]{:S(2)}) collective-permute-start(bf16[32,2048]{1,0:T(8,128)(2,1)S(1)} %get-tuple-element.31), channel_id=1, source_target_pairs={{0,4},{2,6},{4,0},{6,2},{8,12},{10,14},{12,8},{14,10},{1,5},{3,7},... | collective-permute-start | bytes 393224 | tf_op jit(solution)/shard_map/ppermute | solution.py:359
  42.2 9.0 %collective-permute-start.7 = (bf16[32,2048]{1,0:T(8,128)(2,1)S(1)}, bf16[32,2048]{1,0:T(8,128)(2,1)S(1)}, u32[]{:S(2)}, u32[]{:S(2)}) collective-permute-start(bf16[32,2048]{1,0:T(8,128)(2,1)S(1)} %get-tuple-element.32), channel_id=1, source_target_pairs={{0,6},{2,4},{4,2},{6,0},{8,14},{10,12},{12,10},{14,8},{1,7},{3,5},... | collective-permute-start | bytes 393224 | tf_op jit(solution)/shard_map/ppermute | solution.py:359
  45.6 0.7 %copy-start.2 = (f32[128]{0:T(128)S(1)}, f32[128]{0:T(128)}, u32[]{:S(2)}) copy-start(f32[128]{0:T(128)} %param.13) | copy-start | bytes 1540
  46.2 5.0 %copy-start.1 = (bf16[128,128]{1,0:T(8,128)(2,1)S(1)}, bf16[128,128]{1,0:T(8,128)(2,1)}, u32[]{:S(2)}) copy-start(bf16[128,128]{1,0:T(8,128)(2,1)} %w_ref.1) | copy-start | bytes 98308

commit v7 on v5

--- a/solution.py
+++ b/solution.py
@@ -15,6 +15,10 @@
 
 def ceil_to(n, m):
     return -(-n // m) * m
+
+
+def line_step(ch):
+    return (ceil_to(ch, 8) // 8 | 1) * 8
 
 
 def place_of(groups, rows, cols):
@@ -43,10 +47,10 @@
     return i_ok * k_ok
 
 
-def edge_of(normed, w_ref, mask, groups):
-    hidden = w_ref.shape[1] // 2
-    block = normed.shape[0]
-    projected = lax.dot_general(w_ref[...], normed, (((0,), (1,)), ((), ())), preferred_element_type=jnp.float32)
+def edge_of(weights, normed, mask, groups):
+    hidden = weights.shape[0] // 2
+    block = normed.shape[1]
+    projected = jnp.dot(weights, normed, preferred_element_type=jnp.float32)
     edge = sigmoid(projected[:hidden]) * projected[hidden:]
     edge = edge.reshape(hidden // 8, 8, block) * mask[None]
     return edge.reshape(groups, hidden // groups, block).astype(jnp.bfloat16)
@@ -71,30 +75,34 @@
     for copy in pieces[:1] + loads + pieces[1:]:
         copy.start()
     block = chunks[0][1]
+    channels = x_s.shape[1]
     spare = x_s.shape[0] - count
     if spare:
         x_s[pl.ds(count, spare)] = jnp.zeros((spare, x_s.shape[1]), x_s.dtype)
     stores = []
     for n, (at, size) in enumerate(chunks):
         pieces[n].wait()
-        x = x_s[pl.ds(at, block)].astype(jnp.float32)
-        mean = jnp.mean(x, axis=-1, keepdims=True)
-        centred = x - mean
-        variance = jnp.mean(centred * centred, axis=-1, keepdims=True)
+        x = x_s[pl.ds(at, block)].T.astype(jnp.float32)
+        centred = x - jnp.mean(x, axis=0, keepdims=True)
+        variance = jnp.mean(centred * centred, axis=0, keepdims=True)
         if n == 0:
             for copy in loads:
                 copy.wait()
-        normed = (centred * lax.rsqrt(variance + EPS) * gain_s[...]).astype(jnp.bfloat16)
-        normed_s[pl.ds(at, block)] = normed
+            gain = jnp.broadcast_to(gain_s[...], (LANES, channels)).T
+            gain = jnp.concatenate([gain] * (block // LANES), axis=1)
+            right_w, left_w = wr_s[...].T, wl_s[...].T
+        normed = (centred * lax.rsqrt(variance + EPS) * gain).astype(jnp.bfloat16)
         mask = mask_of(cols, first_row, first_col, lens_s, res_s, at, block)
         lanes = pl.ds(at, block)
-        held[:, own:, lanes] = edge_of(normed, wr_s, mask, groups)
-        held[:, :own, lanes] = edge_of(normed, wl_s, mask, groups)
-        sent = [(normed_s.at[pl.ds(at, size)], normed_ref.at[pl.ds(at, size)])]
+        normed_s[:, lanes] = normed
+        held[:, own:, lanes] = edge_of(right_w, normed, mask, groups)
+        held[:, :own, lanes] = edge_of(left_w, normed, mask, groups)
+        sent = []
         for u in range(groups):
             group = jnp.bitwise_xor(mine, u)
             sent.append((held.at[group, pl.ds(own, own), lanes], right_refs[u].at[:, lanes]))
             sent.append((held.at[group, :, lanes], both_refs[u].at[:, lanes]))
+        sent.append((normed_s.at[:, lanes], normed_ref.at[:, lanes]))
         for m, (src, dst) in enumerate(sent):
             stores.append(pltpu.make_async_copy(src, dst, out_sems.at[n, m]))
             stores[-1].start()
@@ -113,7 +121,7 @@
         functools.partial(edges_kernel, groups, rows, cols, chunks),
         in_specs=[here] * 6,
         out_specs=[here] * (1 + 2 * groups),
-        out_shape=[jax.ShapeDtypeStruct((count, channels), jnp.bfloat16)]
+        out_shape=[jax.ShapeDtypeStruct((channels, flat), jnp.bfloat16)]
         + [jax.ShapeDtypeStruct((2 * own, flat), jnp.bfloat16)] * groups
         + [jax.ShapeDtypeStruct((own, flat), jnp.bfloat16)] * groups,
         scratch_shapes=[
@@ -123,7 +131,7 @@
             pltpu.VMEM(w_right.shape, w_right.dtype),
             pltpu.SMEM(lens.shape, lens.dtype),
             pltpu.SMEM(resolved.shape, resolved.dtype),
-            pltpu.VMEM((flat, channels), jnp.bfloat16),
+            pltpu.VMEM((channels, flat), jnp.bfloat16),
             pltpu.VMEM((groups, 2 * own, flat), jnp.bfloat16),
             pltpu.SemaphoreType.DMA((5 + len(chunks),)),
             pltpu.SemaphoreType.DMA((len(chunks), 1 + 2 * groups)),
@@ -186,13 +194,23 @@
     return jnp.concatenate(lines, axis=1).astype(jnp.bfloat16)
 
 
-def near_kernel(groups, rows, cols, after_ref, *refs):
-    got_refs = refs[:groups]
-    left_ref, near_ref, left_s, right_s, prod_s = refs[groups:]
+def early_kernel(groups, rows, cols, far_ref, near_ref, far_lines, left_lines, right_lines):
+    step = far_lines.shape[1] // rows
+    unpack(far_ref, (far_lines,), 0, rows, cols, step)
+    unpack(near_ref, (left_lines, right_lines), 0, rows, cols, step)
+
+
+def near_kernel(groups, rows, cols, left_lines, right_lines, *refs):
+    got_refs = refs[:groups - 1]
+    left_ref, near_ref, left_s, right_s, prod_s = refs[groups - 1:]
     mine = place_of(groups, rows, cols)[2]
     step = left_s.shape[1] // (groups * rows)
-    for u in range(groups):
-        unpack(got_refs[u], (left_s, right_s), jnp.bitwise_xor(mine, u), rows, cols, step)
+    size = rows * step
+    there = pl.ds(pl.multiple_of(jnp.bitwise_xor(mine, 1) * size, 8), size)
+    left_s[:, there, :] = left_lines[...]
+    right_s[:, there, :] = right_lines[...]
+    for got_ref, u in zip(got_refs, [0] + list(range(2, groups))):
+        unpack(got_ref, (left_s, right_s), jnp.bitwise_xor(mine, u), rows, cols, step)
     for d in range(near_ref.shape[1]):
         left_ref[d] = channel_of(left_s, d, groups * rows, step)
         multiply(left_ref[d], channel_of(right_s, d, groups * rows, step), prod_s, d, step)
@@ -200,13 +218,14 @@
         pack(prod_s, near_ref, u, jnp.bitwise_xor(mine, u), rows, cols, step)
 
 
-def lines_kernel(groups, rows, cols, count, *refs):
-    got_refs, lines_ref = refs[:count], refs[-1]
+def late_kernel(groups, rows, cols, after_ref, far_lines, *refs):
+    got_refs, lines_ref = refs[:-1], refs[-1]
     mine = place_of(groups, rows, cols)[2]
-    step = lines_ref.shape[1] // (count * rows)
-    for u in range(count):
-        block = jnp.bitwise_and(jnp.bitwise_xor(mine, u), count - 1)
-        unpack(got_refs[u], (lines_ref,), block, rows, cols, step)
+    step = lines_ref.shape[1] // (groups * rows)
+    size = rows * step
+    lines_ref[:, pl.ds(pl.multiple_of(mine * size, 8), size), :] = far_lines[...]
+    for u in range(1, groups):
+        unpack(got_refs[u - 1], (lines_ref,), jnp.bitwise_xor(mine, u), rows, cols, step)
 
 
 def multiply(left, right, prod_s, d, step):
@@ -219,71 +238,88 @@
         prod_s[t, pl.ds(d, count, stride=step), :] = prod[:, t * LANES:(t + 1) * LANES]
 
 
-def cross_kernel(groups, rows, cols, left_ref, near_ref, early_ref, late_ref, keep_ref, send_ref, right_s, prod_s, pair_s):
+def cross_kernel(groups, rows, cols, left_ref, near_ref, lines_ref, *refs):
+    keep_refs, send_refs = refs[:2], refs[2:4]
+    prod_s, pair_s = refs[4:]
     _, _, mine, half, col = place_of(groups, rows, cols)
     step = prod_s.shape[1] // (groups * rows)
-    size = early_ref.shape[1]
-    base = pl.multiple_of(mine // (groups // 2) * size, 8)
-    right_s[:, pl.ds(base, size), :] = early_ref[...]
-    right_s[:, pl.ds(pl.multiple_of(size - base, 8), size), :] = late_ref[...]
-    for d in range(keep_ref.shape[1]):
-        multiply(left_ref[d], channel_of(right_s, d, groups * rows, step), prod_s, d, step)
+    for d in range(left_ref.shape[0]):
+        multiply(left_ref[d], channel_of(lines_ref, d, groups * rows, step), prod_s, d, step)
     for u in range(groups):
         pack(prod_s, pair_s, u, jnp.bitwise_xor(mine, u), rows, cols, step)
     near_kept = col == half
-    keep_ref[...] = jnp.where(near_kept, near_ref[...], pair_s[...])
-    send_ref[...] = jnp.where(near_kept, pair_s[...], near_ref[...])
-
-
-def make_near(got, after, rows, cols):
-    groups = len(got)
+    for part in range(2):
+        pieces = pl.ds(part * (groups // 2), groups // 2)
+        keep_refs[part][...] = jnp.where(near_kept, near_ref[pieces], pair_s[pieces])
+        send_refs[part][...] = jnp.where(near_kept, pair_s[pieces], near_ref[pieces])
+
+
+def lines_of(blocks, ch, cols):
+    return (pl.cdiv(cols, LANES), blocks * line_step(ch), LANES)
+
+
+def make_early(far, near, groups, rows, cols):
+    ch = far.shape[0]
+    whole = pl.BlockSpec(memory_space=pltpu.VMEM)
+    return pl.pallas_call(
+        functools.partial(early_kernel, groups, rows, cols),
+        in_specs=[whole] * 2,
+        out_specs=[whole] * 3,
+        out_shape=[jax.ShapeDtypeStruct(lines_of(rows, ch, cols), jnp.float32)] * 3,
+        compiler_params=pltpu.CompilerParams(vmem_limit_bytes=VMEM_LIMIT),
+        cost_estimate=pl.CostEstimate(flops=10 ** 5, bytes_accessed=10 ** 8, transcendentals=0),
+    )(far, near)
+
+
+def make_late(after, far_lines, got, groups, rows, cols):
+    ch = got[0].shape[0]
+    whole = pl.BlockSpec(memory_space=pltpu.VMEM)
+    return pl.pallas_call(
+        functools.partial(late_kernel, groups, rows, cols),
+        in_specs=[pl.BlockSpec(memory_space=pl.ANY)] + [whole] * (1 + len(got)),
+        out_specs=whole,
+        out_shape=jax.ShapeDtypeStruct(lines_of(groups * rows, ch, cols), jnp.float32),
+        compiler_params=pltpu.CompilerParams(vmem_limit_bytes=VMEM_LIMIT),
+        cost_estimate=pl.CostEstimate(flops=10 ** 5, bytes_accessed=10 ** 5, transcendentals=0),
+    )(after, far_lines, *got)
+
+
+def make_near(left_lines, right_lines, got, rows, cols):
+    groups = len(got) + 1
     both, flat = got[0].shape
     ch = both // 2
     count = groups * rows
-    tiles = pl.cdiv(cols, LANES)
-    held = pltpu.VMEM((tiles, count * ceil_to(ch, 8), LANES), jnp.float32)
+    held = pltpu.VMEM(lines_of(count, ch, cols), jnp.float32)
     whole = pl.BlockSpec(memory_space=pltpu.VMEM)
     return pl.pallas_call(
         functools.partial(near_kernel, groups, rows, cols),
-        in_specs=[pl.BlockSpec(memory_space=pl.ANY)] + [whole] * groups,
+        in_specs=[whole] * (2 + len(got)),
         out_specs=[whole] * 2,
         out_shape=[
-            jax.ShapeDtypeStruct((ch, count, tiles * LANES), jnp.bfloat16),
+            jax.ShapeDtypeStruct((ch, count, pl.cdiv(cols, LANES) * LANES), jnp.bfloat16),
             jax.ShapeDtypeStruct((groups, ch, flat), jnp.bfloat16),
         ],
         scratch_shapes=[held, held, held],
         compiler_params=pltpu.CompilerParams(vmem_limit_bytes=VMEM_LIMIT),
         cost_estimate=pl.CostEstimate(flops=10 ** 5, bytes_accessed=10 ** 5, transcendentals=0),
-    )(after, *got)
-
-
-def make_lines(got, groups, rows, cols, cost, after=()):
-    ch = got[0].shape[0]
-    whole = pl.BlockSpec(memory_space=pltpu.VMEM)
-    lines = (pl.cdiv(cols, LANES), len(got) * rows * ceil_to(ch, 8), LANES)
-    return pl.pallas_call(
-        functools.partial(lines_kernel, groups, rows, cols, len(got)),
-        in_specs=[whole] * len(got) + [pl.BlockSpec(memory_space=pl.ANY)] * len(after),
-        out_specs=whole,
-        out_shape=jax.ShapeDtypeStruct(lines, jnp.float32),
-        compiler_params=pltpu.CompilerParams(vmem_limit_bytes=VMEM_LIMIT),
-        cost_estimate=pl.CostEstimate(flops=10 ** 5, bytes_accessed=cost, transcendentals=0),
-    )(*got, *after)
-
-
-def make_cross(left, near, early, late, rows, cols):
+    )(left_lines, right_lines, *got)
+
+
+def make_cross(left, near, lines, rows, cols):
     groups, ch, flat = near.shape
     whole = pl.BlockSpec(memory_space=pltpu.VMEM)
-    held = pltpu.VMEM((pl.cdiv(cols, LANES), groups * rows * ceil_to(ch, 8), LANES), jnp.float32)
     return pl.pallas_call(
         functools.partial(cross_kernel, groups, rows, cols),
-        in_specs=[whole] * 4,
-        out_specs=[whole] * 2,
-        out_shape=[jax.ShapeDtypeStruct(near.shape, near.dtype)] * 2,
-        scratch_shapes=[held, held, pltpu.VMEM(near.shape, near.dtype)],
+        in_specs=[whole] * 3,
+        out_specs=[whole] * 4,
+        out_shape=[jax.ShapeDtypeStruct((groups // 2, ch, flat), near.dtype)] * 4,
+        scratch_shapes=[
+            pltpu.VMEM(lines_of(groups * rows, ch, cols), jnp.float32),
+            pltpu.VMEM(near.shape, near.dtype),
+        ],
         compiler_params=pltpu.CompilerParams(vmem_limit_bytes=VMEM_LIMIT),
         cost_estimate=pl.CostEstimate(flops=10 ** 5, bytes_accessed=8 * 10 ** 6, transcendentals=0),
-    )(left, near, early, late)
+    )(left, near, lines)
 
 
 def add_kernel(a_ref, b_ref, *out_refs):
@@ -364,13 +400,18 @@
     both, right = edges[:groups], edges[groups:]
     far_got = [swap(right[u], groups + u) for u in range(groups)]
     near_got = [both[0]] + [swap(both[u], u) for u in range(1, groups)]
-    gate = jax.nn.sigmoid(jnp.dot(normed, w_gate, preferred_element_type=jnp.float32))
-    half = groups // 2
-    early = make_lines(far_got[:half], groups, rows, cols, 10 ** 8)
-    left, near = make_near(near_got, early, rows, cols)
-    late = make_lines(far_got[half:], groups, rows, cols, 10 ** 5, (left,))
-    keep, send = make_cross(left, near, early, late, rows, cols)
-    sums = make_sums(keep, lax.ppermute(send, "col", [(0, 1), (1, 0)]))
+    gate = jax.nn.sigmoid(
+        jnp.einsum("cp,cd->pd", normed[:, :rows * cols], w_gate, preferred_element_type=jnp.float32)
+    )
+    far_lines, *near_lines = make_early(far_got[0], near_got[1], groups, rows, cols)
+    left, near = make_near(*near_lines, near_got[:1] + near_got[2:], rows, cols)
+    lines = make_late(left, far_lines, far_got[1:], groups, rows, cols)
+    parts = make_cross(left, near, lines, rows, cols)
+    sums = [[], []]
+    for part in (1, 0):
+        other = lax.ppermute(parts[2 + part], "col", [(0, 1), (1, 0)])
+        sums[part] = make_sums(parts[part], other)
+    sums = sums[0] + sums[1]
     returned = [sums[0]] + [swap(sums[u], u) for u in range(1, groups)]
     update = make_update(returned, out_gain.reshape(hidden, 1), w_out, gate, rows, cols)
     return update.reshape(rows, cols, channels)

time: 51.1 us -> 54.1 us (1.059)
  waiting for transfers between devices: 19.1 us -> 22.7 us
  Pallas kernels: 12.2 us -> 8.99 us
  starting transfers between devices: 18.4 us -> 20.3 us
    ppermute x10, waiting for transfers between devices: 17.2 us -> 21.7 us  [swap(): lax.ppermute(value, 'row', [(r, r ^ shift) for r in range(lax.axis_size('...]
    pallas_call x1, Pallas kernels: 3.66 us -> 1.74 us  [make_near(): pl.pallas_call(functools.partial(near_kernel, groups, rows, cols), in_spe...]
    ppermute x10, starting transfers between devices: 18.3 us -> 19.8 us  [swap(): lax.ppermute(value, 'row', [(r, r ^ shift) for r in range(lax.axis_size('...]
    pallas_call x1, Pallas kernels: 2.38 us -> 1.15 us  [make_cross(): pl.pallas_call(functools.partial(cross_kernel, groups, rows, cols), in_sp...]
    ppermute x1 -> x2, waiting for transfers between devices: 1.9 us -> 1.03 us  [shards(): other = lax.ppermute(parts[2 + part], 'col', [(0, 1), (1, 0)])]
  transfers between devices with their start and end apart: 11 -> 12, of which waited for: 7 -> 7; matrix products, arithmetic and copies ran while one was open for 1% -> 1% of each run, Pallas kernels for 8% -> 4%
where the time goes in v7:
time: 54.1 us; the launch traced here: 53.9 us
  waiting for transfers between devices  22.7 us (42%)
  starting transfers between devices  20.3 us (38%)
  Pallas kernels  8.99 us (17%)
  local copies, waits for them, and re-layouts  1.24 us (2%)
    ppermute x10, waiting for transfers between devices, swap(): lax.ppermute(value, 'row', [(r, r ^ shift) for r in range(lax.axis_size('...  21.7 us
    ppermute x10, starting transfers between devices, swap(): lax.ppermute(value, 'row', [(r, r ^ shift) for r in range(lax.axis_size('...  19.8 us
    pallas_call x1, Pallas kernels, make_edges(): pl.pallas_call(functools.partial(edges_kernel, groups, rows, cols, chunks...  3.96 us
    pallas_call x1, Pallas kernels, make_near(): pl.pallas_call(functools.partial(near_kernel, groups, rows, cols), in_spe...  1.74 us
    pallas_call x1, Pallas kernels, make_update(): pl.pallas_call(functools.partial(update_kernel, groups, rows, cols, chunk...  1.42 us
    pallas_call x1, Pallas kernels, make_cross(): pl.pallas_call(functools.partial(cross_kernel, groups, rows, cols), in_sp...  1.15 us
    unnamed x10, local copies, waits for them, and re-layouts  1.13 us
  transfers between devices with their start and end apart: 12, of which 7 were waited for; matrix products, arithmetic and copies ran while one was open for 1% of the time, Pallas kernels for 4%

profile of v7, /device:TPU:0, one launch (start us, length us, event | category | flops | bytes accessed | tf_op | source)
XLA Modules:
  0.0 53.9 jit_solution(13448739445200263540)
XLA Ops:
  0.0 0.0 copy-start
  0.0 4.0 %shard_map.91 = (bf16[128,2048]{1,0:T(8,128)(2,1)}, bf16[64,2048]{1,0:T(8,128)(2,1)}, bf16[64,2048]{1,0:T(8,128)(2,1)}, bf16[64,2048]{1,0:T(8,128)(2,1)}, bf16[6...) custom-call(bf16[1936,128]{1,0:T(8,128)(2,1)} %bitcast.5, ...), custom_call_target="tpu_custom_call" | custom-call | tf_op jit(solution)/shard_map/pallas_call | solution.py:120
  4.0 3.0 %collective-permute-start.1 = (bf16[64,2048]{1,0:T(8,128)(2,1)}, bf16[64,2048]{1,0:T(8,128)(2,1)S(1)}, u32[]{:S(2)}, u32[]{:S(2)}) collective-permute-start(bf16[64,2048]{1,0:T(8,128)(2,1)} %get-tuple-element.29), channel_id=1, source_target_pairs={{0,2},{2,0},{4,6},{6,4},{8,10},{10,8},{12,14},{14,12},{1,3},{3,1},... | collective-permute-start | bytes 786440 | tf_op jit(solution)/shard_map/ppermute | solution.py:389
  7.0 1.6 %collective-permute-start.2 = (bf16[64,2048]{1,0:T(8,128)(2,1)}, bf16[64,2048]{1,0:T(8,128)(2,1)S(1)}, u32[]{:S(2)}, u32[]{:S(2)}) collective-permute-start(bf16[64,2048]{1,0:T(8,128)(2,1)} %get-tuple-element.33), channel_id=1, source_target_pairs={{0,4},{2,6},{4,0},{6,2},{8,12},{10,14},{12,8},{14,10},{1,5},{3,7},... | collective-permute-start | bytes 786440 | tf_op jit(solution)/shard_map/ppermute | solution.py:389
  8.6 0.0 collective-permute-start.3
  8.6 3.0 %collective-permute-start = (bf16[32,2048]{1,0:T(8,128)(2,1)}, bf16[32,2048]{1,0:T(8,128)(2,1)S(1)}, u32[]{:S(2)}, u32[]{:S(2)}) collective-permute-start(bf16[32,2048]{1,0:T(8,128)(2,1)} %get-tuple-element.28), channel_id=1, source_target_pairs={{0,8},{2,10},{4,12},{6,14},{8,0},{10,2},{12,4},{14,6},{1,9},{3,11}... | collective-permute-start | bytes 393224 | tf_op jit(solution)/shard_map/ppermute | solution.py:389
  11.6 1.3 %collective-permute-start.4 = (bf16[32,2048]{1,0:T(8,128)(2,1)}, bf16[32,2048]{1,0:T(8,128)(2,1)S(1)}, u32[]{:S(2)}, u32[]{:S(2)}) collective-permute-start(bf16[32,2048]{1,0:T(8,128)(2,1)} %get-tuple-element.38), channel_id=1, source_target_pairs={{0,10},{2,8},{4,14},{6,12},{8,2},{10,0},{12,6},{14,4},{1,11},{3,9}... | collective-permute-start | bytes 393224 | tf_op jit(solution)/shard_map/ppermute | solution.py:389
  12.9 11.2 %collective-permute-done.far_ref = bf16[32,2048]{1,0:T(8,128)(2,1)S(1)} collective-permute-done((bf16[32,2048]{1,0:T(8,128)(2,1)}, bf16[32,2048]{1,0:T(8,128)(2,1)S(1)}, u32[]{:S(2)}, u32[]{:S(2)}) %collective-permute-start) | collective-permute-done | bytes 131104 | tf_op jit(solution)/shard_map/ppermute | solution.py:389
  24.0 2.5 %collective-permute-start.5 = (bf16[32,2048]{1,0:T(8,128)(2,1)}, bf16[32,2048]{1,0:T(8,128)(2,1)S(1)}, u32[]{:S(2)}, u32[]{:S(2)}) collective-permute-start(bf16[32,2048]{1,0:T(8,128)(2,1)} %get-tuple-element.39), channel_id=1, source_target_pairs={{0,12},{2,14},{4,8},{6,10},{8,4},{10,6},{12,0},{14,2},{1,13},{3,15... | collective-permute-start | bytes 393224 | tf_op jit(solution)/shard_map/ppermute | solution.py:389
  26.5 0.0 collective-permute-done.1.near_ref
  26.6 1.2 %collective-permute-start.6 = (bf16[32,2048]{1,0:T(8,128)(2,1)}, bf16[32,2048]{1,0:T(8,128)(2,1)S(1)}, u32[]{:S(2)}, u32[]{:S(2)}) collective-permute-start(bf16[32,2048]{1,0:T(8,128)(2,1)} %get-tuple-element.40), channel_id=1, source_target_pairs={{0,14},{2,12},{4,10},{6,8},{8,6},{10,4},{12,2},{14,0},{1,15},{3,13... | collective-permute-start | bytes 393224 | tf_op jit(solution)/shard_map/ppermute | solution.py:389
  27.8 0.3 shard_map.92
  28.1 0.0 collective-permute-done.2.refs_1_
  28.1 0.0 collective-permute-done.3.refs_2_
  28.1 0.0 copy-start.1
  28.1 0.9 %copy-done.1 = bf16[64,2048]{1,0:T(8,128)(2,1)S(1)} copy-done((bf16[64,2048]{1,0:T(8,128)(2,1)S(1)}, bf16[64,2048]{1,0:T(8,128)(2,1)}, u32[]{:S(2)}) %copy-start.1) | copy-done | bytes 262168
  29.0 1.7 %shard_map.93 = (bf16[32,88,128]{2,1,0:T(8,128)(2,1)S(1)}, bf16[4,32,2048]{2,1,0:T(8,128)(2,1)S(1)}) custom-call(f32[1,880,128]{2,1,0:T(8,128)S(1)} %get-tuple-element.30.left_lines, f32[1,880,128]{2,1,0:T(8,128)S(1)} %get-tuple-element.31.right_lines, bf16[64,2048]{1,0:T(8,128)(2,1)S(1)} %copy-done.1, bf16[64,2048]{1,0:T(8,128)(2,1)S(1)} %collective-permute-done.2.refs_1_, ...), custom_call_target="tpu_custom_call" | custom-call | flops 100000 | bytes 100000 | tf_op jit(solution)/shard_map/pallas_call | solution.py:294
  30.8 0.0 collective-permute-done.4.refs_0_
  30.8 1.7 %collective-permute-done.5.refs_1_ = bf16[32,2048]{1,0:T(8,128)(2,1)S(1)} collective-permute-done((bf16[32,2048]{1,0:T(8,128)(2,1)}, bf16[32,2048]{1,0:T(8,128)(2,1)S(1)}, u32[]{:S(2)}, u32[]{:S(2)}) %collective-permute-start.5) | collective-permute-done | bytes 131104 | tf_op jit(solution)/shard_map/ppermute | solution.py:389
  32.6 2.0 %collective-permute-done.6.refs_2_ = bf16[32,2048]{1,0:T(8,128)(2,1)S(1)} collective-permute-done((bf16[32,2048]{1,0:T(8,128)(2,1)}, bf16[32,2048]{1,0:T(8,128)(2,1)S(1)}, u32[]{:S(2)}, u32[]{:S(2)}) %collective-permute-start.6) | collective-permute-done | bytes 131104 | tf_op jit(solution)/shard_map/ppermute | solution.py:389
  34.5 0.3 shard_map.94.lines_ref
  34.8 0.0 copy-start.4
  34.9 1.1 %shard_map.95 = (bf16[2,32,2048]{2,1,0:T(8,128)(2,1)S(1)}, bf16[2,32,2048]{2,1,0:T(8,128)(2,1)S(1)}, bf16[2,32,2048]{2,1,0:T(8,128)(2,1)S(1)}, bf16[2,32,2048]{2,1,0:T(8,128)(2,1)S(1)}) custom-call(bf16[32,88,128]{2,1,0:T(8,128)(2,1)S(1)} %get-tuple-element.35.after_ref.left_ref, bf16[4,32,2048]{2,1,0:T(8,128)(2,1)S(1)} %get-tuple-element.36.near_ref, ...), custom_call_target="tpu_custom_call" | custom-call | flops 100000 | bytes 8000000 | tf_op jit(solution)/shard_map/pallas_call | solution.py:311
  36.0 0.1 collective-permute-start.9
  36.1 0.5 collective-permute-start.7
  36.6 1.0 %collective-permute-done.9.b_ref = bf16[2,32,2048]{2,1,0:T(8,128)(2,1)S(1)} collective-permute-done((bf16[2,32,2048]{2,1,0:T(8,128)(2,1)S(1)}, bf16[2,32,2048]{2,1,0:T(8,128)(2,1)S(1)}, u32[]{:S(2)}, u32[]{:S(2)}) %collective-permute-start.9) | collective-permute-done | bytes 262176 | tf_op jit(solution)/shard_map/ppermute | solution.py:412
  37.6 0.1 shard_map.97
  37.7 5.5 %collective-permute-start.10 = (bf16[32,2048]{1,0:T(8,128)(2,1)S(1)}, bf16[32,2048]{1,0:T(8,128)(2,1)S(1)}, u32[]{:S(2)}, u32[]{:S(2)}) collective-permute-start(bf16[32,2048]{1,0:T(8,128)(2,1)S(1)} %get-tuple-element.47), channel_id=1, source_target_pairs={{0,4},{2,6},{4,0},{6,2},{8,12},{10,14},{12,8},{14,10},{1,5},{3,7},... | collective-permute-start | bytes 393224 | tf_op jit(solution)/shard_map/ppermute | solution.py:389
  43.2 1.0 %collective-permute-start.11 = (bf16[32,2048]{1,0:T(8,128)(2,1)S(1)}, bf16[32,2048]{1,0:T(8,128)(2,1)S(1)}, u32[]{:S(2)}, u32[]{:S(2)}) collective-permute-start(bf16[32,2048]{1,0:T(8,128)(2,1)S(1)} %get-tuple-element.48), channel_id=1, source_target_pairs={{0,6},{2,4},{4,2},{6,0},{8,14},{10,12},{12,10},{14,8},{1,7},{3,5},... | collective-permute-start | bytes 393224 | tf_op jit(solution)/shard_map/ppermute | solution.py:389
  44.2 0.0 collective-permute-done.7.b_ref
  44.2 0.1 shard_map.96
  44.3 0.6 %collective-permute-start.8 = (bf16[32,2048]{1,0:T(8,128)(2,1)S(1)}, bf16[32,2048]{1,0:T(8,128)(2,1)S(1)}, u32[]{:S(2)}, u32[]{:S(2)}) collective-permute-start(bf16[32,2048]{1,0:T(8,128)(2,1)S(1)} %get-tuple-element.44), channel_id=1, source_target_pairs={{0,2},{2,0},{4,6},{6,4},{8,10},{10,8},{12,14},{14,12},{1,3},{3,1},... | collective-permute-start | bytes 393224 | tf_op jit(solution)/shard_map/ppermute | solution.py:389
  44.9 0.0 copy-done
  44.9 0.0 copy-done.4
  44.9 0.0 copy-start.3
  44.9 0.0 copy-start.2
  44.9 0.5 fusion.2.gate_ref
  45.4 0.2 copy-done.3
  45.5 0.1 copy.10.gain_ref
  45.6 1.7 %collective-permute-done.10.refs_2_ = bf16[32,2048]{1,0:T(8,128)(2,1)S(1)} collective-permute-done((bf16[32,2048]{1,0:T(8,128)(2,1)S(1)}, bf16[32,2048]{1,0:T(8,128)(2,1)S(1)}, u32[]{:S(2)}, u32[]{:S(2)}) %collective-permute-start.10) | collective-permute-done | bytes 131104 | tf_op jit(solution)/shard_map/ppermute | solution.py:389
  47.3 3.5 %collective-permute-done.11.refs_3_ = bf16[32,2048]{1,0:T(8,128)(2,1)S(1)} collective-permute-done((bf16[32,2048]{1,0:T(8,128)(2,1)S(1)}, bf16[32,2048]{1,0:T(8,128)(2,1)S(1)}, u32[]{:S(2)}, u32[]{:S(2)}) %collective-permute-start.11) | collective-permute-done | bytes 131104 | tf_op jit(solution)/shard_map/ppermute | solution.py:389
  50.9 1.6 %collective-permute-done.8.refs_1_ = bf16[32,2048]{1,0:T(8,128)(2,1)S(1)} collective-permute-done((bf16[32,2048]{1,0:T(8,128)(2,1)S(1)}, bf16[32,2048]{1,0:T(8,128)(2,1)S(1)}, u32[]{:S(2)}, u32[]{:S(2)}) %collective-permute-start.8) | collective-permute-done | bytes 131104 | tf_op jit(solution)/shard_map/ppermute | solution.py:389
  52.4 0.0 copy-done.2
  52.4 1.4 %shard_map.98 = bf16[1936,128]{1,0:T(8,128)(2,1)} custom-call(f32[128,1]{1,0:T(8,128)S(1)} %copy.10.gain_ref, bf16[128,128]{1,0:T(8,128)(2,1)S(1)} %copy-done.2, f32[1936,128]{1,0:T(8,128)S(1)} %fusion.2.gate_ref, bf16[32,2048]{1,0:T(8,128)(2,1)S(1)} %get-tuple-element.43.refs_0_, bf16[32,2048]{1,0:T(8,128)(2,1)S(1)} %collective-permute-done.8.refs_1_, ...), custom_call_target="tpu_custom_call" | custom-call | tf_op jit(solution)/shard_map/pallas_call | solution.py:374
Async XLA Ops:
  0.0 44.9 %copy-start = (bf16[128,128]{1,0:T(8,128)(2,1)S(1)}, bf16[128,128]{1,0:T(8,128)(2,1)}, u32[]{:S(2)}) copy-start(bf16[128,128]{1,0:T(8,128)(2,1)} %param.16) | copy-start | bytes 98308
  4.0 22.6 %collective-permute-start.1 = (bf16[64,2048]{1,0:T(8,128)(2,1)}, bf16[64,2048]{1,0:T(8,128)(2,1)S(1)}, u32[]{:S(2)}, u32[]{:S(2)}) collective-permute-start(bf16[64,2048]{1,0:T(8,128)(2,1)} %get-tuple-element.29), channel_id=1, source_target_pairs={{0,2},{2,0},{4,6},{6,4},{8,10},{10,8},{12,14},{14,12},{1,3},{3,1},... | collective-permute-start | bytes 786440 | tf_op jit(solution)/shard_map/ppermute | solution.py:389
  7.0 21.1 %collective-permute-start.2 = (bf16[64,2048]{1,0:T(8,128)(2,1)}, bf16[64,2048]{1,0:T(8,128)(2,1)S(1)}, u32[]{:S(2)}, u32[]{:S(2)}) collective-permute-start(bf16[64,2048]{1,0:T(8,128)(2,1)} %get-tuple-element.33), channel_id=1, source_target_pairs={{0,4},{2,6},{4,0},{6,2},{8,12},{10,14},{12,8},{14,10},{1,5},{3,7},... | collective-permute-start | bytes 786440 | tf_op jit(solution)/shard_map/ppermute | solution.py:389
  8.6 19.5 %collective-permute-start.3 = (bf16[64,2048]{1,0:T(8,128)(2,1)}, bf16[64,2048]{1,0:T(8,128)(2,1)S(1)}, u32[]{:S(2)}, u32[]{:S(2)}) collective-permute-start(bf16[64,2048]{1,0:T(8,128)(2,1)} %get-tuple-element.34), channel_id=1, source_target_pairs={{0,6},{2,4},{4,2},{6,0},{8,14},{10,12},{12,10},{14,8},{1,7},{3,5},... | collective-permute-start | bytes 786440 | tf_op jit(solution)/shard_map/ppermute | solution.py:389
  8.6 15.4 %collective-permute-start = (bf16[32,2048]{1,0:T(8,128)(2,1)}, bf16[32,2048]{1,0:T(8,128)(2,1)S(1)}, u32[]{:S(2)}, u32[]{:S(2)}) collective-permute-start(bf16[32,2048]{1,0:T(8,128)(2,1)} %get-tuple-element.28), channel_id=1, source_target_pairs={{0,8},{2,10},{4,12},{6,14},{8,0},{10,2},{12,4},{14,6},{1,9},{3,11}... | collective-permute-start | bytes 393224 | tf_op jit(solution)/shard_map/ppermute | solution.py:389
  11.6 19.2 %collective-permute-start.4 = (bf16[32,2048]{1,0:T(8,128)(2,1)}, bf16[32,2048]{1,0:T(8,128)(2,1)S(1)}, u32[]{:S(2)}, u32[]{:S(2)}) collective-permute-start(bf16[32,2048]{1,0:T(8,128)(2,1)} %get-tuple-element.38), channel_id=1, source_target_pairs={{0,10},{2,8},{4,14},{6,12},{8,2},{10,0},{12,6},{14,4},{1,11},{3,9}... | collective-permute-start | bytes 393224 | tf_op jit(solution)/shard_map/ppermute | solution.py:389
  24.0 8.5 %collective-permute-start.5 = (bf16[32,2048]{1,0:T(8,128)(2,1)}, bf16[32,2048]{1,0:T(8,128)(2,1)S(1)}, u32[]{:S(2)}, u32[]{:S(2)}) collective-permute-start(bf16[32,2048]{1,0:T(8,128)(2,1)} %get-tuple-element.39), channel_id=1, source_target_pairs={{0,12},{2,14},{4,8},{6,10},{8,4},{10,6},{12,0},{14,2},{1,13},{3,15... | collective-permute-start | bytes 393224 | tf_op jit(solution)/shard_map/ppermute | solution.py:389
  26.6 8.0 %collective-permute-start.6 = (bf16[32,2048]{1,0:T(8,128)(2,1)}, bf16[32,2048]{1,0:T(8,128)(2,1)S(1)}, u32[]{:S(2)}, u32[]{:S(2)}) collective-permute-start(bf16[32,2048]{1,0:T(8,128)(2,1)} %get-tuple-element.40), channel_id=1, source_target_pairs={{0,14},{2,12},{4,10},{6,8},{8,6},{10,4},{12,2},{14,0},{1,15},{3,13... | collective-permute-start | bytes 393224 | tf_op jit(solution)/shard_map/ppermute | solution.py:389
  28.1 1.0 %copy-start.1 = (bf16[64,2048]{1,0:T(8,128)(2,1)S(1)}, bf16[64,2048]{1,0:T(8,128)(2,1)}, u32[]{:S(2)}) copy-start(bf16[64,2048]{1,0:T(8,128)(2,1)} %get-tuple-element.32.refs_0_) | copy-start | bytes 786436
  34.8 10.0 %copy-start.4 = (bf16[128,2048]{1,0:T(8,128)(2,1)S(1)}, bf16[128,2048]{1,0:T(8,128)(2,1)}, u32[]{:S(2)}) copy-start(bf16[128,2048]{1,0:T(8,128)(2,1)} %get-tuple-element.27) | copy-start | bytes 1572868
  36.0 1.6 %collective-permute-start.9 = (bf16[2,32,2048]{2,1,0:T(8,128)(2,1)S(1)}, bf16[2,32,2048]{2,1,0:T(8,128)(2,1)S(1)}, u32[]{:S(2)}, u32[]{:S(2)}) collective-permute-start(bf16[2,32,2048]{2,1,0:T(8,128)(2,1)S(1)} %get-tuple-element.46), channel_id=1, source_target_pairs={{0,1},{1,0},{2,3},{3,2},{4,5},{5,4},{6,7},{7,6},{8,9},{9,8},{10,11... | collective-permute-start | bytes 786440 | tf_op jit(solution)/shard_map/ppermute | solution.py:412
  36.1 8.1 %collective-permute-start.7 = (bf16[2,32,2048]{2,1,0:T(8,128)(2,1)S(1)}, bf16[2,32,2048]{2,1,0:T(8,128)(2,1)S(1)}, u32[]{:S(2)}, u32[]{:S(2)}) collective-permute-start(bf16[2,32,2048]{2,1,0:T(8,128)(2,1)S(1)} %get-tuple-element.42), channel_id=1, source_target_pairs={{0,1},{1,0},{2,3},{3,2},{4,5},{5,4},{6,7},{7,6},{8,9},{9,8},{10,11... | collective-permute-start | bytes 786440 | tf_op jit(solution)/shard_map/ppermute | solution.py:412
  37.7 9.6 %collective-permute-start.10 = (bf16[32,2048]{1,0:T(8,128)(2,1)S(1)}, bf16[32,2048]{1,0:T(8,128)(2,1)S(1)}, u32[]{:S(2)}, u32[]{:S(2)}) collective-permute-start(bf16[32,2048]{1,0:T(8,128)(2,1)S(1)} %get-tuple-element.47), channel_id=1, source_target_pairs={{0,4},{2,6},{4,0},{6,2},{8,12},{10,14},{12,8},{14,10},{1,5},{3,7},... | collective-permute-start | bytes 393224 | tf_op jit(solution)/shard_map/ppermute | solution.py:389
  43.2 7.7 %collective-permute-start.11 = (bf16[32,2048]{1,0:T(8,128)(2,1)S(1)}, bf16[32,2048]{1,0:T(8,128)(2,1)S(1)}, u32[]{:S(2)}, u32[]{:S(2)}) collective-permute-start(bf16[32,2048]{1,0:T(8,128)(2,1)S(1)} %get-tuple-element.48), channel_id=1, source_target_pairs={{0,6},{2,4},{4,2},{6,0},{8,14},{10,12},{12,10},{14,8},{1,7},{3,5},... | collective-permute-start | bytes 393224 | tf_op jit(solution)/shard_map/ppermute | solution.py:389
  44.3 8.1 %collective-permute-start.8 = (bf16[32,2048]{1,0:T(8,128)(2,1)S(1)}, bf16[32,2048]{1,0:T(8,128)(2,1)S(1)}, u32[]{:S(2)}, u32[]{:S(2)}) collective-permute-start(bf16[32,2048]{1,0:T(8,128)(2,1)S(1)} %get-tuple-element.44), channel_id=1, source_target_pairs={{0,2},{2,0},{4,6},{6,4},{8,10},{10,8},{12,14},{14,12},{1,3},{3,1},... | collective-permute-start | bytes 393224 | tf_op jit(solution)/shard_map/ppermute | solution.py:389
  44.9 0.7 %copy-start.3 = (f32[128]{0:T(128)S(1)}, f32[128]{0:T(128)}, u32[]{:S(2)}) copy-start(f32[128]{0:T(128)} %param.13) | copy-start | bytes 1540
  44.9 7.6 %copy-start.2 = (bf16[128,128]{1,0:T(8,128)(2,1)S(1)}, bf16[128,128]{1,0:T(8,128)(2,1)}, u32[]{:S(2)}) copy-start(bf16[128,128]{1,0:T(8,128)(2,1)} %w_ref.1) | copy-start | bytes 98308

commit v8 on v6

--- a/solution.py
+++ b/solution.py
@@ -47,10 +47,10 @@
     return i_ok * k_ok
 
 
-def edge_of(normed, w_ref, mask, groups):
-    hidden = w_ref.shape[1] // 2
-    block = normed.shape[0]
-    projected = lax.dot_general(w_ref[...], normed, (((0,), (1,)), ((), ())), preferred_element_type=jnp.float32)
+def edge_of(weights, normed, mask, groups):
+    hidden = weights.shape[0] // 2
+    block = normed.shape[1]
+    projected = jnp.dot(weights, normed, preferred_element_type=jnp.float32)
     edge = sigmoid(projected[:hidden]) * projected[hidden:]
     edge = edge.reshape(hidden // 8, 8, block) * mask[None]
     return edge.reshape(groups, hidden // groups, block).astype(jnp.bfloat16)
@@ -76,34 +76,33 @@
         copy.start()
     block = chunks[0][1]
     channels = x_s.shape[1]
-    average = jnp.full((2 * channels, channels), 1.0 / channels, jnp.bfloat16)
     spare = x_s.shape[0] - count
     if spare:
         x_s[pl.ds(count, spare)] = jnp.zeros((spare, x_s.shape[1]), x_s.dtype)
     stores = []
     for n, (at, size) in enumerate(chunks):
         pieces[n].wait()
-        x = x_s[pl.ds(at, block)]
-        centred = x.astype(jnp.float32) - jnp.dot(x, average[:channels], preferred_element_type=jnp.float32)
-        square = centred * centred
-        high = square.astype(jnp.bfloat16)
-        low = (square - high.astype(jnp.float32)).astype(jnp.bfloat16)
-        variance = jnp.dot(jnp.concatenate([high, low], axis=1), average, preferred_element_type=jnp.float32)
+        x = x_s[pl.ds(at, block)].T.astype(jnp.float32)
+        centred = x - jnp.mean(x, axis=0, keepdims=True)
+        variance = jnp.mean(centred * centred, axis=0, keepdims=True)
         if n == 0:
             for copy in loads:
                 copy.wait()
-        normed = (centred * lax.rsqrt(variance + EPS) * gain_s[...]).astype(jnp.bfloat16)
-        normed_s[pl.ds(at, block)] = normed
+            gain = jnp.broadcast_to(gain_s[...], (LANES, channels)).T
+            gain = jnp.concatenate([gain] * (block // LANES), axis=1)
+            right_w, left_w = wr_s[...].T, wl_s[...].T
+        normed = (centred * lax.rsqrt(variance + EPS) * gain).astype(jnp.bfloat16)
         mask = mask_of(cols, first_row, first_col, lens_s, res_s, at, block)
         lanes = pl.ds(at, block)
-        held[:, own:, lanes] = edge_of(normed, wr_s, mask, groups)
-        held[:, :own, lanes] = edge_of(normed, wl_s, mask, groups)
+        normed_s[:, lanes] = normed
+        held[:, own:, lanes] = edge_of(right_w, normed, mask, groups)
+        held[:, :own, lanes] = edge_of(left_w, normed, mask, groups)
         sent = [
             (held.at[jnp.bitwise_xor(mine, u), pl.ds(own, own), lanes], right_refs[u].at[:, lanes])
             for u in range(groups)
         ]
         sent.append((held.at[:, :, lanes], both_ref.at[:, :, lanes]))
-        sent.append((normed_s.at[pl.ds(at, size)], normed_ref.at[pl.ds(at, size)]))
+        sent.append((normed_s.at[:, lanes], normed_ref.at[:, lanes]))
         for m, (src, dst) in enumerate(sent):
             stores.append(pltpu.make_async_copy(src, dst, out_sems.at[n, m]))
             stores[-1].start()
@@ -122,7 +121,7 @@
         functools.partial(edges_kernel, groups, rows, cols, chunks),
         in_specs=[here] * 6,
         out_specs=[here] * (2 + groups),
-        out_shape=[jax.ShapeDtypeStruct((count, channels), jnp.bfloat16)]
+        out_shape=[jax.ShapeDtypeStruct((channels, flat), jnp.bfloat16)]
         + [jax.ShapeDtypeStruct((groups, 2 * own, flat), jnp.bfloat16)]
         + [jax.ShapeDtypeStruct((own, flat), jnp.bfloat16)] * groups,
         scratch_shapes=[
@@ -132,7 +131,7 @@
             pltpu.VMEM(w_right.shape, w_right.dtype),
             pltpu.SMEM(lens.shape, lens.dtype),
             pltpu.SMEM(resolved.shape, resolved.dtype),
-            pltpu.VMEM((flat, channels), jnp.bfloat16),
+            pltpu.VMEM((channels, flat), jnp.bfloat16),
             pltpu.VMEM((groups, 2 * own, flat), jnp.bfloat16),
             pltpu.SemaphoreType.DMA((5 + len(chunks),)),
             pltpu.SemaphoreType.DMA((len(chunks), 2 + groups)),
@@ -226,20 +225,24 @@
         prod_s[t, pl.ds(d, count, stride=step), :] = prod[:, t * LANES:(t + 1) * LANES]
 
 
-def cross_kernel(groups, rows, cols, left_ref, near_ref, early_ref, late_ref, keep_ref, send_ref, right_s, prod_s, pair_s):
+def cross_kernel(groups, rows, cols, left_ref, near_ref, early_ref, late_ref, *refs):
+    keep_refs, send_refs = refs[:2], refs[2:4]
+    right_s, prod_s, pair_s = refs[4:]
     _, _, mine, half, col = place_of(groups, rows, cols)
     step = prod_s.shape[1] // (groups * rows)
     size = early_ref.shape[1]
     base = pl.multiple_of(mine // (groups // 2) * size, 8)
     right_s[:, pl.ds(base, size), :] = early_ref[...]
     right_s[:, pl.ds(pl.multiple_of(size - base, 8), size), :] = late_ref[...]
-    for d in range(keep_ref.shape[1]):
+    for d in range(left_ref.shape[0]):
         multiply(left_ref[d], channel_of(right_s, d, groups * rows, step), prod_s, d, step)
     for u in range(groups):
         pack(prod_s, pair_s, u, jnp.bitwise_xor(mine, u), rows, cols, step)
     near_kept = col == half
-    keep_ref[...] = jnp.where(near_kept, near_ref[...], pair_s[...])
-    send_ref[...] = jnp.where(near_kept, pair_s[...], near_ref[...])
+    for part in range(2):
+        pieces = pl.ds(part * (groups // 2), groups // 2)
+        keep_refs[part][...] = jnp.where(near_kept, near_ref[pieces], pair_s[pieces])
+        send_refs[part][...] = jnp.where(near_kept, pair_s[pieces], near_ref[pieces])
 
 
 def make_near(got, after, rows, cols):
@@ -284,8 +287,8 @@
     return pl.pallas_call(
         functools.partial(cross_kernel, groups, rows, cols),
         in_specs=[whole] * 4,
-        out_specs=[whole] * 2,
-        out_shape=[jax.ShapeDtypeStruct(near.shape, near.dtype)] * 2,
+        out_specs=[whole] * 4,
+        out_shape=[jax.ShapeDtypeStruct((groups // 2, ch, flat), near.dtype)] * 4,
         scratch_shapes=[held, held, pltpu.VMEM(near.shape, near.dtype)],
         compiler_params=pltpu.CompilerParams(vmem_limit_bytes=VMEM_LIMIT),
         cost_estimate=pl.CostEstimate(flops=10 ** 5, bytes_accessed=8 * 10 ** 6, transcendentals=0),
@@ -371,13 +374,19 @@
     halves = [[h * groups + r for r in range(groups)] for h in range(2)]
     far_got = [swap(right[u], groups + u) for u in range(groups)]
     near_got = lax.all_to_all(both, "row", split_axis=0, concat_axis=0, tiled=True, axis_index_groups=halves)
-    gate = jax.nn.sigmoid(jnp.dot(normed, w_gate, preferred_element_type=jnp.float32))
+    gate = jax.nn.sigmoid(
+        jnp.einsum("cp,cd->pd", normed[:, :rows * cols], w_gate, preferred_element_type=jnp.float32)
+    )
     half = groups // 2
     early = make_lines(far_got[:half], groups, rows, cols, 10 ** 8)
     left, near = make_near(near_got, early, rows, cols)
     late = make_lines(far_got[half:], groups, rows, cols, 10 ** 5, (left,))
-    keep, send = make_cross(left, near, early, late, rows, cols)
-    sums = make_sums(keep, lax.ppermute(send, "col", [(0, 1), (1, 0)]))
+    parts = make_cross(left, near, early, late, rows, cols)
+    sums = [[], []]
+    for part in (1, 0):
+        other = lax.ppermute(parts[2 + part], "col", [(0, 1), (1, 0)])
+        sums[part] = make_sums(parts[part], other)
+    sums = sums[0] + sums[1]
     returned = [sums[0]] + [swap(sums[u], u) for u in range(1, groups)]
     update = make_update(returned, out_gain.reshape(hidden, 1), w_out, gate, rows, cols)
     return update.reshape(rows, cols, channels)

time: 52.8 us -> 51.9 us (0.983)
  Pallas kernels: 9.75 us -> 8.84 us
  waiting for transfers between devices: 24.6 us -> 24 us
    pallas_call x1, Pallas kernels: 4.76 us -> 3.85 us  [make_edges(): pl.pallas_call(functools.partial(edges_kernel, groups, rows, cols, chunks...]
    ppermute x1 -> x2, waiting for transfers between devices: 1.9 us -> 1.03 us  [shards(): other = lax.ppermute(parts[2 + part], 'col', [(0, 1), (1, 0)])]
  transfers between devices with their start and end apart: 9 -> 10, of which waited for: 9 -> 9; matrix products, arithmetic and copies ran while one was open for 1% -> 1% of each run, Pallas kernels for 4% -> 4%
where the time goes in v8:
time: 51.9 us; the launch traced here: 51.7 us
  waiting for transfers between devices  24 us (46%)
  starting transfers between devices  17.5 us (34%)
  Pallas kernels  8.84 us (17%)
  local copies, waits for them, and re-layouts  0.79 us (2%)
    ppermute x7, waiting for transfers between devices, swap(): lax.ppermute(value, 'row', [(r, r ^ shift) for r in range(lax.axis_size('...  22.1 us
    ppermute x7, starting transfers between devices, swap(): lax.ppermute(value, 'row', [(r, r ^ shift) for r in range(lax.axis_size('...  11.6 us
    all_to_all x1, starting transfers between devices, shards(): lax.all_to_all(both, 'row', split_axis=0, concat_axis=0, tiled=True, axis...  5.39 us
    pallas_call x1, Pallas kernels, make_edges(): pl.pallas_call(functools.partial(edges_kernel, groups, rows, cols, chunks...  3.85 us
    pallas_call x1, Pallas kernels, make_near(): pl.pallas_call(functools.partial(near_kernel, groups, rows, cols), in_spe...  1.75 us
    pallas_call x1, Pallas kernels, make_update(): pl.pallas_call(functools.partial(update_kernel, groups, rows, cols, chunk...  1.41 us
    pallas_call x1, Pallas kernels, make_cross(): pl.pallas_call(functools.partial(cross_kernel, groups, rows, cols), in_sp...  1.28 us
  transfers between devices with their start and end apart: 10, of which 9 were waited for; matrix products, arithmetic and copies ran while one was open for 1% of the time, Pallas kernels for 4%

profile of v8, /device:TPU:0, one launch (start us, length us, event | category | flops | bytes accessed | tf_op | source)
XLA Modules:
  0.0 51.7 jit_solution(7579860521062681652)
XLA Ops:
  0.0 0.0 copy-start
  0.0 3.8 %shard_map.91 = (bf16[128,2048]{1,0:T(8,128)(2,1)}, bf16[4,64,2048]{2,1,0:T(8,128)(2,1)}, bf16[32,2048]{1,0:T(8,128)(2,1)}, bf16[32,2048]{1,0:T(8,128)(2,1)}, bf...) custom-call(bf16[1936,128]{1,0:T(8,128)(2,1)} %bitcast.5, f32[1,128]{1,0:T(1,128)} %bitcast.7, bf16[128,256]{1,0:T(8,128)(2,1)} %wl_ref.1, ...), custom_call_target="tpu_custom_call" | custom-call | tf_op jit(solution)/shard_map/pallas_call | solution.py:120
  3.9 0.0 copy-start.7
  3.9 0.0 copy-start.6
  3.9 0.0 copy-start.5
  3.9 0.0 copy-start.4
  3.9 5.4 %all-to-all-start = ((bf16[4,64,2048]{2,1,0:T(8,128)(2,1)}), bf16[4,64,2048]{2,1,0:T(8,128)(2,1)S(1)}, u32[]{:S(2)}, u32[]{:S(2)}) async-start(bf16[4,64,2048]{2,1,0:T(8,128)(2,1)} %get-tuple-element.24), calls=%async_computation | async-start | bytes 2097152 | tf_op jit(solution)/shard_map/all_to_all | solution.py:376
  9.3 0.0 copy-done.7
  9.3 2.6 %collective-permute-start = (bf16[32,2048]{1,0:T(8,128)(2,1)S(1)}, bf16[32,2048]{1,0:T(8,128)(2,1)S(1)}, u32[]{:S(2)}, u32[]{:S(2)}) collective-permute-start(bf16[32,2048]{1,0:T(8,128)(2,1)S(1)} %copy-done.7), channel_id=1, source_target_pairs={{0,8},{2,10},{4,12},{6,14},{8,0},{10,2},{12,4},{14,6},{1,9},{3,11}... | collective-permute-start | bytes 393224 | tf_op jit(solution)/shard_map/ppermute | solution.py:362
  11.9 0.0 copy-done.6
  11.9 1.8 %collective-permute-start.1 = (bf16[32,2048]{1,0:T(8,128)(2,1)S(1)}, bf16[32,2048]{1,0:T(8,128)(2,1)S(1)}, u32[]{:S(2)}, u32[]{:S(2)}) collective-permute-start(bf16[32,2048]{1,0:T(8,128)(2,1)S(1)} %copy-done.6), channel_id=1, source_target_pairs={{0,10},{2,8},{4,14},{6,12},{8,2},{10,0},{12,6},{14,4},{1,11},{3,9}... | collective-permute-start | bytes 393224 | tf_op jit(solution)/shard_map/ppermute | solution.py:362
  13.7 0.0 copy-done.5
  13.7 3.5 %collective-permute-start.2 = (bf16[32,2048]{1,0:T(8,128)(2,1)S(1)}, bf16[32,2048]{1,0:T(8,128)(2,1)S(1)}, u32[]{:S(2)}, u32[]{:S(2)}) collective-permute-start(bf16[32,2048]{1,0:T(8,128)(2,1)S(1)} %copy-done.5), channel_id=1, source_target_pairs={{0,12},{2,14},{4,8},{6,10},{8,4},{10,6},{12,0},{14,2},{1,13},{3,15... | collective-permute-start | bytes 393224 | tf_op jit(solution)/shard_map/ppermute | solution.py:362
  17.2 0.0 copy-done.4
  17.2 0.1 collective-permute-start.3
  17.3 7.5 %collective-permute-done.refs_0_ = bf16[32,2048]{1,0:T(8,128)(2,1)S(1)} collective-permute-done((bf16[32,2048]{1,0:T(8,128)(2,1)S(1)}, bf16[32,2048]{1,0:T(8,128)(2,1)S(1)}, u32[]{:S(2)}, u32[]{:S(2)}) %collective-permute-start) | collective-permute-done | bytes 131104 | tf_op jit(solution)/shard_map/ppermute | solution.py:362
  24.7 2.8 %collective-permute-done.1.refs_1_ = bf16[32,2048]{1,0:T(8,128)(2,1)S(1)} collective-permute-done((bf16[32,2048]{1,0:T(8,128)(2,1)S(1)}, bf16[32,2048]{1,0:T(8,128)(2,1)S(1)}, u32[]{:S(2)}, u32[]{:S(2)}) %collective-permute-start.1) | collective-permute-done | bytes 131104 | tf_op jit(solution)/shard_map/ppermute | solution.py:362
  27.5 0.2 shard_map.92.after_ref.early_ref
  27.8 0.8 %all-to-all-done.got_ref = bf16[4,64,2048]{2,1,0:T(8,128)(2,1)S(1)} async-done(((bf16[4,64,2048]{2,1,0:T(8,128)(2,1)}), bf16[4,64,2048]{2,1,0:T(8,128)(2,1)S(1)}, u32[]{:S(2)}, u32[]{:S(2)}) %all-to-all-start) | async-done | bytes 1048608 | tf_op jit(solution)/shard_map/all_to_all | solution.py:376
  28.6 1.8 %shard_map.93 = (bf16[32,88,128]{2,1,0:T(8,128)(2,1)S(1)}, bf16[4,32,2048]{2,1,0:T(8,128)(2,1)S(1)}) custom-call(f32[1,1760,128]{2,1,0:T(8,128)S(1)} %shard_map.92.after_ref.early_ref, bf16[4,64,2048]{2,1,0:T(8,128)(2,1)S(1)} %all-to-all-done.got_ref), custom_call_target="tpu_custom_call" | custom-call | flops 100000 | bytes 100000 | tf_op jit(solution)/shard_map/pallas_call | solution.py:255
  30.3 4.5 %collective-permute-done.2.refs_0_ = bf16[32,2048]{1,0:T(8,128)(2,1)S(1)} collective-permute-done((bf16[32,2048]{1,0:T(8,128)(2,1)S(1)}, bf16[32,2048]{1,0:T(8,128)(2,1)S(1)}, u32[]{:S(2)}, u32[]{:S(2)}) %collective-permute-start.2) | collective-permute-done | bytes 131104 | tf_op jit(solution)/shard_map/ppermute | solution.py:362
  34.8 2.3 %collective-permute-done.3.refs_1_ = bf16[32,2048]{1,0:T(8,128)(2,1)S(1)} collective-permute-done((bf16[32,2048]{1,0:T(8,128)(2,1)S(1)}, bf16[32,2048]{1,0:T(8,128)(2,1)S(1)}, u32[]{:S(2)}, u32[]{:S(2)}) %collective-permute-start.3) | collective-permute-done | bytes 131104 | tf_op jit(solution)/shard_map/ppermute | solution.py:362
  37.1 0.2 shard_map.94.late_ref
  37.3 1.3 %shard_map.95 = (bf16[2,32,2048]{2,1,0:T(8,128)(2,1)S(1)}, bf16[2,32,2048]{2,1,0:T(8,128)(2,1)S(1)}, bf16[2,32,2048]{2,1,0:T(8,128)(2,1)S(1)}, bf16[2,32,2048]{2,1,0:T(8,128)(2,1)S(1)}) custom-call(bf16[32,88,128]{2,1,0:T(8,128)(2,1)S(1)} %get-tuple-element.25.refs_2_.left_ref, bf16[4,32,2048]{2,1,0:T(8,128)(2,1)S(1)} %get-tuple-element.26.near_ref, ...), custom_call_target="tpu_custom_call" | custom-call | flops 100000 | bytes 8000000 | tf_op jit(solution)/shard_map/pallas_call | solution.py:287
  38.6 0.1 collective-permute-start.6
  38.7 0.5 collective-permute-start.4
  39.2 1.0 %collective-permute-done.6.b_ref = bf16[2,32,2048]{2,1,0:T(8,128)(2,1)S(1)} collective-permute-done((bf16[2,32,2048]{2,1,0:T(8,128)(2,1)S(1)}, bf16[2,32,2048]{2,1,0:T(8,128)(2,1)S(1)}, u32[]{:S(2)}, u32[]{:S(2)}) %collective-permute-start.6) | collective-permute-done | bytes 262176 | tf_op jit(solution)/shard_map/ppermute | solution.py:387
  40.2 0.0 copy-start.3
  40.2 0.1 shard_map.97
  40.3 0.1 collective-permute-start.7
  40.3 2.0 %collective-permute-start.8 = (bf16[32,2048]{1,0:T(8,128)(2,1)S(1)}, bf16[32,2048]{1,0:T(8,128)(2,1)S(1)}, u32[]{:S(2)}, u32[]{:S(2)}) collective-permute-start(bf16[32,2048]{1,0:T(8,128)(2,1)S(1)} %get-tuple-element.36), channel_id=1, source_target_pairs={{0,6},{2,4},{4,2},{6,0},{8,14},{10,12},{12,10},{14,8},{1,7},{3,5},... | collective-permute-start | bytes 393224 | tf_op jit(solution)/shard_map/ppermute | solution.py:362
  42.4 0.0 collective-permute-done.4.b_ref
  42.4 0.1 shard_map.96
  42.4 1.5 %collective-permute-start.5 = (bf16[32,2048]{1,0:T(8,128)(2,1)S(1)}, bf16[32,2048]{1,0:T(8,128)(2,1)S(1)}, u32[]{:S(2)}, u32[]{:S(2)}) collective-permute-start(bf16[32,2048]{1,0:T(8,128)(2,1)S(1)} %get-tuple-element.32), channel_id=1, source_target_pairs={{0,2},{2,0},{4,6},{6,4},{8,10},{10,8},{12,14},{14,12},{1,3},{3,1},... | collective-permute-start | bytes 393224 | tf_op jit(solution)/shard_map/ppermute | solution.py:362
  43.9 0.0 copy-done
  43.9 0.0 copy-done.3
  44.0 0.5 fusion.2.gate_ref
  44.4 0.0 copy-start.2
  44.4 0.6 %copy-done.2 = f32[128]{0:T(128)S(1)} copy-done((f32[128]{0:T(128)S(1)}, f32[128]{0:T(128)}, u32[]{:S(2)}) %copy-start.2) | copy-done | bytes 536
  45.1 0.0 copy-start.1
  45.1 0.1 copy.10.gain_ref
  45.2 1.5 %collective-permute-done.7.refs_2_ = bf16[32,2048]{1,0:T(8,128)(2,1)S(1)} collective-permute-done((bf16[32,2048]{1,0:T(8,128)(2,1)S(1)}, bf16[32,2048]{1,0:T(8,128)(2,1)S(1)}, u32[]{:S(2)}, u32[]{:S(2)}) %collective-permute-start.7) | collective-permute-done | bytes 131104 | tf_op jit(solution)/shard_map/ppermute | solution.py:362
  46.7 2.1 %collective-permute-done.8.refs_3_ = bf16[32,2048]{1,0:T(8,128)(2,1)S(1)} collective-permute-done((bf16[32,2048]{1,0:T(8,128)(2,1)S(1)}, bf16[32,2048]{1,0:T(8,128)(2,1)S(1)}, u32[]{:S(2)}, u32[]{:S(2)}) %collective-permute-start.8) | collective-permute-done | bytes 131104 | tf_op jit(solution)/shard_map/ppermute | solution.py:362
  48.8 1.5 %collective-permute-done.5.refs_1_ = bf16[32,2048]{1,0:T(8,128)(2,1)S(1)} collective-permute-done((bf16[32,2048]{1,0:T(8,128)(2,1)S(1)}, bf16[32,2048]{1,0:T(8,128)(2,1)S(1)}, u32[]{:S(2)}, u32[]{:S(2)}) %collective-permute-start.5) | collective-permute-done | bytes 131104 | tf_op jit(solution)/shard_map/ppermute | solution.py:362
  50.3 0.0 copy-done.1
  50.3 1.4 %shard_map.98 = bf16[1936,128]{1,0:T(8,128)(2,1)} custom-call(f32[128,1]{1,0:T(8,128)S(1)} %copy.10.gain_ref, bf16[128,128]{1,0:T(8,128)(2,1)S(1)} %copy-done.1, f32[1936,128]{1,0:T(8,128)S(1)} %fusion.2.gate_ref, bf16[32,2048]{1,0:T(8,128)(2,1)S(1)} %get-tuple-element.31.refs_0_, bf16[32,2048]{1,0:T(8,128)(2,1)S(1)} %collective-permute-done.5.refs_1_, ...), custom_call_target="tpu_custom_call" | custom-call | tf_op jit(solution)/shard_map/pallas_call | solution.py:347
Async XLA Ops:
  0.0 43.9 %copy-start = (bf16[128,128]{1,0:T(8,128)(2,1)S(1)}, bf16[128,128]{1,0:T(8,128)(2,1)}, u32[]{:S(2)}) copy-start(bf16[128,128]{1,0:T(8,128)(2,1)} %param.16) | copy-start | bytes 98308
  3.9 5.4 %copy-start.7 = (bf16[32,2048]{1,0:T(8,128)(2,1)S(1)}, bf16[32,2048]{1,0:T(8,128)(2,1)}, u32[]{:S(2)}) copy-start(bf16[32,2048]{1,0:T(8,128)(2,1)} %get-tuple-element.22) | copy-start | bytes 393220
  3.9 8.0 %copy-start.6 = (bf16[32,2048]{1,0:T(8,128)(2,1)S(1)}, bf16[32,2048]{1,0:T(8,128)(2,1)}, u32[]{:S(2)}) copy-start(bf16[32,2048]{1,0:T(8,128)(2,1)} %get-tuple-element.23) | copy-start | bytes 393220
  3.9 9.8 %copy-start.5 = (bf16[32,2048]{1,0:T(8,128)(2,1)S(1)}, bf16[32,2048]{1,0:T(8,128)(2,1)}, u32[]{:S(2)}) copy-start(bf16[32,2048]{1,0:T(8,128)(2,1)} %get-tuple-element.27) | copy-start | bytes 393220
  3.9 13.3 %copy-start.4 = (bf16[32,2048]{1,0:T(8,128)(2,1)S(1)}, bf16[32,2048]{1,0:T(8,128)(2,1)}, u32[]{:S(2)}) copy-start(bf16[32,2048]{1,0:T(8,128)(2,1)} %get-tuple-element.28) | copy-start | bytes 393220
  3.9 24.7 %all-to-all-start = ((bf16[4,64,2048]{2,1,0:T(8,128)(2,1)}), bf16[4,64,2048]{2,1,0:T(8,128)(2,1)S(1)}, u32[]{:S(2)}, u32[]{:S(2)}) async-start(bf16[4,64,2048]{2,1,0:T(8,128)(2,1)} %get-tuple-element.24), calls=%async_computation | async-start | bytes 2097152 | tf_op jit(solution)/shard_map/all_to_all | solution.py:376
  9.3 15.4 %collective-permute-start = (bf16[32,2048]{1,0:T(8,128)(2,1)S(1)}, bf16[32,2048]{1,0:T(8,128)(2,1)S(1)}, u32[]{:S(2)}, u32[]{:S(2)}) collective-permute-start(bf16[32,2048]{1,0:T(8,128)(2,1)S(1)} %copy-done.7), channel_id=1, source_target_pairs={{0,8},{2,10},{4,12},{6,14},{8,0},{10,2},{12,4},{14,6},{1,9},{3,11}... | collective-permute-start | bytes 393224 | tf_op jit(solution)/shard_map/ppermute | solution.py:362
  11.9 15.7 %collective-permute-start.1 = (bf16[32,2048]{1,0:T(8,128)(2,1)S(1)}, bf16[32,2048]{1,0:T(8,128)(2,1)S(1)}, u32[]{:S(2)}, u32[]{:S(2)}) collective-permute-start(bf16[32,2048]{1,0:T(8,128)(2,1)S(1)} %copy-done.6), channel_id=1, source_target_pairs={{0,10},{2,8},{4,14},{6,12},{8,2},{10,0},{12,6},{14,4},{1,11},{3,9}... | collective-permute-start | bytes 393224 | tf_op jit(solution)/shard_map/ppermute | solution.py:362
  13.7 21.1 %collective-permute-start.2 = (bf16[32,2048]{1,0:T(8,128)(2,1)S(1)}, bf16[32,2048]{1,0:T(8,128)(2,1)S(1)}, u32[]{:S(2)}, u32[]{:S(2)}) collective-permute-start(bf16[32,2048]{1,0:T(8,128)(2,1)S(1)} %copy-done.5), channel_id=1, source_target_pairs={{0,12},{2,14},{4,8},{6,10},{8,4},{10,6},{12,0},{14,2},{1,13},{3,15... | collective-permute-start | bytes 393224 | tf_op jit(solution)/shard_map/ppermute | solution.py:362
  17.2 19.9 %collective-permute-start.3 = (bf16[32,2048]{1,0:T(8,128)(2,1)S(1)}, bf16[32,2048]{1,0:T(8,128)(2,1)S(1)}, u32[]{:S(2)}, u32[]{:S(2)}) collective-permute-start(bf16[32,2048]{1,0:T(8,128)(2,1)S(1)} %copy-done.4), channel_id=1, source_target_pairs={{0,14},{2,12},{4,10},{6,8},{8,6},{10,4},{12,2},{14,0},{1,15},{3,13... | collective-permute-start | bytes 393224 | tf_op jit(solution)/shard_map/ppermute | solution.py:362
  38.6 1.6 %collective-permute-start.6 = (bf16[2,32,2048]{2,1,0:T(8,128)(2,1)S(1)}, bf16[2,32,2048]{2,1,0:T(8,128)(2,1)S(1)}, u32[]{:S(2)}, u32[]{:S(2)}) collective-permute-start(bf16[2,32,2048]{2,1,0:T(8,128)(2,1)S(1)} %get-tuple-element.34), channel_id=1, source_target_pairs={{0,1},{1,0},{2,3},{3,2},{4,5},{5,4},{6,7},{7,6},{8,9},{9,8},{10,11... | collective-permute-start | bytes 786440 | tf_op jit(solution)/shard_map/ppermute | solution.py:387
  38.7 3.7 %collective-permute-start.4 = (bf16[2,32,2048]{2,1,0:T(8,128)(2,1)S(1)}, bf16[2,32,2048]{2,1,0:T(8,128)(2,1)S(1)}, u32[]{:S(2)}, u32[]{:S(2)}) collective-permute-start(bf16[2,32,2048]{2,1,0:T(8,128)(2,1)S(1)} %get-tuple-element.30), channel_id=1, source_target_pairs={{0,1},{1,0},{2,3},{3,2},{4,5},{5,4},{6,7},{7,6},{8,9},{9,8},{10,11... | collective-permute-start | bytes 786440 | tf_op jit(solution)/shard_map/ppermute | solution.py:387
  40.2 3.8 %copy-start.3 = (bf16[128,2048]{1,0:T(8,128)(2,1)S(1)}, bf16[128,2048]{1,0:T(8,128)(2,1)}, u32[]{:S(2)}) copy-start(bf16[128,2048]{1,0:T(8,128)(2,1)} %get-tuple-element.21) | copy-start | bytes 1572868
  40.3 6.4 %collective-permute-start.7 = (bf16[32,2048]{1,0:T(8,128)(2,1)S(1)}, bf16[32,2048]{1,0:T(8,128)(2,1)S(1)}, u32[]{:S(2)}, u32[]{:S(2)}) collective-permute-start(bf16[32,2048]{1,0:T(8,128)(2,1)S(1)} %get-tuple-element.35), channel_id=1, source_target_pairs={{0,4},{2,6},{4,0},{6,2},{8,12},{10,14},{12,8},{14,10},{1,5},{3,7},... | collective-permute-start | bytes 393224 | tf_op jit(solution)/shard_map/ppermute | solution.py:362
  40.3 8.4 %collective-permute-start.8 = (bf16[32,2048]{1,0:T(8,128)(2,1)S(1)}, bf16[32,2048]{1,0:T(8,128)(2,1)S(1)}, u32[]{:S(2)}, u32[]{:S(2)}) collective-permute-start(bf16[32,2048]{1,0:T(8,128)(2,1)S(1)} %get-tuple-element.36), channel_id=1, source_target_pairs={{0,6},{2,4},{4,2},{6,0},{8,14},{10,12},{12,10},{14,8},{1,7},{3,5},... | collective-permute-start | bytes 393224 | tf_op jit(solution)/shard_map/ppermute | solution.py:362
  42.4 7.9 %collective-permute-start.5 = (bf16[32,2048]{1,0:T(8,128)(2,1)S(1)}, bf16[32,2048]{1,0:T(8,128)(2,1)S(1)}, u32[]{:S(2)}, u32[]{:S(2)}) collective-permute-start(bf16[32,2048]{1,0:T(8,128)(2,1)S(1)} %get-tuple-element.32), channel_id=1, source_target_pairs={{0,2},{2,0},{4,6},{6,4},{8,10},{10,8},{12,14},{14,12},{1,3},{3,1},... | collective-permute-start | bytes 393224 | tf_op jit(solution)/shard_map/ppermute | solution.py:362
  44.4 0.7 %copy-start.2 = (f32[128]{0:T(128)S(1)}, f32[128]{0:T(128)}, u32[]{:S(2)}) copy-start(f32[128]{0:T(128)} %param.13) | copy-start | bytes 1540
  45.1 5.2 %copy-start.1 = (bf16[128,128]{1,0:T(8,128)(2,1)S(1)}, bf16[128,128]{1,0:T(8,128)(2,1)}, u32[]{:S(2)}) copy-start(bf16[128,128]{1,0:T(8,128)(2,1)} %w_ref.1) | copy-start | bytes 98308

commit v9 on v8

--- a/solution.py
+++ b/solution.py
@@ -57,8 +57,8 @@
 
 
 def edges_kernel(groups, rows, cols, chunks, pair_ref, gain_ref, wl_ref, wr_ref, lens_ref, res_ref, normed_ref, *refs):
-    both_ref, right_refs = refs[0], refs[1:1 + groups]
-    x_s, gain_s, wl_s, wr_s, lens_s, res_s, normed_s, held, in_sems, out_sems = refs[1 + groups:]
+    both_refs, right_refs = refs[:groups], refs[groups:2 * groups]
+    x_s, gain_s, wl_s, wr_s, lens_s, res_s, normed_s, held, in_sems, out_sems = refs[2 * groups:]
     count = rows * cols
     first_row, first_col, mine, _, _ = place_of(groups, rows, cols)
     own = wl_ref.shape[1] // 2 // groups
@@ -97,11 +97,11 @@
         normed_s[:, lanes] = normed
         held[:, own:, lanes] = edge_of(right_w, normed, mask, groups)
         held[:, :own, lanes] = edge_of(left_w, normed, mask, groups)
-        sent = [
-            (held.at[jnp.bitwise_xor(mine, u), pl.ds(own, own), lanes], right_refs[u].at[:, lanes])
-            for u in range(groups)
-        ]
-        sent.append((held.at[:, :, lanes], both_ref.at[:, :, lanes]))
+        sent = []
+        for u in range(groups):
+            group = jnp.bitwise_xor(mine, u)
+            sent.append((held.at[group, pl.ds(own, own), lanes], right_refs[u].at[:, lanes]))
+            sent.append((held.at[group, :, lanes], both_refs[u].at[:, lanes]))
         sent.append((normed_s.at[:, lanes], normed_ref.at[:, lanes]))
         for m, (src, dst) in enumerate(sent):
             stores.append(pltpu.make_async_copy(src, dst, out_sems.at[n, m]))
@@ -120,9 +120,9 @@
     return pl.pallas_call(
         functools.partial(edges_kernel, groups, rows, cols, chunks),
         in_specs=[here] * 6,
-        out_specs=[here] * (2 + groups),
+        out_specs=[here] * (1 + 2 * groups),
         out_shape=[jax.ShapeDtypeStruct((channels, flat), jnp.bfloat16)]
-        + [jax.ShapeDtypeStruct((groups, 2 * own, flat), jnp.bfloat16)]
+        + [jax.ShapeDtypeStruct((2 * own, flat), jnp.bfloat16)] * groups
         + [jax.ShapeDtypeStruct((own, flat), jnp.bfloat16)] * groups,
         scratch_shapes=[
             pltpu.VMEM((flat, channels), pair.dtype),
@@ -134,7 +134,7 @@
             pltpu.VMEM((channels, flat), jnp.bfloat16),
             pltpu.VMEM((groups, 2 * own, flat), jnp.bfloat16),
             pltpu.SemaphoreType.DMA((5 + len(chunks),)),
-            pltpu.SemaphoreType.DMA((len(chunks), 2 + groups)),
+            pltpu.SemaphoreType.DMA((len(chunks), 1 + 2 * groups)),
         ],
         compiler_params=pltpu.CompilerParams(vmem_limit_bytes=VMEM_FIRST),
     )(pair, gain, w_left, w_right, lens, resolved)
@@ -194,11 +194,13 @@
     return jnp.concatenate(lines, axis=1).astype(jnp.bfloat16)
 
 
-def near_kernel(groups, rows, cols, after_ref, got_ref, left_ref, near_ref, left_s, right_s, prod_s):
+def near_kernel(groups, rows, cols, after_ref, *refs):
+    got_refs = refs[:groups]
+    left_ref, near_ref, left_s, right_s, prod_s = refs[groups:]
     mine = place_of(groups, rows, cols)[2]
     step = left_s.shape[1] // (groups * rows)
     for u in range(groups):
-        unpack(got_ref.at[u], (left_s, right_s), u, rows, cols, step)
+        unpack(got_refs[u], (left_s, right_s), jnp.bitwise_xor(mine, u), rows, cols, step)
     for d in range(near_ref.shape[1]):
         left_ref[d] = channel_of(left_s, d, groups * rows, step)
         multiply(left_ref[d], channel_of(right_s, d, groups * rows, step), prod_s, d, step)
@@ -246,7 +248,8 @@
 
 
 def make_near(got, after, rows, cols):
-    groups, both, flat = got.shape
+    groups = len(got)
+    both, flat = got[0].shape
     ch = both // 2
     count = groups * rows
     tiles = pl.cdiv(cols, LANES)
@@ -254,7 +257,7 @@
     whole = pl.BlockSpec(memory_space=pltpu.VMEM)
     return pl.pallas_call(
         functools.partial(near_kernel, groups, rows, cols),
-        in_specs=[pl.BlockSpec(memory_space=pl.ANY), whole],
+        in_specs=[pl.BlockSpec(memory_space=pl.ANY)] + [whole] * groups,
         out_specs=[whole] * 2,
         out_shape=[
             jax.ShapeDtypeStruct((ch, count, tiles * LANES), jnp.bfloat16),
@@ -263,7 +266,7 @@
         scratch_shapes=[held, held, held],
         compiler_params=pltpu.CompilerParams(vmem_limit_bytes=VMEM_LIMIT),
         cost_estimate=pl.CostEstimate(flops=10 ** 5, bytes_accessed=10 ** 5, transcendentals=0),
-    )(after, got)
+    )(after, *got)
 
 
 def make_lines(got, groups, rows, cols, cost, after=()):
@@ -370,17 +373,16 @@
         pair_act.reshape(rows * cols, channels), chain_lengths, resolved,
         in_gain.reshape(1, channels), w_left, w_right, groups, rows, cols,
     )
-    both, right = edges[0], edges[1:]
-    halves = [[h * groups + r for r in range(groups)] for h in range(2)]
+    both, right = edges[:groups], edges[groups:]
     far_got = [swap(right[u], groups + u) for u in range(groups)]
-    near_got = lax.all_to_all(both, "row", split_axis=0, concat_axis=0, tiled=True, axis_index_groups=halves)
+    near_got = [both[0]] + [swap(both[u], u) for u in range(1, groups)]
     gate = jax.nn.sigmoid(
         jnp.einsum("cp,cd->pd", normed[:, :rows * cols], w_gate, preferred_element_type=jnp.float32)
     )
     half = groups // 2
     early = make_lines(far_got[:half], groups, rows, cols, 10 ** 8)
     left, near = make_near(near_got, early, rows, cols)
-    late = make_lines(far_got[half:], groups, rows, cols, 10 ** 5, (left,))
+    late = make_lines(far_got[half:], groups, rows, cols, 10 ** 5)
     parts = make_cross(left, near, early, late, rows, cols)
     sums = [[], []]
     for part in (1, 0):

time: 51.9 us -> 50.5 us (0.973)
  waiting for transfers between devices: 24 us -> 20.5 us
  starting transfers between devices: 17.5 us -> 19.5 us
    ppermute x7 -> x10, starting transfers between devices: 11.6 us -> 18.9 us  [swap(): lax.ppermute(value, 'row', [(r, r ^ shift) for r in range(lax.axis_size('...]
    all_to_all x1 -> x0, starting transfers between devices: 5.39 us -> none  [shards(): lax.all_to_all(both, 'row', split_axis=0, concat_axis=0, tiled=True, axis...]
    ppermute x7 -> x10, waiting for transfers between devices: 22.1 us -> 19.5 us  [swap(): lax.ppermute(value, 'row', [(r, r ^ shift) for r in range(lax.axis_size('...]
    all_to_all x1 -> x0, waiting for transfers between devices: 0.8 us -> none  [shards(): lax.all_to_all(both, 'row', split_axis=0, concat_axis=0, tiled=True, axis...]
  transfers between devices with their start and end apart: 10 -> 12, of which waited for: 9 -> 9; matrix products, arithmetic and copies ran while one was open for 1% -> 1% of each run, Pallas kernels for 4% -> 1%
where the time goes in v9:
time: 50.5 us; the launch traced here: 50.4 us
  waiting for transfers between devices  20.5 us (41%)
  starting transfers between devices  19.5 us (39%)
  Pallas kernels  9.03 us (18%)
  local copies, waits for them, and re-layouts  0.78 us (2%)
    ppermute x10, waiting for transfers between devices, swap(): lax.ppermute(value, 'row', [(r, r ^ shift) for r in range(lax.axis_size('...  19.5 us
    ppermute x10, starting transfers between devices, swap(): lax.ppermute(value, 'row', [(r, r ^ shift) for r in range(lax.axis_size('...  18.9 us
    pallas_call x1, Pallas kernels, make_edges(): pl.pallas_call(functools.partial(edges_kernel, groups, rows, cols, chunks...  3.95 us
    pallas_call x1, Pallas kernels, make_near(): pl.pallas_call(functools.partial(near_kernel, groups, rows, cols), in_spe...  1.83 us
    pallas_call x1, Pallas kernels, make_update(): pl.pallas_call(functools.partial(update_kernel, groups, rows, cols, chunk...  1.42 us
    pallas_call x1, Pallas kernels, make_cross(): pl.pallas_call(functools.partial(cross_kernel, groups, rows, cols), in_sp...  1.27 us
    ppermute x2, waiting for transfers between devices, shards(): other = lax.ppermute(parts[2 + part], 'col', [(0, 1), (1, 0)])  1.03 us
  transfers between devices with their start and end apart: 12, of which 9 were waited for; matrix products, arithmetic and copies ran while one was open for 1% of the time, Pallas kernels for 1%

profile of v9, /device:TPU:0, one launch (start us, length us, event | category | flops | bytes accessed | tf_op | source)
XLA Modules:
  0.0 50.4 jit_solution(16297040204158546170)
XLA Ops:
  0.0 0.0 copy-start
  0.0 4.0 %shard_map.91 = (bf16[128,2048]{1,0:T(8,128)(2,1)}, bf16[64,2048]{1,0:T(8,128)(2,1)}, bf16[64,2048]{1,0:T(8,128)(2,1)}, bf16[64,2048]{1,0:T(8,128)(2,1)}, bf16[6...) custom-call(bf16[1936,128]{1,0:T(8,128)(2,1)} %bitcast.5, ...), custom_call_target="tpu_custom_call" | custom-call | tf_op jit(solution)/shard_map/pallas_call | solution.py:120
  4.0 4.1 %collective-permute-start = (bf16[32,2048]{1,0:T(8,128)(2,1)}, bf16[32,2048]{1,0:T(8,128)(2,1)S(1)}, u32[]{:S(2)}, u32[]{:S(2)}) collective-permute-start(bf16[32,2048]{1,0:T(8,128)(2,1)} %get-tuple-element.25), channel_id=1, source_target_pairs={{0,8},{2,10},{4,12},{6,14},{8,0},{10,2},{12,4},{14,6},{1,9},{3,11}... | collective-permute-start | bytes 393224 | tf_op jit(solution)/shard_map/ppermute | solution.py:365
  8.1 1.3 %collective-permute-start.1 = (bf16[32,2048]{1,0:T(8,128)(2,1)}, bf16[32,2048]{1,0:T(8,128)(2,1)S(1)}, u32[]{:S(2)}, u32[]{:S(2)}) collective-permute-start(bf16[32,2048]{1,0:T(8,128)(2,1)} %get-tuple-element.26), channel_id=1, source_target_pairs={{0,10},{2,8},{4,14},{6,12},{8,2},{10,0},{12,6},{14,4},{1,11},{3,9}... | collective-permute-start | bytes 393224 | tf_op jit(solution)/shard_map/ppermute | solution.py:365
  9.4 0.2 collective-permute-start.2
  9.6 1.8 %collective-permute-start.3 = (bf16[64,2048]{1,0:T(8,128)(2,1)}, bf16[64,2048]{1,0:T(8,128)(2,1)S(1)}, u32[]{:S(2)}, u32[]{:S(2)}) collective-permute-start(bf16[64,2048]{1,0:T(8,128)(2,1)} %get-tuple-element.29), channel_id=1, source_target_pairs={{0,4},{2,6},{4,0},{6,2},{8,12},{10,14},{12,8},{14,10},{1,5},{3,7},... | collective-permute-start | bytes 786440 | tf_op jit(solution)/shard_map/ppermute | solution.py:365
  11.4 1.4 %collective-permute-start.4 = (bf16[64,2048]{1,0:T(8,128)(2,1)}, bf16[64,2048]{1,0:T(8,128)(2,1)S(1)}, u32[]{:S(2)}, u32[]{:S(2)}) collective-permute-start(bf16[64,2048]{1,0:T(8,128)(2,1)} %get-tuple-element.30), channel_id=1, source_target_pairs={{0,6},{2,4},{4,2},{6,0},{8,14},{10,12},{12,10},{14,8},{1,7},{3,5},... | collective-permute-start | bytes 786440 | tf_op jit(solution)/shard_map/ppermute | solution.py:365
  12.8 5.4 %collective-permute-done.refs_0_ = bf16[32,2048]{1,0:T(8,128)(2,1)S(1)} collective-permute-done((bf16[32,2048]{1,0:T(8,128)(2,1)}, bf16[32,2048]{1,0:T(8,128)(2,1)S(1)}, u32[]{:S(2)}, u32[]{:S(2)}) %collective-permute-start) | collective-permute-done | bytes 131104 | tf_op jit(solution)/shard_map/ppermute | solution.py:365
  18.3 2.9 %collective-permute-start.5 = (bf16[32,2048]{1,0:T(8,128)(2,1)}, bf16[32,2048]{1,0:T(8,128)(2,1)S(1)}, u32[]{:S(2)}, u32[]{:S(2)}) collective-permute-start(bf16[32,2048]{1,0:T(8,128)(2,1)} %get-tuple-element.33), channel_id=1, source_target_pairs={{0,12},{2,14},{4,8},{6,10},{8,4},{10,6},{12,0},{14,2},{1,13},{3,15... | collective-permute-start | bytes 393224 | tf_op jit(solution)/shard_map/ppermute | solution.py:365
  21.1 0.1 collective-permute-done.1.refs_1_
  21.2 3.6 %collective-permute-start.6 = (bf16[32,2048]{1,0:T(8,128)(2,1)}, bf16[32,2048]{1,0:T(8,128)(2,1)S(1)}, u32[]{:S(2)}, u32[]{:S(2)}) collective-permute-start(bf16[32,2048]{1,0:T(8,128)(2,1)} %get-tuple-element.34), channel_id=1, source_target_pairs={{0,14},{2,12},{4,10},{6,8},{8,6},{10,4},{12,2},{14,0},{1,15},{3,13... | collective-permute-start | bytes 393224 | tf_op jit(solution)/shard_map/ppermute | solution.py:365
  24.8 0.2 shard_map.92.after_ref.early_ref
  25.0 0.0 copy-start.1
  25.0 6.6 %collective-permute-done.5.refs_0_ = bf16[32,2048]{1,0:T(8,128)(2,1)S(1)} collective-permute-done((bf16[32,2048]{1,0:T(8,128)(2,1)}, bf16[32,2048]{1,0:T(8,128)(2,1)S(1)}, u32[]{:S(2)}, u32[]{:S(2)}) %collective-permute-start.5) | collective-permute-done | bytes 131104 | tf_op jit(solution)/shard_map/ppermute | solution.py:365
  31.6 2.0 %collective-permute-done.6.refs_1_ = bf16[32,2048]{1,0:T(8,128)(2,1)S(1)} collective-permute-done((bf16[32,2048]{1,0:T(8,128)(2,1)}, bf16[32,2048]{1,0:T(8,128)(2,1)S(1)}, u32[]{:S(2)}, u32[]{:S(2)}) %collective-permute-start.6) | collective-permute-done | bytes 131104 | tf_op jit(solution)/shard_map/ppermute | solution.py:365
  33.6 0.2 shard_map.94.late_ref
  33.8 0.0 collective-permute-done.2.refs_1_
  33.8 0.0 collective-permute-done.3.refs_2_
  33.8 0.2 collective-permute-done.4.refs_3_
  34.0 0.0 copy-done.1
  34.0 1.8 %shard_map.93 = (bf16[32,88,128]{2,1,0:T(8,128)(2,1)S(1)}, bf16[4,32,2048]{2,1,0:T(8,128)(2,1)S(1)}) custom-call(f32[1,1760,128]{2,1,0:T(8,128)S(1)} %shard_map.92.after_ref.early_ref, bf16[64,2048]{1,0:T(8,128)(2,1)S(1)} %copy-done.1, bf16[64,2048]{1,0:T(8,128)(2,1)S(1)} %collective-permute-done.2.refs_1_, ...), custom_call_target="tpu_custom_call" | custom-call | flops 100000 | bytes 100000 | tf_op jit(solution)/shard_map/pallas_call | solution.py:258
  35.8 1.3 %shard_map.95 = (bf16[2,32,2048]{2,1,0:T(8,128)(2,1)S(1)}, bf16[2,32,2048]{2,1,0:T(8,128)(2,1)S(1)}, bf16[2,32,2048]{2,1,0:T(8,128)(2,1)S(1)}, bf16[2,32,2048]{2,1,0:T(8,128)(2,1)S(1)}) custom-call(bf16[32,88,128]{2,1,0:T(8,128)(2,1)S(1)} %get-tuple-element.31.left_ref, bf16[4,32,2048]{2,1,0:T(8,128)(2,1)S(1)} %get-tuple-element.32.near_ref, ...), custom_call_target="tpu_custom_call" | custom-call | flops 100000 | bytes 8000000 | tf_op jit(solution)/shard_map/pallas_call | solution.py:290
  37.1 0.1 collective-permute-start.9
  37.2 0.5 collective-permute-start.7
  37.7 1.0 %collective-permute-done.9.b_ref = bf16[2,32,2048]{2,1,0:T(8,128)(2,1)S(1)} collective-permute-done((bf16[2,32,2048]{2,1,0:T(8,128)(2,1)S(1)}, bf16[2,32,2048]{2,1,0:T(8,128)(2,1)S(1)}, u32[]{:S(2)}, u32[]{:S(2)}) %collective-permute-start.9) | collective-permute-done | bytes 262176 | tf_op jit(solution)/shard_map/ppermute | solution.py:389
  38.7 0.0 copy-start.4
  38.7 0.1 shard_map.97
  38.8 0.1 collective-permute-start.10
  38.9 2.2 %collective-permute-start.11 = (bf16[32,2048]{1,0:T(8,128)(2,1)S(1)}, bf16[32,2048]{1,0:T(8,128)(2,1)S(1)}, u32[]{:S(2)}, u32[]{:S(2)}) collective-permute-start(bf16[32,2048]{1,0:T(8,128)(2,1)S(1)} %get-tuple-element.42), channel_id=1, source_target_pairs={{0,6},{2,4},{4,2},{6,0},{8,14},{10,12},{12,10},{14,8},{1,7},{3,5},... | collective-permute-start | bytes 393224 | tf_op jit(solution)/shard_map/ppermute | solution.py:365
  41.0 0.0 collective-permute-done.7.b_ref
  41.0 0.1 shard_map.96
  41.1 1.4 %collective-permute-start.8 = (bf16[32,2048]{1,0:T(8,128)(2,1)S(1)}, bf16[32,2048]{1,0:T(8,128)(2,1)S(1)}, u32[]{:S(2)}, u32[]{:S(2)}) collective-permute-start(bf16[32,2048]{1,0:T(8,128)(2,1)S(1)} %get-tuple-element.38), channel_id=1, source_target_pairs={{0,2},{2,0},{4,6},{6,4},{8,10},{10,8},{12,14},{14,12},{1,3},{3,1},... | collective-permute-start | bytes 393224 | tf_op jit(solution)/shard_map/ppermute | solution.py:365
  42.5 0.0 copy-done
  42.5 0.0 copy-done.4
  42.5 0.5 fusion.2.gate_ref
  43.0 0.0 copy-start.3
  43.0 0.6 %copy-done.3 = f32[128]{0:T(128)S(1)} copy-done((f32[128]{0:T(128)S(1)}, f32[128]{0:T(128)}, u32[]{:S(2)}) %copy-start.3) | copy-done | bytes 536
  43.6 0.0 copy-start.2
  43.6 0.1 copy.10.gain_ref
  43.7 1.5 %collective-permute-done.10.refs_2_ = bf16[32,2048]{1,0:T(8,128)(2,1)S(1)} collective-permute-done((bf16[32,2048]{1,0:T(8,128)(2,1)S(1)}, bf16[32,2048]{1,0:T(8,128)(2,1)S(1)}, u32[]{:S(2)}, u32[]{:S(2)}) %collective-permute-start.10) | collective-permute-done | bytes 131104 | tf_op jit(solution)/shard_map/ppermute | solution.py:365
  45.2 2.3 %collective-permute-done.11.refs_3_ = bf16[32,2048]{1,0:T(8,128)(2,1)S(1)} collective-permute-done((bf16[32,2048]{1,0:T(8,128)(2,1)S(1)}, bf16[32,2048]{1,0:T(8,128)(2,1)S(1)}, u32[]{:S(2)}, u32[]{:S(2)}) %collective-permute-start.11) | collective-permute-done | bytes 131104 | tf_op jit(solution)/shard_map/ppermute | solution.py:365
  47.5 1.5 %collective-permute-done.8.refs_1_ = bf16[32,2048]{1,0:T(8,128)(2,1)S(1)} collective-permute-done((bf16[32,2048]{1,0:T(8,128)(2,1)S(1)}, bf16[32,2048]{1,0:T(8,128)(2,1)S(1)}, u32[]{:S(2)}, u32[]{:S(2)}) %collective-permute-start.8) | collective-permute-done | bytes 131104 | tf_op jit(solution)/shard_map/ppermute | solution.py:365
  49.0 0.0 copy-done.2
  49.0 1.4 %shard_map.98 = bf16[1936,128]{1,0:T(8,128)(2,1)} custom-call(f32[128,1]{1,0:T(8,128)S(1)} %copy.10.gain_ref, bf16[128,128]{1,0:T(8,128)(2,1)S(1)} %copy-done.2, f32[1936,128]{1,0:T(8,128)S(1)} %fusion.2.gate_ref, bf16[32,2048]{1,0:T(8,128)(2,1)S(1)} %get-tuple-element.37.refs_0_, bf16[32,2048]{1,0:T(8,128)(2,1)S(1)} %collective-permute-done.8.refs_1_, ...), custom_call_target="tpu_custom_call" | custom-call | tf_op jit(solution)/shard_map/pallas_call | solution.py:350
Async XLA Ops:
  0.0 42.5 %copy-start = (bf16[128,128]{1,0:T(8,128)(2,1)S(1)}, bf16[128,128]{1,0:T(8,128)(2,1)}, u32[]{:S(2)}) copy-start(bf16[128,128]{1,0:T(8,128)(2,1)} %param.16) | copy-start | bytes 98308
  4.0 14.3 %collective-permute-start = (bf16[32,2048]{1,0:T(8,128)(2,1)}, bf16[32,2048]{1,0:T(8,128)(2,1)S(1)}, u32[]{:S(2)}, u32[]{:S(2)}) collective-permute-start(bf16[32,2048]{1,0:T(8,128)(2,1)} %get-tuple-element.25), channel_id=1, source_target_pairs={{0,8},{2,10},{4,12},{6,14},{8,0},{10,2},{12,4},{14,6},{1,9},{3,11}... | collective-permute-start | bytes 393224 | tf_op jit(solution)/shard_map/ppermute | solution.py:365
  8.1 13.2 %collective-permute-start.1 = (bf16[32,2048]{1,0:T(8,128)(2,1)}, bf16[32,2048]{1,0:T(8,128)(2,1)S(1)}, u32[]{:S(2)}, u32[]{:S(2)}) collective-permute-start(bf16[32,2048]{1,0:T(8,128)(2,1)} %get-tuple-element.26), channel_id=1, source_target_pairs={{0,10},{2,8},{4,14},{6,12},{8,2},{10,0},{12,6},{14,4},{1,11},{3,9}... | collective-permute-start | bytes 393224 | tf_op jit(solution)/shard_map/ppermute | solution.py:365
  9.4 24.5 %collective-permute-start.2 = (bf16[64,2048]{1,0:T(8,128)(2,1)}, bf16[64,2048]{1,0:T(8,128)(2,1)S(1)}, u32[]{:S(2)}, u32[]{:S(2)}) collective-permute-start(bf16[64,2048]{1,0:T(8,128)(2,1)} %get-tuple-element.28), channel_id=1, source_target_pairs={{0,2},{2,0},{4,6},{6,4},{8,10},{10,8},{12,14},{14,12},{1,3},{3,1},... | collective-permute-start | bytes 786440 | tf_op jit(solution)/shard_map/ppermute | solution.py:365
  9.6 24.2 %collective-permute-start.3 = (bf16[64,2048]{1,0:T(8,128)(2,1)}, bf16[64,2048]{1,0:T(8,128)(2,1)S(1)}, u32[]{:S(2)}, u32[]{:S(2)}) collective-permute-start(bf16[64,2048]{1,0:T(8,128)(2,1)} %get-tuple-element.29), channel_id=1, source_target_pairs={{0,4},{2,6},{4,0},{6,2},{8,12},{10,14},{12,8},{14,10},{1,5},{3,7},... | collective-permute-start | bytes 786440 | tf_op jit(solution)/shard_map/ppermute | solution.py:365
  11.4 22.6 %collective-permute-start.4 = (bf16[64,2048]{1,0:T(8,128)(2,1)}, bf16[64,2048]{1,0:T(8,128)(2,1)S(1)}, u32[]{:S(2)}, u32[]{:S(2)}) collective-permute-start(bf16[64,2048]{1,0:T(8,128)(2,1)} %get-tuple-element.30), channel_id=1, source_target_pairs={{0,6},{2,4},{4,2},{6,0},{8,14},{10,12},{12,10},{14,8},{1,7},{3,5},... | collective-permute-start | bytes 786440 | tf_op jit(solution)/shard_map/ppermute | solution.py:365
  18.3 13.3 %collective-permute-start.5 = (bf16[32,2048]{1,0:T(8,128)(2,1)}, bf16[32,2048]{1,0:T(8,128)(2,1)S(1)}, u32[]{:S(2)}, u32[]{:S(2)}) collective-permute-start(bf16[32,2048]{1,0:T(8,128)(2,1)} %get-tuple-element.33), channel_id=1, source_target_pairs={{0,12},{2,14},{4,8},{6,10},{8,4},{10,6},{12,0},{14,2},{1,13},{3,15... | collective-permute-start | bytes 393224 | tf_op jit(solution)/shard_map/ppermute | solution.py:365
  21.2 12.4 %collective-permute-start.6 = (bf16[32,2048]{1,0:T(8,128)(2,1)}, bf16[32,2048]{1,0:T(8,128)(2,1)S(1)}, u32[]{:S(2)}, u32[]{:S(2)}) collective-permute-start(bf16[32,2048]{1,0:T(8,128)(2,1)} %get-tuple-element.34), channel_id=1, source_target_pairs={{0,14},{2,12},{4,10},{6,8},{8,6},{10,4},{12,2},{14,0},{1,15},{3,13... | collective-permute-start | bytes 393224 | tf_op jit(solution)/shard_map/ppermute | solution.py:365
  25.0 9.0 %copy-start.1 = (bf16[64,2048]{1,0:T(8,128)(2,1)S(1)}, bf16[64,2048]{1,0:T(8,128)(2,1)}, u32[]{:S(2)}) copy-start(bf16[64,2048]{1,0:T(8,128)(2,1)} %get-tuple-element.27.refs_0_) | copy-start | bytes 786436
  37.1 1.6 %collective-permute-start.9 = (bf16[2,32,2048]{2,1,0:T(8,128)(2,1)S(1)}, bf16[2,32,2048]{2,1,0:T(8,128)(2,1)S(1)}, u32[]{:S(2)}, u32[]{:S(2)}) collective-permute-start(bf16[2,32,2048]{2,1,0:T(8,128)(2,1)S(1)} %get-tuple-element.40), channel_id=1, source_target_pairs={{0,1},{1,0},{2,3},{3,2},{4,5},{5,4},{6,7},{7,6},{8,9},{9,8},{10,11... | collective-permute-start | bytes 786440 | tf_op jit(solution)/shard_map/ppermute | solution.py:389
  37.2 3.8 %collective-permute-start.7 = (bf16[2,32,2048]{2,1,0:T(8,128)(2,1)S(1)}, bf16[2,32,2048]{2,1,0:T(8,128)(2,1)S(1)}, u32[]{:S(2)}, u32[]{:S(2)}) collective-permute-start(bf16[2,32,2048]{2,1,0:T(8,128)(2,1)S(1)} %get-tuple-element.36), channel_id=1, source_target_pairs={{0,1},{1,0},{2,3},{3,2},{4,5},{5,4},{6,7},{7,6},{8,9},{9,8},{10,11... | collective-permute-start | bytes 786440 | tf_op jit(solution)/shard_map/ppermute | solution.py:389
  38.7 3.8 %copy-start.4 = (bf16[128,2048]{1,0:T(8,128)(2,1)S(1)}, bf16[128,2048]{1,0:T(8,128)(2,1)}, u32[]{:S(2)}) copy-start(bf16[128,2048]{1,0:T(8,128)(2,1)} %get-tuple-element.24) | copy-start | bytes 1572868
  38.8 6.4 %collective-permute-start.10 = (bf16[32,2048]{1,0:T(8,128)(2,1)S(1)}, bf16[32,2048]{1,0:T(8,128)(2,1)S(1)}, u32[]{:S(2)}, u32[]{:S(2)}) collective-permute-start(bf16[32,2048]{1,0:T(8,128)(2,1)S(1)} %get-tuple-element.41), channel_id=1, source_target_pairs={{0,4},{2,6},{4,0},{6,2},{8,12},{10,14},{12,8},{14,10},{1,5},{3,7},... | collective-permute-start | bytes 393224 | tf_op jit(solution)/shard_map/ppermute | solution.py:365
  38.9 8.6 %collective-permute-start.11 = (bf16[32,2048]{1,0:T(8,128)(2,1)S(1)}, bf16[32,2048]{1,0:T(8,128)(2,1)S(1)}, u32[]{:S(2)}, u32[]{:S(2)}) collective-permute-start(bf16[32,2048]{1,0:T(8,128)(2,1)S(1)} %get-tuple-element.42), channel_id=1, source_target_pairs={{0,6},{2,4},{4,2},{6,0},{8,14},{10,12},{12,10},{14,8},{1,7},{3,5},... | collective-permute-start | bytes 393224 | tf_op jit(solution)/shard_map/ppermute | solution.py:365
  41.1 7.9 %collective-permute-start.8 = (bf16[32,2048]{1,0:T(8,128)(2,1)S(1)}, bf16[32,2048]{1,0:T(8,128)(2,1)S(1)}, u32[]{:S(2)}, u32[]{:S(2)}) collective-permute-start(bf16[32,2048]{1,0:T(8,128)(2,1)S(1)} %get-tuple-element.38), channel_id=1, source_target_pairs={{0,2},{2,0},{4,6},{6,4},{8,10},{10,8},{12,14},{14,12},{1,3},{3,1},... | collective-permute-start | bytes 393224 | tf_op jit(solution)/shard_map/ppermute | solution.py:365
  43.0 0.7 %copy-start.3 = (f32[128]{0:T(128)S(1)}, f32[128]{0:T(128)}, u32[]{:S(2)}) copy-start(f32[128]{0:T(128)} %param.13) | copy-start | bytes 1540
  43.6 5.3 %copy-start.2 = (bf16[128,128]{1,0:T(8,128)(2,1)S(1)}, bf16[128,128]{1,0:T(8,128)(2,1)}, u32[]{:S(2)}) copy-start(bf16[128,128]{1,0:T(8,128)(2,1)} %w_ref.1) | copy-start | bytes 98308

commit v10 on v9

--- a/solution.py
+++ b/solution.py
@@ -167,135 +167,111 @@
                 held[tt, pl.ds(base, ch), :] = piece
 
 
-def pack(held, out_ref, u, block, rows, cols, step):
+def packed_tile(held, first, t, block, rows, cols, step, ch):
     tiles = pl.cdiv(cols, LANES)
-    ch = out_ref.shape[1]
     lane = lax.broadcasted_iota(jnp.int32, (ch, LANES), 1)
-    for t in range(out_ref.shape[2] // LANES):
-        tile = None
-        for i in range(rows):
-            for tt in range(tiles):
-                shift = cols * i + LANES * tt - LANES * t
-                length = min(LANES, cols - LANES * tt)
-                if shift >= LANES or shift + length <= 0:
-                    continue
-                base = pl.multiple_of((block * rows + i) * step, 8)
-                piece = held[tt, pl.ds(base, ch), :]
-                if shift % LANES:
-                    piece = pltpu.roll(piece, shift % LANES, 1)
-                tile = piece if tile is None else jnp.where(lane < shift, tile, piece)
-        if tile is None:
-            tile = jnp.zeros((ch, LANES), jnp.float32)
-        out_ref[u, :, pl.ds(t * LANES, LANES)] = tile.astype(jnp.bfloat16)
+    tile = None
+    for i in range(rows):
+        for tt in range(tiles):
+            shift = cols * i + LANES * tt - LANES * t
+            length = min(LANES, cols - LANES * tt)
+            if shift >= LANES or shift + length <= 0:
+                continue
+            base = pl.multiple_of((block * rows + i) * step, 8)
+            piece = held[first + tt, pl.ds(base, ch), :]
+            if shift % LANES:
+                piece = pltpu.roll(piece, shift % LANES, 1)
+            tile = piece if tile is None else jnp.where(lane < shift, tile, piece)
+    return jnp.zeros((ch, LANES), jnp.float32) if tile is None else tile
 
 
 def channel_of(held, d, count, step):
-    lines = [held[t, pl.ds(d, count, stride=step), :] for t in range(held.shape[0])]
-    return jnp.concatenate(lines, axis=1).astype(jnp.bfloat16)
-
-
-def near_kernel(groups, rows, cols, after_ref, *refs):
-    got_refs = refs[:groups]
-    left_ref, near_ref, left_s, right_s, prod_s = refs[groups:]
+    return jnp.concatenate([held[t, pl.ds(d, count, stride=step), :] for t in range(held.shape[0])], axis=1)
+
+
+def lines_kernel(groups, rows, cols, *refs):
+    got_refs, lines_ref = refs[:-1], refs[-1]
     mine = place_of(groups, rows, cols)[2]
-    step = left_s.shape[1] // (groups * rows)
-    for u in range(groups):
-        unpack(got_refs[u], (left_s, right_s), jnp.bitwise_xor(mine, u), rows, cols, step)
-    for d in range(near_ref.shape[1]):
-        left_ref[d] = channel_of(left_s, d, groups * rows, step)
-        multiply(left_ref[d], channel_of(right_s, d, groups * rows, step), prod_s, d, step)
-    for u in range(groups):
-        pack(prod_s, near_ref, u, jnp.bitwise_xor(mine, u), rows, cols, step)
-
-
-def lines_kernel(groups, rows, cols, count, *refs):
-    got_refs, lines_ref = refs[:count], refs[-1]
-    mine = place_of(groups, rows, cols)[2]
+    count = len(got_refs)
     step = lines_ref.shape[1] // (count * rows)
     for u in range(count):
         block = jnp.bitwise_and(jnp.bitwise_xor(mine, u), count - 1)
         unpack(got_refs[u], (lines_ref,), block, rows, cols, step)
 
 
-def multiply(left, right, prod_s, d, step):
-    count = left.shape[0]
-    pad = prod_s.shape[0] * LANES - count
-    if pad:
-        right = jnp.concatenate([right, jnp.zeros((pad, right.shape[1]), right.dtype)], axis=0)
-    prod = lax.dot_general(left, right, (((1,), (1,)), ((), ())), preferred_element_type=jnp.float32)
-    for t in range(prod_s.shape[0]):
-        prod_s[t, pl.ds(d, count, stride=step), :] = prod[:, t * LANES:(t + 1) * LANES]
-
-
-def cross_kernel(groups, rows, cols, left_ref, near_ref, early_ref, late_ref, *refs):
-    keep_refs, send_refs = refs[:2], refs[2:4]
-    right_s, prod_s, pair_s = refs[4:]
-    _, _, mine, half, col = place_of(groups, rows, cols)
-    step = prod_s.shape[1] // (groups * rows)
-    size = early_ref.shape[1]
-    base = pl.multiple_of(mine // (groups // 2) * size, 8)
-    right_s[:, pl.ds(base, size), :] = early_ref[...]
-    right_s[:, pl.ds(pl.multiple_of(size - base, 8), size), :] = late_ref[...]
-    for d in range(left_ref.shape[0]):
-        multiply(left_ref[d], channel_of(right_s, d, groups * rows, step), prod_s, d, step)
+def products_kernel(groups, rows, cols, parts, lines_ref, *refs):
+    half = groups // 2
+    near_refs, far_refs = refs[:groups], refs[groups:groups + half]
+    keep_refs, send_refs = refs[groups + half:groups + half + 2], refs[groups + half + 2:groups + half + 4]
+    left_s, right_s, far_s, prod_s = refs[groups + half + 4:]
+    _, _, mine, own_half, col = place_of(groups, rows, cols)
+    ch = far_refs[0].shape[0]
+    step = left_s.shape[1] // (groups * rows)
+    count = groups * rows
+    tiles = left_s.shape[0]
+    size = lines_ref.shape[1]
+    far_s[:, pl.ds(pl.multiple_of((1 - mine // half) * size, 8), size), :] = lines_ref[...]
     for u in range(groups):
-        pack(prod_s, pair_s, u, jnp.bitwise_xor(mine, u), rows, cols, step)
-    near_kept = col == half
-    for part in range(2):
-        pieces = pl.ds(part * (groups // 2), groups // 2)
-        keep_refs[part][...] = jnp.where(near_kept, near_ref[pieces], pair_s[pieces])
-        send_refs[part][...] = jnp.where(near_kept, pair_s[pieces], near_ref[pieces])
-
-
-def make_near(got, after, rows, cols):
-    groups = len(got)
-    both, flat = got[0].shape
-    ch = both // 2
-    count = groups * rows
-    tiles = pl.cdiv(cols, LANES)
-    held = pltpu.VMEM((tiles, count * line_step(ch), LANES), jnp.float32)
-    whole = pl.BlockSpec(memory_space=pltpu.VMEM)
-    return pl.pallas_call(
-        functools.partial(near_kernel, groups, rows, cols),
-        in_specs=[pl.BlockSpec(memory_space=pl.ANY)] + [whole] * groups,
-        out_specs=[whole] * 2,
-        out_shape=[
-            jax.ShapeDtypeStruct((ch, count, tiles * LANES), jnp.bfloat16),
-            jax.ShapeDtypeStruct((groups, ch, flat), jnp.bfloat16),
-        ],
-        scratch_shapes=[held, held, held],
-        compiler_params=pltpu.CompilerParams(vmem_limit_bytes=VMEM_LIMIT),
-        cost_estimate=pl.CostEstimate(flops=10 ** 5, bytes_accessed=10 ** 5, transcendentals=0),
-    )(after, *got)
-
-
-def make_lines(got, groups, rows, cols, cost, after=()):
+        unpack(near_refs[u], (left_s, right_s), jnp.bitwise_xor(mine, u), rows, cols, step)
+    for u in range(half):
+        unpack(far_refs[u], (far_s,), jnp.bitwise_xor(mine, u), rows, cols, step)
+    pad = [jnp.zeros((tiles * LANES - count, tiles * LANES), jnp.float32)] if count % LANES else []
+    for d in range(ch):
+        left = channel_of(left_s, d, count, step)
+        right = jnp.concatenate(
+            [channel_of(right_s, d, count, step)] + pad + [channel_of(far_s, d, count, step)] + pad, axis=0
+        )
+        prod = lax.dot_general(
+            left.astype(jnp.bfloat16), right.astype(jnp.bfloat16), (((1,), (1,)), ((), ())),
+            preferred_element_type=jnp.float32,
+        )
+        for t in range(2 * tiles):
+            prod_s[t, pl.ds(d, count, stride=step), :] = prod[:, t * LANES:(t + 1) * LANES]
+    near_kept = col == own_half
+    for part, pieces in enumerate(parts):
+        for n, u in enumerate(pieces):
+            block = jnp.bitwise_xor(mine, u)
+            for t in range(keep_refs[part].shape[2] // LANES):
+                near = packed_tile(prod_s, 0, t, block, rows, cols, step, ch)
+                far = packed_tile(prod_s, tiles, t, block, rows, cols, step, ch)
+                lanes = pl.ds(t * LANES, LANES)
+                keep_refs[part][n, :, lanes] = jnp.where(near_kept, near, far).astype(jnp.bfloat16)
+                send_refs[part][n, :, lanes] = jnp.where(near_kept, far, near).astype(jnp.bfloat16)
+
+
+def lines_of(blocks, ch, cols):
+    return (pl.cdiv(cols, LANES), blocks * line_step(ch), LANES)
+
+
+def make_lines(got, groups, rows, cols):
     ch = got[0].shape[0]
     whole = pl.BlockSpec(memory_space=pltpu.VMEM)
-    lines = (pl.cdiv(cols, LANES), len(got) * rows * line_step(ch), LANES)
-    return pl.pallas_call(
-        functools.partial(lines_kernel, groups, rows, cols, len(got)),
-        in_specs=[whole] * len(got) + [pl.BlockSpec(memory_space=pl.ANY)] * len(after),
+    return pl.pallas_call(
+        functools.partial(lines_kernel, groups, rows, cols),
+        in_specs=[whole] * len(got),
         out_specs=whole,
-        out_shape=jax.ShapeDtypeStruct(lines, jnp.float32),
+        out_shape=jax.ShapeDtypeStruct(lines_of(len(got) * rows, ch, cols), jnp.float32),
         compiler_params=pltpu.CompilerParams(vmem_limit_bytes=VMEM_LIMIT),
-        cost_estimate=pl.CostEstimate(flops=10 ** 5, bytes_accessed=cost, transcendentals=0),
-    )(*got, *after)
-
-
-def make_cross(left, near, early, late, rows, cols):
-    groups, ch, flat = near.shape
+        cost_estimate=pl.CostEstimate(flops=10 ** 5, bytes_accessed=10 ** 8, transcendentals=0),
+    )(*got)
+
+
+def make_products(lines, near, far, parts, rows, cols):
+    groups = len(near)
+    ch, flat = far[0].shape
     whole = pl.BlockSpec(memory_space=pltpu.VMEM)
-    held = pltpu.VMEM((pl.cdiv(cols, LANES), groups * rows * line_step(ch), LANES), jnp.float32)
-    return pl.pallas_call(
-        functools.partial(cross_kernel, groups, rows, cols),
-        in_specs=[whole] * 4,
+    tiles, held, _ = lines_of(groups * rows, ch, cols)
+    one = pltpu.VMEM((tiles, held, LANES), jnp.float32)
+    sizes = [len(pieces) for pieces in parts] * 2
+    return pl.pallas_call(
+        functools.partial(products_kernel, groups, rows, cols, parts),
+        in_specs=[whole] * (1 + len(near) + len(far)),
         out_specs=[whole] * 4,
-        out_shape=[jax.ShapeDtypeStruct((groups // 2, ch, flat), near.dtype)] * 4,
-        scratch_shapes=[held, held, pltpu.VMEM(near.shape, near.dtype)],
+        out_shape=[jax.ShapeDtypeStruct((n, ch, flat), jnp.bfloat16) for n in sizes],
+        scratch_shapes=[one, one, one, pltpu.VMEM((2 * tiles, held, LANES), jnp.float32)],
         compiler_params=pltpu.CompilerParams(vmem_limit_bytes=VMEM_LIMIT),
-        cost_estimate=pl.CostEstimate(flops=10 ** 5, bytes_accessed=8 * 10 ** 6, transcendentals=0),
-    )(left, near, early, late)
+        cost_estimate=pl.CostEstimate(flops=10 ** 5, bytes_accessed=10 ** 7, transcendentals=0),
+    )(lines, *near, *far)
 
 
 def add_kernel(a_ref, b_ref, *out_refs):
@@ -380,15 +356,13 @@
         jnp.einsum("cp,cd->pd", normed[:, :rows * cols], w_gate, preferred_element_type=jnp.float32)
     )
     half = groups // 2
-    early = make_lines(far_got[:half], groups, rows, cols, 10 ** 8)
-    left, near = make_near(near_got, early, rows, cols)
-    late = make_lines(far_got[half:], groups, rows, cols, 10 ** 5)
-    parts = make_cross(left, near, early, late, rows, cols)
-    sums = [[], []]
-    for part in (1, 0):
-        other = lax.ppermute(parts[2 + part], "col", [(0, 1), (1, 0)])
-        sums[part] = make_sums(parts[part], other)
-    sums = sums[0] + sums[1]
+    lines = make_lines(far_got[half:], groups, rows, cols)
+    parts = [list(range(1, half + 1)), [0] + list(range(half + 1, groups))]
+    made = make_products(lines, near_got, far_got[:half], parts, rows, cols)
+    sums = {}
+    for part, pieces in enumerate(parts):
+        other = lax.ppermute(made[2 + part], "col", [(0, 1), (1, 0)])
+        sums.update(zip(pieces, make_sums(made[part], other)))
     returned = [sums[0]] + [swap(sums[u], u) for u in range(1, groups)]
     update = make_update(returned, out_gain.reshape(hidden, 1), w_out, gate, rows, cols)
     return update.reshape(rows, cols, channels)

time: 50.5 us -> 48.7 us (0.964)
  waiting for transfers between devices: 20.5 us -> 14.4 us
  starting transfers between devices: 19.5 us -> 24.2 us
    ppermute x10, waiting for transfers between devices: 19.5 us -> 13.4 us  [swap(): lax.ppermute(value, 'row', [(r, r ^ shift) for r in range(lax.axis_size('...]
    ppermute x10, starting transfers between devices: 18.9 us -> 23.6 us  [swap(): lax.ppermute(value, 'row', [(r, r ^ shift) for r in range(lax.axis_size('...]
    pallas_call x4 -> x2, Pallas kernels: 3.53 us -> 3.1 us  [the longest x1 2.89 us: make_products(): pl.pallas_call(functools.partial(products_kernel, groups, rows, cols, par...]
  transfers between devices with their start and end apart: 12 -> 12, of which waited for: 9 -> 6; matrix products, arithmetic and copies ran while one was open for 1% -> 1% of each run, Pallas kernels for 1% -> 1%
where the time goes in v10:
time: 48.7 us; the launch traced here: 48.5 us
  starting transfers between devices  24.2 us (50%)
  waiting for transfers between devices  14.4 us (30%)
  Pallas kernels  8.62 us (18%)
  local copies, waits for them, and re-layouts  0.78 us (2%)
    ppermute x10, starting transfers between devices, swap(): lax.ppermute(value, 'row', [(r, r ^ shift) for r in range(lax.axis_size('...  23.6 us
    ppermute x10, waiting for transfers between devices, swap(): lax.ppermute(value, 'row', [(r, r ^ shift) for r in range(lax.axis_size('...  13.4 us
    pallas_call x1, Pallas kernels, make_edges(): pl.pallas_call(functools.partial(edges_kernel, groups, rows, cols, chunks...  3.97 us
    pallas_call x1, Pallas kernels, make_products(): pl.pallas_call(functools.partial(products_kernel, groups, rows, cols, par...  2.89 us
    pallas_call x1, Pallas kernels, make_update(): pl.pallas_call(functools.partial(update_kernel, groups, rows, cols, chunk...  1.42 us
    ppermute x2, waiting for transfers between devices, shards(): other = lax.ppermute(made[2 + part], 'col', [(0, 1), (1, 0)])  1.03 us
  transfers between devices with their start and end apart: 12, of which 6 were waited for; matrix products, arithmetic and copies ran while one was open for 1% of the time, Pallas kernels for 1%

profile of v10, /device:TPU:0, one launch (start us, length us, event | category | flops | bytes accessed | tf_op | source)
XLA Modules:
  0.0 48.5 jit_solution(3634546355584662947)
XLA Ops:
  0.0 0.0 copy-start
  0.0 4.0 %shard_map.91 = (bf16[128,2048]{1,0:T(8,128)(2,1)}, bf16[64,2048]{1,0:T(8,128)(2,1)}, bf16[64,2048]{1,0:T(8,128)(2,1)}, bf16[64,2048]{1,0:T(8,128)(2,1)}, bf16[6...) custom-call(bf16[1936,128]{1,0:T(8,128)(2,1)} %bitcast.5, ...), custom_call_target="tpu_custom_call" | custom-call | tf_op jit(solution)/shard_map/pallas_call | solution.py:120
  4.0 5.1 %collective-permute-start = (bf16[32,2048]{1,0:T(8,128)(2,1)}, bf16[32,2048]{1,0:T(8,128)(2,1)S(1)}, u32[]{:S(2)}, u32[]{:S(2)}) collective-permute-start(bf16[32,2048]{1,0:T(8,128)(2,1)} %get-tuple-element.23), channel_id=1, source_target_pairs={{0,12},{2,14},{4,8},{6,10},{8,4},{10,6},{12,0},{14,2},{1,13},{3,15... | collective-permute-start | bytes 393224 | tf_op jit(solution)/shard_map/ppermute | solution.py:341
  9.1 1.2 %collective-permute-start.1 = (bf16[32,2048]{1,0:T(8,128)(2,1)}, bf16[32,2048]{1,0:T(8,128)(2,1)S(1)}, u32[]{:S(2)}, u32[]{:S(2)}) collective-permute-start(bf16[32,2048]{1,0:T(8,128)(2,1)} %get-tuple-element.24), channel_id=1, source_target_pairs={{0,14},{2,12},{4,10},{6,8},{8,6},{10,4},{12,2},{14,0},{1,15},{3,13... | collective-permute-start | bytes 393224 | tf_op jit(solution)/shard_map/ppermute | solution.py:341
  10.3 0.4 collective-permute-start.2
  10.6 0.0 collective-permute-start.3
  10.6 3.1 %collective-permute-start.4 = (bf16[64,2048]{1,0:T(8,128)(2,1)}, bf16[64,2048]{1,0:T(8,128)(2,1)S(1)}, u32[]{:S(2)}, u32[]{:S(2)}) collective-permute-start(bf16[64,2048]{1,0:T(8,128)(2,1)} %get-tuple-element.28), channel_id=1, source_target_pairs={{0,6},{2,4},{4,2},{6,0},{8,14},{10,12},{12,10},{14,8},{1,7},{3,5},... | collective-permute-start | bytes 786440 | tf_op jit(solution)/shard_map/ppermute | solution.py:341
  13.8 0.0 collective-permute-done.refs_0_
  13.8 6.5 %collective-permute-start.5 = (bf16[32,2048]{1,0:T(8,128)(2,1)}, bf16[32,2048]{1,0:T(8,128)(2,1)S(1)}, u32[]{:S(2)}, u32[]{:S(2)}) collective-permute-start(bf16[32,2048]{1,0:T(8,128)(2,1)} %get-tuple-element.29), channel_id=1, source_target_pairs={{0,8},{2,10},{4,12},{6,14},{8,0},{10,2},{12,4},{14,6},{1,9},{3,11}... | collective-permute-start | bytes 393224 | tf_op jit(solution)/shard_map/ppermute | solution.py:341
  20.3 0.0 collective-permute-done.1.refs_1_
  20.3 0.0 copy-start.1
  20.3 3.7 %collective-permute-start.6 = (bf16[32,2048]{1,0:T(8,128)(2,1)}, bf16[32,2048]{1,0:T(8,128)(2,1)S(1)}, u32[]{:S(2)}, u32[]{:S(2)}) collective-permute-start(bf16[32,2048]{1,0:T(8,128)(2,1)} %get-tuple-element.30), channel_id=1, source_target_pairs={{0,10},{2,8},{4,14},{6,12},{8,2},{10,0},{12,6},{14,4},{1,11},{3,9}... | collective-permute-start | bytes 393224 | tf_op jit(solution)/shard_map/ppermute | solution.py:341
  24.0 0.2 shard_map.92.lines_ref
  24.2 5.9 %collective-permute-done.5.refs_4_ = bf16[32,2048]{1,0:T(8,128)(2,1)S(1)} collective-permute-done((bf16[32,2048]{1,0:T(8,128)(2,1)}, bf16[32,2048]{1,0:T(8,128)(2,1)S(1)}, u32[]{:S(2)}, u32[]{:S(2)}) %collective-permute-start.5) | collective-permute-done | bytes 131104 | tf_op jit(solution)/shard_map/ppermute | solution.py:341
  30.2 1.7 %collective-permute-done.6.refs_5_ = bf16[32,2048]{1,0:T(8,128)(2,1)S(1)} collective-permute-done((bf16[32,2048]{1,0:T(8,128)(2,1)}, bf16[32,2048]{1,0:T(8,128)(2,1)S(1)}, u32[]{:S(2)}, u32[]{:S(2)}) %collective-permute-start.6) | collective-permute-done | bytes 131104 | tf_op jit(solution)/shard_map/ppermute | solution.py:341
  31.9 0.0 collective-permute-done.2.refs_1_
  31.9 0.0 collective-permute-done.3.refs_2_
  31.9 1.6 %collective-permute-done.4.refs_3_ = bf16[64,2048]{1,0:T(8,128)(2,1)S(1)} collective-permute-done((bf16[64,2048]{1,0:T(8,128)(2,1)}, bf16[64,2048]{1,0:T(8,128)(2,1)S(1)}, u32[]{:S(2)}, u32[]{:S(2)}) %collective-permute-start.4) | collective-permute-done | bytes 262176 | tf_op jit(solution)/shard_map/ppermute | solution.py:341
  33.5 0.0 copy-done.1
  33.5 2.9 %shard_map.93 = (bf16[2,32,2048]{2,1,0:T(8,128)(2,1)S(1)}, bf16[2,32,2048]{2,1,0:T(8,128)(2,1)S(1)}, bf16[2,32,2048]{2,1,0:T(8,128)(2,1)S(1)}, bf16[2,32,2048]{2,1,0:T(8,128)(2,1)S(1)}) custom-call(f32[1,1760,128]{2,1,0:T(8,128)S(1)} %shard_map.92.lines_ref, bf16[64,2048]{1,0:T(8,128)(2,1)S(1)} %copy-done.1, ...), custom_call_target="tpu_custom_call" | custom-call | flops 100000 | bytes 10000000 | tf_op jit(solution)/shard_map/pallas_call | solution.py:266
  36.4 0.1 collective-permute-start.8
  36.5 0.5 %collective-permute-start.7 = (bf16[2,32,2048]{2,1,0:T(8,128)(2,1)S(1)}, bf16[2,32,2048]{2,1,0:T(8,128)(2,1)S(1)}, u32[]{:S(2)}, u32[]{:S(2)}) collective-permute-start(bf16[2,32,2048]{2,1,0:T(8,128)(2,1)S(1)} %get-tuple-element.32), channel_id=1, source_target_pairs={{0,1},{1,0},{2,3},{3,2},{4,5},{5,4},{6,7},{7,6},{8,9},{9,8},{10,11... | collective-permute-start | bytes 786440 | tf_op jit(solution)/shard_map/ppermute | solution.py:364
  37.0 1.0 %collective-permute-done.8.b_ref = bf16[2,32,2048]{2,1,0:T(8,128)(2,1)S(1)} collective-permute-done((bf16[2,32,2048]{2,1,0:T(8,128)(2,1)S(1)}, bf16[2,32,2048]{2,1,0:T(8,128)(2,1)S(1)}, u32[]{:S(2)}, u32[]{:S(2)}) %collective-permute-start.8) | collective-permute-done | bytes 262176 | tf_op jit(solution)/shard_map/ppermute | solution.py:364
  38.0 0.0 copy-start.4
  38.0 0.1 shard_map.95
  38.1 0.9 %collective-permute-start.10 = (bf16[32,2048]{1,0:T(8,128)(2,1)S(1)}, bf16[32,2048]{1,0:T(8,128)(2,1)S(1)}, u32[]{:S(2)}, u32[]{:S(2)}) collective-permute-start(bf16[32,2048]{1,0:T(8,128)(2,1)S(1)} %get-tuple-element.37), channel_id=1, source_target_pairs={{0,4},{2,6},{4,0},{6,2},{8,12},{10,14},{12,8},{14,10},{1,5},{3,7},... | collective-permute-start | bytes 393224 | tf_op jit(solution)/shard_map/ppermute | solution.py:341
  39.0 1.6 %collective-permute-start.9 = (bf16[32,2048]{1,0:T(8,128)(2,1)S(1)}, bf16[32,2048]{1,0:T(8,128)(2,1)S(1)}, u32[]{:S(2)}, u32[]{:S(2)}) collective-permute-start(bf16[32,2048]{1,0:T(8,128)(2,1)S(1)} %get-tuple-element.36), channel_id=1, source_target_pairs={{0,2},{2,0},{4,6},{6,4},{8,10},{10,8},{12,14},{14,12},{1,3},{3,1},... | collective-permute-start | bytes 393224 | tf_op jit(solution)/shard_map/ppermute | solution.py:341
  40.6 0.0 collective-permute-done.7.b_ref
  40.6 0.1 shard_map.94
  40.7 1.1 %collective-permute-start.11 = (bf16[32,2048]{1,0:T(8,128)(2,1)S(1)}, bf16[32,2048]{1,0:T(8,128)(2,1)S(1)}, u32[]{:S(2)}, u32[]{:S(2)}) collective-permute-start(bf16[32,2048]{1,0:T(8,128)(2,1)S(1)} %get-tuple-element.38), channel_id=1, source_target_pairs={{0,6},{2,4},{4,2},{6,0},{8,14},{10,12},{12,10},{14,8},{1,7},{3,5},... | collective-permute-start | bytes 393224 | tf_op jit(solution)/shard_map/ppermute | solution.py:341
  41.8 0.0 copy-done
  41.8 0.0 copy-done.4
  41.8 0.5 fusion.2.gate_ref
  42.3 0.0 copy-start.3
  42.3 0.6 %copy-done.3 = f32[128]{0:T(128)S(1)} copy-done((f32[128]{0:T(128)S(1)}, f32[128]{0:T(128)}, u32[]{:S(2)}) %copy-start.3) | copy-done | bytes 536
  42.9 0.0 copy-start.2
  42.9 0.1 copy.10.gain_ref
  43.0 1.5 %collective-permute-done.10.refs_2_ = bf16[32,2048]{1,0:T(8,128)(2,1)S(1)} collective-permute-done((bf16[32,2048]{1,0:T(8,128)(2,1)S(1)}, bf16[32,2048]{1,0:T(8,128)(2,1)S(1)}, u32[]{:S(2)}, u32[]{:S(2)}) %collective-permute-start.10) | collective-permute-done | bytes 131104 | tf_op jit(solution)/shard_map/ppermute | solution.py:341
  44.5 2.6 %collective-permute-done.9.refs_1_ = bf16[32,2048]{1,0:T(8,128)(2,1)S(1)} collective-permute-done((bf16[32,2048]{1,0:T(8,128)(2,1)S(1)}, bf16[32,2048]{1,0:T(8,128)(2,1)S(1)}, u32[]{:S(2)}, u32[]{:S(2)}) %collective-permute-start.9) | collective-permute-done | bytes 131104 | tf_op jit(solution)/shard_map/ppermute | solution.py:341
  47.1 0.0 collective-permute-done.11.refs_3_
  47.1 0.0 copy-done.2
  47.1 1.4 %shard_map.96 = bf16[1936,128]{1,0:T(8,128)(2,1)} custom-call(f32[128,1]{1,0:T(8,128)S(1)} %copy.10.gain_ref, bf16[128,128]{1,0:T(8,128)(2,1)S(1)} %copy-done.2, f32[1936,128]{1,0:T(8,128)S(1)} %fusion.2.gate_ref, bf16[32,2048]{1,0:T(8,128)(2,1)S(1)} %get-tuple-element.33.refs_0_, bf16[32,2048]{1,0:T(8,128)(2,1)S(1)} %collective-permute-done.9.refs_1_, ...), custom_call_target="tpu_custom_call" | custom-call | tf_op jit(solution)/shard_map/pallas_call | solution.py:326
Async XLA Ops:
  0.0 41.8 %copy-start = (bf16[128,128]{1,0:T(8,128)(2,1)S(1)}, bf16[128,128]{1,0:T(8,128)(2,1)}, u32[]{:S(2)}) copy-start(bf16[128,128]{1,0:T(8,128)(2,1)} %param.16) | copy-start | bytes 98308
  4.0 9.8 %collective-permute-start = (bf16[32,2048]{1,0:T(8,128)(2,1)}, bf16[32,2048]{1,0:T(8,128)(2,1)S(1)}, u32[]{:S(2)}, u32[]{:S(2)}) collective-permute-start(bf16[32,2048]{1,0:T(8,128)(2,1)} %get-tuple-element.23), channel_id=1, source_target_pairs={{0,12},{2,14},{4,8},{6,10},{8,4},{10,6},{12,0},{14,2},{1,13},{3,15... | collective-permute-start | bytes 393224 | tf_op jit(solution)/shard_map/ppermute | solution.py:341
  9.1 11.2 %collective-permute-start.1 = (bf16[32,2048]{1,0:T(8,128)(2,1)}, bf16[32,2048]{1,0:T(8,128)(2,1)S(1)}, u32[]{:S(2)}, u32[]{:S(2)}) collective-permute-start(bf16[32,2048]{1,0:T(8,128)(2,1)} %get-tuple-element.24), channel_id=1, source_target_pairs={{0,14},{2,12},{4,10},{6,8},{8,6},{10,4},{12,2},{14,0},{1,15},{3,13... | collective-permute-start | bytes 393224 | tf_op jit(solution)/shard_map/ppermute | solution.py:341
  10.3 21.6 %collective-permute-start.2 = (bf16[64,2048]{1,0:T(8,128)(2,1)}, bf16[64,2048]{1,0:T(8,128)(2,1)S(1)}, u32[]{:S(2)}, u32[]{:S(2)}) collective-permute-start(bf16[64,2048]{1,0:T(8,128)(2,1)} %get-tuple-element.26), channel_id=1, source_target_pairs={{0,2},{2,0},{4,6},{6,4},{8,10},{10,8},{12,14},{14,12},{1,3},{3,1},... | collective-permute-start | bytes 786440 | tf_op jit(solution)/shard_map/ppermute | solution.py:341
  10.6 21.2 %collective-permute-start.3 = (bf16[64,2048]{1,0:T(8,128)(2,1)}, bf16[64,2048]{1,0:T(8,128)(2,1)S(1)}, u32[]{:S(2)}, u32[]{:S(2)}) collective-permute-start(bf16[64,2048]{1,0:T(8,128)(2,1)} %get-tuple-element.27), channel_id=1, source_target_pairs={{0,4},{2,6},{4,0},{6,2},{8,12},{10,14},{12,8},{14,10},{1,5},{3,7},... | collective-permute-start | bytes 786440 | tf_op jit(solution)/shard_map/ppermute | solution.py:341
  10.6 22.9 %collective-permute-start.4 = (bf16[64,2048]{1,0:T(8,128)(2,1)}, bf16[64,2048]{1,0:T(8,128)(2,1)S(1)}, u32[]{:S(2)}, u32[]{:S(2)}) collective-permute-start(bf16[64,2048]{1,0:T(8,128)(2,1)} %get-tuple-element.28), channel_id=1, source_target_pairs={{0,6},{2,4},{4,2},{6,0},{8,14},{10,12},{12,10},{14,8},{1,7},{3,5},... | collective-permute-start | bytes 786440 | tf_op jit(solution)/shard_map/ppermute | solution.py:341
  13.8 16.4 %collective-permute-start.5 = (bf16[32,2048]{1,0:T(8,128)(2,1)}, bf16[32,2048]{1,0:T(8,128)(2,1)S(1)}, u32[]{:S(2)}, u32[]{:S(2)}) collective-permute-start(bf16[32,2048]{1,0:T(8,128)(2,1)} %get-tuple-element.29), channel_id=1, source_target_pairs={{0,8},{2,10},{4,12},{6,14},{8,0},{10,2},{12,4},{14,6},{1,9},{3,11}... | collective-permute-start | bytes 393224 | tf_op jit(solution)/shard_map/ppermute | solution.py:341
  20.3 13.2 %copy-start.1 = (bf16[64,2048]{1,0:T(8,128)(2,1)S(1)}, bf16[64,2048]{1,0:T(8,128)(2,1)}, u32[]{:S(2)}) copy-start(bf16[64,2048]{1,0:T(8,128)(2,1)} %get-tuple-element.25.refs_0_) | copy-start | bytes 786436
  20.3 11.6 %collective-permute-start.6 = (bf16[32,2048]{1,0:T(8,128)(2,1)}, bf16[32,2048]{1,0:T(8,128)(2,1)S(1)}, u32[]{:S(2)}, u32[]{:S(2)}) collective-permute-start(bf16[32,2048]{1,0:T(8,128)(2,1)} %get-tuple-element.30), channel_id=1, source_target_pairs={{0,10},{2,8},{4,14},{6,12},{8,2},{10,0},{12,6},{14,4},{1,11},{3,9}... | collective-permute-start | bytes 393224 | tf_op jit(solution)/shard_map/ppermute | solution.py:341
  36.4 1.6 %collective-permute-start.8 = (bf16[2,32,2048]{2,1,0:T(8,128)(2,1)S(1)}, bf16[2,32,2048]{2,1,0:T(8,128)(2,1)S(1)}, u32[]{:S(2)}, u32[]{:S(2)}) collective-permute-start(bf16[2,32,2048]{2,1,0:T(8,128)(2,1)S(1)} %get-tuple-element.35), channel_id=1, source_target_pairs={{0,1},{1,0},{2,3},{3,2},{4,5},{5,4},{6,7},{7,6},{8,9},{9,8},{10,11... | collective-permute-start | bytes 786440 | tf_op jit(solution)/shard_map/ppermute | solution.py:364
  36.5 4.1 %collective-permute-start.7 = (bf16[2,32,2048]{2,1,0:T(8,128)(2,1)S(1)}, bf16[2,32,2048]{2,1,0:T(8,128)(2,1)S(1)}, u32[]{:S(2)}, u32[]{:S(2)}) collective-permute-start(bf16[2,32,2048]{2,1,0:T(8,128)(2,1)S(1)} %get-tuple-element.32), channel_id=1, source_target_pairs={{0,1},{1,0},{2,3},{3,2},{4,5},{5,4},{6,7},{7,6},{8,9},{9,8},{10,11... | collective-permute-start | bytes 786440 | tf_op jit(solution)/shard_map/ppermute | solution.py:364
  38.0 3.8 %copy-start.4 = (bf16[128,2048]{1,0:T(8,128)(2,1)S(1)}, bf16[128,2048]{1,0:T(8,128)(2,1)}, u32[]{:S(2)}) copy-start(bf16[128,2048]{1,0:T(8,128)(2,1)} %get-tuple-element.22) | copy-start | bytes 1572868
  38.1 6.4 %collective-permute-start.10 = (bf16[32,2048]{1,0:T(8,128)(2,1)S(1)}, bf16[32,2048]{1,0:T(8,128)(2,1)S(1)}, u32[]{:S(2)}, u32[]{:S(2)}) collective-permute-start(bf16[32,2048]{1,0:T(8,128)(2,1)S(1)} %get-tuple-element.37), channel_id=1, source_target_pairs={{0,4},{2,6},{4,0},{6,2},{8,12},{10,14},{12,8},{14,10},{1,5},{3,7},... | collective-permute-start | bytes 393224 | tf_op jit(solution)/shard_map/ppermute | solution.py:341
  39.0 8.1 %collective-permute-start.9 = (bf16[32,2048]{1,0:T(8,128)(2,1)S(1)}, bf16[32,2048]{1,0:T(8,128)(2,1)S(1)}, u32[]{:S(2)}, u32[]{:S(2)}) collective-permute-start(bf16[32,2048]{1,0:T(8,128)(2,1)S(1)} %get-tuple-element.36), channel_id=1, source_target_pairs={{0,2},{2,0},{4,6},{6,4},{8,10},{10,8},{12,14},{14,12},{1,3},{3,1},... | collective-permute-start | bytes 393224 | tf_op jit(solution)/shard_map/ppermute | solution.py:341
  40.7 6.4 %collective-permute-start.11 = (bf16[32,2048]{1,0:T(8,128)(2,1)S(1)}, bf16[32,2048]{1,0:T(8,128)(2,1)S(1)}, u32[]{:S(2)}, u32[]{:S(2)}) collective-permute-start(bf16[32,2048]{1,0:T(8,128)(2,1)S(1)} %get-tuple-element.38), channel_id=1, source_target_pairs={{0,6},{2,4},{4,2},{6,0},{8,14},{10,12},{12,10},{14,8},{1,7},{3,5},... | collective-permute-start | bytes 393224 | tf_op jit(solution)/shard_map/ppermute | solution.py:341
  42.3 0.7 %copy-start.3 = (f32[128]{0:T(128)S(1)}, f32[128]{0:T(128)}, u32[]{:S(2)}) copy-start(f32[128]{0:T(128)} %param.13) | copy-start | bytes 1540
  42.9 4.2 %copy-start.2 = (bf16[128,128]{1,0:T(8,128)(2,1)S(1)}, bf16[128,128]{1,0:T(8,128)(2,1)}, u32[]{:S(2)}) copy-start(bf16[128,128]{1,0:T(8,128)(2,1)} %w_ref.1) | copy-start | bytes 98308

commit v11 on v10

--- a/solution.py
+++ b/solution.py
@@ -113,7 +113,7 @@
 def make_edges(pair, lens, resolved, gain, w_left, w_right, groups, rows, cols):
     count, channels = pair.shape
     own = w_left.shape[1] // 2 // groups
-    block = 512
+    block = 256
     flat = ceil_to(count, block)
     chunks = [(at, min(block, count - at)) for at in range(0, count, block)]
     here = pl.BlockSpec(memory_space=pltpu.HBM)
@@ -189,32 +189,27 @@
     return jnp.concatenate([held[t, pl.ds(d, count, stride=step), :] for t in range(held.shape[0])], axis=1)
 
 
-def lines_kernel(groups, rows, cols, *refs):
-    got_refs, lines_ref = refs[:-1], refs[-1]
-    mine = place_of(groups, rows, cols)[2]
-    count = len(got_refs)
-    step = lines_ref.shape[1] // (count * rows)
-    for u in range(count):
-        block = jnp.bitwise_and(jnp.bitwise_xor(mine, u), count - 1)
-        unpack(got_refs[u], (lines_ref,), block, rows, cols, step)
-
-
-def products_kernel(groups, rows, cols, parts, lines_ref, *refs):
-    half = groups // 2
-    near_refs, far_refs = refs[:groups], refs[groups:groups + half]
-    keep_refs, send_refs = refs[groups + half:groups + half + 2], refs[groups + half + 2:groups + half + 4]
-    left_s, right_s, far_s, prod_s = refs[groups + half + 4:]
+def lines_kernel(rows, cols, *refs):
+    count = len(refs) // 2
+    for got_ref, lines_ref in zip(refs[:count], refs[count:]):
+        unpack(got_ref, (lines_ref,), 0, rows, cols, lines_ref.shape[1] // rows)
+
+
+def products_kernel(groups, rows, cols, parts, early, late, *refs):
+    lines_refs, near_refs, far_refs = refs[:len(early)], refs[len(early):][:groups], refs[len(early) + groups:][:len(late)]
+    keep_refs, send_refs = refs[2 * groups:2 * groups + 2], refs[2 * groups + 2:2 * groups + 4]
+    left_s, right_s, far_s, prod_s = refs[2 * groups + 4:]
     _, _, mine, own_half, col = place_of(groups, rows, cols)
-    ch = far_refs[0].shape[0]
+    ch = keep_refs[0].shape[1]
     step = left_s.shape[1] // (groups * rows)
     count = groups * rows
     tiles = left_s.shape[0]
-    size = lines_ref.shape[1]
-    far_s[:, pl.ds(pl.multiple_of((1 - mine // half) * size, 8), size), :] = lines_ref[...]
+    for u, lines_ref in zip(early, lines_refs):
+        far_s[:, pl.ds(pl.multiple_of(jnp.bitwise_xor(mine, u) * rows * step, 8), rows * step), :] = lines_ref[...]
     for u in range(groups):
         unpack(near_refs[u], (left_s, right_s), jnp.bitwise_xor(mine, u), rows, cols, step)
-    for u in range(half):
-        unpack(far_refs[u], (far_s,), jnp.bitwise_xor(mine, u), rows, cols, step)
+    for u, far_ref in zip(late, far_refs):
+        unpack(far_ref, (far_s,), jnp.bitwise_xor(mine, u), rows, cols, step)
     pad = [jnp.zeros((tiles * LANES - count, tiles * LANES), jnp.float32)] if count % LANES else []
     for d in range(ch):
         left = channel_of(left_s, d, count, step)
@@ -243,35 +238,35 @@
     return (pl.cdiv(cols, LANES), blocks * line_step(ch), LANES)
 
 
-def make_lines(got, groups, rows, cols):
+def make_lines(got, rows, cols):
     ch = got[0].shape[0]
     whole = pl.BlockSpec(memory_space=pltpu.VMEM)
     return pl.pallas_call(
-        functools.partial(lines_kernel, groups, rows, cols),
+        functools.partial(lines_kernel, rows, cols),
         in_specs=[whole] * len(got),
-        out_specs=whole,
-        out_shape=jax.ShapeDtypeStruct(lines_of(len(got) * rows, ch, cols), jnp.float32),
+        out_specs=[whole] * len(got),
+        out_shape=[jax.ShapeDtypeStruct(lines_of(rows, ch, cols), jnp.float32)] * len(got),
         compiler_params=pltpu.CompilerParams(vmem_limit_bytes=VMEM_LIMIT),
         cost_estimate=pl.CostEstimate(flops=10 ** 5, bytes_accessed=10 ** 8, transcendentals=0),
     )(*got)
 
 
-def make_products(lines, near, far, parts, rows, cols):
+def make_products(lines, near, far, parts, early, late, rows, cols):
     groups = len(near)
-    ch, flat = far[0].shape
+    ch, flat = near[0].shape[0] // 2, near[0].shape[1]
     whole = pl.BlockSpec(memory_space=pltpu.VMEM)
     tiles, held, _ = lines_of(groups * rows, ch, cols)
     one = pltpu.VMEM((tiles, held, LANES), jnp.float32)
     sizes = [len(pieces) for pieces in parts] * 2
     return pl.pallas_call(
-        functools.partial(products_kernel, groups, rows, cols, parts),
-        in_specs=[whole] * (1 + len(near) + len(far)),
+        functools.partial(products_kernel, groups, rows, cols, parts, early, late),
+        in_specs=[whole] * (2 * groups),
         out_specs=[whole] * 4,
         out_shape=[jax.ShapeDtypeStruct((n, ch, flat), jnp.bfloat16) for n in sizes],
         scratch_shapes=[one, one, one, pltpu.VMEM((2 * tiles, held, LANES), jnp.float32)],
         compiler_params=pltpu.CompilerParams(vmem_limit_bytes=VMEM_LIMIT),
         cost_estimate=pl.CostEstimate(flops=10 ** 5, bytes_accessed=10 ** 7, transcendentals=0),
-    )(lines, *near, *far)
+    )(*lines, *near, *far)
 
 
 def add_kernel(a_ref, b_ref, *out_refs):
@@ -294,21 +289,24 @@
 
 def update_kernel(groups, rows, cols, chunks, gain_ref, w_ref, gate_ref, *refs):
     prod_refs = refs[:groups]
-    out_ref, held, out_s, sems = refs[groups:]
+    out_ref, gain_s, w_s, out_s, sems = refs[groups:]
     mine = place_of(groups, rows, cols)[2]
-    ch = held.shape[1]
-    block = held.shape[2]
+    ch = prod_refs[0].shape[0]
+    block = chunks[0][1]
+    for u in range(groups):
+        there = pl.ds(pl.multiple_of(jnp.bitwise_xor(mine, u) * ch, 8), ch)
+        gain_s[u * ch:(u + 1) * ch] = gain_ref[there]
+        w_s[u * ch:(u + 1) * ch] = w_ref[there]
+    gain, weights = gain_s[...], w_s[...].astype(jnp.bfloat16)
     stores = []
     for n, (at, size) in enumerate(chunks):
         lanes = pl.ds(at, block)
-        for u in range(groups):
-            held[jnp.bitwise_xor(mine, u)] = prod_refs[u][:, lanes].astype(jnp.float32)
-        prod = held[...].reshape(groups * ch, block)
+        prod = jnp.concatenate([ref[:, lanes].astype(jnp.float32) for ref in prod_refs], axis=0)
         mean = jnp.mean(prod, axis=0, keepdims=True)
         centred = prod - mean
         variance = jnp.mean(centred * centred, axis=0, keepdims=True)
-        normed = (centred * lax.rsqrt(variance + EPS) * gain_ref[...]).astype(jnp.bfloat16)
-        projected = lax.dot_general(normed, w_ref[...], (((0,), (0,)), ((), ())), preferred_element_type=jnp.float32)
+        normed = (centred * lax.rsqrt(variance + EPS) * gain).astype(jnp.bfloat16)
+        projected = lax.dot_general(normed, weights, (((0,), (0,)), ((), ())), preferred_element_type=jnp.float32)
         out_s[pl.ds(at, size)] = (gate_ref[pl.ds(at, size)] * projected[:size]).astype(out_s.dtype)
         stores.append(pltpu.make_async_copy(out_s.at[pl.ds(at, size)], out_ref.at[pl.ds(at, size)], sems.at[n]))
         stores[-1].start()
@@ -320,7 +318,7 @@
     groups = len(prods)
     ch = prods[0].shape[0]
     count, channels = gate.shape
-    block = 512
+    block = 256
     chunks = [(at, min(block, count - at)) for at in range(0, count, block)]
     whole = pl.BlockSpec(memory_space=pltpu.VMEM)
     return pl.pallas_call(
@@ -329,7 +327,8 @@
         out_specs=pl.BlockSpec(memory_space=pltpu.HBM),
         out_shape=jax.ShapeDtypeStruct((count, channels), jnp.bfloat16),
         scratch_shapes=[
-            pltpu.VMEM((groups, ch, block), jnp.float32),
+            pltpu.VMEM(gain.shape, jnp.float32),
+            pltpu.VMEM(w_out.shape, jnp.float32),
             pltpu.VMEM((count, channels), jnp.bfloat16),
             pltpu.SemaphoreType.DMA((len(chunks),)),
         ],
@@ -356,15 +355,16 @@
         jnp.einsum("cp,cd->pd", normed[:, :rows * cols], w_gate, preferred_element_type=jnp.float32)
     )
     half = groups // 2
-    lines = make_lines(far_got[half:], groups, rows, cols)
+    early, late = list(range(half, groups)) + [0], list(range(1, half))
+    lines = make_lines([far_got[u] for u in early], rows, cols)
     parts = [list(range(1, half + 1)), [0] + list(range(half + 1, groups))]
-    made = make_products(lines, near_got, far_got[:half], parts, rows, cols)
+    made = make_products(lines, near_got, [far_got[u] for u in late], parts, early, late, rows, cols)
     sums = {}
     for part, pieces in enumerate(parts):
         other = lax.ppermute(made[2 + part], "col", [(0, 1), (1, 0)])
         sums.update(zip(pieces, make_sums(made[part], other)))
     returned = [sums[0]] + [swap(sums[u], u) for u in range(1, groups)]
-    update = make_update(returned, out_gain.reshape(hidden, 1), w_out, gate, rows, cols)
+    update = make_update(returned, out_gain.reshape(hidden, 1), w_out.astype(jnp.float32), gate, rows, cols)
     return update.reshape(rows, cols, channels)
 
 

time: 48.7 us -> 49.7 us (1.021)
  Pallas kernels: 8.62 us -> 9.62 us
    pallas_call x1, Pallas kernels: 3.97 us -> 5.11 us  [make_edges(): pl.pallas_call(functools.partial(edges_kernel, groups, rows, cols, chunks...]
where the time goes in v11:
time: 49.7 us; the launch traced here: 49.5 us
  starting transfers between devices  24.2 us (49%)
  waiting for transfers between devices  14 us (28%)
  Pallas kernels  9.62 us (19%)
  local copies, waits for them, and re-layouts  1.06 us (2%)
    ppermute x10, starting transfers between devices, swap(): lax.ppermute(value, 'row', [(r, r ^ shift) for r in range(lax.axis_size('...  23.6 us
    ppermute x10, waiting for transfers between devices, swap(): lax.ppermute(value, 'row', [(r, r ^ shift) for r in range(lax.axis_size('...  13 us
    pallas_call x1, Pallas kernels, make_edges(): pl.pallas_call(functools.partial(edges_kernel, groups, rows, cols, chunks...  5.11 us
    pallas_call x1, Pallas kernels, make_products(): pl.pallas_call(functools.partial(products_kernel, groups, rows, cols, par...  2.81 us
    pallas_call x1, Pallas kernels, make_update(): pl.pallas_call(functools.partial(update_kernel, groups, rows, cols, chunk...  1.28 us
    ppermute x2, waiting for transfers between devices, shards(): other = lax.ppermute(made[2 + part], 'col', [(0, 1), (1, 0)])  1.03 us
  transfers between devices with their start and end apart: 12, of which 6 were waited for; matrix products, arithmetic and copies ran while one was open for 1% of the time, Pallas kernels for 1%

profile of v11, /device:TPU:0, one launch (start us, length us, event | category | flops | bytes accessed | tf_op | source)
XLA Modules:
  0.0 49.5 jit_solution(18227943920811265208)
XLA Ops:
  0.0 0.0 copy-start
  0.0 5.1 %shard_map.91 = (bf16[128,2048]{1,0:T(8,128)(2,1)}, bf16[64,2048]{1,0:T(8,128)(2,1)}, bf16[64,2048]{1,0:T(8,128)(2,1)}, bf16[64,2048]{1,0:T(8,128)(2,1)}, bf16[6...) custom-call(bf16[1936,128]{1,0:T(8,128)(2,1)} %bitcast.5, ...), custom_call_target="tpu_custom_call" | custom-call | tf_op jit(solution)/shard_map/pallas_call | solution.py:120
  5.1 0.0 copy-start.1
  5.1 5.1 %collective-permute-start = (bf16[32,2048]{1,0:T(8,128)(2,1)}, bf16[32,2048]{1,0:T(8,128)(2,1)S(1)}, u32[]{:S(2)}, u32[]{:S(2)}) collective-permute-start(bf16[32,2048]{1,0:T(8,128)(2,1)} %get-tuple-element.26), channel_id=1, source_target_pairs={{0,12},{2,14},{4,8},{6,10},{8,4},{10,6},{12,0},{14,2},{1,13},{3,15... | collective-permute-start | bytes 393224 | tf_op jit(solution)/shard_map/ppermute | solution.py:340
  10.3 1.2 %collective-permute-start.1 = (bf16[32,2048]{1,0:T(8,128)(2,1)}, bf16[32,2048]{1,0:T(8,128)(2,1)S(1)}, u32[]{:S(2)}, u32[]{:S(2)}) collective-permute-start(bf16[32,2048]{1,0:T(8,128)(2,1)} %get-tuple-element.27), channel_id=1, source_target_pairs={{0,14},{2,12},{4,10},{6,8},{8,6},{10,4},{12,2},{14,0},{1,15},{3,13... | collective-permute-start | bytes 393224 | tf_op jit(solution)/shard_map/ppermute | solution.py:340
  11.4 0.4 collective-permute-start.3
  11.8 0.0 collective-permute-start.4
  11.8 3.1 %collective-permute-start.5 = (bf16[64,2048]{1,0:T(8,128)(2,1)}, bf16[64,2048]{1,0:T(8,128)(2,1)S(1)}, u32[]{:S(2)}, u32[]{:S(2)}) collective-permute-start(bf16[64,2048]{1,0:T(8,128)(2,1)} %get-tuple-element.35), channel_id=1, source_target_pairs={{0,6},{2,4},{4,2},{6,0},{8,14},{10,12},{12,10},{14,8},{1,7},{3,5},... | collective-permute-start | bytes 786440 | tf_op jit(solution)/shard_map/ppermute | solution.py:340
  14.9 0.0 collective-permute-done.refs_0_
  14.9 6.5 %collective-permute-start.2 = (bf16[32,2048]{1,0:T(8,128)(2,1)}, bf16[32,2048]{1,0:T(8,128)(2,1)S(1)}, u32[]{:S(2)}, u32[]{:S(2)}) collective-permute-start(bf16[32,2048]{1,0:T(8,128)(2,1)} %get-tuple-element.28), channel_id=1, source_target_pairs={{0,8},{2,10},{4,12},{6,14},{8,0},{10,2},{12,4},{14,6},{1,9},{3,11}... | collective-permute-start | bytes 393224 | tf_op jit(solution)/shard_map/ppermute | solution.py:340
  21.5 0.0 collective-permute-done.1.refs_1_
  21.5 3.7 %collective-permute-start.6 = (bf16[32,2048]{1,0:T(8,128)(2,1)}, bf16[32,2048]{1,0:T(8,128)(2,1)S(1)}, u32[]{:S(2)}, u32[]{:S(2)}) collective-permute-start(bf16[32,2048]{1,0:T(8,128)(2,1)} %get-tuple-element.36), channel_id=1, source_target_pairs={{0,10},{2,8},{4,14},{6,12},{8,2},{10,0},{12,6},{14,4},{1,11},{3,9}... | collective-permute-start | bytes 393224 | tf_op jit(solution)/shard_map/ppermute | solution.py:340
  25.2 6.2 %collective-permute-done.2.refs_2_ = bf16[32,2048]{1,0:T(8,128)(2,1)S(1)} collective-permute-done((bf16[32,2048]{1,0:T(8,128)(2,1)}, bf16[32,2048]{1,0:T(8,128)(2,1)S(1)}, u32[]{:S(2)}, u32[]{:S(2)}) %collective-permute-start.2) | collective-permute-done | bytes 131104 | tf_op jit(solution)/shard_map/ppermute | solution.py:340
  31.3 0.3 shard_map.92
  31.6 1.4 %collective-permute-done.6.refs_7_ = bf16[32,2048]{1,0:T(8,128)(2,1)S(1)} collective-permute-done((bf16[32,2048]{1,0:T(8,128)(2,1)}, bf16[32,2048]{1,0:T(8,128)(2,1)S(1)}, u32[]{:S(2)}, u32[]{:S(2)}) %collective-permute-start.6) | collective-permute-done | bytes 131104 | tf_op jit(solution)/shard_map/ppermute | solution.py:340
  33.0 0.0 collective-permute-done.3.refs_4_
  33.0 0.0 collective-permute-done.4.refs_5_
  33.0 1.6 %collective-permute-done.5.refs_6_ = bf16[64,2048]{1,0:T(8,128)(2,1)S(1)} collective-permute-done((bf16[64,2048]{1,0:T(8,128)(2,1)}, bf16[64,2048]{1,0:T(8,128)(2,1)S(1)}, u32[]{:S(2)}, u32[]{:S(2)}) %collective-permute-start.5) | collective-permute-done | bytes 262176 | tf_op jit(solution)/shard_map/ppermute | solution.py:340
  34.7 0.0 copy-done.1
  34.7 2.8 %shard_map.93 = (bf16[2,32,2048]{2,1,0:T(8,128)(2,1)S(1)}, bf16[2,32,2048]{2,1,0:T(8,128)(2,1)S(1)}, bf16[2,32,2048]{2,1,0:T(8,128)(2,1)S(1)}, bf16[2,32,2048]{2,1,0:T(8,128)(2,1)S(1)}) custom-call(f32[1,880,128]{2,1,0:T(8,128)S(1)} %get-tuple-element.29.refs_0_, f32[1,880,128]{2,1,0:T(8,128)S(1)} %get-tuple-element.30.refs_1_, ...), custom_call_target="tpu_custom_call" | custom-call | flops 100000 | bytes 10000000 | tf_op jit(solution)/shard_map/pallas_call | solution.py:261
  37.5 0.1 collective-permute-start.8
  37.6 0.5 %collective-permute-start.7 = (bf16[2,32,2048]{2,1,0:T(8,128)(2,1)S(1)}, bf16[2,32,2048]{2,1,0:T(8,128)(2,1)S(1)}, u32[]{:S(2)}, u32[]{:S(2)}) collective-permute-start(bf16[2,32,2048]{2,1,0:T(8,128)(2,1)S(1)} %get-tuple-element.38), channel_id=1, source_target_pairs={{0,1},{1,0},{2,3},{3,2},{4,5},{5,4},{6,7},{7,6},{8,9},{9,8},{10,11... | collective-permute-start | bytes 786440 | tf_op jit(solution)/shard_map/ppermute | solution.py:364
  38.1 1.0 %collective-permute-done.8.b_ref = bf16[2,32,2048]{2,1,0:T(8,128)(2,1)S(1)} collective-permute-done((bf16[2,32,2048]{2,1,0:T(8,128)(2,1)S(1)}, bf16[2,32,2048]{2,1,0:T(8,128)(2,1)S(1)}, u32[]{:S(2)}, u32[]{:S(2)}) %collective-permute-start.8) | collective-permute-done | bytes 262176 | tf_op jit(solution)/shard_map/ppermute | solution.py:364
  39.1 0.0 copy-start.4
  39.1 0.1 shard_map.95
  39.2 0.9 %collective-permute-start.10 = (bf16[32,2048]{1,0:T(8,128)(2,1)S(1)}, bf16[32,2048]{1,0:T(8,128)(2,1)S(1)}, u32[]{:S(2)}, u32[]{:S(2)}) collective-permute-start(bf16[32,2048]{1,0:T(8,128)(2,1)S(1)} %get-tuple-element.43), channel_id=1, source_target_pairs={{0,4},{2,6},{4,0},{6,2},{8,12},{10,14},{12,8},{14,10},{1,5},{3,7},... | collective-permute-start | bytes 393224 | tf_op jit(solution)/shard_map/ppermute | solution.py:340
  40.1 1.6 %collective-permute-start.9 = (bf16[32,2048]{1,0:T(8,128)(2,1)S(1)}, bf16[32,2048]{1,0:T(8,128)(2,1)S(1)}, u32[]{:S(2)}, u32[]{:S(2)}) collective-permute-start(bf16[32,2048]{1,0:T(8,128)(2,1)S(1)} %get-tuple-element.42), channel_id=1, source_target_pairs={{0,2},{2,0},{4,6},{6,4},{8,10},{10,8},{12,14},{14,12},{1,3},{3,1},... | collective-permute-start | bytes 393224 | tf_op jit(solution)/shard_map/ppermute | solution.py:340
  41.7 0.0 collective-permute-done.7.b_ref
  41.7 0.1 shard_map.94
  41.8 1.1 %collective-permute-start.11 = (bf16[32,2048]{1,0:T(8,128)(2,1)S(1)}, bf16[32,2048]{1,0:T(8,128)(2,1)S(1)}, u32[]{:S(2)}, u32[]{:S(2)}) collective-permute-start(bf16[32,2048]{1,0:T(8,128)(2,1)S(1)} %get-tuple-element.44), channel_id=1, source_target_pairs={{0,6},{2,4},{4,2},{6,0},{8,14},{10,12},{12,10},{14,8},{1,7},{3,5},... | collective-permute-start | bytes 393224 | tf_op jit(solution)/shard_map/ppermute | solution.py:340
  42.9 0.0 copy-done
  42.9 0.0 copy-done.4
  42.9 0.0 copy-start.2
  42.9 0.5 fusion.2.gate_ref
  43.4 0.3 copy-done.2
  43.6 0.0 copy-start.3
  43.6 0.7 %copy-done.3 = f32[128]{0:T(128)S(1)} copy-done((f32[128]{0:T(128)S(1)}, f32[128]{0:T(128)}, u32[]{:S(2)}) %copy-start.3) | copy-done | bytes 536
  44.3 0.1 copy.10.gain_ref
  44.4 1.2 %collective-permute-done.10.refs_2_ = bf16[32,2048]{1,0:T(8,128)(2,1)S(1)} collective-permute-done((bf16[32,2048]{1,0:T(8,128)(2,1)S(1)}, bf16[32,2048]{1,0:T(8,128)(2,1)S(1)}, u32[]{:S(2)}, u32[]{:S(2)}) %collective-permute-start.10) | collective-permute-done | bytes 131104 | tf_op jit(solution)/shard_map/ppermute | solution.py:340
  45.6 2.6 %collective-permute-done.9.refs_1_ = bf16[32,2048]{1,0:T(8,128)(2,1)S(1)} collective-permute-done((bf16[32,2048]{1,0:T(8,128)(2,1)S(1)}, bf16[32,2048]{1,0:T(8,128)(2,1)S(1)}, u32[]{:S(2)}, u32[]{:S(2)}) %collective-permute-start.9) | collective-permute-done | bytes 131104 | tf_op jit(solution)/shard_map/ppermute | solution.py:340
  48.2 0.0 collective-permute-done.11.refs_3_
  48.2 1.3 %shard_map.96 = bf16[1936,128]{1,0:T(8,128)(2,1)} custom-call(f32[128,1]{1,0:T(8,128)S(1)} %copy.10.gain_ref, f32[128,128]{1,0:T(8,128)S(1)} %convert_element_type.3.w_ref, f32[1936,128]{1,0:T(8,128)S(1)} %fusion.2.gate_ref, bf16[32,2048]{1,0:T(8,128)(2,1)S(1)} %get-tuple-element.39.refs_0_, bf16[32,2048]{1,0:T(8,128)(2,1)S(1)} %collective-permute-done.9.refs_1_, ...), custom_call_target="tpu_custom_call" | custom-call | tf_op jit(solution)/shard_map/pallas_call | solution.py:324
  (1 shorter events, 0.0 us)
Async XLA Ops:
  0.0 42.9 %copy-start = (bf16[128,128]{1,0:T(8,128)(2,1)S(1)}, bf16[128,128]{1,0:T(8,128)(2,1)}, u32[]{:S(2)}) copy-start(bf16[128,128]{1,0:T(8,128)(2,1)} %param.16) | copy-start | bytes 98308
  5.1 29.6 %copy-start.1 = (bf16[64,2048]{1,0:T(8,128)(2,1)S(1)}, bf16[64,2048]{1,0:T(8,128)(2,1)}, u32[]{:S(2)}) copy-start(bf16[64,2048]{1,0:T(8,128)(2,1)} %get-tuple-element.32.refs_3_) | copy-start | bytes 786436
  5.1 9.8 %collective-permute-start = (bf16[32,2048]{1,0:T(8,128)(2,1)}, bf16[32,2048]{1,0:T(8,128)(2,1)S(1)}, u32[]{:S(2)}, u32[]{:S(2)}) collective-permute-start(bf16[32,2048]{1,0:T(8,128)(2,1)} %get-tuple-element.26), channel_id=1, source_target_pairs={{0,12},{2,14},{4,8},{6,10},{8,4},{10,6},{12,0},{14,2},{1,13},{3,15... | collective-permute-start | bytes 393224 | tf_op jit(solution)/shard_map/ppermute | solution.py:340
  10.3 11.2 %collective-permute-start.1 = (bf16[32,2048]{1,0:T(8,128)(2,1)}, bf16[32,2048]{1,0:T(8,128)(2,1)S(1)}, u32[]{:S(2)}, u32[]{:S(2)}) collective-permute-start(bf16[32,2048]{1,0:T(8,128)(2,1)} %get-tuple-element.27), channel_id=1, source_target_pairs={{0,14},{2,12},{4,10},{6,8},{8,6},{10,4},{12,2},{14,0},{1,15},{3,13... | collective-permute-start | bytes 393224 | tf_op jit(solution)/shard_map/ppermute | solution.py:340
  11.4 21.6 %collective-permute-start.3 = (bf16[64,2048]{1,0:T(8,128)(2,1)}, bf16[64,2048]{1,0:T(8,128)(2,1)S(1)}, u32[]{:S(2)}, u32[]{:S(2)}) collective-permute-start(bf16[64,2048]{1,0:T(8,128)(2,1)} %get-tuple-element.33), channel_id=1, source_target_pairs={{0,2},{2,0},{4,6},{6,4},{8,10},{10,8},{12,14},{14,12},{1,3},{3,1},... | collective-permute-start | bytes 786440 | tf_op jit(solution)/shard_map/ppermute | solution.py:340
  11.8 21.2 %collective-permute-start.4 = (bf16[64,2048]{1,0:T(8,128)(2,1)}, bf16[64,2048]{1,0:T(8,128)(2,1)S(1)}, u32[]{:S(2)}, u32[]{:S(2)}) collective-permute-start(bf16[64,2048]{1,0:T(8,128)(2,1)} %get-tuple-element.34), channel_id=1, source_target_pairs={{0,4},{2,6},{4,0},{6,2},{8,12},{10,14},{12,8},{14,10},{1,5},{3,7},... | collective-permute-start | bytes 786440 | tf_op jit(solution)/shard_map/ppermute | solution.py:340
  11.8 22.9 %collective-permute-start.5 = (bf16[64,2048]{1,0:T(8,128)(2,1)}, bf16[64,2048]{1,0:T(8,128)(2,1)S(1)}, u32[]{:S(2)}, u32[]{:S(2)}) collective-permute-start(bf16[64,2048]{1,0:T(8,128)(2,1)} %get-tuple-element.35), channel_id=1, source_target_pairs={{0,6},{2,4},{4,2},{6,0},{8,14},{10,12},{12,10},{14,8},{1,7},{3,5},... | collective-permute-start | bytes 786440 | tf_op jit(solution)/shard_map/ppermute | solution.py:340
  14.9 16.4 %collective-permute-start.2 = (bf16[32,2048]{1,0:T(8,128)(2,1)}, bf16[32,2048]{1,0:T(8,128)(2,1)S(1)}, u32[]{:S(2)}, u32[]{:S(2)}) collective-permute-start(bf16[32,2048]{1,0:T(8,128)(2,1)} %get-tuple-element.28), channel_id=1, source_target_pairs={{0,8},{2,10},{4,12},{6,14},{8,0},{10,2},{12,4},{14,6},{1,9},{3,11}... | collective-permute-start | bytes 393224 | tf_op jit(solution)/shard_map/ppermute | solution.py:340
  21.5 11.6 %collective-permute-start.6 = (bf16[32,2048]{1,0:T(8,128)(2,1)}, bf16[32,2048]{1,0:T(8,128)(2,1)S(1)}, u32[]{:S(2)}, u32[]{:S(2)}) collective-permute-start(bf16[32,2048]{1,0:T(8,128)(2,1)} %get-tuple-element.36), channel_id=1, source_target_pairs={{0,10},{2,8},{4,14},{6,12},{8,2},{10,0},{12,6},{14,4},{1,11},{3,9}... | collective-permute-start | bytes 393224 | tf_op jit(solution)/shard_map/ppermute | solution.py:340
  37.5 1.6 %collective-permute-start.8 = (bf16[2,32,2048]{2,1,0:T(8,128)(2,1)S(1)}, bf16[2,32,2048]{2,1,0:T(8,128)(2,1)S(1)}, u32[]{:S(2)}, u32[]{:S(2)}) collective-permute-start(bf16[2,32,2048]{2,1,0:T(8,128)(2,1)S(1)} %get-tuple-element.41), channel_id=1, source_target_pairs={{0,1},{1,0},{2,3},{3,2},{4,5},{5,4},{6,7},{7,6},{8,9},{9,8},{10,11... | collective-permute-start | bytes 786440 | tf_op jit(solution)/shard_map/ppermute | solution.py:364
  37.6 4.1 %collective-permute-start.7 = (bf16[2,32,2048]{2,1,0:T(8,128)(2,1)S(1)}, bf16[2,32,2048]{2,1,0:T(8,128)(2,1)S(1)}, u32[]{:S(2)}, u32[]{:S(2)}) collective-permute-start(bf16[2,32,2048]{2,1,0:T(8,128)(2,1)S(1)} %get-tuple-element.38), channel_id=1, source_target_pairs={{0,1},{1,0},{2,3},{3,2},{4,5},{5,4},{6,7},{7,6},{8,9},{9,8},{10,11... | collective-permute-start | bytes 786440 | tf_op jit(solution)/shard_map/ppermute | solution.py:364
  39.1 3.8 %copy-start.4 = (bf16[128,2048]{1,0:T(8,128)(2,1)S(1)}, bf16[128,2048]{1,0:T(8,128)(2,1)}, u32[]{:S(2)}) copy-start(bf16[128,2048]{1,0:T(8,128)(2,1)} %get-tuple-element.25) | copy-start | bytes 1572868
  39.2 6.4 %collective-permute-start.10 = (bf16[32,2048]{1,0:T(8,128)(2,1)S(1)}, bf16[32,2048]{1,0:T(8,128)(2,1)S(1)}, u32[]{:S(2)}, u32[]{:S(2)}) collective-permute-start(bf16[32,2048]{1,0:T(8,128)(2,1)S(1)} %get-tuple-element.43), channel_id=1, source_target_pairs={{0,4},{2,6},{4,0},{6,2},{8,12},{10,14},{12,8},{14,10},{1,5},{3,7},... | collective-permute-start | bytes 393224 | tf_op jit(solution)/shard_map/ppermute | solution.py:340
  40.1 8.1 %collective-permute-start.9 = (bf16[32,2048]{1,0:T(8,128)(2,1)S(1)}, bf16[32,2048]{1,0:T(8,128)(2,1)S(1)}, u32[]{:S(2)}, u32[]{:S(2)}) collective-permute-start(bf16[32,2048]{1,0:T(8,128)(2,1)S(1)} %get-tuple-element.42), channel_id=1, source_target_pairs={{0,2},{2,0},{4,6},{6,4},{8,10},{10,8},{12,14},{14,12},{1,3},{3,1},... | collective-permute-start | bytes 393224 | tf_op jit(solution)/shard_map/ppermute | solution.py:340
  41.8 6.4 %collective-permute-start.11 = (bf16[32,2048]{1,0:T(8,128)(2,1)S(1)}, bf16[32,2048]{1,0:T(8,128)(2,1)S(1)}, u32[]{:S(2)}, u32[]{:S(2)}) collective-permute-start(bf16[32,2048]{1,0:T(8,128)(2,1)S(1)} %get-tuple-element.44), channel_id=1, source_target_pairs={{0,6},{2,4},{4,2},{6,0},{8,14},{10,12},{12,10},{14,8},{1,7},{3,5},... | collective-permute-start | bytes 393224 | tf_op jit(solution)/shard_map/ppermute | solution.py:340
  42.9 0.8 %copy-start.2 = (bf16[128,128]{1,0:T(8,128)(2,1)S(1)}, bf16[128,128]{1,0:T(8,128)(2,1)}, u32[]{:S(2)}) copy-start(bf16[128,128]{1,0:T(8,128)(2,1)} %param.17) | copy-start | bytes 98308
  43.6 0.7 %copy-start.3 = (f32[128]{0:T(128)S(1)}, f32[128]{0:T(128)}, u32[]{:S(2)}) copy-start(f32[128]{0:T(128)} %param.13) | copy-start | bytes 1540

commit v12 on v11

--- a/solution.py
+++ b/solution.py
@@ -113,7 +113,7 @@
 def make_edges(pair, lens, resolved, gain, w_left, w_right, groups, rows, cols):
     count, channels = pair.shape
     own = w_left.shape[1] // 2 // groups
-    block = 256
+    block = 1024
     flat = ceil_to(count, block)
     chunks = [(at, min(block, count - at)) for at in range(0, count, block)]
     here = pl.BlockSpec(memory_space=pltpu.HBM)
@@ -318,7 +318,7 @@
     groups = len(prods)
     ch = prods[0].shape[0]
     count, channels = gate.shape
-    block = 256
+    block = 512
     chunks = [(at, min(block, count - at)) for at in range(0, count, block)]
     whole = pl.BlockSpec(memory_space=pltpu.VMEM)
     return pl.pallas_call(

time: 49.7 us -> 48.1 us (0.968)
  Pallas kernels: 9.62 us -> 8.03 us
    pallas_call x1, Pallas kernels: 5.11 us -> 3.52 us  [make_edges(): pl.pallas_call(functools.partial(edges_kernel, groups, rows, cols, chunks...]
where the time goes in v12:
time: 48.1 us; the launch traced here: 47.9 us
  starting transfers between devices  24.2 us (50%)
  waiting for transfers between devices  14 us (29%)
  Pallas kernels  8.03 us (17%)
  local copies, waits for them, and re-layouts  1.06 us (2%)
    ppermute x10, starting transfers between devices, swap(): lax.ppermute(value, 'row', [(r, r ^ shift) for r in range(lax.axis_size('...  23.6 us
    ppermute x10, waiting for transfers between devices, swap(): lax.ppermute(value, 'row', [(r, r ^ shift) for r in range(lax.axis_size('...  13 us
    pallas_call x1, Pallas kernels, make_edges(): pl.pallas_call(functools.partial(edges_kernel, groups, rows, cols, chunks...  3.52 us
    pallas_call x1, Pallas kernels, make_products(): pl.pallas_call(functools.partial(products_kernel, groups, rows, cols, par...  2.81 us
    pallas_call x1, Pallas kernels, make_update(): pl.pallas_call(functools.partial(update_kernel, groups, rows, cols, chunk...  1.29 us
    ppermute x2, waiting for transfers between devices, shards(): other = lax.ppermute(made[2 + part], 'col', [(0, 1), (1, 0)])  1.03 us
  transfers between devices with their start and end apart: 12, of which 6 were waited for; matrix products, arithmetic and copies ran while one was open for 1% of the time, Pallas kernels for 1%

profile of v12, /device:TPU:0, one launch (start us, length us, event | category | flops | bytes accessed | tf_op | source)
XLA Modules:
  0.0 47.9 jit_solution(16607557027127758646)
XLA Ops:
  0.0 0.0 copy-start
  0.0 3.5 %shard_map.91 = (bf16[128,2048]{1,0:T(8,128)(2,1)}, bf16[64,2048]{1,0:T(8,128)(2,1)}, bf16[64,2048]{1,0:T(8,128)(2,1)}, bf16[64,2048]{1,0:T(8,128)(2,1)}, bf16[6...) custom-call(bf16[1936,128]{1,0:T(8,128)(2,1)} %bitcast.5, ...), custom_call_target="tpu_custom_call" | custom-call | tf_op jit(solution)/shard_map/pallas_call | solution.py:120
  3.5 0.0 copy-start.1
  3.5 5.1 %collective-permute-start = (bf16[32,2048]{1,0:T(8,128)(2,1)}, bf16[32,2048]{1,0:T(8,128)(2,1)S(1)}, u32[]{:S(2)}, u32[]{:S(2)}) collective-permute-start(bf16[32,2048]{1,0:T(8,128)(2,1)} %get-tuple-element.26), channel_id=1, source_target_pairs={{0,12},{2,14},{4,8},{6,10},{8,4},{10,6},{12,0},{14,2},{1,13},{3,15... | collective-permute-start | bytes 393224 | tf_op jit(solution)/shard_map/ppermute | solution.py:340
  8.7 1.2 %collective-permute-start.1 = (bf16[32,2048]{1,0:T(8,128)(2,1)}, bf16[32,2048]{1,0:T(8,128)(2,1)S(1)}, u32[]{:S(2)}, u32[]{:S(2)}) collective-permute-start(bf16[32,2048]{1,0:T(8,128)(2,1)} %get-tuple-element.27), channel_id=1, source_target_pairs={{0,14},{2,12},{4,10},{6,8},{8,6},{10,4},{12,2},{14,0},{1,15},{3,13... | collective-permute-start | bytes 393224 | tf_op jit(solution)/shard_map/ppermute | solution.py:340
  9.8 0.4 collective-permute-start.3
  10.2 0.0 collective-permute-start.4
  10.2 3.1 %collective-permute-start.5 = (bf16[64,2048]{1,0:T(8,128)(2,1)}, bf16[64,2048]{1,0:T(8,128)(2,1)S(1)}, u32[]{:S(2)}, u32[]{:S(2)}) collective-permute-start(bf16[64,2048]{1,0:T(8,128)(2,1)} %get-tuple-element.35), channel_id=1, source_target_pairs={{0,6},{2,4},{4,2},{6,0},{8,14},{10,12},{12,10},{14,8},{1,7},{3,5},... | collective-permute-start | bytes 786440 | tf_op jit(solution)/shard_map/ppermute | solution.py:340
  13.3 0.0 collective-permute-done.refs_0_
  13.3 6.5 %collective-permute-start.2 = (bf16[32,2048]{1,0:T(8,128)(2,1)}, bf16[32,2048]{1,0:T(8,128)(2,1)S(1)}, u32[]{:S(2)}, u32[]{:S(2)}) collective-permute-start(bf16[32,2048]{1,0:T(8,128)(2,1)} %get-tuple-element.28), channel_id=1, source_target_pairs={{0,8},{2,10},{4,12},{6,14},{8,0},{10,2},{12,4},{14,6},{1,9},{3,11}... | collective-permute-start | bytes 393224 | tf_op jit(solution)/shard_map/ppermute | solution.py:340
  19.9 0.0 collective-permute-done.1.refs_1_
  19.9 3.7 %collective-permute-start.6 = (bf16[32,2048]{1,0:T(8,128)(2,1)}, bf16[32,2048]{1,0:T(8,128)(2,1)S(1)}, u32[]{:S(2)}, u32[]{:S(2)}) collective-permute-start(bf16[32,2048]{1,0:T(8,128)(2,1)} %get-tuple-element.36), channel_id=1, source_target_pairs={{0,10},{2,8},{4,14},{6,12},{8,2},{10,0},{12,6},{14,4},{1,11},{3,9}... | collective-permute-start | bytes 393224 | tf_op jit(solution)/shard_map/ppermute | solution.py:340
  23.6 6.2 %collective-permute-done.2.refs_2_ = bf16[32,2048]{1,0:T(8,128)(2,1)S(1)} collective-permute-done((bf16[32,2048]{1,0:T(8,128)(2,1)}, bf16[32,2048]{1,0:T(8,128)(2,1)S(1)}, u32[]{:S(2)}, u32[]{:S(2)}) %collective-permute-start.2) | collective-permute-done | bytes 131104 | tf_op jit(solution)/shard_map/ppermute | solution.py:340
  29.7 0.3 shard_map.92
  30.0 1.4 %collective-permute-done.6.refs_7_ = bf16[32,2048]{1,0:T(8,128)(2,1)S(1)} collective-permute-done((bf16[32,2048]{1,0:T(8,128)(2,1)}, bf16[32,2048]{1,0:T(8,128)(2,1)S(1)}, u32[]{:S(2)}, u32[]{:S(2)}) %collective-permute-start.6) | collective-permute-done | bytes 131104 | tf_op jit(solution)/shard_map/ppermute | solution.py:340
  31.4 0.0 collective-permute-done.3.refs_4_
  31.4 0.0 collective-permute-done.4.refs_5_
  31.4 1.6 %collective-permute-done.5.refs_6_ = bf16[64,2048]{1,0:T(8,128)(2,1)S(1)} collective-permute-done((bf16[64,2048]{1,0:T(8,128)(2,1)}, bf16[64,2048]{1,0:T(8,128)(2,1)S(1)}, u32[]{:S(2)}, u32[]{:S(2)}) %collective-permute-start.5) | collective-permute-done | bytes 262176 | tf_op jit(solution)/shard_map/ppermute | solution.py:340
  33.1 0.0 copy-done.1
  33.1 2.8 %shard_map.93 = (bf16[2,32,2048]{2,1,0:T(8,128)(2,1)S(1)}, bf16[2,32,2048]{2,1,0:T(8,128)(2,1)S(1)}, bf16[2,32,2048]{2,1,0:T(8,128)(2,1)S(1)}, bf16[2,32,2048]{2,1,0:T(8,128)(2,1)S(1)}) custom-call(f32[1,880,128]{2,1,0:T(8,128)S(1)} %get-tuple-element.29.refs_0_, f32[1,880,128]{2,1,0:T(8,128)S(1)} %get-tuple-element.30.refs_1_, ...), custom_call_target="tpu_custom_call" | custom-call | flops 100000 | bytes 10000000 | tf_op jit(solution)/shard_map/pallas_call | solution.py:261
  35.9 0.1 collective-permute-start.8
  36.0 0.5 %collective-permute-start.7 = (bf16[2,32,2048]{2,1,0:T(8,128)(2,1)S(1)}, bf16[2,32,2048]{2,1,0:T(8,128)(2,1)S(1)}, u32[]{:S(2)}, u32[]{:S(2)}) collective-permute-start(bf16[2,32,2048]{2,1,0:T(8,128)(2,1)S(1)} %get-tuple-element.38), channel_id=1, source_target_pairs={{0,1},{1,0},{2,3},{3,2},{4,5},{5,4},{6,7},{7,6},{8,9},{9,8},{10,11... | collective-permute-start | bytes 786440 | tf_op jit(solution)/shard_map/ppermute | solution.py:364
  36.5 1.0 %collective-permute-done.8.b_ref = bf16[2,32,2048]{2,1,0:T(8,128)(2,1)S(1)} collective-permute-done((bf16[2,32,2048]{2,1,0:T(8,128)(2,1)S(1)}, bf16[2,32,2048]{2,1,0:T(8,128)(2,1)S(1)}, u32[]{:S(2)}, u32[]{:S(2)}) %collective-permute-start.8) | collective-permute-done | bytes 262176 | tf_op jit(solution)/shard_map/ppermute | solution.py:364
  37.5 0.0 copy-start.4
  37.5 0.1 shard_map.95
  37.6 0.9 %collective-permute-start.10 = (bf16[32,2048]{1,0:T(8,128)(2,1)S(1)}, bf16[32,2048]{1,0:T(8,128)(2,1)S(1)}, u32[]{:S(2)}, u32[]{:S(2)}) collective-permute-start(bf16[32,2048]{1,0:T(8,128)(2,1)S(1)} %get-tuple-element.43), channel_id=1, source_target_pairs={{0,4},{2,6},{4,0},{6,2},{8,12},{10,14},{12,8},{14,10},{1,5},{3,7},... | collective-permute-start | bytes 393224 | tf_op jit(solution)/shard_map/ppermute | solution.py:340
  38.5 1.6 %collective-permute-start.9 = (bf16[32,2048]{1,0:T(8,128)(2,1)S(1)}, bf16[32,2048]{1,0:T(8,128)(2,1)S(1)}, u32[]{:S(2)}, u32[]{:S(2)}) collective-permute-start(bf16[32,2048]{1,0:T(8,128)(2,1)S(1)} %get-tuple-element.42), channel_id=1, source_target_pairs={{0,2},{2,0},{4,6},{6,4},{8,10},{10,8},{12,14},{14,12},{1,3},{3,1},... | collective-permute-start | bytes 393224 | tf_op jit(solution)/shard_map/ppermute | solution.py:340
  40.1 0.0 collective-permute-done.7.b_ref
  40.1 0.1 shard_map.94
  40.2 1.1 %collective-permute-start.11 = (bf16[32,2048]{1,0:T(8,128)(2,1)S(1)}, bf16[32,2048]{1,0:T(8,128)(2,1)S(1)}, u32[]{:S(2)}, u32[]{:S(2)}) collective-permute-start(bf16[32,2048]{1,0:T(8,128)(2,1)S(1)} %get-tuple-element.44), channel_id=1, source_target_pairs={{0,6},{2,4},{4,2},{6,0},{8,14},{10,12},{12,10},{14,8},{1,7},{3,5},... | collective-permute-start | bytes 393224 | tf_op jit(solution)/shard_map/ppermute | solution.py:340
  41.3 0.0 copy-done
  41.3 0.0 copy-done.4
  41.3 0.0 copy-start.2
  41.3 0.5 fusion.2.gate_ref
  41.8 0.3 copy-done.2
  42.0 0.0 copy-start.3
  42.0 0.7 %copy-done.3 = f32[128]{0:T(128)S(1)} copy-done((f32[128]{0:T(128)S(1)}, f32[128]{0:T(128)}, u32[]{:S(2)}) %copy-start.3) | copy-done | bytes 536
  42.7 0.1 copy.10.gain_ref
  42.8 1.2 %collective-permute-done.10.refs_2_ = bf16[32,2048]{1,0:T(8,128)(2,1)S(1)} collective-permute-done((bf16[32,2048]{1,0:T(8,128)(2,1)S(1)}, bf16[32,2048]{1,0:T(8,128)(2,1)S(1)}, u32[]{:S(2)}, u32[]{:S(2)}) %collective-permute-start.10) | collective-permute-done | bytes 131104 | tf_op jit(solution)/shard_map/ppermute | solution.py:340
  44.0 2.6 %collective-permute-done.9.refs_1_ = bf16[32,2048]{1,0:T(8,128)(2,1)S(1)} collective-permute-done((bf16[32,2048]{1,0:T(8,128)(2,1)S(1)}, bf16[32,2048]{1,0:T(8,128)(2,1)S(1)}, u32[]{:S(2)}, u32[]{:S(2)}) %collective-permute-start.9) | collective-permute-done | bytes 131104 | tf_op jit(solution)/shard_map/ppermute | solution.py:340
  46.6 0.0 collective-permute-done.11.refs_3_
  46.6 1.3 %shard_map.96 = bf16[1936,128]{1,0:T(8,128)(2,1)} custom-call(f32[128,1]{1,0:T(8,128)S(1)} %copy.10.gain_ref, f32[128,128]{1,0:T(8,128)S(1)} %convert_element_type.3.w_ref, f32[1936,128]{1,0:T(8,128)S(1)} %fusion.2.gate_ref, bf16[32,2048]{1,0:T(8,128)(2,1)S(1)} %get-tuple-element.39.refs_0_, bf16[32,2048]{1,0:T(8,128)(2,1)S(1)} %collective-permute-done.9.refs_1_, ...), custom_call_target="tpu_custom_call" | custom-call | tf_op jit(solution)/shard_map/pallas_call | solution.py:324
  (1 shorter events, 0.0 us)
Async XLA Ops:
  0.0 41.3 %copy-start = (bf16[128,128]{1,0:T(8,128)(2,1)S(1)}, bf16[128,128]{1,0:T(8,128)(2,1)}, u32[]{:S(2)}) copy-start(bf16[128,128]{1,0:T(8,128)(2,1)} %param.16) | copy-start | bytes 98308
  3.5 29.6 %copy-start.1 = (bf16[64,2048]{1,0:T(8,128)(2,1)S(1)}, bf16[64,2048]{1,0:T(8,128)(2,1)}, u32[]{:S(2)}) copy-start(bf16[64,2048]{1,0:T(8,128)(2,1)} %get-tuple-element.32.refs_3_) | copy-start | bytes 786436
  3.5 9.8 %collective-permute-start = (bf16[32,2048]{1,0:T(8,128)(2,1)}, bf16[32,2048]{1,0:T(8,128)(2,1)S(1)}, u32[]{:S(2)}, u32[]{:S(2)}) collective-permute-start(bf16[32,2048]{1,0:T(8,128)(2,1)} %get-tuple-element.26), channel_id=1, source_target_pairs={{0,12},{2,14},{4,8},{6,10},{8,4},{10,6},{12,0},{14,2},{1,13},{3,15... | collective-permute-start | bytes 393224 | tf_op jit(solution)/shard_map/ppermute | solution.py:340
  8.7 11.2 %collective-permute-start.1 = (bf16[32,2048]{1,0:T(8,128)(2,1)}, bf16[32,2048]{1,0:T(8,128)(2,1)S(1)}, u32[]{:S(2)}, u32[]{:S(2)}) collective-permute-start(bf16[32,2048]{1,0:T(8,128)(2,1)} %get-tuple-element.27), channel_id=1, source_target_pairs={{0,14},{2,12},{4,10},{6,8},{8,6},{10,4},{12,2},{14,0},{1,15},{3,13... | collective-permute-start | bytes 393224 | tf_op jit(solution)/shard_map/ppermute | solution.py:340
  9.8 21.6 %collective-permute-start.3 = (bf16[64,2048]{1,0:T(8,128)(2,1)}, bf16[64,2048]{1,0:T(8,128)(2,1)S(1)}, u32[]{:S(2)}, u32[]{:S(2)}) collective-permute-start(bf16[64,2048]{1,0:T(8,128)(2,1)} %get-tuple-element.33), channel_id=1, source_target_pairs={{0,2},{2,0},{4,6},{6,4},{8,10},{10,8},{12,14},{14,12},{1,3},{3,1},... | collective-permute-start | bytes 786440 | tf_op jit(solution)/shard_map/ppermute | solution.py:340
  10.2 21.2 %collective-permute-start.4 = (bf16[64,2048]{1,0:T(8,128)(2,1)}, bf16[64,2048]{1,0:T(8,128)(2,1)S(1)}, u32[]{:S(2)}, u32[]{:S(2)}) collective-permute-start(bf16[64,2048]{1,0:T(8,128)(2,1)} %get-tuple-element.34), channel_id=1, source_target_pairs={{0,4},{2,6},{4,0},{6,2},{8,12},{10,14},{12,8},{14,10},{1,5},{3,7},... | collective-permute-start | bytes 786440 | tf_op jit(solution)/shard_map/ppermute | solution.py:340
  10.2 22.9 %collective-permute-start.5 = (bf16[64,2048]{1,0:T(8,128)(2,1)}, bf16[64,2048]{1,0:T(8,128)(2,1)S(1)}, u32[]{:S(2)}, u32[]{:S(2)}) collective-permute-start(bf16[64,2048]{1,0:T(8,128)(2,1)} %get-tuple-element.35), channel_id=1, source_target_pairs={{0,6},{2,4},{4,2},{6,0},{8,14},{10,12},{12,10},{14,8},{1,7},{3,5},... | collective-permute-start | bytes 786440 | tf_op jit(solution)/shard_map/ppermute | solution.py:340
  13.3 16.4 %collective-permute-start.2 = (bf16[32,2048]{1,0:T(8,128)(2,1)}, bf16[32,2048]{1,0:T(8,128)(2,1)S(1)}, u32[]{:S(2)}, u32[]{:S(2)}) collective-permute-start(bf16[32,2048]{1,0:T(8,128)(2,1)} %get-tuple-element.28), channel_id=1, source_target_pairs={{0,8},{2,10},{4,12},{6,14},{8,0},{10,2},{12,4},{14,6},{1,9},{3,11}... | collective-permute-start | bytes 393224 | tf_op jit(solution)/shard_map/ppermute | solution.py:340
  19.9 11.6 %collective-permute-start.6 = (bf16[32,2048]{1,0:T(8,128)(2,1)}, bf16[32,2048]{1,0:T(8,128)(2,1)S(1)}, u32[]{:S(2)}, u32[]{:S(2)}) collective-permute-start(bf16[32,2048]{1,0:T(8,128)(2,1)} %get-tuple-element.36), channel_id=1, source_target_pairs={{0,10},{2,8},{4,14},{6,12},{8,2},{10,0},{12,6},{14,4},{1,11},{3,9}... | collective-permute-start | bytes 393224 | tf_op jit(solution)/shard_map/ppermute | solution.py:340
  35.9 1.6 %collective-permute-start.8 = (bf16[2,32,2048]{2,1,0:T(8,128)(2,1)S(1)}, bf16[2,32,2048]{2,1,0:T(8,128)(2,1)S(1)}, u32[]{:S(2)}, u32[]{:S(2)}) collective-permute-start(bf16[2,32,2048]{2,1,0:T(8,128)(2,1)S(1)} %get-tuple-element.41), channel_id=1, source_target_pairs={{0,1},{1,0},{2,3},{3,2},{4,5},{5,4},{6,7},{7,6},{8,9},{9,8},{10,11... | collective-permute-start | bytes 786440 | tf_op jit(solution)/shard_map/ppermute | solution.py:364
  36.0 4.1 %collective-permute-start.7 = (bf16[2,32,2048]{2,1,0:T(8,128)(2,1)S(1)}, bf16[2,32,2048]{2,1,0:T(8,128)(2,1)S(1)}, u32[]{:S(2)}, u32[]{:S(2)}) collective-permute-start(bf16[2,32,2048]{2,1,0:T(8,128)(2,1)S(1)} %get-tuple-element.38), channel_id=1, source_target_pairs={{0,1},{1,0},{2,3},{3,2},{4,5},{5,4},{6,7},{7,6},{8,9},{9,8},{10,11... | collective-permute-start | bytes 786440 | tf_op jit(solution)/shard_map/ppermute | solution.py:364
  37.5 3.8 %copy-start.4 = (bf16[128,2048]{1,0:T(8,128)(2,1)S(1)}, bf16[128,2048]{1,0:T(8,128)(2,1)}, u32[]{:S(2)}) copy-start(bf16[128,2048]{1,0:T(8,128)(2,1)} %get-tuple-element.25) | copy-start | bytes 1572868
  37.6 6.4 %collective-permute-start.10 = (bf16[32,2048]{1,0:T(8,128)(2,1)S(1)}, bf16[32,2048]{1,0:T(8,128)(2,1)S(1)}, u32[]{:S(2)}, u32[]{:S(2)}) collective-permute-start(bf16[32,2048]{1,0:T(8,128)(2,1)S(1)} %get-tuple-element.43), channel_id=1, source_target_pairs={{0,4},{2,6},{4,0},{6,2},{8,12},{10,14},{12,8},{14,10},{1,5},{3,7},... | collective-permute-start | bytes 393224 | tf_op jit(solution)/shard_map/ppermute | solution.py:340
  38.5 8.1 %collective-permute-start.9 = (bf16[32,2048]{1,0:T(8,128)(2,1)S(1)}, bf16[32,2048]{1,0:T(8,128)(2,1)S(1)}, u32[]{:S(2)}, u32[]{:S(2)}) collective-permute-start(bf16[32,2048]{1,0:T(8,128)(2,1)S(1)} %get-tuple-element.42), channel_id=1, source_target_pairs={{0,2},{2,0},{4,6},{6,4},{8,10},{10,8},{12,14},{14,12},{1,3},{3,1},... | collective-permute-start | bytes 393224 | tf_op jit(solution)/shard_map/ppermute | solution.py:340
  40.2 6.4 %collective-permute-start.11 = (bf16[32,2048]{1,0:T(8,128)(2,1)S(1)}, bf16[32,2048]{1,0:T(8,128)(2,1)S(1)}, u32[]{:S(2)}, u32[]{:S(2)}) collective-permute-start(bf16[32,2048]{1,0:T(8,128)(2,1)S(1)} %get-tuple-element.44), channel_id=1, source_target_pairs={{0,6},{2,4},{4,2},{6,0},{8,14},{10,12},{12,10},{14,8},{1,7},{3,5},... | collective-permute-start | bytes 393224 | tf_op jit(solution)/shard_map/ppermute | solution.py:340
  41.3 0.8 %copy-start.2 = (bf16[128,128]{1,0:T(8,128)(2,1)S(1)}, bf16[128,128]{1,0:T(8,128)(2,1)}, u32[]{:S(2)}) copy-start(bf16[128,128]{1,0:T(8,128)(2,1)} %param.17) | copy-start | bytes 98308
  42.0 0.7 %copy-start.3 = (f32[128]{0:T(128)S(1)}, f32[128]{0:T(128)}, u32[]{:S(2)}) copy-start(f32[128]{0:T(128)} %param.13) | copy-start | bytes 1540

commit v13 on v12

--- a/solution.py
+++ b/solution.py
@@ -10,6 +10,7 @@
 EPS = 1e-05
 LANES = 128
 VMEM_LIMIT = 32 * 1024 * 1024
+STRIP = 16
 VMEM_FIRST = 60 * 1024 * 1024
 
 
@@ -53,12 +54,12 @@
     projected = jnp.dot(weights, normed, preferred_element_type=jnp.float32)
     edge = sigmoid(projected[:hidden]) * projected[hidden:]
     edge = edge.reshape(hidden // 8, 8, block) * mask[None]
-    return edge.reshape(groups, hidden // groups, block).astype(jnp.bfloat16)
+    return edge.reshape(groups, hidden // groups, block)
 
 
 def edges_kernel(groups, rows, cols, chunks, pair_ref, gain_ref, wl_ref, wr_ref, lens_ref, res_ref, normed_ref, *refs):
     both_refs, right_refs = refs[:groups], refs[groups:2 * groups]
-    x_s, gain_s, wl_s, wr_s, lens_s, res_s, normed_s, held, in_sems, out_sems = refs[2 * groups:]
+    x_s, gain_s, wl_s, wr_s, lens_s, res_s, normed_s, both_s, right_s, in_sems, out_sems = refs[2 * groups:]
     count = rows * cols
     first_row, first_col, mine, _, _ = place_of(groups, rows, cols)
     own = wl_ref.shape[1] // 2 // groups
@@ -75,6 +76,7 @@
     for copy in pieces[:1] + loads + pieces[1:]:
         copy.start()
     block = chunks[0][1]
+    whole, over = tiles_of(rows, cols)
     channels = x_s.shape[1]
     spare = x_s.shape[0] - count
     if spare:
@@ -95,13 +97,28 @@
         mask = mask_of(cols, first_row, first_col, lens_s, res_s, at, block)
         lanes = pl.ds(at, block)
         normed_s[:, lanes] = normed
-        held[:, own:, lanes] = edge_of(right_w, normed, mask, groups)
-        held[:, :own, lanes] = edge_of(left_w, normed, mask, groups)
+        right = edge_of(right_w, normed, mask, groups)
+        left = edge_of(left_w, normed, mask, groups)
+        begin, end = at // LANES, min((at + block) // LANES, whole)
+        for t in range(begin, end):
+            here = slice(t * LANES - at, (t + 1) * LANES - at)
+            both_s[:, 2 * own * t:2 * own * t + own] = left[:, :, here].astype(jnp.bfloat16)
+            both_s[:, 2 * own * t + own:2 * own * (t + 1)] = right[:, :, here].astype(jnp.bfloat16)
+            right_s[:, own * t:own * (t + 1)] = right[:, :, here].astype(jnp.bfloat16)
+        strip = STRIP if end == whole else 0
+        if strip and over:
+            here = slice(whole * LANES - at, (whole + 1) * LANES - at)
+            for g in range(groups):
+                pair = jnp.concatenate([left[g, :, here], right[g, :, here]], axis=0)
+                both_s[g, 2 * own * whole:2 * own * whole + 8] = strip_of(pair, over).astype(jnp.bfloat16)
+                right_s[g, own * whole:own * whole + 8] = strip_of(right[g, :, here], over).astype(jnp.bfloat16)
+        both_rows = pl.ds(2 * own * begin, 2 * own * (end - begin) + strip)
+        right_rows = pl.ds(own * begin, own * (end - begin) + strip)
         sent = []
         for u in range(groups):
             group = jnp.bitwise_xor(mine, u)
-            sent.append((held.at[group, pl.ds(own, own), lanes], right_refs[u].at[:, lanes]))
-            sent.append((held.at[group, :, lanes], both_refs[u].at[:, lanes]))
+            sent.append((right_s.at[group, right_rows], right_refs[u].at[right_rows]))
+            sent.append((both_s.at[group, both_rows], both_refs[u].at[both_rows]))
         sent.append((normed_s.at[:, lanes], normed_ref.at[:, lanes]))
         for m, (src, dst) in enumerate(sent):
             stores.append(pltpu.make_async_copy(src, dst, out_sems.at[n, m]))
@@ -122,8 +139,8 @@
         in_specs=[here] * 6,
         out_specs=[here] * (1 + 2 * groups),
         out_shape=[jax.ShapeDtypeStruct((channels, flat), jnp.bfloat16)]
-        + [jax.ShapeDtypeStruct((2 * own, flat), jnp.bfloat16)] * groups
-        + [jax.ShapeDtypeStruct((own, flat), jnp.bfloat16)] * groups,
+        + [jax.ShapeDtypeStruct((travel_rows(2 * own, rows, cols), LANES), jnp.bfloat16)] * groups
+        + [jax.ShapeDtypeStruct((travel_rows(own, rows, cols), LANES), jnp.bfloat16)] * groups,
         scratch_shapes=[
             pltpu.VMEM((flat, channels), pair.dtype),
             pltpu.VMEM(gain.shape, gain.dtype),
@@ -132,7 +149,8 @@
             pltpu.SMEM(lens.shape, lens.dtype),
             pltpu.SMEM(resolved.shape, resolved.dtype),
             pltpu.VMEM((channels, flat), jnp.bfloat16),
-            pltpu.VMEM((groups, 2 * own, flat), jnp.bfloat16),
+            pltpu.VMEM((groups, travel_rows(2 * own, rows, cols), LANES), jnp.bfloat16),
+            pltpu.VMEM((groups, travel_rows(own, rows, cols), LANES), jnp.bfloat16),
             pltpu.SemaphoreType.DMA((5 + len(chunks),)),
             pltpu.SemaphoreType.DMA((len(chunks), 1 + 2 * groups)),
         ],
@@ -140,16 +158,47 @@
     )(pair, gain, w_left, w_right, lens, resolved)
 
 
+def tiles_of(rows, cols):
+    return divmod(rows * cols, LANES)
+
+
+def travel_rows(ch, rows, cols):
+    return tiles_of(rows, cols)[0] * ch + STRIP
+
+
+def strip_of(tile, left):
+    lane = lax.broadcasted_iota(jnp.int32, (8, LANES), 1)
+    strip = jnp.zeros((8, LANES), jnp.float32)
+    for g in range(tile.shape[0] // 8):
+        piece = tile[8 * g:8 * g + 8]
+        if g:
+            piece = pltpu.roll(piece, g * left, 1)
+        strip = jnp.where((lane >= g * left) & (lane < (g + 1) * left), piece, strip)
+    return strip
+
+
+def tile_at(ref, t, total, first, ch, rows, cols):
+    whole, left = tiles_of(rows, cols)
+    if t < whole:
+        return ref[t * total + first:t * total + first + ch].astype(jnp.float32)
+    strip = ref[whole * total:whole * total + 8].astype(jnp.float32)
+    pieces = []
+    for g in range(first // 8, (first + ch) // 8):
+        pieces.append(pltpu.roll(strip, LANES - g * left, 1) if g else strip)
+    return jnp.concatenate(pieces, axis=0)
+
+
 def unpack(got_ref, held_refs, block, rows, cols, step):
     tiles = pl.cdiv(cols, LANES)
-    ch = got_ref.shape[0] // len(held_refs)
+    total = (got_ref.shape[0] - STRIP) // tiles_of(rows, cols)[0]
+    ch = total // len(held_refs)
     lane = lax.broadcasted_iota(jnp.int32, (ch, LANES), 1)
     for n, held in enumerate(held_refs):
         seen = {}
 
         def tile_of(t):
             if t not in seen:
-                seen[t] = got_ref[n * ch:(n + 1) * ch, pl.ds(t * LANES, LANES)].astype(jnp.float32)
+                seen[t] = tile_at(got_ref, t, total, n * ch, ch, rows, cols)
             return seen[t]
 
         for i in range(rows):
@@ -200,7 +249,8 @@
     keep_refs, send_refs = refs[2 * groups:2 * groups + 2], refs[2 * groups + 2:2 * groups + 4]
     left_s, right_s, far_s, prod_s = refs[2 * groups + 4:]
     _, _, mine, own_half, col = place_of(groups, rows, cols)
-    ch = keep_refs[0].shape[1]
+    full, over = tiles_of(rows, cols)
+    ch = (keep_refs[0].shape[1] - STRIP) // full
     step = left_s.shape[1] // (groups * rows)
     count = groups * rows
     tiles = left_s.shape[0]
@@ -226,12 +276,14 @@
     for part, pieces in enumerate(parts):
         for n, u in enumerate(pieces):
             block = jnp.bitwise_xor(mine, u)
-            for t in range(keep_refs[part].shape[2] // LANES):
+            for t in range(full + (over > 0)):
                 near = packed_tile(prod_s, 0, t, block, rows, cols, step, ch)
                 far = packed_tile(prod_s, tiles, t, block, rows, cols, step, ch)
-                lanes = pl.ds(t * LANES, LANES)
-                keep_refs[part][n, :, lanes] = jnp.where(near_kept, near, far).astype(jnp.bfloat16)
-                send_refs[part][n, :, lanes] = jnp.where(near_kept, far, near).astype(jnp.bfloat16)
+                if t == full:
+                    near, far = strip_of(near, over), strip_of(far, over)
+                there = pl.ds(t * ch, near.shape[0])
+                keep_refs[part][n, there] = jnp.where(near_kept, near, far).astype(jnp.bfloat16)
+                send_refs[part][n, there] = jnp.where(near_kept, far, near).astype(jnp.bfloat16)
 
 
 def lines_of(blocks, ch, cols):
@@ -239,7 +291,7 @@
 
 
 def make_lines(got, rows, cols):
-    ch = got[0].shape[0]
+    ch = (got[0].shape[0] - STRIP) // tiles_of(rows, cols)[0]
     whole = pl.BlockSpec(memory_space=pltpu.VMEM)
     return pl.pallas_call(
         functools.partial(lines_kernel, rows, cols),
@@ -253,7 +305,7 @@
 
 def make_products(lines, near, far, parts, early, late, rows, cols):
     groups = len(near)
-    ch, flat = near[0].shape[0] // 2, near[0].shape[1]
+    ch = (near[0].shape[0] - STRIP) // tiles_of(rows, cols)[0] // 2
     whole = pl.BlockSpec(memory_space=pltpu.VMEM)
     tiles, held, _ = lines_of(groups * rows, ch, cols)
     one = pltpu.VMEM((tiles, held, LANES), jnp.float32)
@@ -262,7 +314,7 @@
         functools.partial(products_kernel, groups, rows, cols, parts, early, late),
         in_specs=[whole] * (2 * groups),
         out_specs=[whole] * 4,
-        out_shape=[jax.ShapeDtypeStruct((n, ch, flat), jnp.bfloat16) for n in sizes],
+        out_shape=[jax.ShapeDtypeStruct((n, travel_rows(ch, rows, cols), LANES), jnp.bfloat16) for n in sizes],
         scratch_shapes=[one, one, one, pltpu.VMEM((2 * tiles, held, LANES), jnp.float32)],
         compiler_params=pltpu.CompilerParams(vmem_limit_bytes=VMEM_LIMIT),
         cost_estimate=pl.CostEstimate(flops=10 ** 5, bytes_accessed=10 ** 7, transcendentals=0),
@@ -291,7 +343,7 @@
     prod_refs = refs[:groups]
     out_ref, gain_s, w_s, out_s, sems = refs[groups:]
     mine = place_of(groups, rows, cols)[2]
-    ch = prod_refs[0].shape[0]
+    ch = w_ref.shape[0] // groups
     block = chunks[0][1]
     for u in range(groups):
         there = pl.ds(pl.multiple_of(jnp.bitwise_xor(mine, u) * ch, 8), ch)
@@ -300,8 +352,13 @@
     gain, weights = gain_s[...], w_s[...].astype(jnp.bfloat16)
     stores = []
     for n, (at, size) in enumerate(chunks):
-        lanes = pl.ds(at, block)
-        prod = jnp.concatenate([ref[:, lanes].astype(jnp.float32) for ref in prod_refs], axis=0)
+        prod = jnp.concatenate(
+            [
+                jnp.concatenate([tile_at(ref, t, ch, 0, ch, rows, cols) for ref in prod_refs], axis=0)
+                for t in range(at // LANES, pl.cdiv(at + size, LANES))
+            ],
+            axis=1,
+        )
         mean = jnp.mean(prod, axis=0, keepdims=True)
         centred = prod - mean
         variance = jnp.mean(centred * centred, axis=0, keepdims=True)
@@ -316,7 +373,6 @@
 
 def make_update(prods, gain, w_out, gate, rows, cols):
     groups = len(prods)
-    ch = prods[0].shape[0]
     count, channels = gate.shape
     block = 512
     chunks = [(at, min(block, count - at)) for at in range(0, count, block)]

time: 48.1 us -> 47.8 us (level)
  Pallas kernels: 8.03 us -> 8.91 us
  waiting for transfers between devices: 14 us -> 13.2 us
    ppermute x10, waiting for transfers between devices: 13 us -> 12.2 us  [swap(): lax.ppermute(value, 'row', [(r, r ^ shift) for r in range(lax.axis_size('...]
    pallas_call x1, Pallas kernels: 2.81 us -> 3.48 us  [make_products(): pl.pallas_call(functools.partial(products_kernel, groups, rows, cols, par...]
where the time goes in v13:
time: 47.8 us; the launch traced here: 47.6 us
  starting transfers between devices  23.8 us (50%)
  waiting for transfers between devices  13.2 us (28%)
  Pallas kernels  8.91 us (19%)
  local copies, waits for them, and re-layouts  1.06 us (2%)
    ppermute x10, starting transfers between devices, swap(): lax.ppermute(value, 'row', [(r, r ^ shift) for r in range(lax.axis_size('...  23.3 us
    ppermute x10, waiting for transfers between devices, swap(): lax.ppermute(value, 'row', [(r, r ^ shift) for r in range(lax.axis_size('...  12.2 us
    pallas_call x1, Pallas kernels, make_edges(): pl.pallas_call(functools.partial(edges_kernel, groups, rows, cols, chunks...  3.53 us
    pallas_call x1, Pallas kernels, make_products(): pl.pallas_call(functools.partial(products_kernel, groups, rows, cols, par...  3.48 us
    pallas_call x1, Pallas kernels, make_update(): pl.pallas_call(functools.partial(update_kernel, groups, rows, cols, chunk...  1.33 us
    ppermute x2, waiting for transfers between devices, shards(): other = lax.ppermute(made[2 + part], 'col', [(0, 1), (1, 0)])  1.02 us
  transfers between devices with their start and end apart: 12, of which 6 were waited for; matrix products, arithmetic and copies ran while one was open for 1% of the time, Pallas kernels for 1%

profile of v13, /device:TPU:0, one launch (start us, length us, event | category | flops | bytes accessed | tf_op | source)
XLA Modules:
  0.0 47.6 jit_solution(15436586756387014605)
XLA Ops:
  0.0 0.0 copy-start
  0.0 3.5 %shard_map.91 = (bf16[128,2048]{1,0:T(8,128)(2,1)}, bf16[976,128]{1,0:T(8,128)(2,1)}, bf16[976,128]{1,0:T(8,128)(2,1)}, bf16[976,128]{1,0:T(8,128)(2,1)}, bf16[9...) custom-call(bf16[1936,128]{1,0:T(8,128)(2,1)} %bitcast.5, ...), custom_call_target="tpu_custom_call" | custom-call | tf_op jit(solution)/shard_map/pallas_call | solution.py:137
  3.5 0.0 copy-start.1
  3.6 5.1 %collective-permute-start = (bf16[496,128]{1,0:T(8,128)(2,1)}, bf16[496,128]{1,0:T(8,128)(2,1)S(1)}, u32[]{:S(2)}, u32[]{:S(2)}) collective-permute-start(bf16[496,128]{1,0:T(8,128)(2,1)} %get-tuple-element.26), channel_id=1, source_target_pairs={{0,12},{2,14},{4,8},{6,10},{8,4},{10,6},{12,0},{14,2},{1,13},{3,15... | collective-permute-start | bytes 380936 | tf_op jit(solution)/shard_map/ppermute | solution.py:396
  8.7 1.2 %collective-permute-start.1 = (bf16[496,128]{1,0:T(8,128)(2,1)}, bf16[496,128]{1,0:T(8,128)(2,1)S(1)}, u32[]{:S(2)}, u32[]{:S(2)}) collective-permute-start(bf16[496,128]{1,0:T(8,128)(2,1)} %get-tuple-element.27), channel_id=1, source_target_pairs={{0,14},{2,12},{4,10},{6,8},{8,6},{10,4},{12,2},{14,0},{1,15},{3,13... | collective-permute-start | bytes 380936 | tf_op jit(solution)/shard_map/ppermute | solution.py:396
  9.8 0.4 collective-permute-start.3
  10.2 0.0 collective-permute-start.4
  10.2 3.1 %collective-permute-start.5 = (bf16[976,128]{1,0:T(8,128)(2,1)}, bf16[976,128]{1,0:T(8,128)(2,1)S(1)}, u32[]{:S(2)}, u32[]{:S(2)}) collective-permute-start(bf16[976,128]{1,0:T(8,128)(2,1)} %get-tuple-element.35), channel_id=1, source_target_pairs={{0,6},{2,4},{4,2},{6,0},{8,14},{10,12},{12,10},{14,8},{1,7},{3,5},... | collective-permute-start | bytes 749576 | tf_op jit(solution)/shard_map/ppermute | solution.py:396
  13.3 0.0 collective-permute-done.refs_0_
  13.3 6.3 %collective-permute-start.2 = (bf16[496,128]{1,0:T(8,128)(2,1)}, bf16[496,128]{1,0:T(8,128)(2,1)S(1)}, u32[]{:S(2)}, u32[]{:S(2)}) collective-permute-start(bf16[496,128]{1,0:T(8,128)(2,1)} %get-tuple-element.28), channel_id=1, source_target_pairs={{0,8},{2,10},{4,12},{6,14},{8,0},{10,2},{12,4},{14,6},{1,9},{3,11}... | collective-permute-start | bytes 380936 | tf_op jit(solution)/shard_map/ppermute | solution.py:396
  19.6 0.0 collective-permute-done.1.refs_1_
  19.6 3.6 %collective-permute-start.6 = (bf16[496,128]{1,0:T(8,128)(2,1)}, bf16[496,128]{1,0:T(8,128)(2,1)S(1)}, u32[]{:S(2)}, u32[]{:S(2)}) collective-permute-start(bf16[496,128]{1,0:T(8,128)(2,1)} %get-tuple-element.36), channel_id=1, source_target_pairs={{0,10},{2,8},{4,14},{6,12},{8,2},{10,0},{12,6},{14,4},{1,11},{3,9}... | collective-permute-start | bytes 380936 | tf_op jit(solution)/shard_map/ppermute | solution.py:396
  23.2 5.7 %collective-permute-done.2.refs_2_ = bf16[496,128]{1,0:T(8,128)(2,1)S(1)} collective-permute-done((bf16[496,128]{1,0:T(8,128)(2,1)}, bf16[496,128]{1,0:T(8,128)(2,1)S(1)}, u32[]{:S(2)}, u32[]{:S(2)}) %collective-permute-start.2) | collective-permute-done | bytes 127008 | tf_op jit(solution)/shard_map/ppermute | solution.py:396
  29.0 0.5 shard_map.92
  29.4 1.2 %collective-permute-done.6.refs_7_ = bf16[496,128]{1,0:T(8,128)(2,1)S(1)} collective-permute-done((bf16[496,128]{1,0:T(8,128)(2,1)}, bf16[496,128]{1,0:T(8,128)(2,1)S(1)}, u32[]{:S(2)}, u32[]{:S(2)}) %collective-permute-start.6) | collective-permute-done | bytes 127008 | tf_op jit(solution)/shard_map/ppermute | solution.py:396
  30.6 0.0 collective-permute-done.3.refs_4_
  30.6 0.0 collective-permute-done.4.refs_5_
  30.6 1.6 %collective-permute-done.5.refs_6_ = bf16[976,128]{1,0:T(8,128)(2,1)S(1)} collective-permute-done((bf16[976,128]{1,0:T(8,128)(2,1)}, bf16[976,128]{1,0:T(8,128)(2,1)S(1)}, u32[]{:S(2)}, u32[]{:S(2)}) %collective-permute-start.5) | collective-permute-done | bytes 249888 | tf_op jit(solution)/shard_map/ppermute | solution.py:396
  32.2 0.0 copy-done.1
  32.2 3.5 %shard_map.93 = (bf16[2,496,128]{2,1,0:T(8,128)(2,1)S(1)}, bf16[2,496,128]{2,1,0:T(8,128)(2,1)S(1)}, bf16[2,496,128]{2,1,0:T(8,128)(2,1)S(1)}, bf16[2,496,128]{2,1,0:T(8,128)(2,1)S(1)}) custom-call(f32[1,880,128]{2,1,0:T(8,128)S(1)} %get-tuple-element.29.refs_0_, f32[1,880,128]{2,1,0:T(8,128)S(1)} %get-tuple-element.30.refs_1_, ...), custom_call_target="tpu_custom_call" | custom-call | flops 100000 | bytes 10000000 | tf_op jit(solution)/shard_map/pallas_call | solution.py:313
  35.7 0.0 copy-start.4
  35.7 0.1 collective-permute-start.8
  35.8 0.5 %collective-permute-start.7 = (bf16[2,496,128]{2,1,0:T(8,128)(2,1)S(1)}, bf16[2,496,128]{2,1,0:T(8,128)(2,1)S(1)}, u32[]{:S(2)}, u32[]{:S(2)}) collective-permute-start(bf16[2,496,128]{2,1,0:T(8,128)(2,1)S(1)} %get-tuple-element.38), channel_id=1, source_target_pairs={{0,1},{1,0},{2,3},{3,2},{4,5},{5,4},{6,7},{7,6},{8,9},{9,8},{10,11... | collective-permute-start | bytes 761864 | tf_op jit(solution)/shard_map/ppermute | solution.py:420
  36.3 1.0 %collective-permute-done.8.b_ref = bf16[2,496,128]{2,1,0:T(8,128)(2,1)S(1)} collective-permute-done((bf16[2,496,128]{2,1,0:T(8,128)(2,1)S(1)}, bf16[2,496,128]{2,1,0:T(8,128)(2,1)S(1)}, u32[]{:S(2)}, u32[]{:S(2)}) %collective-permute-start.8) | collective-permute-done | bytes 253984 | tf_op jit(solution)/shard_map/ppermute | solution.py:420
  37.3 0.1 shard_map.95
  37.4 1.0 %collective-permute-start.10 = (bf16[496,128]{1,0:T(8,128)(2,1)S(1)}, bf16[496,128]{1,0:T(8,128)(2,1)S(1)}, u32[]{:S(2)}, u32[]{:S(2)}) collective-permute-start(bf16[496,128]{1,0:T(8,128)(2,1)S(1)} %get-tuple-element.43), channel_id=1, source_target_pairs={{0,4},{2,6},{4,0},{6,2},{8,12},{10,14},{12,8},{14,10},{1,5},{3,7},... | collective-permute-start | bytes 380936 | tf_op jit(solution)/shard_map/ppermute | solution.py:396
  38.4 1.6 %collective-permute-start.9 = (bf16[496,128]{1,0:T(8,128)(2,1)S(1)}, bf16[496,128]{1,0:T(8,128)(2,1)S(1)}, u32[]{:S(2)}, u32[]{:S(2)}) collective-permute-start(bf16[496,128]{1,0:T(8,128)(2,1)S(1)} %get-tuple-element.42), channel_id=1, source_target_pairs={{0,2},{2,0},{4,6},{6,4},{8,10},{10,8},{12,14},{14,12},{1,3},{3,1},... | collective-permute-start | bytes 380936 | tf_op jit(solution)/shard_map/ppermute | solution.py:396
  40.0 0.0 collective-permute-done.7.b_ref
  40.0 0.1 shard_map.94
  40.0 1.0 %collective-permute-start.11 = (bf16[496,128]{1,0:T(8,128)(2,1)S(1)}, bf16[496,128]{1,0:T(8,128)(2,1)S(1)}, u32[]{:S(2)}, u32[]{:S(2)}) collective-permute-start(bf16[496,128]{1,0:T(8,128)(2,1)S(1)} %get-tuple-element.44), channel_id=1, source_target_pairs={{0,6},{2,4},{4,2},{6,0},{8,14},{10,12},{12,10},{14,8},{1,7},{3,5},... | collective-permute-start | bytes 380936 | tf_op jit(solution)/shard_map/ppermute | solution.py:396
  41.0 0.0 copy-done
  41.0 0.0 copy-done.4
  41.0 0.0 copy-start.2
  41.0 0.5 fusion.2.gate_ref
  41.5 0.3 copy-done.2
  41.8 0.0 copy-start.3
  41.8 0.7 %copy-done.3 = f32[128]{0:T(128)S(1)} copy-done((f32[128]{0:T(128)S(1)}, f32[128]{0:T(128)}, u32[]{:S(2)}) %copy-start.3) | copy-done | bytes 536
  42.5 0.1 copy.10.gain_ref
  42.6 1.0 %collective-permute-done.10.refs_2_ = bf16[496,128]{1,0:T(8,128)(2,1)S(1)} collective-permute-done((bf16[496,128]{1,0:T(8,128)(2,1)S(1)}, bf16[496,128]{1,0:T(8,128)(2,1)S(1)}, u32[]{:S(2)}, u32[]{:S(2)}) %collective-permute-start.10) | collective-permute-done | bytes 127008 | tf_op jit(solution)/shard_map/ppermute | solution.py:396
  43.6 2.7 %collective-permute-done.9.refs_1_ = bf16[496,128]{1,0:T(8,128)(2,1)S(1)} collective-permute-done((bf16[496,128]{1,0:T(8,128)(2,1)S(1)}, bf16[496,128]{1,0:T(8,128)(2,1)S(1)}, u32[]{:S(2)}, u32[]{:S(2)}) %collective-permute-start.9) | collective-permute-done | bytes 127008 | tf_op jit(solution)/shard_map/ppermute | solution.py:396
  46.3 0.0 collective-permute-done.11.refs_3_
  46.3 1.3 %shard_map.96 = bf16[1936,128]{1,0:T(8,128)(2,1)} custom-call(f32[128,1]{1,0:T(8,128)S(1)} %copy.10.gain_ref, f32[128,128]{1,0:T(8,128)S(1)} %convert_element_type.3.w_ref, f32[1936,128]{1,0:T(8,128)S(1)} %fusion.2.gate_ref, bf16[496,128]{1,0:T(8,128)(2,1)S(1)} %get-tuple-element.39.refs_0_, bf16[496,128]{1,0:T(8,128)(2,1)S(1)} %collective-permute-done.9.refs_1_, ...), custom_call_target="tpu_custom_call" | custom-call | tf_op jit(solution)/shard_map/pallas_call | solution.py:380
  (1 shorter events, 0.0 us)
Async XLA Ops:
  0.0 41.0 %copy-start = (bf16[128,128]{1,0:T(8,128)(2,1)S(1)}, bf16[128,128]{1,0:T(8,128)(2,1)}, u32[]{:S(2)}) copy-start(bf16[128,128]{1,0:T(8,128)(2,1)} %param.16) | copy-start | bytes 98308
  3.5 28.7 %copy-start.1 = (bf16[976,128]{1,0:T(8,128)(2,1)S(1)}, bf16[976,128]{1,0:T(8,128)(2,1)}, u32[]{:S(2)}) copy-start(bf16[976,128]{1,0:T(8,128)(2,1)} %get-tuple-element.32.refs_3_) | copy-start | bytes 749572
  3.6 9.8 %collective-permute-start = (bf16[496,128]{1,0:T(8,128)(2,1)}, bf16[496,128]{1,0:T(8,128)(2,1)S(1)}, u32[]{:S(2)}, u32[]{:S(2)}) collective-permute-start(bf16[496,128]{1,0:T(8,128)(2,1)} %get-tuple-element.26), channel_id=1, source_target_pairs={{0,12},{2,14},{4,8},{6,10},{8,4},{10,6},{12,0},{14,2},{1,13},{3,15... | collective-permute-start | bytes 380936 | tf_op jit(solution)/shard_map/ppermute | solution.py:396
  8.7 10.9 %collective-permute-start.1 = (bf16[496,128]{1,0:T(8,128)(2,1)}, bf16[496,128]{1,0:T(8,128)(2,1)S(1)}, u32[]{:S(2)}, u32[]{:S(2)}) collective-permute-start(bf16[496,128]{1,0:T(8,128)(2,1)} %get-tuple-element.27), channel_id=1, source_target_pairs={{0,14},{2,12},{4,10},{6,8},{8,6},{10,4},{12,2},{14,0},{1,15},{3,13... | collective-permute-start | bytes 380936 | tf_op jit(solution)/shard_map/ppermute | solution.py:396
  9.8 20.7 %collective-permute-start.3 = (bf16[976,128]{1,0:T(8,128)(2,1)}, bf16[976,128]{1,0:T(8,128)(2,1)S(1)}, u32[]{:S(2)}, u32[]{:S(2)}) collective-permute-start(bf16[976,128]{1,0:T(8,128)(2,1)} %get-tuple-element.33), channel_id=1, source_target_pairs={{0,2},{2,0},{4,6},{6,4},{8,10},{10,8},{12,14},{14,12},{1,3},{3,1},... | collective-permute-start | bytes 749576 | tf_op jit(solution)/shard_map/ppermute | solution.py:396
  10.2 20.4 %collective-permute-start.4 = (bf16[976,128]{1,0:T(8,128)(2,1)}, bf16[976,128]{1,0:T(8,128)(2,1)S(1)}, u32[]{:S(2)}, u32[]{:S(2)}) collective-permute-start(bf16[976,128]{1,0:T(8,128)(2,1)} %get-tuple-element.34), channel_id=1, source_target_pairs={{0,4},{2,6},{4,0},{6,2},{8,12},{10,14},{12,8},{14,10},{1,5},{3,7},... | collective-permute-start | bytes 749576 | tf_op jit(solution)/shard_map/ppermute | solution.py:396
  10.2 22.0 %collective-permute-start.5 = (bf16[976,128]{1,0:T(8,128)(2,1)}, bf16[976,128]{1,0:T(8,128)(2,1)S(1)}, u32[]{:S(2)}, u32[]{:S(2)}) collective-permute-start(bf16[976,128]{1,0:T(8,128)(2,1)} %get-tuple-element.35), channel_id=1, source_target_pairs={{0,6},{2,4},{4,2},{6,0},{8,14},{10,12},{12,10},{14,8},{1,7},{3,5},... | collective-permute-start | bytes 749576 | tf_op jit(solution)/shard_map/ppermute | solution.py:396
  13.3 15.6 %collective-permute-start.2 = (bf16[496,128]{1,0:T(8,128)(2,1)}, bf16[496,128]{1,0:T(8,128)(2,1)S(1)}, u32[]{:S(2)}, u32[]{:S(2)}) collective-permute-start(bf16[496,128]{1,0:T(8,128)(2,1)} %get-tuple-element.28), channel_id=1, source_target_pairs={{0,8},{2,10},{4,12},{6,14},{8,0},{10,2},{12,4},{14,6},{1,9},{3,11}... | collective-permute-start | bytes 380936 | tf_op jit(solution)/shard_map/ppermute | solution.py:396
  19.6 11.0 %collective-permute-start.6 = (bf16[496,128]{1,0:T(8,128)(2,1)}, bf16[496,128]{1,0:T(8,128)(2,1)S(1)}, u32[]{:S(2)}, u32[]{:S(2)}) collective-permute-start(bf16[496,128]{1,0:T(8,128)(2,1)} %get-tuple-element.36), channel_id=1, source_target_pairs={{0,10},{2,8},{4,14},{6,12},{8,2},{10,0},{12,6},{14,4},{1,11},{3,9}... | collective-permute-start | bytes 380936 | tf_op jit(solution)/shard_map/ppermute | solution.py:396
  35.7 5.3 %copy-start.4 = (bf16[128,2048]{1,0:T(8,128)(2,1)S(1)}, bf16[128,2048]{1,0:T(8,128)(2,1)}, u32[]{:S(2)}) copy-start(bf16[128,2048]{1,0:T(8,128)(2,1)} %get-tuple-element.25) | copy-start | bytes 1572868
  35.7 1.6 %collective-permute-start.8 = (bf16[2,496,128]{2,1,0:T(8,128)(2,1)S(1)}, bf16[2,496,128]{2,1,0:T(8,128)(2,1)S(1)}, u32[]{:S(2)}, u32[]{:S(2)}) collective-permute-start(bf16[2,496,128]{2,1,0:T(8,128)(2,1)S(1)} %get-tuple-element.41), channel_id=1, source_target_pairs={{0,1},{1,0},{2,3},{3,2},{4,5},{5,4},{6,7},{7,6},{8,9},{9,8},{10,11... | collective-permute-start | bytes 761864 | tf_op jit(solution)/shard_map/ppermute | solution.py:420
  35.8 4.2 %collective-permute-start.7 = (bf16[2,496,128]{2,1,0:T(8,128)(2,1)S(1)}, bf16[2,496,128]{2,1,0:T(8,128)(2,1)S(1)}, u32[]{:S(2)}, u32[]{:S(2)}) collective-permute-start(bf16[2,496,128]{2,1,0:T(8,128)(2,1)S(1)} %get-tuple-element.38), channel_id=1, source_target_pairs={{0,1},{1,0},{2,3},{3,2},{4,5},{5,4},{6,7},{7,6},{8,9},{9,8},{10,11... | collective-permute-start | bytes 761864 | tf_op jit(solution)/shard_map/ppermute | solution.py:420
  37.4 6.2 %collective-permute-start.10 = (bf16[496,128]{1,0:T(8,128)(2,1)S(1)}, bf16[496,128]{1,0:T(8,128)(2,1)S(1)}, u32[]{:S(2)}, u32[]{:S(2)}) collective-permute-start(bf16[496,128]{1,0:T(8,128)(2,1)S(1)} %get-tuple-element.43), channel_id=1, source_target_pairs={{0,4},{2,6},{4,0},{6,2},{8,12},{10,14},{12,8},{14,10},{1,5},{3,7},... | collective-permute-start | bytes 380936 | tf_op jit(solution)/shard_map/ppermute | solution.py:396
  38.4 7.9 %collective-permute-start.9 = (bf16[496,128]{1,0:T(8,128)(2,1)S(1)}, bf16[496,128]{1,0:T(8,128)(2,1)S(1)}, u32[]{:S(2)}, u32[]{:S(2)}) collective-permute-start(bf16[496,128]{1,0:T(8,128)(2,1)S(1)} %get-tuple-element.42), channel_id=1, source_target_pairs={{0,2},{2,0},{4,6},{6,4},{8,10},{10,8},{12,14},{14,12},{1,3},{3,1},... | collective-permute-start | bytes 380936 | tf_op jit(solution)/shard_map/ppermute | solution.py:396
  40.0 6.3 %collective-permute-start.11 = (bf16[496,128]{1,0:T(8,128)(2,1)S(1)}, bf16[496,128]{1,0:T(8,128)(2,1)S(1)}, u32[]{:S(2)}, u32[]{:S(2)}) collective-permute-start(bf16[496,128]{1,0:T(8,128)(2,1)S(1)} %get-tuple-element.44), channel_id=1, source_target_pairs={{0,6},{2,4},{4,2},{6,0},{8,14},{10,12},{12,10},{14,8},{1,7},{3,5},... | collective-permute-start | bytes 380936 | tf_op jit(solution)/shard_map/ppermute | solution.py:396
  41.0 0.8 %copy-start.2 = (bf16[128,128]{1,0:T(8,128)(2,1)S(1)}, bf16[128,128]{1,0:T(8,128)(2,1)}, u32[]{:S(2)}) copy-start(bf16[128,128]{1,0:T(8,128)(2,1)} %param.17) | copy-start | bytes 98308
  41.8 0.7 %copy-start.3 = (f32[128]{0:T(128)S(1)}, f32[128]{0:T(128)}, u32[]{:S(2)}) copy-start(f32[128]{0:T(128)} %param.13) | copy-start | bytes 1540

commit v14 on v13

--- a/solution.py
+++ b/solution.py
@@ -201,6 +201,8 @@
                 seen[t] = tile_at(got_ref, t, total, n * ch, ch, rows, cols)
             return seen[t]
 
+        if tiles_of(rows, cols)[1]:
+            tile_of(tiles_of(rows, cols)[0])
         for i in range(rows):
             for tt in range(tiles):
                 length = min(LANES, cols - LANES * tt)
@@ -276,7 +278,7 @@
     for part, pieces in enumerate(parts):
         for n, u in enumerate(pieces):
             block = jnp.bitwise_xor(mine, u)
-            for t in range(full + (over > 0)):
+            for t in ([full] if over else []) + list(range(full)):
                 near = packed_tile(prod_s, 0, t, block, rows, cols, step, ch)
                 far = packed_tile(prod_s, tiles, t, block, rows, cols, step, ch)
                 if t == full:

time: 47.8 us -> 47.2 us (0.987)
  Pallas kernels: 8.91 us -> 8.1 us
    pallas_call x1, Pallas kernels: 3.48 us -> 2.83 us  [make_products(): pl.pallas_call(functools.partial(products_kernel, groups, rows, cols, par...]
where the time goes in v14:
time: 47.2 us; the launch traced here: 47 us
  starting transfers between devices  23.9 us (51%)
  waiting for transfers between devices  13.4 us (28%)
  Pallas kernels  8.1 us (17%)
  local copies, waits for them, and re-layouts  1.06 us (2%)
    ppermute x10, starting transfers between devices, swap(): lax.ppermute(value, 'row', [(r, r ^ shift) for r in range(lax.axis_size('...  23.3 us
    ppermute x10, waiting for transfers between devices, swap(): lax.ppermute(value, 'row', [(r, r ^ shift) for r in range(lax.axis_size('...  12.4 us
    pallas_call x1, Pallas kernels, make_edges(): pl.pallas_call(functools.partial(edges_kernel, groups, rows, cols, chunks...  3.53 us
    pallas_call x1, Pallas kernels, make_products(): pl.pallas_call(functools.partial(products_kernel, groups, rows, cols, par...  2.83 us
    pallas_call x1, Pallas kernels, make_update(): pl.pallas_call(functools.partial(update_kernel, groups, rows, cols, chunk...  1.32 us
    ppermute x2, waiting for transfers between devices, shards(): other = lax.ppermute(made[2 + part], 'col', [(0, 1), (1, 0)])  1.02 us
    unnamed x10, local copies, waits for them, and re-layouts  0.94 us
  transfers between devices with their start and end apart: 12, of which 6 were waited for; matrix products, arithmetic and copies ran while one was open for 1% of the time, Pallas kernels for 1%

profile of v14, /device:TPU:0, one launch (start us, length us, event | category | flops | bytes accessed | tf_op | source)
XLA Modules:
  0.0 47.0 jit_solution(12163369894126422886)
XLA Ops:
  0.0 0.0 copy-start
  0.0 3.5 %shard_map.91 = (bf16[128,2048]{1,0:T(8,128)(2,1)}, bf16[976,128]{1,0:T(8,128)(2,1)}, bf16[976,128]{1,0:T(8,128)(2,1)}, bf16[976,128]{1,0:T(8,128)(2,1)}, bf16[9...) custom-call(bf16[1936,128]{1,0:T(8,128)(2,1)} %bitcast.5, ...), custom_call_target="tpu_custom_call" | custom-call | tf_op jit(solution)/shard_map/pallas_call | solution.py:137
  3.5 0.0 copy-start.1
  3.6 5.1 %collective-permute-start = (bf16[496,128]{1,0:T(8,128)(2,1)}, bf16[496,128]{1,0:T(8,128)(2,1)S(1)}, u32[]{:S(2)}, u32[]{:S(2)}) collective-permute-start(bf16[496,128]{1,0:T(8,128)(2,1)} %get-tuple-element.26), channel_id=1, source_target_pairs={{0,12},{2,14},{4,8},{6,10},{8,4},{10,6},{12,0},{14,2},{1,13},{3,15... | collective-permute-start | bytes 380936 | tf_op jit(solution)/shard_map/ppermute | solution.py:398
  8.7 1.2 %collective-permute-start.1 = (bf16[496,128]{1,0:T(8,128)(2,1)}, bf16[496,128]{1,0:T(8,128)(2,1)S(1)}, u32[]{:S(2)}, u32[]{:S(2)}) collective-permute-start(bf16[496,128]{1,0:T(8,128)(2,1)} %get-tuple-element.27), channel_id=1, source_target_pairs={{0,14},{2,12},{4,10},{6,8},{8,6},{10,4},{12,2},{14,0},{1,15},{3,13... | collective-permute-start | bytes 380936 | tf_op jit(solution)/shard_map/ppermute | solution.py:398
  9.8 0.4 collective-permute-start.3
  10.2 0.0 collective-permute-start.4
  10.2 3.1 %collective-permute-start.5 = (bf16[976,128]{1,0:T(8,128)(2,1)}, bf16[976,128]{1,0:T(8,128)(2,1)S(1)}, u32[]{:S(2)}, u32[]{:S(2)}) collective-permute-start(bf16[976,128]{1,0:T(8,128)(2,1)} %get-tuple-element.35), channel_id=1, source_target_pairs={{0,6},{2,4},{4,2},{6,0},{8,14},{10,12},{12,10},{14,8},{1,7},{3,5},... | collective-permute-start | bytes 749576 | tf_op jit(solution)/shard_map/ppermute | solution.py:398
  13.3 0.0 collective-permute-done.refs_0_
  13.3 6.3 %collective-permute-start.2 = (bf16[496,128]{1,0:T(8,128)(2,1)}, bf16[496,128]{1,0:T(8,128)(2,1)S(1)}, u32[]{:S(2)}, u32[]{:S(2)}) collective-permute-start(bf16[496,128]{1,0:T(8,128)(2,1)} %get-tuple-element.28), channel_id=1, source_target_pairs={{0,8},{2,10},{4,12},{6,14},{8,0},{10,2},{12,4},{14,6},{1,9},{3,11}... | collective-permute-start | bytes 380936 | tf_op jit(solution)/shard_map/ppermute | solution.py:398
  19.6 0.0 collective-permute-done.1.refs_1_
  19.6 3.6 %collective-permute-start.6 = (bf16[496,128]{1,0:T(8,128)(2,1)}, bf16[496,128]{1,0:T(8,128)(2,1)S(1)}, u32[]{:S(2)}, u32[]{:S(2)}) collective-permute-start(bf16[496,128]{1,0:T(8,128)(2,1)} %get-tuple-element.36), channel_id=1, source_target_pairs={{0,10},{2,8},{4,14},{6,12},{8,2},{10,0},{12,6},{14,4},{1,11},{3,9}... | collective-permute-start | bytes 380936 | tf_op jit(solution)/shard_map/ppermute | solution.py:398
  23.2 5.7 %collective-permute-done.2.refs_2_ = bf16[496,128]{1,0:T(8,128)(2,1)S(1)} collective-permute-done((bf16[496,128]{1,0:T(8,128)(2,1)}, bf16[496,128]{1,0:T(8,128)(2,1)S(1)}, u32[]{:S(2)}, u32[]{:S(2)}) %collective-permute-start.2) | collective-permute-done | bytes 127008 | tf_op jit(solution)/shard_map/ppermute | solution.py:398
  29.0 0.3 shard_map.92
  29.2 1.3 %collective-permute-done.6.refs_7_ = bf16[496,128]{1,0:T(8,128)(2,1)S(1)} collective-permute-done((bf16[496,128]{1,0:T(8,128)(2,1)}, bf16[496,128]{1,0:T(8,128)(2,1)S(1)}, u32[]{:S(2)}, u32[]{:S(2)}) %collective-permute-start.6) | collective-permute-done | bytes 127008 | tf_op jit(solution)/shard_map/ppermute | solution.py:398
  30.6 0.0 collective-permute-done.3.refs_4_
  30.6 0.0 collective-permute-done.4.refs_5_
  30.6 1.6 %collective-permute-done.5.refs_6_ = bf16[976,128]{1,0:T(8,128)(2,1)S(1)} collective-permute-done((bf16[976,128]{1,0:T(8,128)(2,1)}, bf16[976,128]{1,0:T(8,128)(2,1)S(1)}, u32[]{:S(2)}, u32[]{:S(2)}) %collective-permute-start.5) | collective-permute-done | bytes 249888 | tf_op jit(solution)/shard_map/ppermute | solution.py:398
  32.2 0.0 copy-done.1
  32.2 2.8 %shard_map.93 = (bf16[2,496,128]{2,1,0:T(8,128)(2,1)S(1)}, bf16[2,496,128]{2,1,0:T(8,128)(2,1)S(1)}, bf16[2,496,128]{2,1,0:T(8,128)(2,1)S(1)}, bf16[2,496,128]{2,1,0:T(8,128)(2,1)S(1)}) custom-call(f32[1,880,128]{2,1,0:T(8,128)S(1)} %get-tuple-element.29.refs_0_, f32[1,880,128]{2,1,0:T(8,128)S(1)} %get-tuple-element.30.refs_1_, ...), custom_call_target="tpu_custom_call" | custom-call | flops 100000 | bytes 10000000 | tf_op jit(solution)/shard_map/pallas_call | solution.py:315
  35.1 0.0 copy-start.4
  35.1 0.1 collective-permute-start.8
  35.1 0.5 %collective-permute-start.7 = (bf16[2,496,128]{2,1,0:T(8,128)(2,1)S(1)}, bf16[2,496,128]{2,1,0:T(8,128)(2,1)S(1)}, u32[]{:S(2)}, u32[]{:S(2)}) collective-permute-start(bf16[2,496,128]{2,1,0:T(8,128)(2,1)S(1)} %get-tuple-element.38), channel_id=1, source_target_pairs={{0,1},{1,0},{2,3},{3,2},{4,5},{5,4},{6,7},{7,6},{8,9},{9,8},{10,11... | collective-permute-start | bytes 761864 | tf_op jit(solution)/shard_map/ppermute | solution.py:422
  35.6 1.0 %collective-permute-done.8.b_ref = bf16[2,496,128]{2,1,0:T(8,128)(2,1)S(1)} collective-permute-done((bf16[2,496,128]{2,1,0:T(8,128)(2,1)S(1)}, bf16[2,496,128]{2,1,0:T(8,128)(2,1)S(1)}, u32[]{:S(2)}, u32[]{:S(2)}) %collective-permute-start.8) | collective-permute-done | bytes 253984 | tf_op jit(solution)/shard_map/ppermute | solution.py:422
  36.7 0.1 shard_map.95
  36.7 1.0 %collective-permute-start.10 = (bf16[496,128]{1,0:T(8,128)(2,1)S(1)}, bf16[496,128]{1,0:T(8,128)(2,1)S(1)}, u32[]{:S(2)}, u32[]{:S(2)}) collective-permute-start(bf16[496,128]{1,0:T(8,128)(2,1)S(1)} %get-tuple-element.43), channel_id=1, source_target_pairs={{0,4},{2,6},{4,0},{6,2},{8,12},{10,14},{12,8},{14,10},{1,5},{3,7},... | collective-permute-start | bytes 380936 | tf_op jit(solution)/shard_map/ppermute | solution.py:398
  37.8 1.6 %collective-permute-start.9 = (bf16[496,128]{1,0:T(8,128)(2,1)S(1)}, bf16[496,128]{1,0:T(8,128)(2,1)S(1)}, u32[]{:S(2)}, u32[]{:S(2)}) collective-permute-start(bf16[496,128]{1,0:T(8,128)(2,1)S(1)} %get-tuple-element.42), channel_id=1, source_target_pairs={{0,2},{2,0},{4,6},{6,4},{8,10},{10,8},{12,14},{14,12},{1,3},{3,1},... | collective-permute-start | bytes 380936 | tf_op jit(solution)/shard_map/ppermute | solution.py:398
  39.3 0.0 collective-permute-done.7.b_ref
  39.3 0.1 shard_map.94
  39.4 1.0 %collective-permute-start.11 = (bf16[496,128]{1,0:T(8,128)(2,1)S(1)}, bf16[496,128]{1,0:T(8,128)(2,1)S(1)}, u32[]{:S(2)}, u32[]{:S(2)}) collective-permute-start(bf16[496,128]{1,0:T(8,128)(2,1)S(1)} %get-tuple-element.44), channel_id=1, source_target_pairs={{0,6},{2,4},{4,2},{6,0},{8,14},{10,12},{12,10},{14,8},{1,7},{3,5},... | collective-permute-start | bytes 380936 | tf_op jit(solution)/shard_map/ppermute | solution.py:398
  40.4 0.0 copy-done
  40.4 0.0 copy-done.4
  40.4 0.0 copy-start.2
  40.4 0.5 %fusion.2.gate_ref = f32[1936,128]{1,0:T(8,128)S(1)} fusion(bf16[128,128]{1,0:T(8,128)(2,1)S(1)} %copy-done, bf16[128,2048]{1,0:T(8,128)(2,1)S(1)} %copy-done.4), kind=kOutput, calls=%fused_computation.3 | convolution fusion | flops 64182272 | bytes 1548288 | tf_op jit(solution)/shard_map/cp,cd->pd/dot_general | solution.py:413
  40.9 0.3 copy-done.2
  41.2 0.0 copy-start.3
  41.2 0.7 %copy-done.3 = f32[128]{0:T(128)S(1)} copy-done((f32[128]{0:T(128)S(1)}, f32[128]{0:T(128)}, u32[]{:S(2)}) %copy-start.3) | copy-done | bytes 536
  41.8 0.1 copy.10.gain_ref
  42.0 1.0 %collective-permute-done.10.refs_2_ = bf16[496,128]{1,0:T(8,128)(2,1)S(1)} collective-permute-done((bf16[496,128]{1,0:T(8,128)(2,1)S(1)}, bf16[496,128]{1,0:T(8,128)(2,1)S(1)}, u32[]{:S(2)}, u32[]{:S(2)}) %collective-permute-start.10) | collective-permute-done | bytes 127008 | tf_op jit(solution)/shard_map/ppermute | solution.py:398
  42.9 2.7 %collective-permute-done.9.refs_1_ = bf16[496,128]{1,0:T(8,128)(2,1)S(1)} collective-permute-done((bf16[496,128]{1,0:T(8,128)(2,1)S(1)}, bf16[496,128]{1,0:T(8,128)(2,1)S(1)}, u32[]{:S(2)}, u32[]{:S(2)}) %collective-permute-start.9) | collective-permute-done | bytes 127008 | tf_op jit(solution)/shard_map/ppermute | solution.py:398
  45.6 0.0 collective-permute-done.11.refs_3_
  45.6 1.3 %shard_map.96 = bf16[1936,128]{1,0:T(8,128)(2,1)} custom-call(f32[128,1]{1,0:T(8,128)S(1)} %copy.10.gain_ref, f32[128,128]{1,0:T(8,128)S(1)} %convert_element_type.3.w_ref, f32[1936,128]{1,0:T(8,128)S(1)} %fusion.2.gate_ref, bf16[496,128]{1,0:T(8,128)(2,1)S(1)} %get-tuple-element.39.refs_0_, bf16[496,128]{1,0:T(8,128)(2,1)S(1)} %collective-permute-done.9.refs_1_, ...), custom_call_target="tpu_custom_call" | custom-call | tf_op jit(solution)/shard_map/pallas_call | solution.py:382
  (1 shorter events, 0.0 us)
Async XLA Ops:
  0.0 40.4 %copy-start = (bf16[128,128]{1,0:T(8,128)(2,1)S(1)}, bf16[128,128]{1,0:T(8,128)(2,1)}, u32[]{:S(2)}) copy-start(bf16[128,128]{1,0:T(8,128)(2,1)} %param.16) | copy-start | bytes 98308
  3.5 28.7 %copy-start.1 = (bf16[976,128]{1,0:T(8,128)(2,1)S(1)}, bf16[976,128]{1,0:T(8,128)(2,1)}, u32[]{:S(2)}) copy-start(bf16[976,128]{1,0:T(8,128)(2,1)} %get-tuple-element.32.refs_3_) | copy-start | bytes 749572
  3.6 9.8 %collective-permute-start = (bf16[496,128]{1,0:T(8,128)(2,1)}, bf16[496,128]{1,0:T(8,128)(2,1)S(1)}, u32[]{:S(2)}, u32[]{:S(2)}) collective-permute-start(bf16[496,128]{1,0:T(8,128)(2,1)} %get-tuple-element.26), channel_id=1, source_target_pairs={{0,12},{2,14},{4,8},{6,10},{8,4},{10,6},{12,0},{14,2},{1,13},{3,15... | collective-permute-start | bytes 380936 | tf_op jit(solution)/shard_map/ppermute | solution.py:398
  8.7 10.9 %collective-permute-start.1 = (bf16[496,128]{1,0:T(8,128)(2,1)}, bf16[496,128]{1,0:T(8,128)(2,1)S(1)}, u32[]{:S(2)}, u32[]{:S(2)}) collective-permute-start(bf16[496,128]{1,0:T(8,128)(2,1)} %get-tuple-element.27), channel_id=1, source_target_pairs={{0,14},{2,12},{4,10},{6,8},{8,6},{10,4},{12,2},{14,0},{1,15},{3,13... | collective-permute-start | bytes 380936 | tf_op jit(solution)/shard_map/ppermute | solution.py:398
  9.8 20.7 %collective-permute-start.3 = (bf16[976,128]{1,0:T(8,128)(2,1)}, bf16[976,128]{1,0:T(8,128)(2,1)S(1)}, u32[]{:S(2)}, u32[]{:S(2)}) collective-permute-start(bf16[976,128]{1,0:T(8,128)(2,1)} %get-tuple-element.33), channel_id=1, source_target_pairs={{0,2},{2,0},{4,6},{6,4},{8,10},{10,8},{12,14},{14,12},{1,3},{3,1},... | collective-permute-start | bytes 749576 | tf_op jit(solution)/shard_map/ppermute | solution.py:398
  10.2 20.4 %collective-permute-start.4 = (bf16[976,128]{1,0:T(8,128)(2,1)}, bf16[976,128]{1,0:T(8,128)(2,1)S(1)}, u32[]{:S(2)}, u32[]{:S(2)}) collective-permute-start(bf16[976,128]{1,0:T(8,128)(2,1)} %get-tuple-element.34), channel_id=1, source_target_pairs={{0,4},{2,6},{4,0},{6,2},{8,12},{10,14},{12,8},{14,10},{1,5},{3,7},... | collective-permute-start | bytes 749576 | tf_op jit(solution)/shard_map/ppermute | solution.py:398
  10.2 22.0 %collective-permute-start.5 = (bf16[976,128]{1,0:T(8,128)(2,1)}, bf16[976,128]{1,0:T(8,128)(2,1)S(1)}, u32[]{:S(2)}, u32[]{:S(2)}) collective-permute-start(bf16[976,128]{1,0:T(8,128)(2,1)} %get-tuple-element.35), channel_id=1, source_target_pairs={{0,6},{2,4},{4,2},{6,0},{8,14},{10,12},{12,10},{14,8},{1,7},{3,5},... | collective-permute-start | bytes 749576 | tf_op jit(solution)/shard_map/ppermute | solution.py:398
  13.3 15.6 %collective-permute-start.2 = (bf16[496,128]{1,0:T(8,128)(2,1)}, bf16[496,128]{1,0:T(8,128)(2,1)S(1)}, u32[]{:S(2)}, u32[]{:S(2)}) collective-permute-start(bf16[496,128]{1,0:T(8,128)(2,1)} %get-tuple-element.28), channel_id=1, source_target_pairs={{0,8},{2,10},{4,12},{6,14},{8,0},{10,2},{12,4},{14,6},{1,9},{3,11}... | collective-permute-start | bytes 380936 | tf_op jit(solution)/shard_map/ppermute | solution.py:398
  19.6 11.0 %collective-permute-start.6 = (bf16[496,128]{1,0:T(8,128)(2,1)}, bf16[496,128]{1,0:T(8,128)(2,1)S(1)}, u32[]{:S(2)}, u32[]{:S(2)}) collective-permute-start(bf16[496,128]{1,0:T(8,128)(2,1)} %get-tuple-element.36), channel_id=1, source_target_pairs={{0,10},{2,8},{4,14},{6,12},{8,2},{10,0},{12,6},{14,4},{1,11},{3,9}... | collective-permute-start | bytes 380936 | tf_op jit(solution)/shard_map/ppermute | solution.py:398
  35.1 5.4 %copy-start.4 = (bf16[128,2048]{1,0:T(8,128)(2,1)S(1)}, bf16[128,2048]{1,0:T(8,128)(2,1)}, u32[]{:S(2)}) copy-start(bf16[128,2048]{1,0:T(8,128)(2,1)} %get-tuple-element.25) | copy-start | bytes 1572868
  35.1 1.6 %collective-permute-start.8 = (bf16[2,496,128]{2,1,0:T(8,128)(2,1)S(1)}, bf16[2,496,128]{2,1,0:T(8,128)(2,1)S(1)}, u32[]{:S(2)}, u32[]{:S(2)}) collective-permute-start(bf16[2,496,128]{2,1,0:T(8,128)(2,1)S(1)} %get-tuple-element.41), channel_id=1, source_target_pairs={{0,1},{1,0},{2,3},{3,2},{4,5},{5,4},{6,7},{7,6},{8,9},{9,8},{10,11... | collective-permute-start | bytes 761864 | tf_op jit(solution)/shard_map/ppermute | solution.py:422
  35.1 4.2 %collective-permute-start.7 = (bf16[2,496,128]{2,1,0:T(8,128)(2,1)S(1)}, bf16[2,496,128]{2,1,0:T(8,128)(2,1)S(1)}, u32[]{:S(2)}, u32[]{:S(2)}) collective-permute-start(bf16[2,496,128]{2,1,0:T(8,128)(2,1)S(1)} %get-tuple-element.38), channel_id=1, source_target_pairs={{0,1},{1,0},{2,3},{3,2},{4,5},{5,4},{6,7},{7,6},{8,9},{9,8},{10,11... | collective-permute-start | bytes 761864 | tf_op jit(solution)/shard_map/ppermute | solution.py:422
  36.7 6.2 %collective-permute-start.10 = (bf16[496,128]{1,0:T(8,128)(2,1)S(1)}, bf16[496,128]{1,0:T(8,128)(2,1)S(1)}, u32[]{:S(2)}, u32[]{:S(2)}) collective-permute-start(bf16[496,128]{1,0:T(8,128)(2,1)S(1)} %get-tuple-element.43), channel_id=1, source_target_pairs={{0,4},{2,6},{4,0},{6,2},{8,12},{10,14},{12,8},{14,10},{1,5},{3,7},... | collective-permute-start | bytes 380936 | tf_op jit(solution)/shard_map/ppermute | solution.py:398
  37.8 7.9 %collective-permute-start.9 = (bf16[496,128]{1,0:T(8,128)(2,1)S(1)}, bf16[496,128]{1,0:T(8,128)(2,1)S(1)}, u32[]{:S(2)}, u32[]{:S(2)}) collective-permute-start(bf16[496,128]{1,0:T(8,128)(2,1)S(1)} %get-tuple-element.42), channel_id=1, source_target_pairs={{0,2},{2,0},{4,6},{6,4},{8,10},{10,8},{12,14},{14,12},{1,3},{3,1},... | collective-permute-start | bytes 380936 | tf_op jit(solution)/shard_map/ppermute | solution.py:398
  39.4 6.3 %collective-permute-start.11 = (bf16[496,128]{1,0:T(8,128)(2,1)S(1)}, bf16[496,128]{1,0:T(8,128)(2,1)S(1)}, u32[]{:S(2)}, u32[]{:S(2)}) collective-permute-start(bf16[496,128]{1,0:T(8,128)(2,1)S(1)} %get-tuple-element.44), channel_id=1, source_target_pairs={{0,6},{2,4},{4,2},{6,0},{8,14},{10,12},{12,10},{14,8},{1,7},{3,5},... | collective-permute-start | bytes 380936 | tf_op jit(solution)/shard_map/ppermute | solution.py:398
  40.4 0.8 %copy-start.2 = (bf16[128,128]{1,0:T(8,128)(2,1)S(1)}, bf16[128,128]{1,0:T(8,128)(2,1)}, u32[]{:S(2)}) copy-start(bf16[128,128]{1,0:T(8,128)(2,1)} %param.17) | copy-start | bytes 98308
  41.2 0.7 %copy-start.3 = (f32[128]{0:T(128)S(1)}, f32[128]{0:T(128)}, u32[]{:S(2)}) copy-start(f32[128]{0:T(128)} %param.13) | copy-start | bytes 1540

commit v15 on v14

--- a/solution.py
+++ b/solution.py
@@ -259,7 +259,7 @@
     for u, lines_ref in zip(early, lines_refs):
         far_s[:, pl.ds(pl.multiple_of(jnp.bitwise_xor(mine, u) * rows * step, 8), rows * step), :] = lines_ref[...]
     for u in range(groups):
-        unpack(near_refs[u], (left_s, right_s), jnp.bitwise_xor(mine, u), rows, cols, step)
+        unpack(near_refs[(groups - u) % groups], (left_s, right_s), jnp.bitwise_xor(mine, u), rows, cols, step)
     for u, far_ref in zip(late, far_refs):
         unpack(far_ref, (far_s,), jnp.bitwise_xor(mine, u), rows, cols, step)
     pad = [jnp.zeros((tiles * LANES - count, tiles * LANES), jnp.float32)] if count % LANES else []
@@ -320,7 +320,7 @@
         scratch_shapes=[one, one, one, pltpu.VMEM((2 * tiles, held, LANES), jnp.float32)],
         compiler_params=pltpu.CompilerParams(vmem_limit_bytes=VMEM_LIMIT),
         cost_estimate=pl.CostEstimate(flops=10 ** 5, bytes_accessed=10 ** 7, transcendentals=0),
-    )(*lines, *near, *far)
+    )(*lines, *near[:1], *near[:0:-1], *far)
 
 
 def add_kernel(a_ref, b_ref, *out_refs):
@@ -376,7 +376,7 @@
 def make_update(prods, gain, w_out, gate, rows, cols):
     groups = len(prods)
     count, channels = gate.shape
-    block = 512
+    block = 1024
     chunks = [(at, min(block, count - at)) for at in range(0, count, block)]
     whole = pl.BlockSpec(memory_space=pltpu.VMEM)
     return pl.pallas_call(

time: 47.2 us -> 48 us (1.017)
  starting transfers between devices: 23.9 us -> 24.8 us
    ppermute x10, starting transfers between devices: 23.3 us -> 24.2 us  [swap(): lax.ppermute(value, 'row', [(r, r ^ shift) for r in range(lax.axis_size('...]
  transfers between devices with their start and end apart: 12 -> 12, of which waited for: 6 -> 5; matrix products, arithmetic and copies ran while one was open for 1% -> 1% of each run, Pallas kernels for 1% -> 1%
where the time goes in v15:
time: 48 us; the launch traced here: 47.8 us
  starting transfers between devices  24.8 us (52%)
  waiting for transfers between devices  13.3 us (28%)
  Pallas kernels  8.17 us (17%)
  local copies, waits for them, and re-layouts  1.06 us (2%)
    ppermute x10, starting transfers between devices, swap(): lax.ppermute(value, 'row', [(r, r ^ shift) for r in range(lax.axis_size('...  24.2 us
    ppermute x10, waiting for transfers between devices, swap(): lax.ppermute(value, 'row', [(r, r ^ shift) for r in range(lax.axis_size('...  12.3 us
    pallas_call x1, Pallas kernels, make_edges(): pl.pallas_call(functools.partial(edges_kernel, groups, rows, cols, chunks...  3.53 us
    pallas_call x1, Pallas kernels, make_products(): pl.pallas_call(functools.partial(products_kernel, groups, rows, cols, par...  2.83 us
    pallas_call x1, Pallas kernels, make_update(): pl.pallas_call(functools.partial(update_kernel, groups, rows, cols, chunk...  1.39 us
    ppermute x2, waiting for transfers between devices, shards(): other = lax.ppermute(made[2 + part], 'col', [(0, 1), (1, 0)])  1.02 us
  transfers between devices with their start and end apart: 12, of which 5 were waited for; matrix products, arithmetic and copies ran while one was open for 1% of the time, Pallas kernels for 1%

profile of v15, /device:TPU:0, one launch (start us, length us, event | category | flops | bytes accessed | tf_op | source)
XLA Modules:
  0.0 47.8 jit_solution(1439345390410339881)
XLA Ops:
  0.0 0.0 copy-start
  0.0 3.5 %shard_map.91 = (bf16[128,2048]{1,0:T(8,128)(2,1)}, bf16[976,128]{1,0:T(8,128)(2,1)}, bf16[976,128]{1,0:T(8,128)(2,1)}, bf16[976,128]{1,0:T(8,128)(2,1)}, bf16[9...) custom-call(bf16[1936,128]{1,0:T(8,128)(2,1)} %bitcast.5, ...), custom_call_target="tpu_custom_call" | custom-call | tf_op jit(solution)/shard_map/pallas_call | solution.py:137
  3.5 0.0 copy-start.1
  3.6 5.1 %collective-permute-start = (bf16[496,128]{1,0:T(8,128)(2,1)}, bf16[496,128]{1,0:T(8,128)(2,1)S(1)}, u32[]{:S(2)}, u32[]{:S(2)}) collective-permute-start(bf16[496,128]{1,0:T(8,128)(2,1)} %get-tuple-element.26), channel_id=1, source_target_pairs={{0,12},{2,14},{4,8},{6,10},{8,4},{10,6},{12,0},{14,2},{1,13},{3,15... | collective-permute-start | bytes 380936 | tf_op jit(solution)/shard_map/ppermute | solution.py:398
  8.7 1.2 %collective-permute-start.1 = (bf16[496,128]{1,0:T(8,128)(2,1)}, bf16[496,128]{1,0:T(8,128)(2,1)S(1)}, u32[]{:S(2)}, u32[]{:S(2)}) collective-permute-start(bf16[496,128]{1,0:T(8,128)(2,1)} %get-tuple-element.27), channel_id=1, source_target_pairs={{0,14},{2,12},{4,10},{6,8},{8,6},{10,4},{12,2},{14,0},{1,15},{3,13... | collective-permute-start | bytes 380936 | tf_op jit(solution)/shard_map/ppermute | solution.py:398
  9.8 0.0 collective-permute-start.3
  9.9 1.8 %collective-permute-start.4 = (bf16[976,128]{1,0:T(8,128)(2,1)}, bf16[976,128]{1,0:T(8,128)(2,1)S(1)}, u32[]{:S(2)}, u32[]{:S(2)}) collective-permute-start(bf16[976,128]{1,0:T(8,128)(2,1)} %get-tuple-element.34), channel_id=1, source_target_pairs={{0,4},{2,6},{4,0},{6,2},{8,12},{10,14},{12,8},{14,10},{1,5},{3,7},... | collective-permute-start | bytes 749576 | tf_op jit(solution)/shard_map/ppermute | solution.py:398
  11.7 1.7 %collective-permute-start.5 = (bf16[976,128]{1,0:T(8,128)(2,1)}, bf16[976,128]{1,0:T(8,128)(2,1)S(1)}, u32[]{:S(2)}, u32[]{:S(2)}) collective-permute-start(bf16[976,128]{1,0:T(8,128)(2,1)} %get-tuple-element.35), channel_id=1, source_target_pairs={{0,2},{2,0},{4,6},{6,4},{8,10},{10,8},{12,14},{14,12},{1,3},{3,1},... | collective-permute-start | bytes 749576 | tf_op jit(solution)/shard_map/ppermute | solution.py:398
  13.3 0.0 collective-permute-done.refs_0_
  13.3 6.3 %collective-permute-start.2 = (bf16[496,128]{1,0:T(8,128)(2,1)}, bf16[496,128]{1,0:T(8,128)(2,1)S(1)}, u32[]{:S(2)}, u32[]{:S(2)}) collective-permute-start(bf16[496,128]{1,0:T(8,128)(2,1)} %get-tuple-element.28), channel_id=1, source_target_pairs={{0,8},{2,10},{4,12},{6,14},{8,0},{10,2},{12,4},{14,6},{1,9},{3,11}... | collective-permute-start | bytes 380936 | tf_op jit(solution)/shard_map/ppermute | solution.py:398
  19.6 0.0 collective-permute-done.1.refs_1_
  19.6 4.5 %collective-permute-start.6 = (bf16[496,128]{1,0:T(8,128)(2,1)}, bf16[496,128]{1,0:T(8,128)(2,1)S(1)}, u32[]{:S(2)}, u32[]{:S(2)}) collective-permute-start(bf16[496,128]{1,0:T(8,128)(2,1)} %get-tuple-element.36), channel_id=1, source_target_pairs={{0,10},{2,8},{4,14},{6,12},{8,2},{10,0},{12,6},{14,4},{1,11},{3,9}... | collective-permute-start | bytes 380936 | tf_op jit(solution)/shard_map/ppermute | solution.py:398
  24.1 6.5 %collective-permute-done.2.refs_2_ = bf16[496,128]{1,0:T(8,128)(2,1)S(1)} collective-permute-done((bf16[496,128]{1,0:T(8,128)(2,1)}, bf16[496,128]{1,0:T(8,128)(2,1)S(1)}, u32[]{:S(2)}, u32[]{:S(2)}) %collective-permute-start.2) | collective-permute-done | bytes 127008 | tf_op jit(solution)/shard_map/ppermute | solution.py:398
  30.7 0.3 shard_map.92
  30.9 1.3 %collective-permute-done.6.refs_7_ = bf16[496,128]{1,0:T(8,128)(2,1)S(1)} collective-permute-done((bf16[496,128]{1,0:T(8,128)(2,1)}, bf16[496,128]{1,0:T(8,128)(2,1)S(1)}, u32[]{:S(2)}, u32[]{:S(2)}) %collective-permute-start.6) | collective-permute-done | bytes 127008 | tf_op jit(solution)/shard_map/ppermute | solution.py:398
  32.3 0.0 collective-permute-done.3.refs_4_
  32.3 0.0 collective-permute-done.4.refs_5_
  32.3 0.0 collective-permute-done.5.refs_6_
  32.3 0.0 copy-done.1
  32.3 2.8 %shard_map.93 = (bf16[2,496,128]{2,1,0:T(8,128)(2,1)S(1)}, bf16[2,496,128]{2,1,0:T(8,128)(2,1)S(1)}, bf16[2,496,128]{2,1,0:T(8,128)(2,1)S(1)}, bf16[2,496,128]{2,1,0:T(8,128)(2,1)S(1)}) custom-call(f32[1,880,128]{2,1,0:T(8,128)S(1)} %get-tuple-element.29.refs_0_, f32[1,880,128]{2,1,0:T(8,128)S(1)} %get-tuple-element.30.refs_1_, ...), custom_call_target="tpu_custom_call" | custom-call | flops 100000 | bytes 10000000 | tf_op jit(solution)/shard_map/pallas_call | solution.py:315
  35.1 0.0 copy-start.4
  35.1 0.1 collective-permute-start.8
  35.2 0.5 %collective-permute-start.7 = (bf16[2,496,128]{2,1,0:T(8,128)(2,1)S(1)}, bf16[2,496,128]{2,1,0:T(8,128)(2,1)S(1)}, u32[]{:S(2)}, u32[]{:S(2)}) collective-permute-start(bf16[2,496,128]{2,1,0:T(8,128)(2,1)S(1)} %get-tuple-element.38), channel_id=1, source_target_pairs={{0,1},{1,0},{2,3},{3,2},{4,5},{5,4},{6,7},{7,6},{8,9},{9,8},{10,11... | collective-permute-start | bytes 761864 | tf_op jit(solution)/shard_map/ppermute | solution.py:422
  35.7 1.0 %collective-permute-done.8.b_ref = bf16[2,496,128]{2,1,0:T(8,128)(2,1)S(1)} collective-permute-done((bf16[2,496,128]{2,1,0:T(8,128)(2,1)S(1)}, bf16[2,496,128]{2,1,0:T(8,128)(2,1)S(1)}, u32[]{:S(2)}, u32[]{:S(2)}) %collective-permute-start.8) | collective-permute-done | bytes 253984 | tf_op jit(solution)/shard_map/ppermute | solution.py:422
  36.7 0.1 shard_map.95
  36.8 1.4 %collective-permute-start.10 = (bf16[496,128]{1,0:T(8,128)(2,1)S(1)}, bf16[496,128]{1,0:T(8,128)(2,1)S(1)}, u32[]{:S(2)}, u32[]{:S(2)}) collective-permute-start(bf16[496,128]{1,0:T(8,128)(2,1)S(1)} %get-tuple-element.43), channel_id=1, source_target_pairs={{0,4},{2,6},{4,0},{6,2},{8,12},{10,14},{12,8},{14,10},{1,5},{3,7},... | collective-permute-start | bytes 380936 | tf_op jit(solution)/shard_map/ppermute | solution.py:398
  38.2 2.1 %collective-permute-start.9 = (bf16[496,128]{1,0:T(8,128)(2,1)S(1)}, bf16[496,128]{1,0:T(8,128)(2,1)S(1)}, u32[]{:S(2)}, u32[]{:S(2)}) collective-permute-start(bf16[496,128]{1,0:T(8,128)(2,1)S(1)} %get-tuple-element.42), channel_id=1, source_target_pairs={{0,2},{2,0},{4,6},{6,4},{8,10},{10,8},{12,14},{14,12},{1,3},{3,1},... | collective-permute-start | bytes 380936 | tf_op jit(solution)/shard_map/ppermute | solution.py:398
  40.3 0.0 collective-permute-done.7.b_ref
  40.3 0.1 shard_map.94
  40.4 0.1 collective-permute-start.11
  40.5 0.0 copy-done
  40.5 0.0 copy-done.4
  40.5 0.0 copy-start.2
  40.5 0.5 fusion.2.gate_ref
  41.0 0.3 copy-done.2
  41.3 0.0 copy-start.3
  41.3 0.7 %copy-done.3 = f32[128]{0:T(128)S(1)} copy-done((f32[128]{0:T(128)S(1)}, f32[128]{0:T(128)}, u32[]{:S(2)}) %copy-start.3) | copy-done | bytes 536
  41.9 0.1 copy.10.gain_ref
  42.0 0.3 collective-permute-done.10.refs_2_
  42.3 4.1 %collective-permute-done.9.refs_1_ = bf16[496,128]{1,0:T(8,128)(2,1)S(1)} collective-permute-done((bf16[496,128]{1,0:T(8,128)(2,1)S(1)}, bf16[496,128]{1,0:T(8,128)(2,1)S(1)}, u32[]{:S(2)}, u32[]{:S(2)}) %collective-permute-start.9) | collective-permute-done | bytes 127008 | tf_op jit(solution)/shard_map/ppermute | solution.py:398
  46.4 0.0 collective-permute-done.11.refs_3_
  46.4 1.4 %shard_map.96 = bf16[1936,128]{1,0:T(8,128)(2,1)} custom-call(f32[128,1]{1,0:T(8,128)S(1)} %copy.10.gain_ref, f32[128,128]{1,0:T(8,128)S(1)} %convert_element_type.3.w_ref, f32[1936,128]{1,0:T(8,128)S(1)} %fusion.2.gate_ref, bf16[496,128]{1,0:T(8,128)(2,1)S(1)} %get-tuple-element.39.refs_0_, bf16[496,128]{1,0:T(8,128)(2,1)S(1)} %collective-permute-done.9.refs_1_, ...), custom_call_target="tpu_custom_call" | custom-call | tf_op jit(solution)/shard_map/pallas_call | solution.py:382
  (1 shorter events, 0.0 us)
Async XLA Ops:
  0.0 40.5 %copy-start = (bf16[128,128]{1,0:T(8,128)(2,1)S(1)}, bf16[128,128]{1,0:T(8,128)(2,1)}, u32[]{:S(2)}) copy-start(bf16[128,128]{1,0:T(8,128)(2,1)} %param.16) | copy-start | bytes 98308
  3.5 28.7 %copy-start.1 = (bf16[976,128]{1,0:T(8,128)(2,1)S(1)}, bf16[976,128]{1,0:T(8,128)(2,1)}, u32[]{:S(2)}) copy-start(bf16[976,128]{1,0:T(8,128)(2,1)} %get-tuple-element.32.refs_3_) | copy-start | bytes 749572
  3.6 9.8 %collective-permute-start = (bf16[496,128]{1,0:T(8,128)(2,1)}, bf16[496,128]{1,0:T(8,128)(2,1)S(1)}, u32[]{:S(2)}, u32[]{:S(2)}) collective-permute-start(bf16[496,128]{1,0:T(8,128)(2,1)} %get-tuple-element.26), channel_id=1, source_target_pairs={{0,12},{2,14},{4,8},{6,10},{8,4},{10,6},{12,0},{14,2},{1,13},{3,15... | collective-permute-start | bytes 380936 | tf_op jit(solution)/shard_map/ppermute | solution.py:398
  8.7 10.9 %collective-permute-start.1 = (bf16[496,128]{1,0:T(8,128)(2,1)}, bf16[496,128]{1,0:T(8,128)(2,1)S(1)}, u32[]{:S(2)}, u32[]{:S(2)}) collective-permute-start(bf16[496,128]{1,0:T(8,128)(2,1)} %get-tuple-element.27), channel_id=1, source_target_pairs={{0,14},{2,12},{4,10},{6,8},{8,6},{10,4},{12,2},{14,0},{1,15},{3,13... | collective-permute-start | bytes 380936 | tf_op jit(solution)/shard_map/ppermute | solution.py:398
  9.8 22.4 %collective-permute-start.3 = (bf16[976,128]{1,0:T(8,128)(2,1)}, bf16[976,128]{1,0:T(8,128)(2,1)S(1)}, u32[]{:S(2)}, u32[]{:S(2)}) collective-permute-start(bf16[976,128]{1,0:T(8,128)(2,1)} %get-tuple-element.33), channel_id=1, source_target_pairs={{0,6},{2,4},{4,2},{6,0},{8,14},{10,12},{12,10},{14,8},{1,7},{3,5},... | collective-permute-start | bytes 749576 | tf_op jit(solution)/shard_map/ppermute | solution.py:398
  9.9 22.4 %collective-permute-start.4 = (bf16[976,128]{1,0:T(8,128)(2,1)}, bf16[976,128]{1,0:T(8,128)(2,1)S(1)}, u32[]{:S(2)}, u32[]{:S(2)}) collective-permute-start(bf16[976,128]{1,0:T(8,128)(2,1)} %get-tuple-element.34), channel_id=1, source_target_pairs={{0,4},{2,6},{4,0},{6,2},{8,12},{10,14},{12,8},{14,10},{1,5},{3,7},... | collective-permute-start | bytes 749576 | tf_op jit(solution)/shard_map/ppermute | solution.py:398
  11.7 20.6 %collective-permute-start.5 = (bf16[976,128]{1,0:T(8,128)(2,1)}, bf16[976,128]{1,0:T(8,128)(2,1)S(1)}, u32[]{:S(2)}, u32[]{:S(2)}) collective-permute-start(bf16[976,128]{1,0:T(8,128)(2,1)} %get-tuple-element.35), channel_id=1, source_target_pairs={{0,2},{2,0},{4,6},{6,4},{8,10},{10,8},{12,14},{14,12},{1,3},{3,1},... | collective-permute-start | bytes 749576 | tf_op jit(solution)/shard_map/ppermute | solution.py:398
  13.3 17.3 %collective-permute-start.2 = (bf16[496,128]{1,0:T(8,128)(2,1)}, bf16[496,128]{1,0:T(8,128)(2,1)S(1)}, u32[]{:S(2)}, u32[]{:S(2)}) collective-permute-start(bf16[496,128]{1,0:T(8,128)(2,1)} %get-tuple-element.28), channel_id=1, source_target_pairs={{0,8},{2,10},{4,12},{6,14},{8,0},{10,2},{12,4},{14,6},{1,9},{3,11}... | collective-permute-start | bytes 380936 | tf_op jit(solution)/shard_map/ppermute | solution.py:398
  19.6 12.7 %collective-permute-start.6 = (bf16[496,128]{1,0:T(8,128)(2,1)}, bf16[496,128]{1,0:T(8,128)(2,1)S(1)}, u32[]{:S(2)}, u32[]{:S(2)}) collective-permute-start(bf16[496,128]{1,0:T(8,128)(2,1)} %get-tuple-element.36), channel_id=1, source_target_pairs={{0,10},{2,8},{4,14},{6,12},{8,2},{10,0},{12,6},{14,4},{1,11},{3,9}... | collective-permute-start | bytes 380936 | tf_op jit(solution)/shard_map/ppermute | solution.py:398
  35.1 5.4 %copy-start.4 = (bf16[128,2048]{1,0:T(8,128)(2,1)S(1)}, bf16[128,2048]{1,0:T(8,128)(2,1)}, u32[]{:S(2)}) copy-start(bf16[128,2048]{1,0:T(8,128)(2,1)} %get-tuple-element.25) | copy-start | bytes 1572868
  35.1 1.6 %collective-permute-start.8 = (bf16[2,496,128]{2,1,0:T(8,128)(2,1)S(1)}, bf16[2,496,128]{2,1,0:T(8,128)(2,1)S(1)}, u32[]{:S(2)}, u32[]{:S(2)}) collective-permute-start(bf16[2,496,128]{2,1,0:T(8,128)(2,1)S(1)} %get-tuple-element.41), channel_id=1, source_target_pairs={{0,1},{1,0},{2,3},{3,2},{4,5},{5,4},{6,7},{7,6},{8,9},{9,8},{10,11... | collective-permute-start | bytes 761864 | tf_op jit(solution)/shard_map/ppermute | solution.py:422
  35.2 5.1 %collective-permute-start.7 = (bf16[2,496,128]{2,1,0:T(8,128)(2,1)S(1)}, bf16[2,496,128]{2,1,0:T(8,128)(2,1)S(1)}, u32[]{:S(2)}, u32[]{:S(2)}) collective-permute-start(bf16[2,496,128]{2,1,0:T(8,128)(2,1)S(1)} %get-tuple-element.38), channel_id=1, source_target_pairs={{0,1},{1,0},{2,3},{3,2},{4,5},{5,4},{6,7},{7,6},{8,9},{9,8},{10,11... | collective-permute-start | bytes 761864 | tf_op jit(solution)/shard_map/ppermute | solution.py:422
  36.8 5.5 %collective-permute-start.10 = (bf16[496,128]{1,0:T(8,128)(2,1)S(1)}, bf16[496,128]{1,0:T(8,128)(2,1)S(1)}, u32[]{:S(2)}, u32[]{:S(2)}) collective-permute-start(bf16[496,128]{1,0:T(8,128)(2,1)S(1)} %get-tuple-element.43), channel_id=1, source_target_pairs={{0,4},{2,6},{4,0},{6,2},{8,12},{10,14},{12,8},{14,10},{1,5},{3,7},... | collective-permute-start | bytes 380936 | tf_op jit(solution)/shard_map/ppermute | solution.py:398
  38.2 8.3 %collective-permute-start.9 = (bf16[496,128]{1,0:T(8,128)(2,1)S(1)}, bf16[496,128]{1,0:T(8,128)(2,1)S(1)}, u32[]{:S(2)}, u32[]{:S(2)}) collective-permute-start(bf16[496,128]{1,0:T(8,128)(2,1)S(1)} %get-tuple-element.42), channel_id=1, source_target_pairs={{0,2},{2,0},{4,6},{6,4},{8,10},{10,8},{12,14},{14,12},{1,3},{3,1},... | collective-permute-start | bytes 380936 | tf_op jit(solution)/shard_map/ppermute | solution.py:398
  40.4 6.1 %collective-permute-start.11 = (bf16[496,128]{1,0:T(8,128)(2,1)S(1)}, bf16[496,128]{1,0:T(8,128)(2,1)S(1)}, u32[]{:S(2)}, u32[]{:S(2)}) collective-permute-start(bf16[496,128]{1,0:T(8,128)(2,1)S(1)} %get-tuple-element.44), channel_id=1, source_target_pairs={{0,6},{2,4},{4,2},{6,0},{8,14},{10,12},{12,10},{14,8},{1,7},{3,5},... | collective-permute-start | bytes 380936 | tf_op jit(solution)/shard_map/ppermute | solution.py:398
  40.5 0.8 %copy-start.2 = (bf16[128,128]{1,0:T(8,128)(2,1)S(1)}, bf16[128,128]{1,0:T(8,128)(2,1)}, u32[]{:S(2)}) copy-start(bf16[128,128]{1,0:T(8,128)(2,1)} %param.17) | copy-start | bytes 98308
  41.3 0.7 %copy-start.3 = (f32[128]{0:T(128)S(1)}, f32[128]{0:T(128)}, u32[]{:S(2)}) copy-start(f32[128]{0:T(128)} %param.13) | copy-start | bytes 1540

commit v16 on v14

--- a/solution.py
+++ b/solution.py
@@ -415,7 +415,7 @@
     half = groups // 2
     early, late = list(range(half, groups)) + [0], list(range(1, half))
     lines = make_lines([far_got[u] for u in early], rows, cols)
-    parts = [list(range(1, half + 1)), [0] + list(range(half + 1, groups))]
+    parts = [list(range(half)), list(range(half, groups))]
     made = make_products(lines, near_got, [far_got[u] for u in late], parts, early, late, rows, cols)
     sums = {}
     for part, pieces in enumerate(parts):

time: 47.2 us -> 48.4 us (1.025)
  waiting for transfers between devices: 13.4 us -> 14.6 us
    ppermute x10, waiting for transfers between devices: 12.4 us -> 13.6 us  [swap(): lax.ppermute(value, 'row', [(r, r ^ shift) for r in range(lax.axis_size('...]
  transfers between devices with their start and end apart: 12 -> 12, of which waited for: 6 -> 7; matrix products, arithmetic and copies ran while one was open for 1% -> 1% of each run, Pallas kernels for 1% -> 1%
where the time goes in v16:
time: 48.4 us; the launch traced here: 48.2 us
  starting transfers between devices  23.9 us (49%)
  waiting for transfers between devices  14.6 us (30%)
  Pallas kernels  8.11 us (17%)
  local copies, waits for them, and re-layouts  1.06 us (2%)
    ppermute x10, starting transfers between devices, swap(): lax.ppermute(value, 'row', [(r, r ^ shift) for r in range(lax.axis_size('...  23.3 us
    ppermute x10, waiting for transfers between devices, swap(): lax.ppermute(value, 'row', [(r, r ^ shift) for r in range(lax.axis_size('...  13.6 us
    pallas_call x1, Pallas kernels, make_edges(): pl.pallas_call(functools.partial(edges_kernel, groups, rows, cols, chunks...  3.53 us
    pallas_call x1, Pallas kernels, make_products(): pl.pallas_call(functools.partial(products_kernel, groups, rows, cols, par...  2.84 us
    pallas_call x1, Pallas kernels, make_update(): pl.pallas_call(functools.partial(update_kernel, groups, rows, cols, chunk...  1.32 us
    ppermute x2, waiting for transfers between devices, shards(): other = lax.ppermute(made[2 + part], 'col', [(0, 1), (1, 0)])  1.02 us
  transfers between devices with their start and end apart: 12, of which 7 were waited for; matrix products, arithmetic and copies ran while one was open for 1% of the time, Pallas kernels for 1%

profile of v16, /device:TPU:0, one launch (start us, length us, event | category | flops | bytes accessed | tf_op | source)
XLA Modules:
  0.0 48.2 jit_solution(246048202126638566)
XLA Ops:
  0.0 0.0 copy-start
  0.0 3.5 %shard_map.91 = (bf16[128,2048]{1,0:T(8,128)(2,1)}, bf16[976,128]{1,0:T(8,128)(2,1)}, bf16[976,128]{1,0:T(8,128)(2,1)}, bf16[976,128]{1,0:T(8,128)(2,1)}, bf16[9...) custom-call(bf16[1936,128]{1,0:T(8,128)(2,1)} %bitcast.5, ...), custom_call_target="tpu_custom_call" | custom-call | tf_op jit(solution)/shard_map/pallas_call | solution.py:137
  3.5 0.0 copy-start.1
  3.6 5.1 %collective-permute-start = (bf16[496,128]{1,0:T(8,128)(2,1)}, bf16[496,128]{1,0:T(8,128)(2,1)S(1)}, u32[]{:S(2)}, u32[]{:S(2)}) collective-permute-start(bf16[496,128]{1,0:T(8,128)(2,1)} %get-tuple-element.26), channel_id=1, source_target_pairs={{0,12},{2,14},{4,8},{6,10},{8,4},{10,6},{12,0},{14,2},{1,13},{3,15... | collective-permute-start | bytes 380936 | tf_op jit(solution)/shard_map/ppermute | solution.py:398
  8.7 1.2 %collective-permute-start.1 = (bf16[496,128]{1,0:T(8,128)(2,1)}, bf16[496,128]{1,0:T(8,128)(2,1)S(1)}, u32[]{:S(2)}, u32[]{:S(2)}) collective-permute-start(bf16[496,128]{1,0:T(8,128)(2,1)} %get-tuple-element.27), channel_id=1, source_target_pairs={{0,14},{2,12},{4,10},{6,8},{8,6},{10,4},{12,2},{14,0},{1,15},{3,13... | collective-permute-start | bytes 380936 | tf_op jit(solution)/shard_map/ppermute | solution.py:398
  9.8 0.4 collective-permute-start.3
  10.2 0.0 collective-permute-start.4
  10.2 3.1 %collective-permute-start.5 = (bf16[976,128]{1,0:T(8,128)(2,1)}, bf16[976,128]{1,0:T(8,128)(2,1)S(1)}, u32[]{:S(2)}, u32[]{:S(2)}) collective-permute-start(bf16[976,128]{1,0:T(8,128)(2,1)} %get-tuple-element.35), channel_id=1, source_target_pairs={{0,6},{2,4},{4,2},{6,0},{8,14},{10,12},{12,10},{14,8},{1,7},{3,5},... | collective-permute-start | bytes 749576 | tf_op jit(solution)/shard_map/ppermute | solution.py:398
  13.3 0.0 collective-permute-done.refs_0_
  13.3 6.3 %collective-permute-start.2 = (bf16[496,128]{1,0:T(8,128)(2,1)}, bf16[496,128]{1,0:T(8,128)(2,1)S(1)}, u32[]{:S(2)}, u32[]{:S(2)}) collective-permute-start(bf16[496,128]{1,0:T(8,128)(2,1)} %get-tuple-element.28), channel_id=1, source_target_pairs={{0,8},{2,10},{4,12},{6,14},{8,0},{10,2},{12,4},{14,6},{1,9},{3,11}... | collective-permute-start | bytes 380936 | tf_op jit(solution)/shard_map/ppermute | solution.py:398
  19.6 0.0 collective-permute-done.1.refs_1_
  19.6 3.6 %collective-permute-start.6 = (bf16[496,128]{1,0:T(8,128)(2,1)}, bf16[496,128]{1,0:T(8,128)(2,1)S(1)}, u32[]{:S(2)}, u32[]{:S(2)}) collective-permute-start(bf16[496,128]{1,0:T(8,128)(2,1)} %get-tuple-element.36), channel_id=1, source_target_pairs={{0,10},{2,8},{4,14},{6,12},{8,2},{10,0},{12,6},{14,4},{1,11},{3,9}... | collective-permute-start | bytes 380936 | tf_op jit(solution)/shard_map/ppermute | solution.py:398
  23.2 5.7 %collective-permute-done.2.refs_2_ = bf16[496,128]{1,0:T(8,128)(2,1)S(1)} collective-permute-done((bf16[496,128]{1,0:T(8,128)(2,1)}, bf16[496,128]{1,0:T(8,128)(2,1)S(1)}, u32[]{:S(2)}, u32[]{:S(2)}) %collective-permute-start.2) | collective-permute-done | bytes 127008 | tf_op jit(solution)/shard_map/ppermute | solution.py:398
  29.0 0.3 shard_map.92
  29.2 1.3 %collective-permute-done.6.refs_7_ = bf16[496,128]{1,0:T(8,128)(2,1)S(1)} collective-permute-done((bf16[496,128]{1,0:T(8,128)(2,1)}, bf16[496,128]{1,0:T(8,128)(2,1)S(1)}, u32[]{:S(2)}, u32[]{:S(2)}) %collective-permute-start.6) | collective-permute-done | bytes 127008 | tf_op jit(solution)/shard_map/ppermute | solution.py:398
  30.6 0.0 collective-permute-done.3.refs_4_
  30.6 0.0 collective-permute-done.4.refs_5_
  30.6 1.6 %collective-permute-done.5.refs_6_ = bf16[976,128]{1,0:T(8,128)(2,1)S(1)} collective-permute-done((bf16[976,128]{1,0:T(8,128)(2,1)}, bf16[976,128]{1,0:T(8,128)(2,1)S(1)}, u32[]{:S(2)}, u32[]{:S(2)}) %collective-permute-start.5) | collective-permute-done | bytes 249888 | tf_op jit(solution)/shard_map/ppermute | solution.py:398
  32.2 0.0 copy-done.1
  32.2 2.8 %shard_map.93 = (bf16[2,496,128]{2,1,0:T(8,128)(2,1)S(1)}, bf16[2,496,128]{2,1,0:T(8,128)(2,1)S(1)}, bf16[2,496,128]{2,1,0:T(8,128)(2,1)S(1)}, bf16[2,496,128]{2,1,0:T(8,128)(2,1)S(1)}) custom-call(f32[1,880,128]{2,1,0:T(8,128)S(1)} %get-tuple-element.29.refs_0_, f32[1,880,128]{2,1,0:T(8,128)S(1)} %get-tuple-element.30.refs_1_, ...), custom_call_target="tpu_custom_call" | custom-call | flops 100000 | bytes 10000000 | tf_op jit(solution)/shard_map/pallas_call | solution.py:315
  35.1 0.0 copy-start.4
  35.1 0.1 collective-permute-start.9
  35.2 0.5 %collective-permute-start.7 = (bf16[2,496,128]{2,1,0:T(8,128)(2,1)S(1)}, bf16[2,496,128]{2,1,0:T(8,128)(2,1)S(1)}, u32[]{:S(2)}, u32[]{:S(2)}) collective-permute-start(bf16[2,496,128]{2,1,0:T(8,128)(2,1)S(1)} %get-tuple-element.38), channel_id=1, source_target_pairs={{0,1},{1,0},{2,3},{3,2},{4,5},{5,4},{6,7},{7,6},{8,9},{9,8},{10,11... | collective-permute-start | bytes 761864 | tf_op jit(solution)/shard_map/ppermute | solution.py:422
  35.7 1.0 %collective-permute-done.9.b_ref = bf16[2,496,128]{2,1,0:T(8,128)(2,1)S(1)} collective-permute-done((bf16[2,496,128]{2,1,0:T(8,128)(2,1)S(1)}, bf16[2,496,128]{2,1,0:T(8,128)(2,1)S(1)}, u32[]{:S(2)}, u32[]{:S(2)}) %collective-permute-start.9) | collective-permute-done | bytes 253984 | tf_op jit(solution)/shard_map/ppermute | solution.py:422
  36.7 0.1 shard_map.95
  36.7 1.0 %collective-permute-start.10 = (bf16[496,128]{1,0:T(8,128)(2,1)S(1)}, bf16[496,128]{1,0:T(8,128)(2,1)S(1)}, u32[]{:S(2)}, u32[]{:S(2)}) collective-permute-start(bf16[496,128]{1,0:T(8,128)(2,1)S(1)} %get-tuple-element.43), channel_id=1, source_target_pairs={{0,4},{2,6},{4,0},{6,2},{8,12},{10,14},{12,8},{14,10},{1,5},{3,7},... | collective-permute-start | bytes 380936 | tf_op jit(solution)/shard_map/ppermute | solution.py:398
  37.8 1.1 %collective-permute-start.11 = (bf16[496,128]{1,0:T(8,128)(2,1)S(1)}, bf16[496,128]{1,0:T(8,128)(2,1)S(1)}, u32[]{:S(2)}, u32[]{:S(2)}) collective-permute-start(bf16[496,128]{1,0:T(8,128)(2,1)S(1)} %get-tuple-element.44), channel_id=1, source_target_pairs={{0,6},{2,4},{4,2},{6,0},{8,14},{10,12},{12,10},{14,8},{1,7},{3,5},... | collective-permute-start | bytes 380936 | tf_op jit(solution)/shard_map/ppermute | solution.py:398
  38.9 0.0 collective-permute-done.7.b_ref
  38.9 0.1 shard_map.94
  38.9 1.5 %collective-permute-start.8 = (bf16[496,128]{1,0:T(8,128)(2,1)S(1)}, bf16[496,128]{1,0:T(8,128)(2,1)S(1)}, u32[]{:S(2)}, u32[]{:S(2)}) collective-permute-start(bf16[496,128]{1,0:T(8,128)(2,1)S(1)} %get-tuple-element.40), channel_id=1, source_target_pairs={{0,2},{2,0},{4,6},{6,4},{8,10},{10,8},{12,14},{14,12},{1,3},{3,1},... | collective-permute-start | bytes 380936 | tf_op jit(solution)/shard_map/ppermute | solution.py:398
  40.4 0.0 copy-done
  40.4 0.0 copy-done.4
  40.4 0.0 copy-start.2
  40.4 0.5 fusion.2.gate_ref
  40.9 0.3 copy-done.2
  41.2 0.0 copy-start.3
  41.2 0.7 %copy-done.3 = f32[128]{0:T(128)S(1)} copy-done((f32[128]{0:T(128)S(1)}, f32[128]{0:T(128)}, u32[]{:S(2)}) %copy-start.3) | copy-done | bytes 536
  41.9 0.1 copy.10.gain_ref
  42.0 1.1 %collective-permute-done.10.refs_2_ = bf16[496,128]{1,0:T(8,128)(2,1)S(1)} collective-permute-done((bf16[496,128]{1,0:T(8,128)(2,1)S(1)}, bf16[496,128]{1,0:T(8,128)(2,1)S(1)}, u32[]{:S(2)}, u32[]{:S(2)}) %collective-permute-start.10) | collective-permute-done | bytes 127008 | tf_op jit(solution)/shard_map/ppermute | solution.py:398
  43.1 2.3 %collective-permute-done.11.refs_3_ = bf16[496,128]{1,0:T(8,128)(2,1)S(1)} collective-permute-done((bf16[496,128]{1,0:T(8,128)(2,1)S(1)}, bf16[496,128]{1,0:T(8,128)(2,1)S(1)}, u32[]{:S(2)}, u32[]{:S(2)}) %collective-permute-start.11) | collective-permute-done | bytes 127008 | tf_op jit(solution)/shard_map/ppermute | solution.py:398
  45.3 1.6 %collective-permute-done.8.refs_1_ = bf16[496,128]{1,0:T(8,128)(2,1)S(1)} collective-permute-done((bf16[496,128]{1,0:T(8,128)(2,1)S(1)}, bf16[496,128]{1,0:T(8,128)(2,1)S(1)}, u32[]{:S(2)}, u32[]{:S(2)}) %collective-permute-start.8) | collective-permute-done | bytes 127008 | tf_op jit(solution)/shard_map/ppermute | solution.py:398
  46.9 1.3 %shard_map.96 = bf16[1936,128]{1,0:T(8,128)(2,1)} custom-call(f32[128,1]{1,0:T(8,128)S(1)} %copy.10.gain_ref, f32[128,128]{1,0:T(8,128)S(1)} %convert_element_type.3.w_ref, f32[1936,128]{1,0:T(8,128)S(1)} %fusion.2.gate_ref, bf16[496,128]{1,0:T(8,128)(2,1)S(1)} %get-tuple-element.39.refs_0_, bf16[496,128]{1,0:T(8,128)(2,1)S(1)} %collective-permute-done.8.refs_1_, ...), custom_call_target="tpu_custom_call" | custom-call | tf_op jit(solution)/shard_map/pallas_call | solution.py:382
  (1 shorter events, 0.0 us)
Async XLA Ops:
  0.0 40.4 %copy-start = (bf16[128,128]{1,0:T(8,128)(2,1)S(1)}, bf16[128,128]{1,0:T(8,128)(2,1)}, u32[]{:S(2)}) copy-start(bf16[128,128]{1,0:T(8,128)(2,1)} %param.16) | copy-start | bytes 98308
  3.5 28.7 %copy-start.1 = (bf16[976,128]{1,0:T(8,128)(2,1)S(1)}, bf16[976,128]{1,0:T(8,128)(2,1)}, u32[]{:S(2)}) copy-start(bf16[976,128]{1,0:T(8,128)(2,1)} %get-tuple-element.32.refs_3_) | copy-start | bytes 749572
  3.6 9.8 %collective-permute-start = (bf16[496,128]{1,0:T(8,128)(2,1)}, bf16[496,128]{1,0:T(8,128)(2,1)S(1)}, u32[]{:S(2)}, u32[]{:S(2)}) collective-permute-start(bf16[496,128]{1,0:T(8,128)(2,1)} %get-tuple-element.26), channel_id=1, source_target_pairs={{0,12},{2,14},{4,8},{6,10},{8,4},{10,6},{12,0},{14,2},{1,13},{3,15... | collective-permute-start | bytes 380936 | tf_op jit(solution)/shard_map/ppermute | solution.py:398
  8.7 10.9 %collective-permute-start.1 = (bf16[496,128]{1,0:T(8,128)(2,1)}, bf16[496,128]{1,0:T(8,128)(2,1)S(1)}, u32[]{:S(2)}, u32[]{:S(2)}) collective-permute-start(bf16[496,128]{1,0:T(8,128)(2,1)} %get-tuple-element.27), channel_id=1, source_target_pairs={{0,14},{2,12},{4,10},{6,8},{8,6},{10,4},{12,2},{14,0},{1,15},{3,13... | collective-permute-start | bytes 380936 | tf_op jit(solution)/shard_map/ppermute | solution.py:398
  9.8 20.7 %collective-permute-start.3 = (bf16[976,128]{1,0:T(8,128)(2,1)}, bf16[976,128]{1,0:T(8,128)(2,1)S(1)}, u32[]{:S(2)}, u32[]{:S(2)}) collective-permute-start(bf16[976,128]{1,0:T(8,128)(2,1)} %get-tuple-element.33), channel_id=1, source_target_pairs={{0,2},{2,0},{4,6},{6,4},{8,10},{10,8},{12,14},{14,12},{1,3},{3,1},... | collective-permute-start | bytes 749576 | tf_op jit(solution)/shard_map/ppermute | solution.py:398
  10.2 20.4 %collective-permute-start.4 = (bf16[976,128]{1,0:T(8,128)(2,1)}, bf16[976,128]{1,0:T(8,128)(2,1)S(1)}, u32[]{:S(2)}, u32[]{:S(2)}) collective-permute-start(bf16[976,128]{1,0:T(8,128)(2,1)} %get-tuple-element.34), channel_id=1, source_target_pairs={{0,4},{2,6},{4,0},{6,2},{8,12},{10,14},{12,8},{14,10},{1,5},{3,7},... | collective-permute-start | bytes 749576 | tf_op jit(solution)/shard_map/ppermute | solution.py:398
  10.2 22.0 %collective-permute-start.5 = (bf16[976,128]{1,0:T(8,128)(2,1)}, bf16[976,128]{1,0:T(8,128)(2,1)S(1)}, u32[]{:S(2)}, u32[]{:S(2)}) collective-permute-start(bf16[976,128]{1,0:T(8,128)(2,1)} %get-tuple-element.35), channel_id=1, source_target_pairs={{0,6},{2,4},{4,2},{6,0},{8,14},{10,12},{12,10},{14,8},{1,7},{3,5},... | collective-permute-start | bytes 749576 | tf_op jit(solution)/shard_map/ppermute | solution.py:398
  13.3 15.6 %collective-permute-start.2 = (bf16[496,128]{1,0:T(8,128)(2,1)}, bf16[496,128]{1,0:T(8,128)(2,1)S(1)}, u32[]{:S(2)}, u32[]{:S(2)}) collective-permute-start(bf16[496,128]{1,0:T(8,128)(2,1)} %get-tuple-element.28), channel_id=1, source_target_pairs={{0,8},{2,10},{4,12},{6,14},{8,0},{10,2},{12,4},{14,6},{1,9},{3,11}... | collective-permute-start | bytes 380936 | tf_op jit(solution)/shard_map/ppermute | solution.py:398
  19.6 11.0 %collective-permute-start.6 = (bf16[496,128]{1,0:T(8,128)(2,1)}, bf16[496,128]{1,0:T(8,128)(2,1)S(1)}, u32[]{:S(2)}, u32[]{:S(2)}) collective-permute-start(bf16[496,128]{1,0:T(8,128)(2,1)} %get-tuple-element.36), channel_id=1, source_target_pairs={{0,10},{2,8},{4,14},{6,12},{8,2},{10,0},{12,6},{14,4},{1,11},{3,9}... | collective-permute-start | bytes 380936 | tf_op jit(solution)/shard_map/ppermute | solution.py:398
  35.1 5.4 %copy-start.4 = (bf16[128,2048]{1,0:T(8,128)(2,1)S(1)}, bf16[128,2048]{1,0:T(8,128)(2,1)}, u32[]{:S(2)}) copy-start(bf16[128,2048]{1,0:T(8,128)(2,1)} %get-tuple-element.25) | copy-start | bytes 1572868
  35.1 1.6 %collective-permute-start.9 = (bf16[2,496,128]{2,1,0:T(8,128)(2,1)S(1)}, bf16[2,496,128]{2,1,0:T(8,128)(2,1)S(1)}, u32[]{:S(2)}, u32[]{:S(2)}) collective-permute-start(bf16[2,496,128]{2,1,0:T(8,128)(2,1)S(1)} %get-tuple-element.42), channel_id=1, source_target_pairs={{0,1},{1,0},{2,3},{3,2},{4,5},{5,4},{6,7},{7,6},{8,9},{9,8},{10,11... | collective-permute-start | bytes 761864 | tf_op jit(solution)/shard_map/ppermute | solution.py:422
  35.2 3.7 %collective-permute-start.7 = (bf16[2,496,128]{2,1,0:T(8,128)(2,1)S(1)}, bf16[2,496,128]{2,1,0:T(8,128)(2,1)S(1)}, u32[]{:S(2)}, u32[]{:S(2)}) collective-permute-start(bf16[2,496,128]{2,1,0:T(8,128)(2,1)S(1)} %get-tuple-element.38), channel_id=1, source_target_pairs={{0,1},{1,0},{2,3},{3,2},{4,5},{5,4},{6,7},{7,6},{8,9},{9,8},{10,11... | collective-permute-start | bytes 761864 | tf_op jit(solution)/shard_map/ppermute | solution.py:422
  36.7 6.3 %collective-permute-start.10 = (bf16[496,128]{1,0:T(8,128)(2,1)S(1)}, bf16[496,128]{1,0:T(8,128)(2,1)S(1)}, u32[]{:S(2)}, u32[]{:S(2)}) collective-permute-start(bf16[496,128]{1,0:T(8,128)(2,1)S(1)} %get-tuple-element.43), channel_id=1, source_target_pairs={{0,4},{2,6},{4,0},{6,2},{8,12},{10,14},{12,8},{14,10},{1,5},{3,7},... | collective-permute-start | bytes 380936 | tf_op jit(solution)/shard_map/ppermute | solution.py:398
  37.8 7.5 %collective-permute-start.11 = (bf16[496,128]{1,0:T(8,128)(2,1)S(1)}, bf16[496,128]{1,0:T(8,128)(2,1)S(1)}, u32[]{:S(2)}, u32[]{:S(2)}) collective-permute-start(bf16[496,128]{1,0:T(8,128)(2,1)S(1)} %get-tuple-element.44), channel_id=1, source_target_pairs={{0,6},{2,4},{4,2},{6,0},{8,14},{10,12},{12,10},{14,8},{1,7},{3,5},... | collective-permute-start | bytes 380936 | tf_op jit(solution)/shard_map/ppermute | solution.py:398
  38.9 8.0 %collective-permute-start.8 = (bf16[496,128]{1,0:T(8,128)(2,1)S(1)}, bf16[496,128]{1,0:T(8,128)(2,1)S(1)}, u32[]{:S(2)}, u32[]{:S(2)}) collective-permute-start(bf16[496,128]{1,0:T(8,128)(2,1)S(1)} %get-tuple-element.40), channel_id=1, source_target_pairs={{0,2},{2,0},{4,6},{6,4},{8,10},{10,8},{12,14},{14,12},{1,3},{3,1},... | collective-permute-start | bytes 380936 | tf_op jit(solution)/shard_map/ppermute | solution.py:398
  40.4 0.8 %copy-start.2 = (bf16[128,128]{1,0:T(8,128)(2,1)S(1)}, bf16[128,128]{1,0:T(8,128)(2,1)}, u32[]{:S(2)}) copy-start(bf16[128,128]{1,0:T(8,128)(2,1)} %param.17) | copy-start | bytes 98308
  41.2 0.7 %copy-start.3 = (f32[128]{0:T(128)S(1)}, f32[128]{0:T(128)}, u32[]{:S(2)}) copy-start(f32[128]{0:T(128)} %param.13) | copy-start | bytes 1540
